TPU v7x, 128 devices: a whole 4x4x4 slice. The times are simulated.
128 devices in a mesh: pts: 16 (over x, z), cent: 8 (over y, core).
Axes of the slice: x: 4, y: 4, z: 4, core: 2. Of those that a mesh axis runs over, the one named last changes fastest.
Arguments:
- points: bfloat16 [262144, 1024], P(('pts', 'cent')), may hold values from -40 to 40, as said below
- centroids: bfloat16 [65536, 1024], P('cent'), may hold values from -3 to 3, as said below
- prev_loads: bfloat16 [65536], P('cent'), may hold values from 0.25 to 4
- candidates: int32 [256, 4], P(('pts', 'cent')), may hold values from 0 to 511, as said below
- panel_home: int32 [512], replicated, may hold values from 0 to 511, as said below
Outputs:
- new_centroids: bfloat16 [65536, 1024], P(('cent', 'pts'))
- new_loads: float32 [65536], P(('cent', 'pts'))
Inputs may be any that keep to these rules, and one draw needn't show every extreme that they name: `candidates`: within a row the 4 panels sit in slots of 4 different owners (slot // 64); the 2 rows of one device name the same owner in each column, so one device asks each of 4 owners for 2 panels, not always distinct, and the others for none. Low slots of an owner are asked for more often. `panel_home`: A permutation of the panel ids. `points`: Real-valued embeddings. Real-valued centroids.
All inputs are finite; a program needn't handle non-finite values.
Results may differ from a plain program's by a relative error of at most 0.0095.
Values may be sent and summed in bfloat16 or wider, within the bound.
No kernel may reach another device: no remote copies, remote signals or barrier semaphores. Data moves between devices by JAX's collectives and lax.ppermute only.
A program may use at most 320 MiB of HBM per device.

v0:
```python
import jax
import jax.numpy as jnp
from jax import lax
from jax.sharding import PartitionSpec as P

PANEL = 128
GROUP = 1024


sharpness_divisor = 16.0
evenness_coefficient = 1.0
prior_mass = 1.0


def score_group(members, centers, evenness_surcharge):
    inner_pairwise_matrix = lax.dot_general(
        members, centers, (((1,), (1,)), ((), ())), preferred_element_type=jnp.float32
    )
    length_quadratics = jnp.sum(jnp.square(centers.astype(jnp.float32)), axis=1)
    cluster_affinity_scores = (
        2.0 * inner_pairwise_matrix - length_quadratics[None, :]
    ) / sharpness_divisor - evenness_coefficient * evenness_surcharge[None, :]
    highest = jnp.max(cluster_affinity_scores, axis=1, keepdims=True)
    raised = jnp.exp(cluster_affinity_scores - highest)
    shares = (raised / jnp.sum(raised, axis=1, keepdims=True)).astype(jnp.bfloat16)
    partial_sums = lax.dot_general(
        shares, members, (((0,), (0,)), ((), ())), preferred_element_type=jnp.float32
    ).astype(jnp.bfloat16)
    membership_weights = jnp.sum(shares.astype(jnp.float32), axis=0).astype(jnp.bfloat16)
    return (partial_sums, membership_weights)


def local(points, centroids, prev_loads, candidates, panel_home):
    groups_here = candidates.shape[0]
    chosen = candidates.shape[1]
    owners = lax.axis_size("cent")
    width = points.shape[1]
    pan_here = centroids.shape[0] // PANEL
    requests = groups_here * chosen
    slot_ids = jnp.take(panel_home, candidates.reshape(-1), axis=0)
    owner_ids = slot_ids // pan_here
    local_ids = slot_ids % pan_here
    order = jnp.arange(requests, dtype=jnp.int32)
    before = (order[None, :] < order[:, None]) & (owner_ids[None, :] == owner_ids[:, None])
    position = jnp.sum(before.astype(jnp.int32), axis=1)
    target = owner_ids * groups_here + position
    places = jnp.arange(owners * groups_here, dtype=jnp.int32)
    wanted = jnp.sum(jnp.where(target[:, None] == places[None, :], local_ids[:, None], 0), axis=0)
    wanted = wanted.reshape(owners, groups_here)
    asked = lax.all_to_all(wanted, "cent", split_axis=0, concat_axis=0, tiled=True)
    shelf = centroids.reshape(pan_here, PANEL, width)
    load_shelf = prev_loads.reshape(pan_here, PANEL)
    flat_asked = asked.reshape(-1)
    sending = jnp.take(shelf, flat_asked, axis=0).reshape(owners, groups_here, PANEL, width)
    sending_loads = jnp.take(load_shelf, flat_asked, axis=0).reshape(owners, groups_here, PANEL)
    arrived, arrived_loads = (
        lax.all_to_all(sending, "cent", split_axis=0, concat_axis=0, tiled=True),
        lax.all_to_all(sending_loads, "cent", split_axis=0, concat_axis=0, tiled=True),
    )
    fetched = jnp.take(arrived.reshape(owners * groups_here, PANEL, width), target, axis=0)
    fetched_loads = jnp.take(arrived_loads.reshape(owners * groups_here, PANEL), target, axis=0)
    members = points.reshape(groups_here, GROUP, width)
    centers = fetched.reshape(groups_here, chosen * PANEL, width)
    evenness_surcharge = jnp.log(
        fetched_loads.reshape(groups_here, chosen * PANEL).astype(jnp.float32)
    )
    partial_sums, membership_weights = lax.map(
        lambda sample_matrix: score_group(sample_matrix[0], sample_matrix[1], sample_matrix[2]),
        (members, centers, evenness_surcharge),
    )
    outgoing = (
        jnp.zeros((owners * groups_here, PANEL, width), jnp.bfloat16)
        .at[target]
        .set(partial_sums.reshape(requests, PANEL, width))
    )
    outgoing_weights = (
        jnp.zeros((owners * groups_here, PANEL), jnp.bfloat16)
        .at[target]
        .set(membership_weights.reshape(requests, PANEL))
    )
    returned, returned_weights = (
        lax.all_to_all(
            outgoing.reshape(owners, groups_here, PANEL, width),
            "cent",
            split_axis=0,
            concat_axis=0,
            tiled=True,
        ),
        lax.all_to_all(
            outgoing_weights.reshape(owners, groups_here, PANEL),
            "cent",
            split_axis=0,
            concat_axis=0,
            tiled=True,
        ),
    )
    owner_asked = asked.reshape(-1)
    sum_acc = (
        jnp.zeros((pan_here, PANEL, width), jnp.float32)
        .at[owner_asked]
        .add(returned.reshape(owners * groups_here, PANEL, width).astype(jnp.float32))
    )
    weight_acc = (
        jnp.zeros((pan_here, PANEL), jnp.float32)
        .at[owner_asked]
        .add(returned_weights.reshape(owners * groups_here, PANEL).astype(jnp.float32))
    )
    total, weight_rows = (
        lax.psum_scatter(
            sum_acc.reshape(pan_here * PANEL, width), "pts", scatter_dimension=0, tiled=True
        ),
        lax.psum_scatter(
            weight_acc.reshape(pan_here * PANEL), "pts", scatter_dimension=0, tiled=True
        ),
    )
    row_count = total.shape[0]
    old_rows = lax.dynamic_slice_in_dim(
        centroids, lax.axis_index("pts") * row_count, row_count, 0
    ).astype(jnp.float32)
    new_centroids = ((total + prior_mass * old_rows) / (weight_rows[:, None] + prior_mass)).astype(
        jnp.bfloat16
    )
    return (new_centroids, weight_rows)


def solution(mesh):
    placed = (P(("pts", "cent"), None), P("cent", None), P("cent"), P(("pts", "cent"), None), P())
    return jax.shard_map(
        local,
        mesh=mesh,
        in_specs=placed,
        out_specs=(P(("cent", "pts"), None), P(("cent", "pts"))),
        check_vma=False,
    )
```

profile of v0, /device:TPU:24, one launch (start us, length us, event | category | flops | bytes accessed | tf_op | source)
XLA Modules:
  0.0 417.4 jit_solution(9318035895987598615)
XLA Ops:
  10.4 7.7 %all_to_all.29 = s32[8,1,2]{2,1,0:T(1,128)S(1)} all-to-all(s32[8,1,2]{2,1,0:T(1,128)S(1)} %bitcast.98), channel_id=1, replica_groups=mesh['pts'=16,'cent'=8] {'cent'}, dimensions={0} | all-to-all | bytes 128 | tf_op jit(solution)/shard_map/all_to_all | solution.py:50
  19.6 8.5 %gather_fusion.1 = bf16[16,128,1024]{2,1,0:T(8,128)(2,1)} fusion(bf16[64,128,1024]{2,1,0:T(8,128)(2,1)} %bitcast.92, s32[1024]{0:T(1024)S(1)} %pad_clamp_fusion.1), kind=kCustom, calls=%fused_computation.1 | custom fusion | bytes 8388672 | tf_op jit(solution)/shard_map/jit(_take)/gather | solution.py:54
  29.3 5.3 %all-to-all-start.2 = ((bf16[8,2,128]{2,1,0:T(2,128)(2,1)}), bf16[8,2,128]{2,1,0:T(2,128)(2,1)S(1)}, u32[]{:S(2)}, u32[]{:S(2)}) async-start(bf16[8,2,128]{2,1,0:T(2,128)(2,1)} %broadcast_select_fusion.1), calls=%async_computation.2 | async-start | bytes 8192 | tf_op jit(solution)/shard_map/all_to_all | solution.py:58
  34.7 4.6 %broadcast_select_fusion = bf16[8,2,128,1024]{3,2,1,0:T(8,128)(2,1)} fusion(bf16[8,2,128,1024]{3,2,1,0:T(8,128)(2,1)} %bitcast.89, pred[8,2]{1,0:T(8,128)(4,1)S(1)} %copy.19), kind=kLoop, calls=%fused_computation.29 | loop fusion | flops 2097152 | bytes 8388624 | tf_op jit(solution)/shard_map/jit(_take)/select_n | solution.py:54
  39.3 5.0 %all-to-all-start.1 = ((bf16[8,2,128,1024]{3,2,1,0:T(8,128)(2,1)}), bf16[8,2,128,1024]{3,2,1,0:T(8,128)(2,1)}, u32[]{:S(2)}, u32[]{:S(2)}) async-start(bf16[8,2,128,1024]{3,2,1,0:T(8,128)(2,1)} %broadcast_select_fusion), calls=%async_computation.1 | async-start | bytes 8388608 | tf_op jit(solution)/shard_map/all_to_all | solution.py:57
  45.2 46.8 %all-to-all-done.1 = bf16[8,2,128,1024]{3,2,1,0:T(8,128)(2,1)} async-done(((bf16[8,2,128,1024]{3,2,1,0:T(8,128)(2,1)}), bf16[8,2,128,1024]{3,2,1,0:T(8,128)(2,1)}, u32[]{:S(2)}, u32[]{:S(2)}) %all-to-all-start.1) | async-done | bytes 4194336 | tf_op jit(solution)/shard_map/all_to_all | solution.py:57
  92.0 4.2 %gather_fusion.2 = bf16[8,128,1024]{2,1,0:T(8,128)(2,1)} fusion(bf16[16,128,1024]{2,1,0:T(8,128)(2,1)} %bitcast.14, s32[1024]{0:T(1024)S(1)} %pad_clamp_fusion), kind=kCustom, calls=%fused_computation.2 | custom fusion | bytes 4194336 | tf_op jit(solution)/shard_map/jit(_take)/gather | solution.py:60
  96.2 1.9 bitcast_select_fusion
  98.0 16.2 %while.14 = (s32[]{:T(128)}, bf16[2,512,1024]{2,1,0:T(8,128)(2,1)}, bf16[2,512]{1,0:T(2,128)(2,1)S(1)}, bf16[2,1024,1024]{2,1,0:T(8,128)(2,1)}, bf16[2,512,1024]...) while((s32[]{:T(128)}, bf16[2,512,1024]{2,1,0:T(8,128)(2,1)}, ...), condition=%wide.region_7.8_spmd, body=%wide.region_2.7_spmd.sunk | while | flops 2155344896 | bytes 49321140 | solution.py:67
  98.4 3.1 fusion.42
  104.7 1.4 copy-done.3
  106.5 3.1 fusion.42
  112.9 1.4 copy-done.3
  114.3 2.5 broadcast_in_dim.107
  116.7 5.0 %scatter_fusion = bf16[16,128,1024]{2,1,0:T(8,128)(2,1)} fusion(bf16[16,128,1024]{2,1,0:T(8,128)(2,1)} %broadcast_in_dim.107, s32[8]{0:T(128)S(1)} %fusion.29, bf16[8,128,1024]{2,1,0:T(8,128)(2,1)S(1)} %bitcast.91), kind=kCustom, calls=%fused_computation.5 | custom fusion | bytes 6291488 | tf_op jit(solution)/shard_map/scatter | solution.py:74
  121.8 53.9 %all_to_all.30 = bf16[8,2,128,1024]{3,2,1,0:T(8,128)(2,1)S(1)} all-to-all(bf16[8,2,128,1024]{3,2,1,0:T(8,128)(2,1)} %bitcast.88), channel_id=1, replica_groups=mesh['pts'=16,'cent'=8] {'cent'}, dimensions={0} | all-to-all | bytes 8388608 | tf_op jit(solution)/shard_map/all_to_all | solution.py:82
  175.7 4.5 %bitcast_convert_fusion = f32[16,128,1024]{2,1,0:T(8,128)} fusion(bf16[8,2,128,1024]{3,2,1,0:T(8,128)(2,1)S(1)} %all_to_all.30), kind=kLoop, calls=%fused_computation.28 | loop fusion | flops 2097152 | bytes 12582912 | tf_op jit(solution)/shard_map/convert_element_type | solution.py:101
  180.2 11.2 %broadcast_in_dim.104 = f32[64,128,1024]{2,1,0:T(8,128)} broadcast(f32[]{:T(128)} %constant.149.clone.1), dimensions={} | broadcast | bytes 33554436 | tf_op jit(solution)/shard_map/broadcast_in_dim | solution.py:99
  191.4 18.0 %scatter_fusion.1 = f32[64,128,1024]{2,1,0:T(8,128)} fusion(f32[64,128,1024]{2,1,0:T(8,128)} %broadcast_in_dim.104, s32[16]{0:T(128)S(1)} %fusion.28, f32[16,128,1024]{2,1,0:T(8,128)} %bitcast_convert_fusion), kind=kCustom, calls=%fused_computation.6 | custom fusion | flops 2097152 | bytes 25165888 | tf_op jit(solution)/shard_map/scatter-add | solution.py:101
  210.6 4.5 %all-to-all-start.4 = ((bf16[8,2,128]{2,1,0:T(2,128)(2,1)}), bf16[8,2,128]{2,1,0:T(2,128)(2,1)S(1)}, u32[]{:S(2)}, u32[]{:S(2)}) async-start(bf16[8,2,128]{2,1,0:T(2,128)(2,1)} %bitcast.23), calls=%async_computation.5 | async-start | bytes 8192 | tf_op jit(solution)/shard_map/all_to_all | solution.py:89
  216.4 1.9 all-to-all-done.4
  218.9 79.0 %all-reduce = f32[8192]{0:T(1024)S(1)} all-reduce(f32[8192]{0:T(1024)S(1)} %bitcast.93), channel_id=3, replica_groups=mesh['pts'=16,'cent'=8] {'pts'}, use_global_device_ids=true, to_apply=%region_13.14.clone | all-reduce | flops 8192 | bytes 65536
  298.6 108.7 %reduce-scatter.2.cloned.1.call-done = f32[512,1024]{1,0:T(8,128)} async-done(((f32[8192,1024]{1,0:T(8,128)}), f32[512,1024]{1,0:T(8,128)}) %reduce-scatter.2.cloned.1.call-update) | async-done | bytes 2097168 | tf_op jit(solution)/shard_map/reduce_scatter | solution.py:109
  407.3 3.2 divide_convert_fusion.1
  (74 shorter events, 17.0 us)
Async XLA Ops:
  7.2 20.9 %copy-start = (bf16[8192]{0:T(1024)(128)(2,1)S(1)}, bf16[8192]{0:T(1024)(128)(2,1)}, u32[]{:S(2)}) copy-start(bf16[8192]{0:T(1024)(128)(2,1)} %param.9) | copy-start | bytes 49156
  29.3 9.9 %all-to-all-start.2 = ((bf16[8,2,128]{2,1,0:T(2,128)(2,1)}), bf16[8,2,128]{2,1,0:T(2,128)(2,1)S(1)}, u32[]{:S(2)}, u32[]{:S(2)}) async-start(bf16[8,2,128]{2,1,0:T(2,128)(2,1)} %broadcast_select_fusion.1), calls=%async_computation.2 | async-start | bytes 8192 | tf_op jit(solution)/shard_map/all_to_all | solution.py:58
  39.3 5.2 %copy-start.5 = (s32[2,4]{1,0:T(2,128)S(1)}, s32[2,4]{1,0:T(2,128)}, u32[]{:S(2)}) copy-start(s32[2,4]{1,0:T(2,128)} %param.10) | copy-start | bytes 100
  39.3 52.7 %all-to-all-start.1 = ((bf16[8,2,128,1024]{3,2,1,0:T(8,128)(2,1)}), bf16[8,2,128,1024]{3,2,1,0:T(8,128)(2,1)}, u32[]{:S(2)}, u32[]{:S(2)}) async-start(bf16[8,2,128,1024]{3,2,1,0:T(8,128)(2,1)} %broadcast_select_fusion), calls=%async_computation.1 | async-start | bytes 8388608 | tf_op jit(solution)/shard_map/all_to_all | solution.py:57
  44.3 363.0 %reduce-scatter.2.cloned.1.call-start = ((), (), s32[]{:S(2)}) async-start(), calls=%async_computation.6 | async-start | bytes 35651584 | tf_op jit(solution)/shard_map/reduce_scatter | solution.py:109
  98.3 4.0 copy-start.6
  101.8 1.6 copy-start.2
  104.7 1.4 copy-start.3
  106.5 4.0 copy-start.6
  110.0 1.6 copy-start.2
  112.8 1.4 copy-start.3
  114.3 2.5 copy-start.4
  209.4 5.7 %copy-start.7 = (u32[128]{0:T(128)S(1)}, u32[128]{0:T(128)}, u32[]{:S(2)}) copy-start(u32[128]{0:T(128)} %constant.171) | copy-start | bytes 1540
  210.6 7.6 %all-to-all-start.4 = ((bf16[8,2,128]{2,1,0:T(2,128)(2,1)}), bf16[8,2,128]{2,1,0:T(2,128)(2,1)S(1)}, u32[]{:S(2)}, u32[]{:S(2)}) async-start(bf16[8,2,128]{2,1,0:T(2,128)(2,1)} %bitcast.23), calls=%async_computation.5 | async-start | bytes 8192 | tf_op jit(solution)/shard_map/all_to_all | solution.py:89
  407.3 3.2 copy-start.1
Sparse Core Ops, SparseCore 0:
  209.6 197.6 reduce-scatter.1
where the time goes:
time: 419 us; the launch traced here: 417 us
  waiting for transfers between devices  157 us (37%)
  blocking collectives  141 us (34%)
  local copies, waits for them, and re-layouts  43.4 us (10%)
  other arithmetic  37.4 us (9%)
  starting transfers between devices  14.8 us (4%)
  between operations  14.8 us (4%)
  matrix products  8.84 us (2%)
    reduce_scatter x1, waiting for transfers between devices, local(): lax.psum_scatter(sum_acc.reshape(pan_here * PANEL, width), 'pts', scatter...  109 us
    unnamed x1, blocking collectives  79 us
    all_to_all x1, blocking collectives, local(): lax.all_to_all(outgoing.reshape(owners, groups_here, PANEL, width), 'cent...  53.9 us
    all_to_all x1, waiting for transfers between devices, local(): lax.all_to_all(sending, 'cent', split_axis=0, concat_axis=0, tiled=True)  46.8 us
    scatter-add x1, other arithmetic, local(): sum_acc = jnp.zeros((pan_here, PANEL, width), jnp.float32).at[owner_asked...  18 us
    broadcast_in_dim x1, local copies, waits for them, and re-layouts, local(): jnp.zeros((pan_here, PANEL, width), jnp.float32).at[owner_asked]  11.2 us
    gather x1, local copies, waits for them, and re-layouts, local(): jnp.take(shelf, flat_asked, axis=0)  8.51 us
  transfers between devices with their start and end apart: 4, of which 3 were waited for; matrix products, arithmetic and copies ran while one was open for 2% of the time, Pallas kernels for 0%

commit v1 on v0

v1 whole, which is shorter than its diff:
```python
import functools

import jax
import jax.numpy as jnp
from jax import lax
from jax.experimental import pallas as pl
from jax.experimental.pallas import tpu as pltpu
from jax.sharding import PartitionSpec as P

PANEL = 128
GROUP = 1024
CAND = 4
GROUPS_DEV = 2
REQ = CAND * GROUPS_DEV
PAN_DEV = 64
WIDTH = 1024
N_CENT = 8
CHIPS = 4
N_PTS = 16
ROWS = 16
HALF = 512
LANE = 128
TILES = HALF // LANE
SEND_TILES = REQ * TILES + 1
DENSE = PAN_DEV * TILES
CHUNK_TILES = DENSE + 1
LAST_TILES = CAND * TILES + 1

sharpness_divisor = 16.0
evenness_coefficient = 1.0
prior_mass = 1.0

BF16 = jnp.bfloat16
F32 = jnp.float32
MIB = 1 << 20


def params(mib):
    return pltpu.CompilerParams(vmem_limit_bytes=mib * MIB)


def pick_kernel(ids, table, out, sems):
    for n in range(ids.shape[0]):
        pltpu.make_async_copy(table.at[ids[n]], out.at[n], sems.at[n]).start()
    for n in range(ids.shape[0]):
        pltpu.make_async_copy(table.at[ids[n]], out.at[n], sems.at[n]).wait()


def pick_panels(ids, table):
    count = ids.shape[0]
    return pl.pallas_call(
        pick_kernel,
        out_shape=jax.ShapeDtypeStruct((count, PANEL, WIDTH), BF16),
        in_specs=[pl.BlockSpec(memory_space=pltpu.SMEM), pl.BlockSpec(memory_space=pl.ANY)],
        out_specs=pl.BlockSpec(memory_space=pl.ANY),
        scratch_shapes=[pltpu.SemaphoreType.DMA((count,))],
        cost_estimate=pl.CostEstimate(flops=0, bytes_accessed=4 * count * PANEL * WIDTH, transcendentals=0),
    )(ids, table)


def score_kernel(target, points, c0, c1, c2, c3, surcharge, tags, out, centers, shares, marks):
    del target
    group = pl.program_id(0)
    for j, panel in enumerate((c0, c1, c2, c3)):
        centers[j * PANEL : (j + 1) * PANEL, :] = panel[0]
    wide = centers[...].astype(F32)
    squares = jnp.sum(wide * wide, axis=1, keepdims=True)
    bias = squares * (1.0 / sharpness_divisor) + evenness_coefficient * surcharge[0]
    step = 256
    weights = jnp.zeros((CAND * PANEL, LANE), F32)
    for s in range(GROUP // step):
        block = points[s * step : (s + 1) * step, :]
        inner = lax.dot_general(centers[...], block, (((1,), (1,)), ((), ())), preferred_element_type=F32)
        logits = inner * (2.0 / sharpness_divisor) - bias
        highest = jnp.max(logits, axis=0, keepdims=True)
        raised = jnp.exp(logits - highest)
        scale = 1.0 / jnp.sum(raised, axis=0, keepdims=True)
        share = (raised * scale).astype(BF16)
        shares[:, s * step : (s + 1) * step] = share
        rounded = share.astype(F32)
        for part in range(step // LANE):
            weights = weights + rounded[:, part * LANE : (part + 1) * LANE]
    weight = jnp.sum(weights, axis=1, keepdims=True)
    coarse = weight.astype(BF16).astype(F32)
    fine = weight - coarse
    lane = lax.broadcasted_iota(jnp.int32, (PANEL, LANE), 1)

    @pl.when(group == 0)
    def _():
        marks[...] = jnp.broadcast_to(tags[0:1, :], (PANEL, LANE))

    tile = marks[...]
    for j in range(CAND):
        place = group * CAND + j
        rows = slice(j * PANEL, (j + 1) * PANEL)
        tile = jnp.where(lane == place, coarse[rows], tile)
        tile = jnp.where(lane == REQ + place, fine[rows], tile)
    marks[...] = tile

    wide_step = 256
    for s in range(WIDTH // wide_step):
        part = lax.dot_general(
            shares[...], points[:, s * wide_step : (s + 1) * wide_step], (((1,), (0,)), ((), ())),
            preferred_element_type=F32,
        ).astype(BF16)
        for t in range(wide_step // LANE):
            column = s * (wide_step // LANE) + t
            half, tile_at = divmod(column, TILES)
            for j in range(CAND):
                for block_at in range(PANEL // ROWS):
                    row = j * PANEL + block_at * ROWS
                    out[block_at * 2 + half, (group * CAND + j) * TILES + tile_at] = part[
                        row : row + ROWS, t * LANE : (t + 1) * LANE
                    ]

    @pl.when(group == GROUPS_DEV - 1)
    def _():
        last = marks[...].astype(BF16)
        for block_at in range(PANEL // ROWS):
            for half in range(2):
                out[block_at * 2 + half, REQ * TILES] = last[block_at * ROWS : (block_at + 1) * ROWS]


def score(target, points, arrived, surcharge, tags):
    def panel(j):
        return pl.BlockSpec((1, PANEL, WIDTH), lambda g, t: (t[g * CAND + j], 0, 0))

    return pl.pallas_call(
        score_kernel,
        grid_spec=pltpu.PrefetchScalarGridSpec(
            num_scalar_prefetch=1,
            grid=(GROUPS_DEV,),
            in_specs=[
                pl.BlockSpec((GROUP, WIDTH), lambda g, t: (g, 0)),
                panel(0), panel(1), panel(2), panel(3),
                pl.BlockSpec((1, CAND * PANEL, 1), lambda g, t: (g, 0, 0)),
                pl.BlockSpec((ROWS, LANE), lambda g, t: (0, 0)),
            ],
            out_specs=pl.BlockSpec((N_PTS, SEND_TILES, ROWS, LANE), lambda g, t: (0, 0, 0, 0)),
            scratch_shapes=[
                pltpu.VMEM((CAND * PANEL, WIDTH), BF16),
                pltpu.VMEM((CAND * PANEL, GROUP), BF16),
                pltpu.VMEM((PANEL, LANE), F32),
            ],
        ),
        out_shape=jax.ShapeDtypeStruct((N_PTS, SEND_TILES, ROWS, LANE), BF16),
        compiler_params=params(48),
        cost_estimate=pl.CostEstimate(flops=4294967296, bytes_accessed=10 * MIB, transcendentals=1 << 20),
    )(target, points, arrived, arrived, arrived, arrived, surcharge, tags)


def spread_kernel(places, mine, mate, lanes, own, own_weights, out1, out2, out3, total):
    total[...] = jnp.zeros_like(total)
    count = N_PTS * REQ
    for first, source in ((0, mine), (count, mate)):
        def add(s, carry, first=first, source=source):
            for i in range(REQ):
                at = places[first + s * REQ + i] * TILES
                total[pl.ds(at, TILES)] += source[s, i * TILES : (i + 1) * TILES].astype(F32)
            return carry

        lax.fori_loop(0, N_PTS, add, 0)
    panel = lax.broadcasted_iota(jnp.int32, (CHIPS * PAN_DEV, LANE), 0)
    weights = jnp.zeros((ROWS, CHIPS * PAN_DEV), F32)
    for n in range(2 * N_PTS):
        source = mine if n < N_PTS else mate
        chosen = jnp.where(panel == lanes[n : n + 1, :], 1.0, 0.0).astype(BF16)
        weights = weights + lax.dot_general(
            source[n % N_PTS, REQ * TILES], chosen, (((1,), (1,)), ((), ())), preferred_element_type=F32
        )
    own[...] = total[0:DENSE]
    coarse = weights.astype(BF16)
    fine = (weights - coarse.astype(F32)).astype(BF16)
    own_weights[...] = weights[:, 0:LANE]
    for d, out in ((1, out1), (2, out2), (3, out3)):
        out[0:DENSE] = total[d * DENSE : (d + 1) * DENSE].astype(BF16)
        out[DENSE, :, 0:PAN_DEV] = coarse[:, d * PAN_DEV : (d + 1) * PAN_DEV]
        out[DENSE, :, PAN_DEV:LANE] = fine[:, d * PAN_DEV : (d + 1) * PAN_DEV]


def spread(places, mine, mate, lanes):
    vmem = pl.BlockSpec(memory_space=pltpu.VMEM)
    chunk = jax.ShapeDtypeStruct((CHUNK_TILES, ROWS, LANE), BF16)
    return pl.pallas_call(
        spread_kernel,
        in_specs=[pl.BlockSpec(memory_space=pltpu.SMEM), vmem, vmem, vmem],
        out_specs=[vmem] * 5,
        out_shape=[
            jax.ShapeDtypeStruct((DENSE, ROWS, LANE), F32),
            jax.ShapeDtypeStruct((ROWS, LANE), F32),
            chunk, chunk, chunk,
        ],
        scratch_shapes=[pltpu.VMEM((CHIPS * DENSE + TILES, ROWS, LANE), F32)],
        compiler_params=params(48),
        cost_estimate=pl.CostEstimate(flops=1 << 22, bytes_accessed=10 * MIB, transcendentals=0),
    )(places, mine, mate, lanes)


def finish_kernel(me, own, own_weights, in1, in2, in3, old, out):
    del me
    weights = own_weights[:, 0:PAN_DEV]
    for arrived in (in1, in2, in3):
        pair = arrived[DENSE].astype(F32)
        weights = weights + (pair[:, 0:PAN_DEV] + pair[:, PAN_DEV:LANE])
    inverse = 1.0 / (weights + prior_mass)
    for q in range(PAN_DEV):
        scale = jnp.broadcast_to(inverse[:, q : q + 1], (ROWS, LANE))
        for t in range(TILES):
            at = q * TILES + t
            total = own[at] + in1[at].astype(F32) + in2[at].astype(F32) + in3[at].astype(F32)
            previous = old[q, :, t * LANE : (t + 1) * LANE].astype(F32)
            fresh = (total + prior_mass * previous) * scale
            out[q // CAND, (q % CAND) * TILES + t] = fresh.astype(BF16)
    coarse = weights.astype(BF16)
    fine = (weights - coarse.astype(F32)).astype(BF16)
    for p in range(N_PTS):
        out[p, CAND * TILES, :, 0:PAN_DEV] = coarse
        out[p, CAND * TILES, :, PAN_DEV:LANE] = fine


def finish(me, own, own_weights, arrived, table):
    whole = lambda shape: pl.BlockSpec(shape, lambda g, me: (0,) * len(shape))
    chunk = whole((CHUNK_TILES, ROWS, LANE))
    return pl.pallas_call(
        finish_kernel,
        grid_spec=pltpu.PrefetchScalarGridSpec(
            num_scalar_prefetch=1,
            grid=(1,),
            in_specs=[
                whole((DENSE, ROWS, LANE)), whole((ROWS, LANE)), chunk, chunk, chunk,
                pl.BlockSpec((PAN_DEV, ROWS, HALF), lambda g, me: (0, me[0] // 2, me[0] % 2)),
            ],
            out_specs=whole((N_PTS, LAST_TILES, ROWS, LANE)),
        ),
        out_shape=jax.ShapeDtypeStruct((N_PTS, LAST_TILES, ROWS, LANE), BF16),
        compiler_params=params(48),
        cost_estimate=pl.CostEstimate(flops=1 << 22, bytes_accessed=8 * MIB, transcendentals=0),
    )(me, own, own_weights, *arrived, table)


def place_kernel(me, pieces, out, loads):
    for block_at in range(PANEL // ROWS):
        for half in range(2):
            for q in range(CAND):
                for t in range(TILES):
                    column = half * HALF + t * LANE
                    out[q, block_at * ROWS : (block_at + 1) * ROWS, column : column + LANE] = pieces[
                        block_at * 2 + half, q * TILES + t
                    ]
    lane = lax.broadcasted_iota(jnp.int32, (ROWS, LANE), 1)
    row = lax.broadcasted_iota(jnp.int32, (ROWS, LANE), 0)
    wanted = me[0] * CAND + row
    chosen = jnp.where((row < CAND) & (lane % PAN_DEV == wanted), 1.0, 0.0).astype(BF16)
    for block_at in range(PANEL // ROWS):
        pair = pieces[block_at * 2, CAND * TILES]
        part = lax.dot_general(chosen, pair, (((1,), (1,)), ((), ())), preferred_element_type=F32)
        loads[:, block_at * ROWS : (block_at + 1) * ROWS] = part[0:8]


def place(me, pieces):
    vmem = pl.BlockSpec(memory_space=pltpu.VMEM)
    return pl.pallas_call(
        place_kernel,
        in_specs=[pl.BlockSpec(memory_space=pltpu.SMEM), vmem],
        out_specs=[vmem, vmem],
        out_shape=[
            jax.ShapeDtypeStruct((CAND, PANEL, WIDTH), BF16),
            jax.ShapeDtypeStruct((8, PANEL), F32),
        ],
        compiler_params=params(32),
        cost_estimate=pl.CostEstimate(flops=1 << 20, bytes_accessed=2 * MIB, transcendentals=0),
    )(me, pieces)


def shift(dy, dk):
    return [(y * 2 + k, ((y + dy) % CHIPS) * 2 + (k + dk) % 2) for y in range(CHIPS) for k in range(2)]


def exchange(x, axis):
    return lax.all_to_all(x, axis, split_axis=0, concat_axis=0, tiled=True)


def local(points, centroids, prev_loads, candidates, panel_home):
    me = lax.axis_index("pts")
    here = lax.axis_index("cent")
    chip, core = here // 2, here % 2
    shelf = centroids.reshape(PAN_DEV, PANEL, WIDTH)

    with jax.named_scope("requests"):
        wanted_ids = candidates.reshape(REQ)
        slots = jnp.sum(
            jnp.where(wanted_ids[:, None] == jnp.arange(panel_home.shape[0], dtype=jnp.int32), panel_home[None, :], 0),
            axis=1,
        )
        owners, local_ids = slots // PAN_DEV, slots % PAN_DEV
        target = owners * GROUPS_DEV + jnp.arange(REQ, dtype=jnp.int32) // CAND
        spots = jnp.arange(N_CENT * GROUPS_DEV, dtype=jnp.int32)
        wanted = jnp.sum(jnp.where(target[None, :] == spots[:, None], local_ids[None, :], 0), axis=1)
        ask = jnp.zeros((N_CENT, 1, ROWS, LANE), BF16)
        ask = ask.at[:, 0, 0, 0:GROUPS_DEV].set(wanted.reshape(N_CENT, GROUPS_DEV).astype(BF16))
        table = jnp.broadcast_to(
            prev_loads.reshape(1, PAN_DEV // ROWS, ROWS, LANE), (N_CENT, PAN_DEV // ROWS, ROWS, LANE)
        )
        answered = exchange(jnp.concatenate([table, ask], axis=1), "cent")
        asked = answered[:, PAN_DEV // ROWS, 0, 0:GROUPS_DEV].astype(jnp.int32).reshape(-1)

    with jax.named_scope("gather_panels"):
        arrived = exchange(pick_panels(asked, shelf).reshape(N_CENT, GROUPS_DEV, PANEL, WIDTH), "cent")
        arrived = arrived.reshape(N_CENT * GROUPS_DEV, PANEL, WIDTH)

    with jax.named_scope("loads"):
        load_table = answered[:, : PAN_DEV // ROWS].reshape(N_CENT * PAN_DEV, PANEL)
        loads = jnp.take(load_table, slots, axis=0, mode="clip").astype(F32)
        surcharge = jnp.log(loads).reshape(GROUPS_DEV, CAND * PANEL, 1)
        marks = jnp.concatenate([jnp.zeros((2 * REQ,), F32), (slots // 16).astype(F32), (slots % 16).astype(F32)])
        tags = jnp.broadcast_to(jnp.pad(marks, (0, LANE - 4 * REQ)), (ROWS, LANE))

    with jax.named_scope("score"):
        pieces = score(target, points, arrived, surcharge, tags)

    with jax.named_scope("split_pieces"):
        mine = exchange(pieces, "pts")
        mate = lax.ppermute(mine, "cent", shift(0, 1))

    with jax.named_scope("spread"):
        heads = jnp.stack([mine[:, REQ * TILES, 0, 2 * REQ : 4 * REQ], mate[:, REQ * TILES, 0, 2 * REQ : 4 * REQ]])
        heads = heads.reshape(2 * N_PTS, 2, REQ).astype(jnp.int32)
        homes = heads[:, 0] * 16 + heads[:, 1]
        owner = homes // PAN_DEV
        relative = (owner // 2 - chip) % CHIPS
        places = jnp.where(owner % 2 == core, relative * PAN_DEV + homes % PAN_DEV, CHIPS * PAN_DEV)
        lanes = jnp.pad(
            jnp.concatenate([places, places], axis=1), ((0, 0), (0, LANE - 2 * REQ)), constant_values=CHIPS * PAN_DEV
        )
        own, own_weights, far1, far2, far3 = spread(places.reshape(-1), mine, mate, lanes)

    with jax.named_scope("sum_over_chips"):
        back = [lax.ppermute(far, "cent", shift(d, 0)) for d, far in ((2, far2), (1, far1), (3, far3))]

    with jax.named_scope("finish"):
        where = me.reshape(1)
        fresh = finish(where, own, own_weights, back, shelf)
        new_centroids, new_loads = place(where, exchange(fresh, "pts"))
    return new_centroids.reshape(CAND * PANEL, WIDTH), new_loads[0:CAND].reshape(CAND * PANEL)


def solution(mesh):
    placed = (P(("pts", "cent"), None), P("cent", None), P("cent"), P(("pts", "cent"), None), P())
    return jax.shard_map(
        local,
        mesh=mesh,
        in_specs=placed,
        out_specs=(P(("cent", "pts"), None), P(("cent", "pts"))),
        check_vma=False,
    )
```

time: 419 us -> 333 us (0.79)
  Pallas kernels: 0 us -> 148 us
  blocking collectives: 141 us -> 66.8 us
  waiting for transfers between devices: 157 us -> 96.5 us
  local copies, waits for them, and re-layouts: 43.4 us -> 6.35 us
  other arithmetic: 37.4 us -> 1.27 us
  between operations: 14.8 us -> 0.73 us
  matrix products: 8.84 us -> 0 us
    pallas_call x0 -> x5, Pallas kernels: none -> 148 us  [the longest x1 129 us: pick_panels(): pl.pallas_call(pick_kernel, out_shape=jax.ShapeDtypeStruct((count, PANEL,...]
    reduce_scatter x1 -> x0, waiting for transfers between devices: 109 us -> none  [local(): lax.psum_scatter(sum_acc.reshape(pan_here * PANEL, width), 'pts', scatter...]
    unnamed x1 -> x0, blocking collectives: 79 us -> none
    ppermute x0 -> x4, waiting for transfers between devices: none -> 49.8 us  [the longest x3 45.5 us: local(): lax.ppermute(far, 'cent', shift(d, 0))]
    scatter-add x2 -> x0, other arithmetic: 18.6 us -> none  [the longest x1 18 us: local(): sum_acc = jnp.zeros((pan_here, PANEL, width), jnp.float32).at[owner_asked...]
    gather x7 -> x1, local copies, waits for them, and re-layouts: 15.3 us -> 0.57 us  [local(): loads = jnp.take(load_table, slots, axis=0, mode='clip').astype(F32)]
    broadcast_in_dim x4 -> x2, local copies, waits for them, and re-layouts: 13.7 us -> 0.74 us  [the longest x1 0.74 us: local(): jnp.broadcast_to(prev_loads.reshape(1, PAN_DEV // ROWS, ROWS, LANE), (N_C...]
    dot_general x4 -> x0, matrix products: 8.84 us -> none  [the longest x2 6.28 us: score_group(): lax.dot_general(members, centers, (((1,), (1,)), ((), ())), preferred_ele...]
  transfers between devices with their start and end apart: 4 -> 5, of which waited for: 3 -> 5; matrix products, arithmetic and copies ran while one was open for 2% -> 0% of each run, Pallas kernels for 0% -> 0%
where the time goes in v1:
time: 333 us; the launch traced here: 331 us
  Pallas kernels  148 us (44%)
  waiting for transfers between devices  96.5 us (29%)
  blocking collectives  66.8 us (20%)
  starting transfers between devices  10.7 us (3%)
  local copies, waits for them, and re-layouts  6.35 us (2%)
    pallas_call x1, Pallas kernels, pick_panels(): pl.pallas_call(pick_kernel, out_shape=jax.ShapeDtypeStruct((count, PANEL,...  129 us
    all_to_all x3, blocking collectives, exchange(): return lax.all_to_all(x, axis, split_axis=0, concat_axis=0, tiled=True)  66.8 us
    all_to_all x1, waiting for transfers between devices, exchange(): return lax.all_to_all(x, axis, split_axis=0, concat_axis=0, tiled=True)  46.7 us
    ppermute x3, waiting for transfers between devices, local(): lax.ppermute(far, 'cent', shift(d, 0))  45.5 us
    pallas_call x1, Pallas kernels, score(): pl.pallas_call(score_kernel, grid_spec=pltpu.PrefetchScalarGridSpec(num_s...  8.93 us
  transfers between devices with their start and end apart: 5, of which 5 were waited for; matrix products, arithmetic and copies ran while one was open for 0% of the time, Pallas kernels for 0%

profile of v1, /device:TPU:24, one launch (start us, length us, event | category | flops | bytes accessed | tf_op | source)
XLA Modules:
  0.0 330.7 jit_solution(3532713285755844744)
XLA Ops:
  0.6 0.8 eq.48
  1.4 0.9 select_reduce_fusion
  2.5 0.7 broadcast_in_dim.53
  3.2 8.9 %all_to_all.20 = bf16[8,5,16,128]{3,2,1,0:T(8,128)(2,1)S(1)} all-to-all(bf16[8,5,16,128]{3,2,1,0:T(8,128)(2,1)S(1)} %fusion.1), channel_id=1, replica_groups=mesh['pts'=16,'cent'=8] {'cent'}, dimensions={0} | all-to-all | bytes 327680 | tf_op jit(solution)/shard_map/requests/all_to_all | solution.py:280
  12.2 0.6 reshape.163.ids
  12.7 129.0 %gather_panels.1 = bf16[16,128,1024]{2,1,0:T(8,128)(2,1)} custom-call(s32[16]{0:T(128)} %reshape.163.ids, bf16[64,128,1024]{2,1,0:T(8,128)(2,1)} %bitcast.37), custom_call_target="tpu_custom_call" | custom-call | bytes 8388608 | tf_op jit(solution)/shard_map/gather_panels/pallas_call | solution.py:51
  141.7 6.5 %all-to-all-start.1 = ((bf16[8,2,128,1024]{3,2,1,0:T(8,128)(2,1)}), bf16[8,2,128,1024]{3,2,1,0:T(8,128)(2,1)}, u32[]{:S(2)}, u32[]{:S(2)}) async-start(bf16[8,2,128,1024]{3,2,1,0:T(8,128)(2,1)} %bitcast.39), calls=%async_computation.1 | async-start | bytes 8388608 | tf_op jit(solution)/shard_map/gather_panels/all_to_all | solution.py:280
  149.3 46.7 %all-to-all-done.1 = bf16[8,2,128,1024]{3,2,1,0:T(8,128)(2,1)} async-done(((bf16[8,2,128,1024]{3,2,1,0:T(8,128)(2,1)}), bf16[8,2,128,1024]{3,2,1,0:T(8,128)(2,1)}, u32[]{:S(2)}, u32[]{:S(2)}) %all-to-all-start.1) | async-done | bytes 4194336 | tf_op jit(solution)/shard_map/gather_panels/all_to_all | solution.py:280
  195.9 8.9 %score.1 = bf16[16,33,16,128]{3,2,1,0:T(8,128)(2,1)S(1)} custom-call(s32[8]{0:T(128)S(1)} %get-tuple-element.35.target, bf16[2048,1024]{1,0:T(8,128)(2,1)} %points.1, bf16[16,128,1024]{2,1,0:T(8,128)(2,1)} %bitcast.4.c0.c1.c2.c3, bf16[16,128,1024]{2,1,0:T(8,128)(2,1)} %bitcast.4.c0.c1.c2.c3, bf16[16,128,1024]{2,1,0:T(8,128)(2,1)} %bitcast.4.c0.c1.c2.c3, ...), custom_call_target="tpu_custom_call" | custom-call | flops 4294967296 | bytes 10485760 | tf_op jit(solution)/shard_map/score/pallas_call | solution.py:128
  204.9 36.6 %all_to_all.21.mine = bf16[16,33,16,128]{3,2,1,0:T(8,128)(2,1)S(1)} all-to-all(bf16[16,33,16,128]{3,2,1,0:T(8,128)(2,1)S(1)} %score.1), channel_id=1, replica_groups=mesh['pts'=16,'cent'=8] {'pts'}, dimensions={0} | all-to-all | bytes 4325376 | tf_op jit(solution)/shard_map/split_pieces/all_to_all | solution.py:280
  241.5 4.3 %collective-permute-done.mate = bf16[16,33,16,128]{3,2,1,0:T(8,128)(2,1)} collective-permute-done((bf16[16,33,16,128]{3,2,1,0:T(8,128)(2,1)S(1)}, bf16[16,33,16,128]{3,2,1,0:T(8,128)(2,1)}, u32[]{:S(2)}, u32[]{:S(2)}) %collective-permute-start) | collective-permute-done | bytes 2162720 | tf_op jit(solution)/shard_map/split_pieces/ppermute | solution.py:323
  245.8 0.8 slice.61
  247.3 6.5 %spread.1 = (f32[256,16,128]{2,1,0:T(8,128)S(1)}, f32[16,128]{1,0:T(8,128)S(1)}, bf16[257,16,128]{2,1,0:T(8,128)(2,1)}, bf16[257,16,128]{2,1,0:T(8,128)(2,1)}, bf16[257,16,128]{2,1,0:T(8,128)(2,1)}) custom-call(s32[256]{0:T(256)S(1)} %compare_select_fusion.2.places, bf16[16,33,16,128]{3,2,1,0:T(8,128)(2,1)} %copy-done.1, ...), custom_call_target="tpu_custom_call" | custom-call | flops 4194304 | bytes 10485760 | tf_op jit(solution)/shard_map/spread/pallas_call | solution.py:184
  253.8 1.3 copy-done
  255.2 2.1 collective-permute-start.1
  257.3 0.8 collective-permute-start.2
  258.1 1.2 collective-permute-start.3
  259.3 23.7 %collective-permute-done.1.in1 = bf16[257,16,128]{2,1,0:T(8,128)(2,1)S(1)} collective-permute-done((bf16[257,16,128]{2,1,0:T(8,128)(2,1)}, bf16[257,16,128]{2,1,0:T(8,128)(2,1)S(1)}, u32[]{:S(2)}, u32[]{:S(2)}) %collective-permute-start.1) | collective-permute-done | bytes 1052704 | tf_op jit(solution)/shard_map/sum_over_chips/ppermute | solution.py:338
  283.0 21.2 %collective-permute-done.2.in2 = bf16[257,16,128]{2,1,0:T(8,128)(2,1)S(1)} collective-permute-done((bf16[257,16,128]{2,1,0:T(8,128)(2,1)}, bf16[257,16,128]{2,1,0:T(8,128)(2,1)S(1)}, u32[]{:S(2)}, u32[]{:S(2)}) %collective-permute-start.2) | collective-permute-done | bytes 1052704 | tf_op jit(solution)/shard_map/sum_over_chips/ppermute | solution.py:338
  304.2 0.6 collective-permute-done.3.in3
  304.8 2.8 finish.2
  307.5 21.4 %all_to_all.22.pieces = bf16[16,17,16,128]{3,2,1,0:T(8,128)(2,1)S(1)} all-to-all(bf16[16,17,16,128]{3,2,1,0:T(8,128)(2,1)S(1)} %finish.2), channel_id=1, replica_groups=mesh['pts'=16,'cent'=8] {'pts'}, dimensions={0} | all-to-all | bytes 2228224 | tf_op jit(solution)/shard_map/finish/all_to_all | solution.py:280
  328.9 1.2 finish.3
  330.1 0.6 slice_bitcast_fusion
  (32 shorter events, 1.9 us)
Async XLA Ops:
  141.7 54.2 %all-to-all-start.1 = ((bf16[8,2,128,1024]{3,2,1,0:T(8,128)(2,1)}), bf16[8,2,128,1024]{3,2,1,0:T(8,128)(2,1)}, u32[]{:S(2)}, u32[]{:S(2)}) async-start(bf16[8,2,128,1024]{3,2,1,0:T(8,128)(2,1)} %bitcast.39), calls=%async_computation.1 | async-start | bytes 8388608 | tf_op jit(solution)/shard_map/gather_panels/all_to_all | solution.py:280
  241.4 5.8 %copy-start.1 = (bf16[16,33,16,128]{3,2,1,0:T(8,128)(2,1)}, bf16[16,33,16,128]{3,2,1,0:T(8,128)(2,1)S(1)}, u32[]{:S(2)}) copy-start(bf16[16,33,16,128]{3,2,1,0:T(8,128)(2,1)S(1)} %all_to_all.21.mine) | copy-start | bytes 6488068
  241.4 4.4 %collective-permute-start = (bf16[16,33,16,128]{3,2,1,0:T(8,128)(2,1)S(1)}, bf16[16,33,16,128]{3,2,1,0:T(8,128)(2,1)}, u32[]{:S(2)}, u32[]{:S(2)}) collective-permute-start(bf16[16,33,16,128]{3,2,1,0:T(8,128)(2,1)S(1)} %all_to_all.21.mine), channel_id=1, source_target_pairs={{0,1},{1,0},{2,3},{3,2},{4,5},{5,4},{6,7},{7,6},{8,9},{9,8},{10,11... | collective-permute-start | bytes 6488072 | tf_op jit(solution)/shard_map/split_pieces/ppermute | solution.py:323
  253.8 1.3 copy-start
  255.2 27.8 %collective-permute-start.1 = (bf16[257,16,128]{2,1,0:T(8,128)(2,1)}, bf16[257,16,128]{2,1,0:T(8,128)(2,1)S(1)}, u32[]{:S(2)}, u32[]{:S(2)}) collective-permute-start(bf16[257,16,128]{2,1,0:T(8,128)(2,1)} %get-tuple-element.23), channel_id=1, source_target_pairs={{0,4},{1,5},{2,6},{3,7},{4,0},{5,1},{6,2},{7,3},{8,12},{9,13},{10,... | collective-permute-start | bytes 3158024 | tf_op jit(solution)/shard_map/sum_over_chips/ppermute | solution.py:338
  257.3 46.9 %collective-permute-start.2 = (bf16[257,16,128]{2,1,0:T(8,128)(2,1)}, bf16[257,16,128]{2,1,0:T(8,128)(2,1)S(1)}, u32[]{:S(2)}, u32[]{:S(2)}) collective-permute-start(bf16[257,16,128]{2,1,0:T(8,128)(2,1)} %get-tuple-element.24), channel_id=1, source_target_pairs={{0,2},{1,3},{2,4},{3,5},{4,6},{5,7},{6,0},{7,1},{8,10},{9,11},{10,... | collective-permute-start | bytes 3158024 | tf_op jit(solution)/shard_map/sum_over_chips/ppermute | solution.py:338
  258.1 46.7 %collective-permute-start.3 = (bf16[257,16,128]{2,1,0:T(8,128)(2,1)}, bf16[257,16,128]{2,1,0:T(8,128)(2,1)S(1)}, u32[]{:S(2)}, u32[]{:S(2)}) collective-permute-start(bf16[257,16,128]{2,1,0:T(8,128)(2,1)} %get-tuple-element.25), channel_id=1, source_target_pairs={{0,6},{1,7},{2,0},{3,1},{4,2},{5,3},{6,4},{7,5},{8,14},{9,15},{10,... | collective-permute-start | bytes 3158024 | tf_op jit(solution)/shard_map/sum_over_chips/ppermute | solution.py:338

commit v2 on v1

--- a/solution.py
+++ b/solution.py
@@ -52,8 +52,9 @@
         pick_kernel,
         out_shape=jax.ShapeDtypeStruct((count, PANEL, WIDTH), BF16),
         in_specs=[pl.BlockSpec(memory_space=pltpu.SMEM), pl.BlockSpec(memory_space=pl.ANY)],
-        out_specs=pl.BlockSpec(memory_space=pl.ANY),
+        out_specs=pl.BlockSpec(memory_space=pltpu.VMEM),
         scratch_shapes=[pltpu.SemaphoreType.DMA((count,))],
+        compiler_params=params(16),
         cost_estimate=pl.CostEstimate(flops=0, bytes_accessed=4 * count * PANEL * WIDTH, transcendentals=0),
     )(ids, table)
 

time: 333 us -> 212 us (0.64)
  Pallas kernels: 148 us -> 20.5 us
  local copies, waits for them, and re-layouts: 6.35 us -> 13.6 us
    pallas_call x1, Pallas kernels: 129 us -> 1.06 us  [pick_panels(): pl.pallas_call(pick_kernel, out_shape=jax.ShapeDtypeStruct((count, PANEL,...]
    unnamed x8 -> x12, local copies, waits for them, and re-layouts: 1.5 us -> 9.26 us
  transfers between devices with their start and end apart: 5 -> 5, of which waited for: 5 -> 5; matrix products, arithmetic and copies ran while one was open for 0% -> 1% of each run, Pallas kernels for 0% -> 0%
where the time goes in v2:
time: 212 us; the launch traced here: 210 us
  waiting for transfers between devices  96.4 us (45%)
  blocking collectives  66.8 us (32%)
  Pallas kernels  20.5 us (10%)
  local copies, waits for them, and re-layouts  13.6 us (6%)
  starting transfers between devices  10.6 us (5%)
    all_to_all x3, blocking collectives, exchange(): return lax.all_to_all(x, axis, split_axis=0, concat_axis=0, tiled=True)  66.8 us
    all_to_all x1, waiting for transfers between devices, exchange(): return lax.all_to_all(x, axis, split_axis=0, concat_axis=0, tiled=True)  46.7 us
    ppermute x3, waiting for transfers between devices, local(): lax.ppermute(far, 'cent', shift(d, 0))  45.4 us
    unnamed x12, local copies, waits for them, and re-layouts  9.26 us
    pallas_call x1, Pallas kernels, score(): pl.pallas_call(score_kernel, grid_spec=pltpu.PrefetchScalarGridSpec(num_s...  8.93 us
    pallas_call x1, Pallas kernels, spread(): pl.pallas_call(spread_kernel, in_specs=[pl.BlockSpec(memory_space=pltpu.S...  6.58 us
    all_to_all x1, starting transfers between devices, exchange(): return lax.all_to_all(x, axis, split_axis=0, concat_axis=0, tiled=True)  6.52 us
    ppermute x1, waiting for transfers between devices, local(): mate = lax.ppermute(mine, 'cent', shift(0, 1))  4.3 us
  transfers between devices with their start and end apart: 5, of which 5 were waited for; matrix products, arithmetic and copies ran while one was open for 1% of the time, Pallas kernels for 0%

profile of v2, /device:TPU:24, one launch (start us, length us, event | category | flops | bytes accessed | tf_op | source)
XLA Modules:
  0.0 209.9 jit_solution(17012907334815155818)
XLA Ops:
  0.6 0.8 eq.48
  1.4 0.9 select_reduce_fusion
  2.5 0.7 broadcast_in_dim.53
  3.2 8.9 %all_to_all.20 = bf16[8,5,16,128]{3,2,1,0:T(8,128)(2,1)S(1)} all-to-all(bf16[8,5,16,128]{3,2,1,0:T(8,128)(2,1)S(1)} %fusion.1), channel_id=1, replica_groups=mesh['pts'=16,'cent'=8] {'cent'}, dimensions={0} | all-to-all | bytes 327680 | tf_op jit(solution)/shard_map/requests/all_to_all | solution.py:281
  12.2 5.8 %copy-done = bf16[8192,1024]{1,0:T(8,128)(2,1)S(1)} copy-done((bf16[8192,1024]{1,0:T(8,128)(2,1)S(1)}, bf16[8192,1024]{1,0:T(8,128)(2,1)}, u32[]{:S(2)}) %copy-start) | copy-done | bytes 16777240
  18.0 1.1 gather_panels.1
  19.1 2.0 copy-done.1
  21.1 6.5 %all-to-all-start.1 = ((bf16[8,2,128,1024]{3,2,1,0:T(8,128)(2,1)}), bf16[8,2,128,1024]{3,2,1,0:T(8,128)(2,1)}, u32[]{:S(2)}, u32[]{:S(2)}) async-start(bf16[8,2,128,1024]{3,2,1,0:T(8,128)(2,1)} %bitcast.39), calls=%async_computation.1 | async-start | bytes 8388608 | tf_op jit(solution)/shard_map/gather_panels/all_to_all | solution.py:281
  28.6 46.7 %all-to-all-done.1 = bf16[8,2,128,1024]{3,2,1,0:T(8,128)(2,1)} async-done(((bf16[8,2,128,1024]{3,2,1,0:T(8,128)(2,1)}), bf16[8,2,128,1024]{3,2,1,0:T(8,128)(2,1)}, u32[]{:S(2)}, u32[]{:S(2)}) %all-to-all-start.1) | async-done | bytes 4194336 | tf_op jit(solution)/shard_map/gather_panels/all_to_all | solution.py:281
  75.3 8.9 %score.1 = bf16[16,33,16,128]{3,2,1,0:T(8,128)(2,1)S(1)} custom-call(s32[8]{0:T(128)S(1)} %get-tuple-element.35.target, bf16[2048,1024]{1,0:T(8,128)(2,1)} %points.1, bf16[16,128,1024]{2,1,0:T(8,128)(2,1)} %bitcast.4.c0.c1.c2.c3, bf16[16,128,1024]{2,1,0:T(8,128)(2,1)} %bitcast.4.c0.c1.c2.c3, bf16[16,128,1024]{2,1,0:T(8,128)(2,1)} %bitcast.4.c0.c1.c2.c3, ...), custom_call_target="tpu_custom_call" | custom-call | flops 4294967296 | bytes 10485760 | tf_op jit(solution)/shard_map/score/pallas_call | solution.py:129
  84.2 36.6 %all_to_all.21.mine = bf16[16,33,16,128]{3,2,1,0:T(8,128)(2,1)S(1)} all-to-all(bf16[16,33,16,128]{3,2,1,0:T(8,128)(2,1)S(1)} %score.1), channel_id=1, replica_groups=mesh['pts'=16,'cent'=8] {'pts'}, dimensions={0} | all-to-all | bytes 4325376 | tf_op jit(solution)/shard_map/split_pieces/all_to_all | solution.py:281
  120.8 4.3 %collective-permute-done.mate = bf16[16,33,16,128]{3,2,1,0:T(8,128)(2,1)} collective-permute-done((bf16[16,33,16,128]{3,2,1,0:T(8,128)(2,1)S(1)}, bf16[16,33,16,128]{3,2,1,0:T(8,128)(2,1)}, u32[]{:S(2)}, u32[]{:S(2)}) %collective-permute-start) | collective-permute-done | bytes 2162720 | tf_op jit(solution)/shard_map/split_pieces/ppermute | solution.py:324
  125.1 0.8 slice.61
  126.6 6.6 %spread.1 = (f32[256,16,128]{2,1,0:T(8,128)S(1)}, f32[16,128]{1,0:T(8,128)S(1)}, bf16[257,16,128]{2,1,0:T(8,128)(2,1)}, bf16[257,16,128]{2,1,0:T(8,128)(2,1)}, bf16[257,16,128]{2,1,0:T(8,128)(2,1)}) custom-call(s32[256]{0:T(256)S(1)} %compare_select_fusion.2.places, bf16[16,33,16,128]{3,2,1,0:T(8,128)(2,1)} %copy-done.3, ...), custom_call_target="tpu_custom_call" | custom-call | flops 4194304 | bytes 10485760 | tf_op jit(solution)/shard_map/spread/pallas_call | solution.py:185
  133.2 1.4 copy-done.2
  134.5 2.1 collective-permute-start.1
  136.6 0.8 collective-permute-start.2
  137.4 1.2 collective-permute-start.3
  138.6 23.8 %collective-permute-done.1.in1 = bf16[257,16,128]{2,1,0:T(8,128)(2,1)S(1)} collective-permute-done((bf16[257,16,128]{2,1,0:T(8,128)(2,1)}, bf16[257,16,128]{2,1,0:T(8,128)(2,1)S(1)}, u32[]{:S(2)}, u32[]{:S(2)}) %collective-permute-start.1) | collective-permute-done | bytes 1052704 | tf_op jit(solution)/shard_map/sum_over_chips/ppermute | solution.py:339
  162.4 21.1 %collective-permute-done.2.in2 = bf16[257,16,128]{2,1,0:T(8,128)(2,1)S(1)} collective-permute-done((bf16[257,16,128]{2,1,0:T(8,128)(2,1)}, bf16[257,16,128]{2,1,0:T(8,128)(2,1)S(1)}, u32[]{:S(2)}, u32[]{:S(2)}) %collective-permute-start.2) | collective-permute-done | bytes 1052704 | tf_op jit(solution)/shard_map/sum_over_chips/ppermute | solution.py:339
  184.0 2.7 %finish.2 = bf16[16,17,16,128]{3,2,1,0:T(8,128)(2,1)S(1)} custom-call(s32[1]{0:T(128)} %bitcast.me, f32[256,16,128]{2,1,0:T(8,128)} %copy-done.2, f32[16,128]{1,0:T(8,128)S(1)} %get-tuple-element.22.own_weights, bf16[257,16,128]{2,1,0:T(8,128)(2,1)S(1)} %collective-permute-done.1.in1, bf16[257,16,128]{2,1,0:T(8,128)(2,1)S(1)} %collective-permute-done.2.in2, ...), custom_call_target="tpu_custom_call" | custom-call | flops 4194304 | bytes 8388608 | tf_op jit(solution)/shard_map/finish/pallas_call | solution.py:225
  186.8 21.4 %all_to_all.22.pieces = bf16[16,17,16,128]{3,2,1,0:T(8,128)(2,1)S(1)} all-to-all(bf16[16,17,16,128]{3,2,1,0:T(8,128)(2,1)S(1)} %finish.2), channel_id=1, replica_groups=mesh['pts'=16,'cent'=8] {'pts'}, dimensions={0} | all-to-all | bytes 2228224 | tf_op jit(solution)/shard_map/finish/all_to_all | solution.py:281
  208.2 1.2 finish.3
  209.4 0.6 slice_bitcast_fusion
  (36 shorter events, 2.5 us)
Async XLA Ops:
  12.2 5.8 %copy-start = (bf16[8192,1024]{1,0:T(8,128)(2,1)S(1)}, bf16[8192,1024]{1,0:T(8,128)(2,1)}, u32[]{:S(2)}) copy-start(bf16[8192,1024]{1,0:T(8,128)(2,1)} %param.8) | copy-start | bytes 50331652
  19.1 2.0 copy-start.1
  21.1 54.2 %all-to-all-start.1 = ((bf16[8,2,128,1024]{3,2,1,0:T(8,128)(2,1)}), bf16[8,2,128,1024]{3,2,1,0:T(8,128)(2,1)}, u32[]{:S(2)}, u32[]{:S(2)}) async-start(bf16[8,2,128,1024]{3,2,1,0:T(8,128)(2,1)} %bitcast.39), calls=%async_computation.1 | async-start | bytes 8388608 | tf_op jit(solution)/shard_map/gather_panels/all_to_all | solution.py:281
  120.8 5.8 %copy-start.3 = (bf16[16,33,16,128]{3,2,1,0:T(8,128)(2,1)}, bf16[16,33,16,128]{3,2,1,0:T(8,128)(2,1)S(1)}, u32[]{:S(2)}) copy-start(bf16[16,33,16,128]{3,2,1,0:T(8,128)(2,1)S(1)} %all_to_all.21.mine) | copy-start | bytes 6488068
  120.8 4.4 %collective-permute-start = (bf16[16,33,16,128]{3,2,1,0:T(8,128)(2,1)S(1)}, bf16[16,33,16,128]{3,2,1,0:T(8,128)(2,1)}, u32[]{:S(2)}, u32[]{:S(2)}) collective-permute-start(bf16[16,33,16,128]{3,2,1,0:T(8,128)(2,1)S(1)} %all_to_all.21.mine), channel_id=1, source_target_pairs={{0,1},{1,0},{2,3},{3,2},{4,5},{5,4},{6,7},{7,6},{8,9},{9,8},{10,11... | collective-permute-start | bytes 6488072 | tf_op jit(solution)/shard_map/split_pieces/ppermute | solution.py:324
  133.2 1.4 copy-start.2
  134.5 27.9 %collective-permute-start.1 = (bf16[257,16,128]{2,1,0:T(8,128)(2,1)}, bf16[257,16,128]{2,1,0:T(8,128)(2,1)S(1)}, u32[]{:S(2)}, u32[]{:S(2)}) collective-permute-start(bf16[257,16,128]{2,1,0:T(8,128)(2,1)} %get-tuple-element.23), channel_id=1, source_target_pairs={{0,4},{1,5},{2,6},{3,7},{4,0},{5,1},{6,2},{7,3},{8,12},{9,13},{10,... | collective-permute-start | bytes 3158024 | tf_op jit(solution)/shard_map/sum_over_chips/ppermute | solution.py:339
  136.6 46.9 %collective-permute-start.2 = (bf16[257,16,128]{2,1,0:T(8,128)(2,1)}, bf16[257,16,128]{2,1,0:T(8,128)(2,1)S(1)}, u32[]{:S(2)}, u32[]{:S(2)}) collective-permute-start(bf16[257,16,128]{2,1,0:T(8,128)(2,1)} %get-tuple-element.24), channel_id=1, source_target_pairs={{0,2},{1,3},{2,4},{3,5},{4,6},{5,7},{6,0},{7,1},{8,10},{9,11},{10,... | collective-permute-start | bytes 3158024 | tf_op jit(solution)/shard_map/sum_over_chips/ppermute | solution.py:339
  137.4 46.6 %collective-permute-start.3 = (bf16[257,16,128]{2,1,0:T(8,128)(2,1)}, bf16[257,16,128]{2,1,0:T(8,128)(2,1)S(1)}, u32[]{:S(2)}, u32[]{:S(2)}) collective-permute-start(bf16[257,16,128]{2,1,0:T(8,128)(2,1)} %get-tuple-element.25), channel_id=1, source_target_pairs={{0,6},{1,7},{2,0},{3,1},{4,2},{5,3},{6,4},{7,5},{8,14},{9,15},{10,... | collective-permute-start | bytes 3158024 | tf_op jit(solution)/shard_map/sum_over_chips/ppermute | solution.py:339

commit v3 on v1

v3 whole, which is shorter than its diff:
```python
import functools

import jax
import jax.numpy as jnp
from jax import lax
from jax.experimental import pallas as pl
from jax.experimental.pallas import tpu as pltpu
from jax.sharding import PartitionSpec as P

PANEL = 128
GROUP = 1024
CAND = 4
GROUPS_DEV = 2
REQ = CAND * GROUPS_DEV
PAN_DEV = 64
WIDTH = 1024
N_CENT = 8
CHIPS = 4
N_PTS = 16
SIDE = 4
ROWS = 16
HALF = 512
LANE = 128
TILES = HALF // LANE
PARTS = 2
WIDE = TILES // PARTS
DENSE = PAN_DEV * WIDE

sharpness_divisor = 16.0
evenness_coefficient = 1.0
prior_mass = 1.0

BF16 = jnp.bfloat16
F32 = jnp.float32
MIB = 1 << 20


def params(mib):
    return pltpu.CompilerParams(vmem_limit_bytes=mib * MIB)


def pick_kernel(ids, table, out, held, sems):
    def fetch(n):
        return pltpu.make_async_copy(table.at[ids[n]], held.at[n], sems.at[0, n])

    def put(n):
        return pltpu.make_async_copy(held.at[n], out.at[n], sems.at[1, n])

    for n in range(ids.shape[0]):
        fetch(n).start()
    for n in range(ids.shape[0]):
        fetch(n).wait()
        put(n).start()
    for n in range(ids.shape[0]):
        put(n).wait()


def pick_panels(ids, table):
    count = ids.shape[0]
    return pl.pallas_call(
        pick_kernel,
        out_shape=jax.ShapeDtypeStruct((count, PANEL, WIDTH), BF16),
        in_specs=[pl.BlockSpec(memory_space=pltpu.SMEM), pl.BlockSpec(memory_space=pltpu.HBM)],
        out_specs=pl.BlockSpec(memory_space=pltpu.HBM),
        scratch_shapes=[pltpu.VMEM((count, PANEL, WIDTH), BF16), pltpu.SemaphoreType.DMA((2, count))],
        compiler_params=params(60),
        cost_estimate=pl.CostEstimate(flops=0, bytes_accessed=4 * count * PANEL * WIDTH, transcendentals=0),
    )(ids, table)


def whole(shape):
    return pl.BlockSpec(shape, lambda *_: (0,) * len(shape))


def smem_spec():
    return pl.BlockSpec(memory_space=pltpu.SMEM)


def send_part(h, group, shares, columns, out):
    for half in range(2):
        part = lax.dot_general(
            shares, columns(half), (((1,), (0,)), ((), ())), preferred_element_type=F32
        ).astype(BF16)
        for t in range(WIDE):
            for j in range(CAND):
                for block_at in range(PANEL // ROWS):
                    row = j * PANEL + block_at * ROWS
                    out[block_at * 2 + half, (group * CAND + j) * WIDE + t] = part[
                        row : row + ROWS, t * LANE : (t + 1) * LANE
                    ]


def score_kernel(target, points, c0, c1, c2, c3, surcharge, out, shares, centers, marks):
    del target
    group = pl.program_id(0)
    for j, panel in enumerate((c0, c1, c2, c3)):
        centers[j * PANEL : (j + 1) * PANEL, :] = panel[0]
    wide = centers[...].astype(F32)
    squares = jnp.sum(wide * wide, axis=1, keepdims=True)
    bias = squares * (1.0 / sharpness_divisor) + evenness_coefficient * surcharge[0]
    step = 256
    weights = jnp.zeros((CAND * PANEL, LANE), F32)
    for s in range(GROUP // step):
        block = points[s * step : (s + 1) * step, :]
        inner = lax.dot_general(centers[...], block, (((1,), (1,)), ((), ())), preferred_element_type=F32)
        logits = inner * (2.0 / sharpness_divisor) - bias
        highest = jnp.max(logits, axis=0, keepdims=True)
        raised = jnp.exp(logits - highest)
        scale = 1.0 / jnp.sum(raised, axis=0, keepdims=True)
        share = (raised * scale).astype(BF16)
        shares[0, :, s * step : (s + 1) * step] = share
        rounded = share.astype(F32)
        for part in range(step // LANE):
            weights = weights + rounded[:, part * LANE : (part + 1) * LANE]
    weight = jnp.sum(weights, axis=1, keepdims=True)
    coarse = weight.astype(BF16).astype(F32)
    fine = weight - coarse
    lane = lax.broadcasted_iota(jnp.int32, (PANEL, LANE), 1)

    @pl.when(group == 0)
    def _():
        marks[...] = jnp.zeros_like(marks)

    tile = marks[...]
    for j in range(CAND):
        place = group * CAND + j
        rows = slice(j * PANEL, (j + 1) * PANEL)
        tile = jnp.where(lane == place, coarse[rows], tile)
        tile = jnp.where(lane == REQ + place, fine[rows], tile)
    marks[...] = tile
    send_part(0, group, shares[0], lambda half: points[:, half * HALF : half * HALF + WIDE * LANE], out)

    @pl.when(group == GROUPS_DEV - 1)
    def _():
        last = marks[...].astype(BF16)
        for block_at in range(PANEL // ROWS):
            for half in range(2):
                out[block_at * 2 + half, REQ * WIDE] = last[block_at * ROWS : (block_at + 1) * ROWS]


def score(target, points, arrived, surcharge):
    def panel(j):
        return pl.BlockSpec((1, PANEL, WIDTH), lambda g, t: (t[g * CAND + j], 0, 0))

    tiles = REQ * WIDE + 1
    return pl.pallas_call(
        score_kernel,
        grid_spec=pltpu.PrefetchScalarGridSpec(
            num_scalar_prefetch=1,
            grid=(GROUPS_DEV,),
            in_specs=[
                pl.BlockSpec((GROUP, WIDTH), lambda g, t: (g, 0)),
                panel(0), panel(1), panel(2), panel(3),
                pl.BlockSpec((1, CAND * PANEL, 1), lambda g, t: (g, 0, 0)),
            ],
            out_specs=[
                pl.BlockSpec((N_PTS, tiles, ROWS, LANE), lambda g, t: (0, 0, 0, 0)),
                pl.BlockSpec((1, CAND * PANEL, GROUP), lambda g, t: (g, 0, 0)),
            ],
            scratch_shapes=[pltpu.VMEM((CAND * PANEL, WIDTH), BF16), pltpu.VMEM((PANEL, LANE), F32)],
        ),
        out_shape=[
            jax.ShapeDtypeStruct((N_PTS, tiles, ROWS, LANE), BF16),
            jax.ShapeDtypeStruct((GROUPS_DEV, CAND * PANEL, GROUP), BF16),
        ],
        compiler_params=params(48),
        cost_estimate=pl.CostEstimate(flops=3 << 30, bytes_accessed=10 * MIB, transcendentals=1 << 20),
    )(target, points, arrived, arrived, arrived, arrived, surcharge)


def second_kernel(shares, left, right, out):
    group = pl.program_id(0)
    send_part(1, group, shares[0], lambda half: (left, right)[half][...], out)


def second(shares, points):
    width = WIDE * LANE
    tiles = REQ * WIDE
    return pl.pallas_call(
        second_kernel,
        grid=(GROUPS_DEV,),
        in_specs=[
            pl.BlockSpec((1, CAND * PANEL, GROUP), lambda g: (g, 0, 0)),
            pl.BlockSpec((GROUP, width), lambda g: (g, 1)),
            pl.BlockSpec((GROUP, width), lambda g: (g, HALF // width + 1)),
        ],
        out_specs=pl.BlockSpec((N_PTS, tiles, ROWS, LANE), lambda g: (0, 0, 0, 0)),
        out_shape=jax.ShapeDtypeStruct((N_PTS, tiles, ROWS, LANE), BF16),
        compiler_params=params(48),
        cost_estimate=pl.CostEstimate(flops=1 << 30, bytes_accessed=6 * MIB, transcendentals=0),
    )(shares, points, points)


def spread_kernel(has_weights, places, mine, mate, *refs):
    if has_weights:
        lanes, own, own_weights, out1, out2, out3, total = refs
    else:
        own, out1, out2, out3, total = refs
    total[...] = jnp.zeros_like(total)
    sources = (mine, mate)
    for n, source in enumerate(sources):
        def add(s, carry, n=n, source=source):
            for i in range(REQ):
                at = places[(n * N_PTS + s) * REQ + i] * WIDE
                total[pl.ds(at, WIDE)] += source[s, i * WIDE : (i + 1) * WIDE].astype(F32)
            return carry

        lax.fori_loop(0, N_PTS, add, 0)
    own[...] = total[0:DENSE]
    for d, out in ((1, out1), (2, out2), (3, out3)):
        out[0:DENSE] = total[d * DENSE : (d + 1) * DENSE].astype(BF16)
    if has_weights:
        panel = lax.broadcasted_iota(jnp.int32, (CHIPS * PAN_DEV, LANE), 0)
        weights = jnp.zeros((ROWS, CHIPS * PAN_DEV), F32)
        for n in range(2 * N_PTS):
            chosen = jnp.where(panel == lanes[n : n + 1, :], 1.0, 0.0).astype(BF16)
            weights = weights + lax.dot_general(
                sources[n // N_PTS][n % N_PTS, REQ * WIDE], chosen, (((1,), (1,)), ((), ())),
                preferred_element_type=F32,
            )
        coarse = weights.astype(BF16)
        fine = (weights - coarse.astype(F32)).astype(BF16)
        own_weights[...] = weights[:, 0:LANE]
        for d, out in ((1, out1), (2, out2), (3, out3)):
            out[DENSE, :, 0:PAN_DEV] = coarse[:, d * PAN_DEV : (d + 1) * PAN_DEV]
            out[DENSE, :, PAN_DEV:LANE] = fine[:, d * PAN_DEV : (d + 1) * PAN_DEV]


def spread(places, mine, mate, lanes=None):
    has_weights = lanes is not None
    chunk = jax.ShapeDtypeStruct((DENSE + has_weights, ROWS, LANE), BF16)
    return pl.pallas_call(
        functools.partial(spread_kernel, has_weights),
        grid=(1,),
        in_specs=[smem_spec()] + [whole(mine.shape)] * 2 + [whole((2 * N_PTS, LANE))] * has_weights,
        out_specs=[whole((DENSE, ROWS, LANE))] + [whole((ROWS, LANE))] * has_weights + [whole(chunk.shape)] * 3,
        out_shape=[jax.ShapeDtypeStruct((DENSE, ROWS, LANE), F32)]
        + [jax.ShapeDtypeStruct((ROWS, LANE), F32)] * has_weights
        + [chunk, chunk, chunk],
        scratch_shapes=[pltpu.VMEM((CHIPS * DENSE + WIDE, ROWS, LANE), F32)],
        compiler_params=params(48),
        cost_estimate=pl.CostEstimate(flops=1 << 22, bytes_accessed=5 * MIB, transcendentals=0),
    )(places, mine, mate, *([lanes] if has_weights else []))


def finish_kernel(has_weights, me, own, in1, in2, in3, old, *refs):
    del me
    if has_weights:
        own_weights, out, scales = refs
        weights = own_weights[:, 0:PAN_DEV]
        for arrived in (in1, in2, in3):
            pair = arrived[DENSE].astype(F32)
            weights = weights + (pair[:, 0:PAN_DEV] + pair[:, PAN_DEV:LANE])
        inverse = 1.0 / (weights + prior_mass)
        scales[:, 0:PAN_DEV] = inverse
        coarse = weights.astype(BF16)
        fine = (weights - coarse.astype(F32)).astype(BF16)
        for p in range(N_PTS):
            out[p, CAND * WIDE, :, 0:PAN_DEV] = coarse
            out[p, CAND * WIDE, :, PAN_DEV:LANE] = fine
    else:
        scales, out = refs
        inverse = scales[:, 0:PAN_DEV]
    for q in range(PAN_DEV):
        scale = jnp.broadcast_to(inverse[:, q : q + 1], (ROWS, LANE))
        for t in range(WIDE):
            at = q * WIDE + t
            total = own[at] + in1[at].astype(F32) + in2[at].astype(F32) + in3[at].astype(F32)
            previous = old[q, :, t * LANE : (t + 1) * LANE].astype(F32)
            fresh = (total + prior_mass * previous) * scale
            out[q // CAND, (q % CAND) * WIDE + t] = fresh.astype(BF16)


def finish(h, me, own, arrived, table, weights):
    has_weights = h == 0
    chunk = whole((DENSE + has_weights, ROWS, LANE))
    fresh = (N_PTS, CAND * WIDE + has_weights, ROWS, LANE)
    return pl.pallas_call(
        functools.partial(finish_kernel, has_weights),
        grid_spec=pltpu.PrefetchScalarGridSpec(
            num_scalar_prefetch=1,
            grid=(1,),
            in_specs=[
                whole((DENSE, ROWS, LANE)), chunk, chunk, chunk,
                pl.BlockSpec((PAN_DEV, ROWS, WIDE * LANE), lambda g, me: (0, me[0] // 2, (me[0] % 2) * PARTS + h)),
                whole((ROWS, LANE)),
            ],
            out_specs=[whole(fresh)] + [whole((ROWS, LANE))] * has_weights,
        ),
        out_shape=[jax.ShapeDtypeStruct(fresh, BF16)] + [jax.ShapeDtypeStruct((ROWS, LANE), F32)] * has_weights,
        compiler_params=params(48),
        cost_estimate=pl.CostEstimate(flops=1 << 22, bytes_accessed=4 * MIB, transcendentals=0),
    )(me, own, *arrived, table, weights)


def place_kernel(me, part0, part1, out, loads):
    for h, pieces in enumerate((part0, part1)):
        for block_at in range(PANEL // ROWS):
            for half in range(2):
                for q in range(CAND):
                    for t in range(WIDE):
                        column = half * HALF + (h * WIDE + t) * LANE
                        out[q, block_at * ROWS : (block_at + 1) * ROWS, column : column + LANE] = pieces[
                            block_at * 2 + half, q * WIDE + t
                        ]
    lane = lax.broadcasted_iota(jnp.int32, (ROWS, LANE), 1)
    row = lax.broadcasted_iota(jnp.int32, (ROWS, LANE), 0)
    wanted = me[0] * CAND + row
    chosen = jnp.where((row < CAND) & (lane % PAN_DEV == wanted), 1.0, 0.0).astype(BF16)
    for block_at in range(PANEL // ROWS):
        pair = part0[block_at * 2, CAND * WIDE]
        part = lax.dot_general(chosen, pair, (((1,), (1,)), ((), ())), preferred_element_type=F32)
        loads[:, block_at * ROWS : (block_at + 1) * ROWS] = part[0:8]


def place(me, part0, part1):
    return pl.pallas_call(
        place_kernel,
        grid=(1,),
        in_specs=[smem_spec(), whole(part0.shape), whole(part1.shape)],
        out_specs=[whole((CAND, PANEL, WIDTH)), whole((8, PANEL))],
        out_shape=[
            jax.ShapeDtypeStruct((CAND, PANEL, WIDTH), BF16),
            jax.ShapeDtypeStruct((8, PANEL), F32),
        ],
        compiler_params=params(32),
        cost_estimate=pl.CostEstimate(flops=1 << 20, bytes_accessed=2 * MIB, transcendentals=0),
    )(me, part0, part1)


def shift(dy, dk):
    return [(y * 2 + k, ((y + dy) % CHIPS) * 2 + (k + dk) % 2) for y in range(CHIPS) for k in range(2)]


def spread_out(x, place, dz, dx):
    held = [x]
    for d in range(1, SIDE):
        pairs = [
            (ix * SIDE + iz, (ix + d * dx) % SIDE * SIDE + (iz + d * dz) % SIDE)
            for ix in range(SIDE)
            for iz in range(SIDE)
        ]
        held.append(lax.ppermute(x, "pts", pairs))
    held = jnp.stack(held)
    at = (place - jnp.arange(SIDE, dtype=jnp.int32)) % SIDE
    return jnp.stack([jnp.sum(jnp.where((at == n).reshape((SIDE,) + (1,) * x.ndim), held, 0), axis=0) for n in range(SIDE)])


def exchange(x, axis):
    return lax.all_to_all(x, axis, split_axis=0, concat_axis=0, tiled=True)


def local(points, centroids, prev_loads, candidates, panel_home):
    me = lax.axis_index("pts")
    here = lax.axis_index("cent")
    chip, core = here // 2, here % 2
    shelf = centroids.reshape(PAN_DEV, PANEL, WIDTH)

    with jax.named_scope("requests"):
        wanted_ids = candidates.reshape(REQ)
        slots = jnp.sum(
            jnp.where(wanted_ids[:, None] == jnp.arange(panel_home.shape[0], dtype=jnp.int32), panel_home[None, :], 0),
            axis=1,
        )
        owners, local_ids = slots // PAN_DEV, slots % PAN_DEV
        target = owners * GROUPS_DEV + jnp.arange(REQ, dtype=jnp.int32) // CAND
        spots = jnp.arange(N_CENT * GROUPS_DEV, dtype=jnp.int32)
        wanted = jnp.sum(jnp.where(target[None, :] == spots[:, None], local_ids[None, :], 0), axis=1)
        ask = jnp.stack(
            [
                jnp.pad(wanted.reshape(N_CENT, GROUPS_DEV), ((0, 0), (0, LANE - GROUPS_DEV))),
                jnp.broadcast_to(jnp.pad(owners, (0, LANE - REQ)), (N_CENT, LANE)),
                jnp.broadcast_to(jnp.pad(local_ids, (0, LANE - REQ)), (N_CENT, LANE)),
            ],
            axis=1,
        ).astype(BF16)
        ask = jnp.pad(ask, ((0, 0), (0, ROWS - 3), (0, 0))).reshape(N_CENT, 1, ROWS, LANE)
        table = jnp.broadcast_to(
            prev_loads.reshape(1, PAN_DEV // ROWS, ROWS, LANE), (N_CENT, PAN_DEV // ROWS, ROWS, LANE)
        )
        answered = exchange(jnp.concatenate([table, ask], axis=1), "cent")
        asked = answered[:, PAN_DEV // ROWS, 0, 0:GROUPS_DEV].astype(jnp.int32).reshape(-1)

    with jax.named_scope("gather_panels"):
        arrived = exchange(pick_panels(asked, shelf).reshape(N_CENT, GROUPS_DEV, PANEL, WIDTH), "cent")
        arrived = arrived.reshape(N_CENT * GROUPS_DEV, PANEL, WIDTH)

    with jax.named_scope("all_requests"):
        ring = answered[:, PAN_DEV // ROWS, 1:3, 0:REQ].astype(jnp.int32)
        ring = ring[:, 0] * PAN_DEV + ring[:, 1]
        line = spread_out(ring, me % SIDE, 1, 0)
        everyone = spread_out(line, me // SIDE, 0, 1).reshape(N_PTS, N_CENT, REQ)
        pair = jnp.stack(
            [lax.dynamic_index_in_dim(everyone, at, 1, keepdims=False) for at in (here, chip * 2 + 1 - core)]
        ).reshape(2 * N_PTS, REQ)
        owner = pair // PAN_DEV
        relative = (owner // 2 - chip) % CHIPS
        places = jnp.where(owner % 2 == core, relative * PAN_DEV + pair % PAN_DEV, CHIPS * PAN_DEV)
        lanes = jnp.pad(
            jnp.concatenate([places, places], axis=1), ((0, 0), (0, LANE - 2 * REQ)), constant_values=CHIPS * PAN_DEV
        )
        places = places.reshape(-1)
        target, places, lanes = lax.optimization_barrier((target, places, lanes))

    with jax.named_scope("loads"):
        load_table = answered[:, : PAN_DEV // ROWS].reshape(N_CENT * PAN_DEV, PANEL)
        loads = jnp.take(load_table, slots, axis=0, mode="clip").astype(F32)
        surcharge = jnp.log(loads).reshape(GROUPS_DEV, CAND * PANEL, 1)

    with jax.named_scope("score"):
        pieces0, shares = score(target, points, arrived, surcharge)
        pieces1 = second(shares, points)

    where = me.reshape(1)
    tie = lax.optimization_barrier
    with jax.named_scope("split_pieces"):
        mine0 = exchange(pieces0, "pts")
        mine0, pieces1 = tie((mine0, pieces1))
        mine1 = exchange(pieces1, "pts")
        mate0 = lax.ppermute(mine0, "cent", shift(0, 1))
    with jax.named_scope("spread"):
        own0, weights, *far0 = spread(places, mine0, mate0, lanes)
    with jax.named_scope("sum_over_chips"):
        back0 = [lax.ppermute(far0[d - 1], "cent", shift(d, 0)) for d in (2, 1, 3)]
    with jax.named_scope("split_pieces"):
        mine1, back0 = tie((mine1, back0))
        mate1 = lax.ppermute(mine1, "cent", shift(0, 1))
    with jax.named_scope("spread"):
        own1, *far1 = spread(places, mine1, mate1)
    with jax.named_scope("sum_over_chips"):
        back1 = [lax.ppermute(far1[d - 1], "cent", shift(d, 0)) for d in (2, 1, 3)]
    with jax.named_scope("finish"):
        own0, own1 = tie((own0, own1))
        fresh0, scales = finish(0, where, own0, back0, shelf, weights)
        done0 = exchange(fresh0, "pts")
        own1, done0 = tie((own1, done0))
        fresh1, = finish(1, where, own1, back1, shelf, scales)
        done1 = exchange(fresh1, "pts")
    with jax.named_scope("place"):
        new_centroids, new_loads = place(where, done0, done1)
    return new_centroids.reshape(CAND * PANEL, WIDTH), new_loads[0:CAND].reshape(CAND * PANEL)


def solution(mesh):
    placed = (P(("pts", "cent"), None), P("cent", None), P("cent"), P(("pts", "cent"), None), P())
    return jax.shard_map(
        local,
        mesh=mesh,
        in_specs=placed,
        out_specs=(P(("cent", "pts"), None), P(("cent", "pts"))),
        check_vma=False,
    )
```

time: 333 us -> 213 us (0.64)
  Pallas kernels: 148 us -> 28.3 us
  blocking collectives: 66.8 us -> 27.2 us
  starting transfers between devices: 10.7 us -> 44.4 us
  local copies, waits for them, and re-layouts: 6.35 us -> 9.85 us
    pallas_call x1, Pallas kernels: 129 us -> 5.72 us  [pick_panels(): pl.pallas_call(pick_kernel, out_shape=jax.ShapeDtypeStruct((count, PANEL,...]
    all_to_all x3 -> x2, blocking collectives: 66.8 us -> 27.2 us  [exchange(): return lax.all_to_all(x, axis, split_axis=0, concat_axis=0, tiled=True)]
    all_to_all x1 -> x4, starting transfers between devices: 6.54 us -> 25.2 us  [exchange(): return lax.all_to_all(x, axis, split_axis=0, concat_axis=0, tiled=True)]
    all_to_all x1 -> x4, waiting for transfers between devices: 46.7 us -> 61.9 us  [exchange(): return lax.all_to_all(x, axis, split_axis=0, concat_axis=0, tiled=True)]
    ppermute x4 -> x14, starting transfers between devices: 4.13 us -> 19.2 us  [the longest x6 10.9 us: spread_out(): held.append(lax.ppermute(x, 'pts', pairs))]
    ppermute x4 -> x14, waiting for transfers between devices: 49.8 us -> 36.2 us  [the longest x3 14.2 us: local(): back1 = [lax.ppermute(far1[d - 1], 'cent', shift(d, 0)) for d in (2, 1, 3)]]
    unnamed x8 -> x16, local copies, waits for them, and re-layouts: 1.5 us -> 5.81 us
    pallas_call x3 -> x6, Pallas kernels: 10.5 us -> 14.7 us  [the longest x2 6.13 us: spread(): pl.pallas_call(functools.partial(spread_kernel, has_weights), grid=(1,),...]
  transfers between devices with their start and end apart: 5 -> 18, of which waited for: 5 -> 15; matrix products, arithmetic and copies ran while one was open for 0% -> 1% of each run, Pallas kernels for 0% -> 4%
where the time goes in v3:
time: 213 us; the launch traced here: 210 us
  waiting for transfers between devices  98 us (46%)
  starting transfers between devices  44.4 us (21%)
  Pallas kernels  28.3 us (13%)
  blocking collectives  27.2 us (13%)
  local copies, waits for them, and re-layouts  9.85 us (5%)
    all_to_all x4, waiting for transfers between devices, exchange(): return lax.all_to_all(x, axis, split_axis=0, concat_axis=0, tiled=True)  61.9 us
    all_to_all x2, blocking collectives, exchange(): return lax.all_to_all(x, axis, split_axis=0, concat_axis=0, tiled=True)  27.2 us
    all_to_all x4, starting transfers between devices, exchange(): return lax.all_to_all(x, axis, split_axis=0, concat_axis=0, tiled=True)  25.2 us
    ppermute x3, waiting for transfers between devices, local(): back1 = [lax.ppermute(far1[d - 1], 'cent', shift(d, 0)) for d in (2, 1, 3)]  14.2 us
    ppermute x3, waiting for transfers between devices, local(): back0 = [lax.ppermute(far0[d - 1], 'cent', shift(d, 0)) for d in (2, 1, 3)]  13.4 us
    ppermute x6, starting transfers between devices, spread_out(): held.append(lax.ppermute(x, 'pts', pairs))  10.9 us
    pallas_call x1, Pallas kernels, score(): pl.pallas_call(score_kernel, grid_spec=pltpu.PrefetchScalarGridSpec(num_s...  7.84 us
    pallas_call x2, Pallas kernels, spread(): pl.pallas_call(functools.partial(spread_kernel, has_weights), grid=(1,),...  6.13 us
  transfers between devices with their start and end apart: 18, of which 15 were waited for; matrix products, arithmetic and copies ran while one was open for 1% of the time, Pallas kernels for 4%

profile of v3, /device:TPU:24, one launch (start us, length us, event | category | flops | bytes accessed | tf_op | source)
XLA Modules:
  0.0 210.2 jit_solution(11270187509651694029)
XLA Ops:
  3.3 8.9 %all_to_all.30 = bf16[8,5,16,128]{3,2,1,0:T(8,128)(2,1)S(1)} all-to-all(bf16[8,5,16,128]{3,2,1,0:T(8,128)(2,1)S(1)} %pad_maximum_fusion), channel_id=1, replica_groups=mesh['pts'=16,'cent'=8] {'cent'}, dimensions={0} | all-to-all | bytes 327680 | tf_op jit(solution)/shard_map/requests/all_to_all | solution.py:350
  12.8 5.7 %gather_panels.1 = bf16[16,128,1024]{2,1,0:T(8,128)(2,1)} custom-call(s32[16]{0:T(128)} %reshape.213.ids, bf16[64,128,1024]{2,1,0:T(8,128)(2,1)} %bitcast.59), custom_call_target="tpu_custom_call" | custom-call | bytes 8388608 | tf_op jit(solution)/shard_map/gather_panels/pallas_call | solution.py:60
  18.5 6.6 %all-to-all-start.1 = ((bf16[8,2,128,1024]{3,2,1,0:T(8,128)(2,1)}), bf16[8,2,128,1024]{3,2,1,0:T(8,128)(2,1)}, u32[]{:S(2)}, u32[]{:S(2)}) async-start(bf16[8,2,128,1024]{3,2,1,0:T(8,128)(2,1)} %bitcast.62), calls=%async_computation.1 | async-start | bytes 8388608 | tf_op jit(solution)/shard_map/gather_panels/all_to_all | solution.py:350
  25.2 4.3 %collective-permute-start.2 = (s32[8,8]{1,0:T(8,128)S(1)}, s32[8,8]{1,0:T(8,128)S(1)}, u32[]{:S(2)}, u32[]{:S(2)}) collective-permute-start(s32[8,8]{1,0:T(8,128)S(1)} %get-tuple-element.73), channel_id=1, source_target_pairs={{0,24},{8,0},{16,8},{24,16},{32,56},{40,32},{48,40},{56,48},{64,88... | collective-permute-start | bytes 776 | tf_op jit(solution)/shard_map/all_requests/ppermute | solution.py:343
  31.7 2.7 %collective-permute-done = s32[8,8]{1,0:T(8,128)S(1)} collective-permute-done((s32[8,8]{1,0:T(8,128)S(1)}, s32[8,8]{1,0:T(8,128)S(1)}, u32[]{:S(2)}, u32[]{:S(2)}) %collective-permute-start) | collective-permute-done | bytes 288 | tf_op jit(solution)/shard_map/all_requests/ppermute | solution.py:343
  35.4 4.0 %collective-permute-start.4 = (s32[4,8,8]{2,1,0:T(8,128)S(1)}, s32[4,8,8]{2,1,0:T(8,128)S(1)}, u32[]{:S(2)}, u32[]{:S(2)}) collective-permute-start(s32[4,8,8]{2,1,0:T(8,128)S(1)} %get-tuple-element.70), channel_id=1, source_target_pairs={{0,64},{8,72},{16,80},{24,88},{32,96},{40,104},{48,112},{56,120},{... | collective-permute-start | bytes 3080 | tf_op jit(solution)/shard_map/all_requests/ppermute | solution.py:343
  43.7 29.1 %all-to-all-done.1 = bf16[8,2,128,1024]{3,2,1,0:T(8,128)(2,1)} async-done(((bf16[8,2,128,1024]{3,2,1,0:T(8,128)(2,1)}), bf16[8,2,128,1024]{3,2,1,0:T(8,128)(2,1)}, u32[]{:S(2)}, u32[]{:S(2)}) %all-to-all-start.1) | async-done | bytes 4194336 | tf_op jit(solution)/shard_map/gather_panels/all_to_all | solution.py:350
  72.8 7.8 %score.2 = (bf16[16,17,16,128]{3,2,1,0:T(8,128)(2,1)S(1)}, bf16[2,512,1024]{2,1,0:T(8,128)(2,1)S(1)}) custom-call(s32[8]{0:T(128)S(1)} %get-tuple-element.31.target, bf16[2048,1024]{1,0:T(8,128)(2,1)} %right.1, bf16[16,128,1024]{2,1,0:T(8,128)(2,1)} %bitcast.29.c0.c1.c2.c3, bf16[16,128,1024]{2,1,0:T(8,128)(2,1)} %bitcast.29.c0.c1.c2.c3, ...), custom_call_target="tpu_custom_call" | custom-call | flops 3221225472 | bytes 10485760 | tf_op jit(solution)/shard_map/score/pallas_call | solution.py:146
  81.7 8.1 %all-to-all-start.2 = ((bf16[16,17,16,128]{3,2,1,0:T(8,128)(2,1)}), bf16[16,17,16,128]{3,2,1,0:T(8,128)(2,1)S(1)}, u32[]{:S(2)}, u32[]{:S(2)}) async-start(bf16[16,17,16,128]{3,2,1,0:T(8,128)(2,1)} %copy-done), calls=%async_computation.2 | async-start | bytes 2228224 | tf_op jit(solution)/shard_map/split_pieces/all_to_all | solution.py:350
  89.8 3.7 %score.3 = bf16[16,16,16,128]{3,2,1,0:T(8,128)(2,1)} custom-call(bf16[2,512,1024]{2,1,0:T(8,128)(2,1)S(1)} %get-tuple-element.33.shares, bf16[2048,1024]{1,0:T(8,128)(2,1)} %right.1, bf16[2048,1024]{1,0:T(8,128)(2,1)} %right.1), custom_call_target="tpu_custom_call" | custom-call | flops 1073741824 | bytes 6291456 | tf_op jit(solution)/shard_map/score/pallas_call | solution.py:179
  93.5 14.5 %all-to-all-done.2.mine = bf16[16,17,16,128]{3,2,1,0:T(8,128)(2,1)S(1)} async-done(((bf16[16,17,16,128]{3,2,1,0:T(8,128)(2,1)}), bf16[16,17,16,128]{3,2,1,0:T(8,128)(2,1)S(1)}, u32[]{:S(2)}, u32[]{:S(2)}) %all-to-all-start.2) | async-done | bytes 1114144 | tf_op jit(solution)/shard_map/split_pieces/all_to_all | solution.py:350
  108.0 3.7 %all-to-all-start.3 = ((bf16[16,16,16,128]{3,2,1,0:T(8,128)(2,1)}), bf16[16,16,16,128]{3,2,1,0:T(8,128)(2,1)S(1)}, u32[]{:S(2)}, u32[]{:S(2)}) async-start(bf16[16,16,16,128]{3,2,1,0:T(8,128)(2,1)} %score.3), calls=%async_computation.3 | async-start | bytes 2097152 | tf_op jit(solution)/shard_map/split_pieces/all_to_all | solution.py:350
  111.7 4.0 %spread.2 = (f32[128,16,128]{2,1,0:T(8,128)S(1)}, f32[16,128]{1,0:T(8,128)S(1)}, bf16[129,16,128]{2,1,0:T(8,128)(2,1)}, bf16[129,16,128]{2,1,0:T(8,128)(2,1)}, bf16[129,16,128]{2,1,0:T(8,128)(2,1)}) custom-call(s32[256]{0:T(256)S(1)} %compare_select_fusion.6.places, bf16[16,17,16,128]{3,2,1,0:T(8,128)(2,1)S(1)} %all-to-all-done.2.mine, ...), custom_call_target="tpu_custom_call" | custom-call | flops 4194304 | bytes 5242880 | tf_op jit(solution)/shard_map/spread/pallas_call | solution.py:232
  120.7 9.9 %all-to-all-done.3.mine = bf16[16,16,16,128]{3,2,1,0:T(8,128)(2,1)S(1)} async-done(((bf16[16,16,16,128]{3,2,1,0:T(8,128)(2,1)}), bf16[16,16,16,128]{3,2,1,0:T(8,128)(2,1)S(1)}, u32[]{:S(2)}, u32[]{:S(2)}) %all-to-all-start.3) | async-done | bytes 1048608 | tf_op jit(solution)/shard_map/split_pieces/all_to_all | solution.py:350
  130.6 2.5 %collective-permute-done.7.in1 = bf16[129,16,128]{2,1,0:T(8,128)(2,1)S(1)} collective-permute-done((bf16[129,16,128]{2,1,0:T(8,128)(2,1)}, bf16[129,16,128]{2,1,0:T(8,128)(2,1)S(1)}, u32[]{:S(2)}, u32[]{:S(2)}) %collective-permute-start.7) | collective-permute-done | bytes 528416 | tf_op jit(solution)/shard_map/sum_over_chips/ppermute | solution.py:424
  133.2 10.3 %collective-permute-done.8.in2 = bf16[129,16,128]{2,1,0:T(8,128)(2,1)S(1)} collective-permute-done((bf16[129,16,128]{2,1,0:T(8,128)(2,1)}, bf16[129,16,128]{2,1,0:T(8,128)(2,1)S(1)}, u32[]{:S(2)}, u32[]{:S(2)}) %collective-permute-start.8) | collective-permute-done | bytes 528416 | tf_op jit(solution)/shard_map/sum_over_chips/ppermute | solution.py:424
  144.9 2.6 %collective-permute-done.10.mate = bf16[16,16,16,128]{3,2,1,0:T(8,128)(2,1)S(1)} collective-permute-done((bf16[16,16,16,128]{3,2,1,0:T(8,128)(2,1)S(1)}, bf16[16,16,16,128]{3,2,1,0:T(8,128)(2,1)S(1)}, u32[]{:S(2)}, u32[]{:S(2)}) %collective-permute-start.10) | collective-permute-done | bytes 1048608 | tf_op jit(solution)/shard_map/split_pieces/ppermute | solution.py:427
  147.5 2.2 %spread.3 = (f32[128,16,128]{2,1,0:T(8,128)S(1)}, bf16[128,16,128]{2,1,0:T(8,128)(2,1)S(1)}, bf16[128,16,128]{2,1,0:T(8,128)(2,1)S(1)}, bf16[128,16,128]{2,1,0:T(8,128)(2,1)S(1)}) custom-call(s32[256]{0:T(256)S(1)} %compare_select_fusion.6.places, bf16[16,16,16,128]{3,2,1,0:T(8,128)(2,1)S(1)} %all-to-all-done.3.mine, ...), custom_call_target="tpu_custom_call" | custom-call | flops 4194304 | bytes 5242880 | tf_op jit(solution)/shard_map/spread/pallas_call | solution.py:232
  152.8 2.3 %finish.2 = (bf16[16,9,16,128]{3,2,1,0:T(8,128)(2,1)}, f32[16,128]{1,0:T(8,128)S(1)}) custom-call(s32[1]{0:T(128)} %bitcast.me, f32[128,16,128]{2,1,0:T(8,128)S(1)} %copy-done.2, bf16[129,16,128]{2,1,0:T(8,128)(2,1)S(1)} %collective-permute-done.7.in1, bf16[129,16,128]{2,1,0:T(8,128)(2,1)S(1)} %collective-permute-done.8.in2, ...), custom_call_target="tpu_custom_call" | custom-call | flops 4194304 | bytes 4194304 | tf_op jit(solution)/shard_map/finish/pallas_call | solution.py:278
  155.1 6.9 %all-to-all-start.4 = ((bf16[16,9,16,128]{3,2,1,0:T(8,128)(2,1)}), bf16[16,9,16,128]{3,2,1,0:T(8,128)(2,1)S(1)}, u32[]{:S(2)}, u32[]{:S(2)}) async-start(bf16[16,9,16,128]{3,2,1,0:T(8,128)(2,1)} %get-tuple-element.49), calls=%async_computation.4 | async-start | bytes 1179648 | tf_op jit(solution)/shard_map/finish/all_to_all | solution.py:350
  166.1 8.3 %all-to-all-done.4.part0 = bf16[16,9,16,128]{3,2,1,0:T(8,128)(2,1)S(1)} async-done(((bf16[16,9,16,128]{3,2,1,0:T(8,128)(2,1)}), bf16[16,9,16,128]{3,2,1,0:T(8,128)(2,1)S(1)}, u32[]{:S(2)}, u32[]{:S(2)}) %all-to-all-start.4) | async-done | bytes 589856 | tf_op jit(solution)/shard_map/finish/all_to_all | solution.py:350
  174.5 4.2 %collective-permute-done.11.in1 = bf16[128,16,128]{2,1,0:T(8,128)(2,1)S(1)} collective-permute-done((bf16[128,16,128]{2,1,0:T(8,128)(2,1)}, bf16[128,16,128]{2,1,0:T(8,128)(2,1)S(1)}, u32[]{:S(2)}, u32[]{:S(2)}) %collective-permute-start.11) | collective-permute-done | bytes 524320 | tf_op jit(solution)/shard_map/sum_over_chips/ppermute | solution.py:431
  178.6 9.4 %collective-permute-done.12.in2 = bf16[128,16,128]{2,1,0:T(8,128)(2,1)S(1)} collective-permute-done((bf16[128,16,128]{2,1,0:T(8,128)(2,1)}, bf16[128,16,128]{2,1,0:T(8,128)(2,1)S(1)}, u32[]{:S(2)}, u32[]{:S(2)}) %collective-permute-start.12) | collective-permute-done | bytes 524320 | tf_op jit(solution)/shard_map/sum_over_chips/ppermute | solution.py:431
  190.1 18.3 %all_to_all.31.part1 = bf16[16,8,16,128]{3,2,1,0:T(8,128)(2,1)S(1)} all-to-all(bf16[16,8,16,128]{3,2,1,0:T(8,128)(2,1)S(1)} %finish.3), channel_id=1, replica_groups=mesh['pts'=16,'cent'=8] {'pts'}, dimensions={0} | all-to-all | bytes 1048576 | tf_op jit(solution)/shard_map/finish/all_to_all | solution.py:350
  (81 shorter events, 29.2 us)
Async XLA Ops:
  18.5 54.3 %all-to-all-start.1 = ((bf16[8,2,128,1024]{3,2,1,0:T(8,128)(2,1)}), bf16[8,2,128,1024]{3,2,1,0:T(8,128)(2,1)}, u32[]{:S(2)}, u32[]{:S(2)}) async-start(bf16[8,2,128,1024]{3,2,1,0:T(8,128)(2,1)} %bitcast.62), calls=%async_computation.1 | async-start | bytes 8388608 | tf_op jit(solution)/shard_map/gather_panels/all_to_all | solution.py:350
  25.2 6.4 %collective-permute-start.2 = (s32[8,8]{1,0:T(8,128)S(1)}, s32[8,8]{1,0:T(8,128)S(1)}, u32[]{:S(2)}, u32[]{:S(2)}) collective-permute-start(s32[8,8]{1,0:T(8,128)S(1)} %get-tuple-element.73), channel_id=1, source_target_pairs={{0,24},{8,0},{16,8},{24,16},{32,56},{40,32},{48,40},{56,48},{64,88... | collective-permute-start | bytes 776 | tf_op jit(solution)/shard_map/all_requests/ppermute | solution.py:343
  29.5 4.8 %collective-permute-start = (s32[8,8]{1,0:T(8,128)S(1)}, s32[8,8]{1,0:T(8,128)S(1)}, u32[]{:S(2)}, u32[]{:S(2)}) collective-permute-start(s32[8,8]{1,0:T(8,128)S(1)} %get-tuple-element.73), channel_id=1, source_target_pairs={{0,8},{8,16},{16,24},{24,0},{32,40},{40,48},{48,56},{56,32},{64,72... | collective-permute-start | bytes 776 | tf_op jit(solution)/shard_map/all_requests/ppermute | solution.py:343
  29.5 5.1 %collective-permute-start.1 = (s32[8,8]{1,0:T(8,128)S(1)}, s32[8,8]{1,0:T(8,128)S(1)}, u32[]{:S(2)}, u32[]{:S(2)}) collective-permute-start(s32[8,8]{1,0:T(8,128)S(1)} %get-tuple-element.73), channel_id=1, source_target_pairs={{0,16},{8,24},{16,0},{24,8},{32,48},{40,56},{48,32},{56,40},{64,80... | collective-permute-start | bytes 776 | tf_op jit(solution)/shard_map/all_requests/ppermute | solution.py:343
  34.8 5.5 %collective-permute-start.3 = (s32[4,8,8]{2,1,0:T(8,128)S(1)}, s32[4,8,8]{2,1,0:T(8,128)S(1)}, u32[]{:S(2)}, u32[]{:S(2)}) collective-permute-start(s32[4,8,8]{2,1,0:T(8,128)S(1)} %get-tuple-element.70), channel_id=1, source_target_pairs={{0,32},{8,40},{16,48},{24,56},{32,64},{40,72},{48,80},{56,88},{64,... | collective-permute-start | bytes 3080 | tf_op jit(solution)/shard_map/all_requests/ppermute | solution.py:343
  35.4 5.9 %collective-permute-start.4 = (s32[4,8,8]{2,1,0:T(8,128)S(1)}, s32[4,8,8]{2,1,0:T(8,128)S(1)}, u32[]{:S(2)}, u32[]{:S(2)}) collective-permute-start(s32[4,8,8]{2,1,0:T(8,128)S(1)} %get-tuple-element.70), channel_id=1, source_target_pairs={{0,64},{8,72},{16,80},{24,88},{32,96},{40,104},{48,112},{56,120},{... | collective-permute-start | bytes 3080 | tf_op jit(solution)/shard_map/all_requests/ppermute | solution.py:343
  39.4 3.7 %collective-permute-start.5 = (s32[4,8,8]{2,1,0:T(8,128)S(1)}, s32[4,8,8]{2,1,0:T(8,128)S(1)}, u32[]{:S(2)}, u32[]{:S(2)}) collective-permute-start(s32[4,8,8]{2,1,0:T(8,128)S(1)} %get-tuple-element.70), channel_id=1, source_target_pairs={{0,96},{8,104},{16,112},{24,120},{32,0},{40,8},{48,16},{56,24},{64... | collective-permute-start | bytes 3080 | tf_op jit(solution)/shard_map/all_requests/ppermute | solution.py:343
  80.7 1.0 copy-start
  81.7 26.3 %all-to-all-start.2 = ((bf16[16,17,16,128]{3,2,1,0:T(8,128)(2,1)}), bf16[16,17,16,128]{3,2,1,0:T(8,128)(2,1)S(1)}, u32[]{:S(2)}, u32[]{:S(2)}) async-start(bf16[16,17,16,128]{3,2,1,0:T(8,128)(2,1)} %copy-done), calls=%async_computation.2 | async-start | bytes 2228224 | tf_op jit(solution)/shard_map/split_pieces/all_to_all | solution.py:350
  108.0 3.7 %collective-permute-start.6 = (bf16[16,17,16,128]{3,2,1,0:T(8,128)(2,1)S(1)}, bf16[16,17,16,128]{3,2,1,0:T(8,128)(2,1)S(1)}, u32[]{:S(2)}, u32[]{:S(2)}) collective-permute-start(bf16[16,17,16,128]{3,2,1,0:T(8,128)(2,1)S(1)} %all-to-all-done.2.mine), channel_id=1, source_target_pairs={{0,1},{1,0},{2,3},{3,2},{4,5},{5,4},{6,7},{7,6},{8,9},{9,8},{10,11... | collective-permute-start | bytes 3342344 | tf_op jit(solution)/shard_map/split_pieces/ppermute | solution.py:420
  108.0 22.6 %all-to-all-start.3 = ((bf16[16,16,16,128]{3,2,1,0:T(8,128)(2,1)}), bf16[16,16,16,128]{3,2,1,0:T(8,128)(2,1)S(1)}, u32[]{:S(2)}, u32[]{:S(2)}) async-start(bf16[16,16,16,128]{3,2,1,0:T(8,128)(2,1)} %score.3), calls=%async_computation.3 | async-start | bytes 2097152 | tf_op jit(solution)/shard_map/split_pieces/all_to_all | solution.py:350
  115.6 1.0 copy-start.1
  116.6 16.6 %collective-permute-start.7 = (bf16[129,16,128]{2,1,0:T(8,128)(2,1)}, bf16[129,16,128]{2,1,0:T(8,128)(2,1)S(1)}, u32[]{:S(2)}, u32[]{:S(2)}) collective-permute-start(bf16[129,16,128]{2,1,0:T(8,128)(2,1)} %get-tuple-element.38), channel_id=1, source_target_pairs={{0,4},{1,5},{2,6},{3,7},{4,0},{5,1},{6,2},{7,3},{8,12},{9,13},{10,... | collective-permute-start | bytes 1585160 | tf_op jit(solution)/shard_map/sum_over_chips/ppermute | solution.py:424
  118.7 24.8 %collective-permute-start.8 = (bf16[129,16,128]{2,1,0:T(8,128)(2,1)}, bf16[129,16,128]{2,1,0:T(8,128)(2,1)S(1)}, u32[]{:S(2)}, u32[]{:S(2)}) collective-permute-start(bf16[129,16,128]{2,1,0:T(8,128)(2,1)} %get-tuple-element.39), channel_id=1, source_target_pairs={{0,2},{1,3},{2,4},{3,5},{4,6},{5,7},{6,0},{7,1},{8,10},{9,11},{10,... | collective-permute-start | bytes 1585160 | tf_op jit(solution)/shard_map/sum_over_chips/ppermute | solution.py:424
  119.4 24.7 %collective-permute-start.9 = (bf16[129,16,128]{2,1,0:T(8,128)(2,1)}, bf16[129,16,128]{2,1,0:T(8,128)(2,1)S(1)}, u32[]{:S(2)}, u32[]{:S(2)}) collective-permute-start(bf16[129,16,128]{2,1,0:T(8,128)(2,1)} %get-tuple-element.40), channel_id=1, source_target_pairs={{0,6},{1,7},{2,0},{3,1},{4,2},{5,3},{6,4},{7,5},{8,14},{9,15},{10,... | collective-permute-start | bytes 1585160 | tf_op jit(solution)/shard_map/sum_over_chips/ppermute | solution.py:424
  144.8 2.7 %collective-permute-start.10 = (bf16[16,16,16,128]{3,2,1,0:T(8,128)(2,1)S(1)}, bf16[16,16,16,128]{3,2,1,0:T(8,128)(2,1)S(1)}, u32[]{:S(2)}, u32[]{:S(2)}) collective-permute-start(bf16[16,16,16,128]{3,2,1,0:T(8,128)(2,1)S(1)} %all-to-all-done.3.mine), channel_id=1, source_target_pairs={{0,1},{1,0},{2,3},{3,2},{4,5},{5,4},{6,7},{7,6},{8,9},{9,8},{10,11... | collective-permute-start | bytes 3145736 | tf_op jit(solution)/shard_map/split_pieces/ppermute | solution.py:427
  149.7 5.4 %copy-start.6 = (bf16[128,16,128]{2,1,0:T(8,128)(2,1)}, bf16[128,16,128]{2,1,0:T(8,128)(2,1)S(1)}, u32[]{:S(2)}) copy-start(bf16[128,16,128]{2,1,0:T(8,128)(2,1)S(1)} %get-tuple-element.53) | copy-start | bytes 1572868
  149.7 5.4 %copy-start.7 = (bf16[128,16,128]{2,1,0:T(8,128)(2,1)}, bf16[128,16,128]{2,1,0:T(8,128)(2,1)S(1)}, u32[]{:S(2)}) copy-start(bf16[128,16,128]{2,1,0:T(8,128)(2,1)S(1)} %get-tuple-element.52) | copy-start | bytes 1572868
  150.5 1.2 copy-start.2
  151.7 1.0 copy-start.4
  155.1 19.4 %all-to-all-start.4 = ((bf16[16,9,16,128]{3,2,1,0:T(8,128)(2,1)}), bf16[16,9,16,128]{3,2,1,0:T(8,128)(2,1)S(1)}, u32[]{:S(2)}, u32[]{:S(2)}) async-start(bf16[16,9,16,128]{3,2,1,0:T(8,128)(2,1)} %get-tuple-element.49), calls=%async_computation.4 | async-start | bytes 1179648 | tf_op jit(solution)/shard_map/finish/all_to_all | solution.py:350
  162.0 16.7 %collective-permute-start.11 = (bf16[128,16,128]{2,1,0:T(8,128)(2,1)}, bf16[128,16,128]{2,1,0:T(8,128)(2,1)S(1)}, u32[]{:S(2)}, u32[]{:S(2)}) collective-permute-start(bf16[128,16,128]{2,1,0:T(8,128)(2,1)} %copy-done.7), channel_id=1, source_target_pairs={{0,4},{1,5},{2,6},{3,7},{4,0},{5,1},{6,2},{7,3},{8,12},{9,13},{10,... | collective-permute-start | bytes 1572872 | tf_op jit(solution)/shard_map/sum_over_chips/ppermute | solution.py:431
  164.1 24.0 %collective-permute-start.12 = (bf16[128,16,128]{2,1,0:T(8,128)(2,1)}, bf16[128,16,128]{2,1,0:T(8,128)(2,1)S(1)}, u32[]{:S(2)}, u32[]{:S(2)}) collective-permute-start(bf16[128,16,128]{2,1,0:T(8,128)(2,1)} %copy-done.6), channel_id=1, source_target_pairs={{0,2},{1,3},{2,4},{3,5},{4,6},{5,7},{6,0},{7,1},{8,10},{9,11},{10,... | collective-permute-start | bytes 1572872 | tf_op jit(solution)/shard_map/sum_over_chips/ppermute | solution.py:431
  165.3 23.4 %collective-permute-start.13 = (bf16[128,16,128]{2,1,0:T(8,128)(2,1)}, bf16[128,16,128]{2,1,0:T(8,128)(2,1)S(1)}, u32[]{:S(2)}, u32[]{:S(2)}) collective-permute-start(bf16[128,16,128]{2,1,0:T(8,128)(2,1)} %copy-done.5), channel_id=1, source_target_pairs={{0,6},{1,7},{2,0},{3,1},{4,2},{5,3},{6,4},{7,5},{8,14},{9,15},{10,... | collective-permute-start | bytes 1572872 | tf_op jit(solution)/shard_map/sum_over_chips/ppermute | solution.py:431
  (2 other events, 1.6 us)

commit v4 on v1

v4 whole, which is shorter than its diff:
```python
import functools

import jax
import jax.numpy as jnp
from jax import lax
from jax.experimental import pallas as pl
from jax.experimental.pallas import tpu as pltpu
from jax.sharding import PartitionSpec as P

PANEL = 128
GROUP = 1024
CAND = 4
GROUPS_DEV = 2
REQ = CAND * GROUPS_DEV
PAN_DEV = 64
WIDTH = 1024
N_CENT = 8
CHIPS = 4
N_PTS = 16
SIDE = 4
ROWS = 16
HALF = 512
LANE = 128
TILES = HALF // LANE
SEND_TILES = REQ * TILES + 1
DENSE = PAN_DEV * TILES
LISTED = 36

sharpness_divisor = 16.0
evenness_coefficient = 1.0
prior_mass = 1.0

BF16 = jnp.bfloat16
F32 = jnp.float32
MIB = 1 << 20


def params(mib):
    return pltpu.CompilerParams(vmem_limit_bytes=mib * MIB)


def pick_kernel(ids, table, out, held, sems):
    def fetch(n):
        return pltpu.make_async_copy(table.at[ids[n]], held.at[n], sems.at[0, n])

    def put(n):
        return pltpu.make_async_copy(held.at[n], out.at[n], sems.at[1, n])

    for n in range(ids.shape[0]):
        fetch(n).start()
    for n in range(ids.shape[0]):
        fetch(n).wait()
        put(n).start()
    for n in range(ids.shape[0]):
        put(n).wait()


def pick_panels(ids, table):
    count = ids.shape[0]
    return pl.pallas_call(
        pick_kernel,
        out_shape=jax.ShapeDtypeStruct((count, PANEL, WIDTH), BF16),
        in_specs=[pl.BlockSpec(memory_space=pltpu.SMEM), pl.BlockSpec(memory_space=pltpu.HBM)],
        out_specs=pl.BlockSpec(memory_space=pltpu.HBM),
        scratch_shapes=[pltpu.VMEM((count, PANEL, WIDTH), BF16), pltpu.SemaphoreType.DMA((2, count))],
        compiler_params=params(60),
        cost_estimate=pl.CostEstimate(flops=0, bytes_accessed=4 * count * PANEL * WIDTH, transcendentals=0),
    )(ids, table)


def whole(shape):
    return pl.BlockSpec(shape, lambda *_: (0,) * len(shape))


def smem_spec():
    return pl.BlockSpec(memory_space=pltpu.SMEM)


def score_kernel(target, points, c0, c1, c2, c3, surcharge, out, centers, shares, marks):
    del target
    group = pl.program_id(0)
    for j, panel in enumerate((c0, c1, c2, c3)):
        centers[j * PANEL : (j + 1) * PANEL, :] = panel[0]
    wide = centers[...].astype(F32)
    squares = jnp.sum(wide * wide, axis=1, keepdims=True)
    bias = squares * (1.0 / sharpness_divisor) + evenness_coefficient * surcharge[0]
    step = 256
    weights = jnp.zeros((CAND * PANEL, LANE), F32)
    for s in range(GROUP // step):
        block = points[s * step : (s + 1) * step, :]
        inner = lax.dot_general(centers[...], block, (((1,), (1,)), ((), ())), preferred_element_type=F32)
        logits = inner * (2.0 / sharpness_divisor) - bias
        highest = jnp.max(logits, axis=0, keepdims=True)
        raised = jnp.exp(logits - highest)
        scale = 1.0 / jnp.sum(raised, axis=0, keepdims=True)
        share = (raised * scale).astype(BF16)
        shares[:, s * step : (s + 1) * step] = share
        rounded = share.astype(F32)
        for part in range(step // LANE):
            weights = weights + rounded[:, part * LANE : (part + 1) * LANE]
    weight = jnp.sum(weights, axis=1, keepdims=True)
    coarse = weight.astype(BF16).astype(F32)
    fine = weight - coarse
    lane = lax.broadcasted_iota(jnp.int32, (PANEL, LANE), 1)

    @pl.when(group == 0)
    def _():
        marks[...] = jnp.zeros_like(marks)

    tile = marks[...]
    for j in range(CAND):
        place = group * CAND + j
        rows = slice(j * PANEL, (j + 1) * PANEL)
        tile = jnp.where(lane == place, coarse[rows], tile)
        tile = jnp.where(lane == REQ + place, fine[rows], tile)
    marks[...] = tile

    wide_step = 256
    for s in range(WIDTH // wide_step):
        part = lax.dot_general(
            shares[...], points[:, s * wide_step : (s + 1) * wide_step], (((1,), (0,)), ((), ())),
            preferred_element_type=F32,
        ).astype(BF16)
        for t in range(wide_step // LANE):
            column = s * (wide_step // LANE) + t
            half, tile_at = divmod(column, TILES)
            for j in range(CAND):
                for block_at in range(PANEL // ROWS):
                    row = j * PANEL + block_at * ROWS
                    out[block_at * 2 + half, (group * CAND + j) * TILES + tile_at] = part[
                        row : row + ROWS, t * LANE : (t + 1) * LANE
                    ]

    @pl.when(group == GROUPS_DEV - 1)
    def _():
        last = marks[...].astype(BF16)
        for block_at in range(PANEL // ROWS):
            for half in range(2):
                out[block_at * 2 + half, REQ * TILES] = last[block_at * ROWS : (block_at + 1) * ROWS]


def score(target, points, arrived, surcharge):
    def panel(j):
        return pl.BlockSpec((1, PANEL, WIDTH), lambda g, t: (t[g * CAND + j], 0, 0))

    return pl.pallas_call(
        score_kernel,
        grid_spec=pltpu.PrefetchScalarGridSpec(
            num_scalar_prefetch=1,
            grid=(GROUPS_DEV,),
            in_specs=[
                pl.BlockSpec((GROUP, WIDTH), lambda g, t: (g, 0)),
                panel(0), panel(1), panel(2), panel(3),
                pl.BlockSpec((1, CAND * PANEL, 1), lambda g, t: (g, 0, 0)),
            ],
            out_specs=pl.BlockSpec((N_PTS, SEND_TILES, ROWS, LANE), lambda g, t: (0, 0, 0, 0)),
            scratch_shapes=[
                pltpu.VMEM((CAND * PANEL, WIDTH), BF16),
                pltpu.VMEM((CAND * PANEL, GROUP), BF16),
                pltpu.VMEM((PANEL, LANE), F32),
            ],
        ),
        out_shape=jax.ShapeDtypeStruct((N_PTS, SEND_TILES, ROWS, LANE), BF16),
        compiler_params=params(48),
        cost_estimate=pl.CostEstimate(flops=4294967296, bytes_accessed=10 * MIB, transcendentals=1 << 20),
    )(target, points, arrived, arrived, arrived, arrived, surcharge)


def spread_kernel(rows, places, mine, mate, lanes, own, own_weights, out1, out2, out3, total):
    total[...] = jnp.zeros_like(total)
    sources = (mine, mate)
    for n, source in enumerate(sources):
        def add(s, carry, n=n, source=source):
            for i in range(REQ):
                at = places[(n * N_PTS + s) * REQ + i] * TILES
                total[pl.ds(at, TILES)] += source[s, i * TILES : (i + 1) * TILES].astype(F32)
            return carry

        lax.fori_loop(0, N_PTS, add, 0)
    panel = lax.broadcasted_iota(jnp.int32, (CHIPS * PAN_DEV, LANE), 0)
    weights = jnp.zeros((ROWS, CHIPS * PAN_DEV), F32)
    for n in range(2 * N_PTS):
        chosen = jnp.where(panel == lanes[n : n + 1, :], 1.0, 0.0).astype(BF16)
        weights = weights + lax.dot_general(
            sources[n // N_PTS][n % N_PTS, REQ * TILES], chosen, (((1,), (1,)), ((), ())),
            preferred_element_type=F32,
        )
    own[...] = total[0:DENSE]
    coarse = weights.astype(BF16)
    fine = (weights - coarse.astype(F32)).astype(BF16)
    own_weights[...] = weights[:, 0:LANE]
    for d, out in ((1, out1), (2, out2), (3, out3)):
        first = DENSE + (d - 1) * rows * TILES
        out[0 : rows * TILES] = total[first : first + rows * TILES].astype(BF16)
        out[rows * TILES, :, 0:PAN_DEV] = coarse[:, d * PAN_DEV : (d + 1) * PAN_DEV]
        out[rows * TILES, :, PAN_DEV:LANE] = fine[:, d * PAN_DEV : (d + 1) * PAN_DEV]


def spread(rows, places, mine, mate, lanes):
    chunk = jax.ShapeDtypeStruct((rows * TILES + 1, ROWS, LANE), BF16)
    return pl.pallas_call(
        functools.partial(spread_kernel, rows),
        grid=(1,),
        in_specs=[smem_spec()] + [whole(mine.shape)] * 2 + [whole((2 * N_PTS, LANE))],
        out_specs=[whole((DENSE, ROWS, LANE)), whole((ROWS, LANE))] + [whole(chunk.shape)] * 3,
        out_shape=[
            jax.ShapeDtypeStruct((DENSE, ROWS, LANE), F32), jax.ShapeDtypeStruct((ROWS, LANE), F32),
            chunk, chunk, chunk,
        ],
        scratch_shapes=[pltpu.VMEM(((PAN_DEV + 3 * rows + 1) * TILES, ROWS, LANE), F32)],
        compiler_params=params(48),
        cost_estimate=pl.CostEstimate(flops=1 << 22, bytes_accessed=8 * MIB, transcendentals=0),
    )(places, mine, mate, lanes)


def finish_kernel(rows, numbers, own, own_weights, in1, in2, in3, lanes, old, out, total):
    weights = own_weights[:, 0:PAN_DEV]
    panel = lax.broadcasted_iota(jnp.int32, (PAN_DEV, LANE), 0)
    total[...] = own[...]
    for d, arrived in enumerate((in1, in2, in3)):
        chosen = jnp.where(panel == lanes[d : d + 1, :], 1.0, 0.0).astype(BF16)
        weights = weights + lax.dot_general(
            arrived[rows * TILES], chosen, (((1,), (1,)), ((), ())), preferred_element_type=F32
        )
        first = 4 + d * rows

        def add(n, carry, arrived=arrived, first=first):
            at = numbers[first + n] * TILES
            total[pl.ds(at, TILES)] += arrived[pl.ds(n * TILES, TILES)].astype(F32)
            return carry

        lax.fori_loop(0, numbers[1 + d], add, 0)
    inverse = 1.0 / (weights + prior_mass)
    for q in range(PAN_DEV):
        scale = jnp.broadcast_to(inverse[:, q : q + 1], (ROWS, LANE))
        for t in range(TILES):
            previous = old[q, :, t * LANE : (t + 1) * LANE].astype(F32)
            fresh = (total[q * TILES + t] + prior_mass * previous) * scale
            out[q // CAND, (q % CAND) * TILES + t] = fresh.astype(BF16)
    coarse = weights.astype(BF16)
    fine = (weights - coarse.astype(F32)).astype(BF16)
    for p in range(N_PTS):
        out[p, CAND * TILES, :, 0:PAN_DEV] = coarse
        out[p, CAND * TILES, :, PAN_DEV:LANE] = fine


def finish(rows, numbers, own, own_weights, arrived, lanes, table):
    chunk = whole((rows * TILES + 1, ROWS, LANE))
    fresh = (N_PTS, CAND * TILES + 1, ROWS, LANE)
    return pl.pallas_call(
        functools.partial(finish_kernel, rows),
        grid_spec=pltpu.PrefetchScalarGridSpec(
            num_scalar_prefetch=1,
            grid=(1,),
            in_specs=[
                whole((DENSE, ROWS, LANE)), whole((ROWS, LANE)), chunk, chunk, chunk, whole((CHIPS - 1, LANE)),
                pl.BlockSpec((PAN_DEV, ROWS, HALF), lambda g, n: (0, n[0] // 2, n[0] % 2)),
            ],
            out_specs=whole(fresh),
            scratch_shapes=[pltpu.VMEM((DENSE, ROWS, LANE), F32)],
        ),
        out_shape=jax.ShapeDtypeStruct(fresh, BF16),
        compiler_params=params(48),
        cost_estimate=pl.CostEstimate(flops=1 << 22, bytes_accessed=6 * MIB, transcendentals=0),
    )(numbers, own, own_weights, *arrived, lanes, table)


def place_kernel(me, pieces, out, loads):
    for block_at in range(PANEL // ROWS):
        for half in range(2):
            for q in range(CAND):
                for t in range(TILES):
                    column = half * HALF + t * LANE
                    out[q, block_at * ROWS : (block_at + 1) * ROWS, column : column + LANE] = pieces[
                        block_at * 2 + half, q * TILES + t
                    ]
    lane = lax.broadcasted_iota(jnp.int32, (ROWS, LANE), 1)
    row = lax.broadcasted_iota(jnp.int32, (ROWS, LANE), 0)
    wanted = me[0] * CAND + row
    chosen = jnp.where((row < CAND) & (lane % PAN_DEV == wanted), 1.0, 0.0).astype(BF16)
    for block_at in range(PANEL // ROWS):
        pair = pieces[block_at * 2, CAND * TILES]
        part = lax.dot_general(chosen, pair, (((1,), (1,)), ((), ())), preferred_element_type=F32)
        loads[:, block_at * ROWS : (block_at + 1) * ROWS] = part[0:8]


def place(me, pieces):
    return pl.pallas_call(
        place_kernel,
        grid=(1,),
        in_specs=[smem_spec(), whole(pieces.shape)],
        out_specs=[whole((CAND, PANEL, WIDTH)), whole((8, PANEL))],
        out_shape=[
            jax.ShapeDtypeStruct((CAND, PANEL, WIDTH), BF16),
            jax.ShapeDtypeStruct((8, PANEL), F32),
        ],
        compiler_params=params(32),
        cost_estimate=pl.CostEstimate(flops=1 << 20, bytes_accessed=2 * MIB, transcendentals=0),
    )(me, pieces)


def shift(dy, dk):
    return [(y * 2 + k, ((y + dy) % CHIPS) * 2 + (k + dk) % 2) for y in range(CHIPS) for k in range(2)]


def spread_out(x, place, dz, dx):
    held = [x]
    for d in range(1, SIDE):
        pairs = [
            (ix * SIDE + iz, (ix + d * dx) % SIDE * SIDE + (iz + d * dz) % SIDE)
            for ix in range(SIDE)
            for iz in range(SIDE)
        ]
        held.append(lax.ppermute(x, "pts", pairs))
    held = jnp.stack(held)
    at = (place - jnp.arange(SIDE, dtype=jnp.int32)) % SIDE
    return jnp.stack([jnp.sum(jnp.where((at == n).reshape((SIDE,) + (1,) * x.ndim), held, 0), axis=0) for n in range(SIDE)])


def exchange(x, axis):
    return lax.all_to_all(x, axis, split_axis=0, concat_axis=0, tiled=True)


def local(points, centroids, prev_loads, candidates, panel_home):
    me = lax.axis_index("pts")
    here = lax.axis_index("cent")
    chip, core = here // 2, here % 2
    shelf = centroids.reshape(PAN_DEV, PANEL, WIDTH)

    with jax.named_scope("requests"):
        wanted_ids = candidates.reshape(REQ)
        slots = jnp.sum(
            jnp.where(wanted_ids[:, None] == jnp.arange(panel_home.shape[0], dtype=jnp.int32), panel_home[None, :], 0),
            axis=1,
        )
        owners, local_ids = slots // PAN_DEV, slots % PAN_DEV
        target = owners * GROUPS_DEV + jnp.arange(REQ, dtype=jnp.int32) // CAND
        spots = jnp.arange(N_CENT * GROUPS_DEV, dtype=jnp.int32)
        wanted = jnp.sum(jnp.where(target[None, :] == spots[:, None], local_ids[None, :], 0), axis=1)
        ask = jnp.stack(
            [
                jnp.pad(wanted.reshape(N_CENT, GROUPS_DEV), ((0, 0), (0, LANE - GROUPS_DEV))),
                jnp.broadcast_to(jnp.pad(owners, (0, LANE - REQ)), (N_CENT, LANE)),
                jnp.broadcast_to(jnp.pad(local_ids, (0, LANE - REQ)), (N_CENT, LANE)),
            ],
            axis=1,
        ).astype(BF16)
        ask = jnp.pad(ask, ((0, 0), (0, ROWS - 3), (0, 0))).reshape(N_CENT, 1, ROWS, LANE)
        table = jnp.broadcast_to(
            prev_loads.reshape(1, PAN_DEV // ROWS, ROWS, LANE), (N_CENT, PAN_DEV // ROWS, ROWS, LANE)
        )
        answered = exchange(jnp.concatenate([table, ask], axis=1), "cent")
        asked = answered[:, PAN_DEV // ROWS, 0, 0:GROUPS_DEV].astype(jnp.int32).reshape(-1)

    with jax.named_scope("gather_panels"):
        arrived = exchange(pick_panels(asked, shelf).reshape(N_CENT, GROUPS_DEV, PANEL, WIDTH), "cent")
        arrived = arrived.reshape(N_CENT * GROUPS_DEV, PANEL, WIDTH)

    with jax.named_scope("all_requests"):
        ring = answered[:, PAN_DEV // ROWS, 1:3, 0:REQ].astype(jnp.int32)
        ring = ring[:, 0] * PAN_DEV + ring[:, 1]
        line = spread_out(ring, me % SIDE, 1, 0)
        everyone = spread_out(line, me // SIDE, 0, 1).reshape(N_PTS, N_CENT, REQ)
        numbers = jnp.arange(N_CENT * PAN_DEV, dtype=jnp.int32)
        by_chip = jnp.transpose(everyone.reshape(N_PTS, CHIPS, 2 * REQ), (1, 0, 2)).reshape(CHIPS, -1)
        asked_by = jnp.any(by_chip[:, :, None] == numbers, axis=1).reshape(CHIPS, N_CENT, PAN_DEV)
        below = jnp.arange(PAN_DEV)[:, None] < jnp.arange(PAN_DEV)[None, :]
        ranks = lax.dot_general(
            asked_by.astype(BF16), below.astype(BF16), (((2,), (0,)), ((), ())), preferred_element_type=F32
        ).astype(jnp.int32)
        lengths = jnp.sum(asked_by.astype(jnp.int32), axis=2)
        off_chip = jnp.arange(N_CENT)[None, :] // 2 != jnp.arange(CHIPS)[:, None]
        too_long = jnp.any(off_chip & (lengths > LISTED))

        pair = jnp.stack(
            [lax.dynamic_index_in_dim(everyone, at, 1, keepdims=False) for at in (here, chip * 2 + 1 - core)]
        ).reshape(2 * N_PTS, REQ)
        owner = pair // PAN_DEV
        relative = (owner // 2 - chip) % CHIPS
        my_ranks = lax.dynamic_index_in_dim(ranks, chip, 0, keepdims=False).reshape(-1)
        rank = jnp.sum(jnp.where(pair[:, :, None] == numbers, my_ranks, 0), axis=2)
        ours = owner % 2 == core

        def sender(rows, rank):
            at = jnp.where(relative == 0, pair % PAN_DEV, rank)
            known = ours & ((relative == 0) | (rank < rows))
            first = jnp.where(relative == 0, 0, PAN_DEV + (relative - 1) * rows)
            places = jnp.where(known, first + at, PAN_DEV + 3 * rows).reshape(-1)
            lane = jnp.where(known, relative * PAN_DEV + at, CHIPS * PAN_DEV)
            lanes = jnp.pad(
                jnp.concatenate([lane, lane], axis=1), ((0, 0), (0, LANE - 2 * REQ)), constant_values=CHIPS * PAN_DEV
            )
            return places, lanes

        def receiver(rows, count, panels):
            numbers = jnp.concatenate([me.reshape(1), count, panels[:, :rows].reshape(-1)])
            lane = jnp.where(jnp.arange(PAN_DEV) < jnp.minimum(count, rows)[:, None], panels, PAN_DEV)
            return numbers, jnp.concatenate([lane, lane], axis=1)

        behind = [(chip - d) % CHIPS for d in range(1, CHIPS)]
        pick = lambda x, y: lax.dynamic_index_in_dim(lax.dynamic_index_in_dim(x, y, 0, False), here, 0, False)
        named = jnp.stack([pick(asked_by, y) for y in behind])
        order = jnp.stack([pick(ranks, y) for y in behind])
        spots = jnp.arange(PAN_DEV, dtype=jnp.int32)
        listed = jnp.sum(
            jnp.where(named[:, None, :] & (order[:, None, :] == spots[None, :, None]), spots, 0), axis=2
        )
        count = jnp.minimum(jnp.sum(named.astype(jnp.int32), axis=1), LISTED)
        short = sender(LISTED, rank) + receiver(LISTED, count, listed)
        target, too_long, short = lax.optimization_barrier((target, too_long, short))

    with jax.named_scope("loads"):
        load_table = answered[:, : PAN_DEV // ROWS].reshape(N_CENT * PAN_DEV, PANEL)
        loads = jnp.take(load_table, slots, axis=0, mode="clip").astype(F32)
        surcharge = jnp.log(loads).reshape(GROUPS_DEV, CAND * PANEL, 1)

    with jax.named_scope("score"):
        pieces = score(target, points, arrived, surcharge)

    with jax.named_scope("split_pieces"):
        mine = exchange(pieces, "pts")
        mate = lax.ppermute(mine, "cent", shift(0, 1))

    def sum_over_chips(rows, places, lanes, numbers, back_lanes):
        own, own_weights, *far = spread(rows, places, mine, mate, lanes)
        back = [lax.ppermute(far[d - 1], "cent", shift(d, 0)) for d in range(1, CHIPS)]
        return finish(rows, numbers, own, own_weights, back, back_lanes, shelf)

    def send_all():
        everything = jnp.broadcast_to(spots, (CHIPS - 1, PAN_DEV))
        count = jnp.full((CHIPS - 1,), PAN_DEV, jnp.int32)
        return sum_over_chips(PAN_DEV, *sender(PAN_DEV, pair % PAN_DEV), *receiver(PAN_DEV, count, everything))

    with jax.named_scope("sum_over_chips"):
        fresh = lax.cond(too_long, send_all, lambda: sum_over_chips(LISTED, *short))

    with jax.named_scope("place"):
        new_centroids, new_loads = place(me.reshape(1), exchange(fresh, "pts"))
    return new_centroids.reshape(CAND * PANEL, WIDTH), new_loads[0:CAND].reshape(CAND * PANEL)


def solution(mesh):
    placed = (P(("pts", "cent"), None), P("cent", None), P("cent"), P(("pts", "cent"), None), P())
    return jax.shard_map(
        local,
        mesh=mesh,
        in_specs=placed,
        out_specs=(P(("cent", "pts"), None), P(("cent", "pts"))),
        check_vma=False,
    )
```

time: 333 us -> 188 us (0.56)
  Pallas kernels: 148 us -> 23.9 us
  waiting for transfers between devices: 96.5 us -> 67.5 us
  starting transfers between devices: 10.7 us -> 26.5 us
  blocking collectives: 66.8 us -> 57.7 us
    pallas_call x1, Pallas kernels: 129 us -> 5.49 us  [pick_panels(): pl.pallas_call(pick_kernel, out_shape=jax.ShapeDtypeStruct((count, PANEL,...]
    all_to_all x1 -> x2, waiting for transfers between devices: 46.7 us -> 31 us  [exchange(): return lax.all_to_all(x, axis, split_axis=0, concat_axis=0, tiled=True)]
    ppermute x3 -> x9, waiting for transfers between devices: 45.5 us -> 32.7 us  [the longest x3 27.8 us: sum_over_chips(): lax.ppermute(far[d - 1], 'cent', shift(d, 0))]
    ppermute x3 -> x9, starting transfers between devices: 4.13 us -> 14.4 us  [the longest x6 10.9 us: spread_out(): held.append(lax.ppermute(x, 'pts', pairs))]
    all_to_all x3 -> x2, blocking collectives: 66.8 us -> 57.7 us  [exchange(): return lax.all_to_all(x, axis, split_axis=0, concat_axis=0, tiled=True)]
    all_to_all x1 -> x2, starting transfers between devices: 6.54 us -> 12 us  [exchange(): return lax.all_to_all(x, axis, split_axis=0, concat_axis=0, tiled=True)]
  transfers between devices with their start and end apart: 5 -> 12, of which waited for: 5 -> 7; matrix products, arithmetic and copies ran while one was open for 0% -> 3% of each run, Pallas kernels for 0% -> 0%
where the time goes in v4:
time: 188 us; the launch traced here: 187 us
  waiting for transfers between devices  67.5 us (36%)
  blocking collectives  57.7 us (31%)
  starting transfers between devices  26.5 us (14%)
  Pallas kernels  23.9 us (13%)
  local copies, waits for them, and re-layouts  4.74 us (3%)
  other arithmetic  4.59 us (2%)
    all_to_all x2, blocking collectives, exchange(): return lax.all_to_all(x, axis, split_axis=0, concat_axis=0, tiled=True)  57.7 us
    all_to_all x2, waiting for transfers between devices, exchange(): return lax.all_to_all(x, axis, split_axis=0, concat_axis=0, tiled=True)  31 us
    ppermute x3, waiting for transfers between devices, sum_over_chips(): lax.ppermute(far[d - 1], 'cent', shift(d, 0))  27.8 us
    all_to_all x2, starting transfers between devices, exchange(): return lax.all_to_all(x, axis, split_axis=0, concat_axis=0, tiled=True)  12 us
    ppermute x6, starting transfers between devices, spread_out(): held.append(lax.ppermute(x, 'pts', pairs))  10.9 us
    pallas_call x1, Pallas kernels, score(): pl.pallas_call(score_kernel, grid_spec=pltpu.PrefetchScalarGridSpec(num_s...  8.93 us
    pallas_call x1, Pallas kernels, pick_panels(): pl.pallas_call(pick_kernel, out_shape=jax.ShapeDtypeStruct((count, PANEL,...  5.49 us
    ppermute x6, waiting for transfers between devices, spread_out(): held.append(lax.ppermute(x, 'pts', pairs))  4.93 us
  transfers between devices with their start and end apart: 12, of which 7 were waited for; matrix products, arithmetic and copies ran while one was open for 3% of the time, Pallas kernels for 0%

profile of v4, /device:TPU:24, one launch (start us, length us, event | category | flops | bytes accessed | tf_op | source)
XLA Modules:
  0.0 186.7 jit_solution(9785618113431317050)
XLA Ops:
  1.4 0.9 select_reduce_fusion.10
  4.0 4.7 %all-to-all-start = ((bf16[8,5,16,128]{3,2,1,0:T(8,128)(2,1)}), bf16[8,5,16,128]{3,2,1,0:T(8,128)(2,1)S(1)}, u32[]{:S(2)}, u32[]{:S(2)}) async-start(bf16[8,5,16,128]{3,2,1,0:T(8,128)(2,1)} %pad_maximum_fusion), calls=%async_computation | async-start | bytes 327680 | tf_op jit(solution)/shard_map/requests/all_to_all | solution.py:321
  8.9 4.1 %all-to-all-done = bf16[8,5,16,128]{3,2,1,0:T(8,128)(2,1)S(1)} async-done(((bf16[8,5,16,128]{3,2,1,0:T(8,128)(2,1)}), bf16[8,5,16,128]{3,2,1,0:T(8,128)(2,1)S(1)}, u32[]{:S(2)}, u32[]{:S(2)}) %all-to-all-start) | async-done | bytes 163872 | tf_op jit(solution)/shard_map/requests/all_to_all | solution.py:321
  13.7 5.5 %gather_panels.1 = bf16[16,128,1024]{2,1,0:T(8,128)(2,1)} custom-call(s32[16]{0:T(128)} %reshape.288.ids, bf16[64,128,1024]{2,1,0:T(8,128)(2,1)} %bitcast.64), custom_call_target="tpu_custom_call" | custom-call | bytes 8388608 | tf_op jit(solution)/shard_map/gather_panels/pallas_call | solution.py:60
  19.2 7.3 %all-to-all-start.1 = ((bf16[8,2,128,1024]{3,2,1,0:T(8,128)(2,1)}), bf16[8,2,128,1024]{3,2,1,0:T(8,128)(2,1)}, u32[]{:S(2)}, u32[]{:S(2)}) async-start(bf16[8,2,128,1024]{3,2,1,0:T(8,128)(2,1)} %bitcast.67), calls=%async_computation.1 | async-start | bytes 8388608 | tf_op jit(solution)/shard_map/gather_panels/all_to_all | solution.py:321
  26.5 3.4 %collective-permute-start.8 = (s32[8,8]{1,0:T(8,128)S(1)}, s32[8,8]{1,0:T(8,128)S(1)}, u32[]{:S(2)}, u32[]{:S(2)}) collective-permute-start(s32[8,8]{1,0:T(8,128)S(1)} %get-tuple-element.150), channel_id=1, source_target_pairs={{0,24},{8,0},{16,8},{24,16},{32,56},{40,32},{48,40},{56,48},{64,88... | collective-permute-start | bytes 776 | tf_op jit(solution)/shard_map/all_requests/ppermute | solution.py:314
  30.1 0.9 collective-permute-start.6
  31.5 3.6 %collective-permute-done.7 = s32[8,8]{1,0:T(8,128)S(1)} collective-permute-done((s32[8,8]{1,0:T(8,128)S(1)}, s32[8,8]{1,0:T(8,128)S(1)}, u32[]{:S(2)}, u32[]{:S(2)}) %collective-permute-start.7) | collective-permute-done | bytes 288 | tf_op jit(solution)/shard_map/all_requests/ppermute | solution.py:314
  35.2 3.2 %collective-permute-start.10 = (s32[4,8,8]{2,1,0:T(8,128)S(1)}, s32[4,8,8]{2,1,0:T(8,128)S(1)}, u32[]{:S(2)}, u32[]{:S(2)}) collective-permute-start(s32[4,8,8]{2,1,0:T(8,128)S(1)} %get-tuple-element.147), channel_id=1, source_target_pairs={{0,64},{8,72},{16,80},{24,88},{32,96},{40,104},{48,112},{56,120},{... | collective-permute-start | bytes 3080 | tf_op jit(solution)/shard_map/all_requests/ppermute | solution.py:314
  38.5 3.2 %collective-permute-start.11 = (s32[4,8,8]{2,1,0:T(8,128)S(1)}, s32[4,8,8]{2,1,0:T(8,128)S(1)}, u32[]{:S(2)}, u32[]{:S(2)}) collective-permute-start(s32[4,8,8]{2,1,0:T(8,128)S(1)} %get-tuple-element.147), channel_id=1, source_target_pairs={{0,96},{8,104},{16,112},{24,120},{32,0},{40,8},{48,16},{56,24},{64... | collective-permute-start | bytes 3080 | tf_op jit(solution)/shard_map/all_requests/ppermute | solution.py:314
  42.1 1.3 collective-permute-done.9
  47.3 26.9 %all-to-all-done.1 = bf16[8,2,128,1024]{3,2,1,0:T(8,128)(2,1)} async-done(((bf16[8,2,128,1024]{3,2,1,0:T(8,128)(2,1)}), bf16[8,2,128,1024]{3,2,1,0:T(8,128)(2,1)}, u32[]{:S(2)}, u32[]{:S(2)}) %all-to-all-start.1) | async-done | bytes 4194336 | tf_op jit(solution)/shard_map/gather_panels/all_to_all | solution.py:321
  74.2 8.9 %score.1 = bf16[16,33,16,128]{3,2,1,0:T(8,128)(2,1)S(1)} custom-call(s32[8]{0:T(128)S(1)} %get-tuple-element.74.target, bf16[2048,1024]{1,0:T(8,128)(2,1)} %points.1, bf16[16,128,1024]{2,1,0:T(8,128)(2,1)} %bitcast.37.c0.c1.c2.c3, bf16[16,128,1024]{2,1,0:T(8,128)(2,1)} %bitcast.37.c0.c1.c2.c3, bf16[16,128,1024]{2,1,0:T(8,128)(2,1)} %bitcast.37.c0.c1.c2.c3, ...), custom_call_target="tpu_custom_call" | custom-call | flops 4294967296 | bytes 10485760 | tf_op jit(solution)/shard_map/score/pallas_call | solution.py:146
  83.1 36.0 %all_to_all.20 = bf16[16,33,16,128]{3,2,1,0:T(8,128)(2,1)S(1)} all-to-all(bf16[16,33,16,128]{3,2,1,0:T(8,128)(2,1)S(1)} %score.1), channel_id=1, replica_groups=mesh['pts'=16,'cent'=8] {'pts'}, dimensions={0} | all-to-all | bytes 4325376 | tf_op jit(solution)/shard_map/split_pieces/all_to_all | solution.py:321
  119.9 3.7 %collective-permute-done.12 = bf16[16,33,16,128]{3,2,1,0:T(8,128)(2,1)} collective-permute-done((bf16[16,33,16,128]{3,2,1,0:T(8,128)(2,1)S(1)}, bf16[16,33,16,128]{3,2,1,0:T(8,128)(2,1)}, u32[]{:S(2)}, u32[]{:S(2)}) %collective-permute-start.12) | collective-permute-done | bytes 2162720 | tf_op jit(solution)/shard_map/split_pieces/ppermute | solution.py:422
  123.6 39.7 %conditional.1 = (bf16[16,17,16,128]{3,2,1,0:T(8,128)(2,1)}) conditional(s32[]{:T(128)} %convert_element_type.46, (s32[256]{0:T(256)S(1)}, bf16[16,33,16,128]{3,2,1,0:T(8,128)(2,1)S(1)}, bf16[16,33,16,128]{3,2,1,0:T(8,128)(2,1)}, s32[32,128]{1,0:T(8,128)S(1)}, s32[112]{0:T(128)S(1)}, /*index=5*/s32[3,128]{1,0:T(4,128)S(1)}, ...), branch_computations={%region_16.17_spmd, %region_17.18_spmd} | conditional | flops 8396488 | bytes 36002384 | solution.py:435
  123.6 4.2 %branch_0_fun.2 = (f32[256,16,128]{2,1,0:T(8,128)S(1)}, f32[16,128]{1,0:T(8,128)S(1)}, bf16[145,16,128]{2,1,0:T(8,128)(2,1)S(1)}, bf16[145,16,128]{2,1,0:T(8,128)(2,1)S(1)}, bf16[145,16,128]{2,1,0:T(8,128)(2,1)S(1)}) custom-call(s32[256]{0:T(256)S(1)} %get-tuple-element.20.places, bf16[16,33,16,128]{3,2,1,0:T(8,128)(2,1)S(1)} %get-tuple-element.21.mine, ...), custom_call_target="tpu_custom_call" | custom-call | flops 4194304 | bytes 8388608 | tf_op jit(solution)/shard_map/sum_over_chips/cond/branch_0_fun/pallas_call | solution.py:201
  127.8 2.1 %collective-permute-start = (bf16[145,16,128]{2,1,0:T(8,128)(2,1)S(1)}, bf16[145,16,128]{2,1,0:T(8,128)(2,1)S(1)}, u32[]{:S(2)}, u32[]{:S(2)}) collective-permute-start(bf16[145,16,128]{2,1,0:T(8,128)(2,1)S(1)} %get-tuple-element.42), channel_id=1, source_target_pairs={{0,2},{1,3},{2,4},{3,5},{4,6},{5,7},{6,0},{7,1},{8,10},{9,11},{10,... | collective-permute-start | bytes 1781768 | tf_op jit(solution)/shard_map/sum_over_chips/cond/branch_0_fun/ppermute | solution.py:426
  130.2 1.2 collective-permute-start.2
  131.3 24.4 %collective-permute-done.in1 = bf16[145,16,128]{2,1,0:T(8,128)(2,1)S(1)} collective-permute-done((bf16[145,16,128]{2,1,0:T(8,128)(2,1)S(1)}, bf16[145,16,128]{2,1,0:T(8,128)(2,1)S(1)}, u32[]{:S(2)}, u32[]{:S(2)}) %collective-permute-start) | collective-permute-done | bytes 593952 | tf_op jit(solution)/shard_map/sum_over_chips/cond/branch_0_fun/ppermute | solution.py:426
  155.7 3.4 %collective-permute-done.2.in3 = bf16[145,16,128]{2,1,0:T(8,128)(2,1)S(1)} collective-permute-done((bf16[145,16,128]{2,1,0:T(8,128)(2,1)S(1)}, bf16[145,16,128]{2,1,0:T(8,128)(2,1)S(1)}, u32[]{:S(2)}, u32[]{:S(2)}) %collective-permute-start.2) | collective-permute-done | bytes 593952 | tf_op jit(solution)/shard_map/sum_over_chips/cond/branch_0_fun/ppermute | solution.py:426
  159.2 4.1 %branch_0_fun.3 = bf16[16,17,16,128]{3,2,1,0:T(8,128)(2,1)} custom-call(s32[112]{0:T(128)S(1)} %get-tuple-element.19.numbers, f32[256,16,128]{2,1,0:T(8,128)S(1)} %get-tuple-element.40.own, f32[16,128]{1,0:T(8,128)S(1)} %get-tuple-element.41.own_weights, bf16[145,16,128]{2,1,0:T(8,128)(2,1)S(1)} %collective-permute-done.in1, ...), custom_call_target="tpu_custom_call" | custom-call | flops 4194304 | bytes 6291456 | tf_op jit(solution)/shard_map/sum_over_chips/cond/branch_0_fun/pallas_call | solution.py:250
  163.2 21.7 %all_to_all.21.pieces = bf16[16,17,16,128]{3,2,1,0:T(8,128)(2,1)S(1)} all-to-all(bf16[16,17,16,128]{3,2,1,0:T(8,128)(2,1)} %get-tuple-element.156), channel_id=1, replica_groups=mesh['pts'=16,'cent'=8] {'pts'}, dimensions={0} | all-to-all | bytes 2228224 | tf_op jit(solution)/shard_map/place/all_to_all | solution.py:321
  184.9 1.2 place.1
  (83 shorter events, 9.0 us)
Async XLA Ops:
  4.0 9.1 %all-to-all-start = ((bf16[8,5,16,128]{3,2,1,0:T(8,128)(2,1)}), bf16[8,5,16,128]{3,2,1,0:T(8,128)(2,1)S(1)}, u32[]{:S(2)}, u32[]{:S(2)}) async-start(bf16[8,5,16,128]{3,2,1,0:T(8,128)(2,1)} %pad_maximum_fusion), calls=%async_computation | async-start | bytes 327680 | tf_op jit(solution)/shard_map/requests/all_to_all | solution.py:321
  19.2 55.0 %all-to-all-start.1 = ((bf16[8,2,128,1024]{3,2,1,0:T(8,128)(2,1)}), bf16[8,2,128,1024]{3,2,1,0:T(8,128)(2,1)}, u32[]{:S(2)}, u32[]{:S(2)}) async-start(bf16[8,2,128,1024]{3,2,1,0:T(8,128)(2,1)} %bitcast.67), calls=%async_computation.1 | async-start | bytes 8388608 | tf_op jit(solution)/shard_map/gather_panels/all_to_all | solution.py:321
  26.5 5.0 %collective-permute-start.8 = (s32[8,8]{1,0:T(8,128)S(1)}, s32[8,8]{1,0:T(8,128)S(1)}, u32[]{:S(2)}, u32[]{:S(2)}) collective-permute-start(s32[8,8]{1,0:T(8,128)S(1)} %get-tuple-element.150), channel_id=1, source_target_pairs={{0,24},{8,0},{16,8},{24,16},{32,56},{40,32},{48,40},{56,48},{64,88... | collective-permute-start | bytes 776 | tf_op jit(solution)/shard_map/all_requests/ppermute | solution.py:314
  30.0 5.1 %collective-permute-start.7 = (s32[8,8]{1,0:T(8,128)S(1)}, s32[8,8]{1,0:T(8,128)S(1)}, u32[]{:S(2)}, u32[]{:S(2)}) collective-permute-start(s32[8,8]{1,0:T(8,128)S(1)} %get-tuple-element.150), channel_id=1, source_target_pairs={{0,16},{8,24},{16,0},{24,8},{32,48},{40,56},{48,32},{56,40},{64,80... | collective-permute-start | bytes 776 | tf_op jit(solution)/shard_map/all_requests/ppermute | solution.py:314
  30.1 5.0 %collective-permute-start.6 = (s32[8,8]{1,0:T(8,128)S(1)}, s32[8,8]{1,0:T(8,128)S(1)}, u32[]{:S(2)}, u32[]{:S(2)}) collective-permute-start(s32[8,8]{1,0:T(8,128)S(1)} %get-tuple-element.150), channel_id=1, source_target_pairs={{0,8},{8,16},{16,24},{24,0},{32,40},{40,48},{48,56},{56,32},{64,72... | collective-permute-start | bytes 776 | tf_op jit(solution)/shard_map/all_requests/ppermute | solution.py:314
  35.2 6.8 %collective-permute-start.10 = (s32[4,8,8]{2,1,0:T(8,128)S(1)}, s32[4,8,8]{2,1,0:T(8,128)S(1)}, u32[]{:S(2)}, u32[]{:S(2)}) collective-permute-start(s32[4,8,8]{2,1,0:T(8,128)S(1)} %get-tuple-element.147), channel_id=1, source_target_pairs={{0,64},{8,72},{16,80},{24,88},{32,96},{40,104},{48,112},{56,120},{... | collective-permute-start | bytes 3080 | tf_op jit(solution)/shard_map/all_requests/ppermute | solution.py:314
  38.5 4.9 %collective-permute-start.9 = (s32[4,8,8]{2,1,0:T(8,128)S(1)}, s32[4,8,8]{2,1,0:T(8,128)S(1)}, u32[]{:S(2)}, u32[]{:S(2)}) collective-permute-start(s32[4,8,8]{2,1,0:T(8,128)S(1)} %get-tuple-element.147), channel_id=1, source_target_pairs={{0,32},{8,40},{16,48},{24,56},{32,64},{40,72},{48,80},{56,88},{64,... | collective-permute-start | bytes 3080 | tf_op jit(solution)/shard_map/all_requests/ppermute | solution.py:314
  38.5 4.9 %collective-permute-start.11 = (s32[4,8,8]{2,1,0:T(8,128)S(1)}, s32[4,8,8]{2,1,0:T(8,128)S(1)}, u32[]{:S(2)}, u32[]{:S(2)}) collective-permute-start(s32[4,8,8]{2,1,0:T(8,128)S(1)} %get-tuple-element.147), channel_id=1, source_target_pairs={{0,96},{8,104},{16,112},{24,120},{32,0},{40,8},{48,16},{56,24},{64... | collective-permute-start | bytes 3080 | tf_op jit(solution)/shard_map/all_requests/ppermute | solution.py:314
  119.2 4.4 %collective-permute-start.12 = (bf16[16,33,16,128]{3,2,1,0:T(8,128)(2,1)S(1)}, bf16[16,33,16,128]{3,2,1,0:T(8,128)(2,1)}, u32[]{:S(2)}, u32[]{:S(2)}) collective-permute-start(bf16[16,33,16,128]{3,2,1,0:T(8,128)(2,1)S(1)} %all_to_all.20), channel_id=1, source_target_pairs={{0,1},{1,0},{2,3},{3,2},{4,5},{5,4},{6,7},{7,6},{8,9},{9,8},{10,11... | collective-permute-start | bytes 6488072 | tf_op jit(solution)/shard_map/split_pieces/ppermute | solution.py:422
  127.8 27.9 %collective-permute-start = (bf16[145,16,128]{2,1,0:T(8,128)(2,1)S(1)}, bf16[145,16,128]{2,1,0:T(8,128)(2,1)S(1)}, u32[]{:S(2)}, u32[]{:S(2)}) collective-permute-start(bf16[145,16,128]{2,1,0:T(8,128)(2,1)S(1)} %get-tuple-element.42), channel_id=1, source_target_pairs={{0,2},{1,3},{2,4},{3,5},{4,6},{5,7},{6,0},{7,1},{8,10},{9,11},{10,... | collective-permute-start | bytes 1781768 | tf_op jit(solution)/shard_map/sum_over_chips/cond/branch_0_fun/ppermute | solution.py:426
  129.9 25.8 %collective-permute-start.1 = (bf16[145,16,128]{2,1,0:T(8,128)(2,1)S(1)}, bf16[145,16,128]{2,1,0:T(8,128)(2,1)S(1)}, u32[]{:S(2)}, u32[]{:S(2)}) collective-permute-start(bf16[145,16,128]{2,1,0:T(8,128)(2,1)S(1)} %get-tuple-element.43), channel_id=1, source_target_pairs={{0,4},{1,5},{2,6},{3,7},{4,0},{5,1},{6,2},{7,3},{8,12},{9,13},{10,... | collective-permute-start | bytes 1781768 | tf_op jit(solution)/shard_map/sum_over_chips/cond/branch_0_fun/ppermute | solution.py:426
  130.2 29.0 %collective-permute-start.2 = (bf16[145,16,128]{2,1,0:T(8,128)(2,1)S(1)}, bf16[145,16,128]{2,1,0:T(8,128)(2,1)S(1)}, u32[]{:S(2)}, u32[]{:S(2)}) collective-permute-start(bf16[145,16,128]{2,1,0:T(8,128)(2,1)S(1)} %get-tuple-element.44), channel_id=1, source_target_pairs={{0,6},{1,7},{2,0},{3,1},{4,2},{5,3},{6,4},{7,5},{8,14},{9,15},{10,... | collective-permute-start | bytes 1781768 | tf_op jit(solution)/shard_map/sum_over_chips/cond/branch_0_fun/ppermute | solution.py:426

commit v5 on v4

v5 whole, which is shorter than its diff:
```python
import functools

import jax
import jax.numpy as jnp
from jax import lax
from jax.experimental import pallas as pl
from jax.experimental.pallas import tpu as pltpu
from jax.sharding import PartitionSpec as P

PANEL = 128
GROUP = 1024
CAND = 4
GROUPS_DEV = 2
REQ = CAND * GROUPS_DEV
PAN_DEV = 64
WIDTH = 1024
N_CENT = 8
CHIPS = 4
N_PTS = 16
SIDE = 4
ROWS = 16
HALF = 512
LANE = 128
TILES = HALF // LANE
SEND_TILES = CAND * TILES + 1
DENSE = PAN_DEV * TILES
LOAD_TILES = PAN_DEV // ROWS
LISTED = 24

sharpness_divisor = 16.0
evenness_coefficient = 1.0
prior_mass = 1.0

BF16 = jnp.bfloat16
F32 = jnp.float32
MIB = 1 << 20


def params(mib):
    return pltpu.CompilerParams(vmem_limit_bytes=mib * MIB)


def whole(shape):
    return pl.BlockSpec(shape, lambda *_: (0,) * len(shape))


def smem_spec():
    return pl.BlockSpec(memory_space=pltpu.SMEM)


def hbm_spec():
    return pl.BlockSpec(memory_space=pltpu.HBM)


def ask_kernel(candidates, home, loads, out):
    row = lax.broadcasted_iota(jnp.int32, (ROWS, LANE), 0)
    lane = lax.broadcasted_iota(jnp.int32, (ROWS, LANE), 1)
    slots = [home[candidates[n // CAND, n % CAND]] for n in range(REQ)]
    common = jnp.zeros((ROWS, LANE), F32)
    for n, slot in enumerate(slots):
        common = jnp.where((row == 1) & (lane == n), (slot // PAN_DEV).astype(F32), common)
        common = jnp.where((row == 2) & (lane == n), (slot % PAN_DEV).astype(F32), common)
    for o in range(N_CENT):
        tile = common
        for n, slot in enumerate(slots):
            here = jnp.where(slot // PAN_DEV == o, slot % PAN_DEV, 0).astype(F32)
            tile = jnp.where((row == 0) & (lane == n // CAND), tile + here, tile)
        for t in range(LOAD_TILES):
            out[o, t] = loads[t * ROWS : (t + 1) * ROWS]
        out[o, LOAD_TILES] = tile.astype(BF16)


def ask(candidates, home, loads):
    shape = (N_CENT, LOAD_TILES + 1, ROWS, LANE)
    return pl.pallas_call(
        ask_kernel,
        grid=(1,),
        in_specs=[smem_spec(), smem_spec(), whole((PAN_DEV, LANE))],
        out_specs=whole(shape),
        out_shape=jax.ShapeDtypeStruct(shape, BF16),
        compiler_params=params(8),
        cost_estimate=pl.CostEstimate(flops=1 << 16, bytes_accessed=1 << 18, transcendentals=0),
    )(candidates, home, loads)


def pick_kernel(group, ids, place, table, *refs):
    *outs, held, sems = refs

    def fetch(n):
        if len(outs) == 1:
            reader = n
        else:
            reader = (place[0] // 2 + n // 2) % CHIPS * 2 + (place[0] + n) % 2
        return pltpu.make_async_copy(table.at[ids[reader * GROUPS_DEV + group]], held.at[n], sems.at[0, n])

    def put(n):
        target = outs[0].at[n] if len(outs) == 1 else outs[n]
        return pltpu.make_async_copy(held.at[n], target, sems.at[1, n])

    depth = 4
    for n in range(depth):
        fetch(n).start()
    for n in range(N_CENT):
        fetch(n).wait()
        put(n).start()
        if n + depth < N_CENT:
            fetch(n + depth).start()
    for n in range(N_CENT):
        put(n).wait()


def pick_panels(group, apart, ids, place, table):
    one = jax.ShapeDtypeStruct((PANEL, WIDTH), BF16)
    out = [one] * N_CENT if apart else [jax.ShapeDtypeStruct((N_CENT, PANEL, WIDTH), BF16)]
    return pl.pallas_call(
        functools.partial(pick_kernel, group),
        out_shape=out,
        in_specs=[smem_spec(), smem_spec(), hbm_spec()],
        out_specs=[hbm_spec()] * len(out),
        scratch_shapes=[pltpu.VMEM((N_CENT, PANEL, WIDTH), BF16), pltpu.SemaphoreType.DMA((2, N_CENT))],
        compiler_params=params(60),
        cost_estimate=pl.CostEstimate(flops=0, bytes_accessed=4 * N_CENT * PANEL * WIDTH, transcendentals=0),
    )(ids, place, table)


def score_kernel(group, sources, owners, *refs):
    panels, (points, surcharge, out, members, centers, shares, sems) = refs[:sources], refs[sources:]
    step = 256
    steps = GROUP // step

    def bring(s):
        rows = pl.ds(s * step, step)
        return pltpu.make_async_copy(points.at[pl.ds(group * GROUP + s * step, step)], members.at[rows], sems.at[s])

    def land(j, source):
        return pltpu.make_async_copy(source, centers.at[pl.ds(j * PANEL, PANEL)], sems.at[steps + j])

    for j in range(CAND):
        if sources == 1:
            land(j, panels[0].at[owners[j]]).start()
        else:
            for o in range(N_CENT):

                @pl.when(owners[j] == o)
                def _(j=j, o=o):
                    land(j, panels[o]).start()

    for s in range(steps):
        bring(s).start()
    for j in range(CAND):
        land(j, panels[0].at[0] if sources == 1 else panels[0]).wait()
    wide = centers[...].astype(F32)
    squares = jnp.sum(wide * wide, axis=1, keepdims=True)
    bias = squares * (1.0 / sharpness_divisor) + evenness_coefficient * surcharge[0]
    weights = jnp.zeros((CAND * PANEL, LANE), F32)
    for s in range(steps):
        bring(s).wait()
        block = members[s * step : (s + 1) * step, :]
        inner = lax.dot_general(centers[...], block, (((1,), (1,)), ((), ())), preferred_element_type=F32)
        logits = inner * (2.0 / sharpness_divisor) - bias
        highest = jnp.max(logits, axis=0, keepdims=True)
        raised = jnp.exp(logits - highest)
        scale = 1.0 / jnp.sum(raised, axis=0, keepdims=True)
        share = (raised * scale).astype(BF16)
        shares[:, s * step : (s + 1) * step] = share
        rounded = share.astype(F32)
        for part in range(step // LANE):
            weights = weights + rounded[:, part * LANE : (part + 1) * LANE]
    weight = jnp.sum(weights, axis=1, keepdims=True)
    coarse = weight.astype(BF16).astype(F32)
    fine = weight - coarse
    lane = lax.broadcasted_iota(jnp.int32, (PANEL, LANE), 1)
    tile = jnp.zeros((PANEL, LANE), F32)
    for j in range(CAND):
        rows = slice(j * PANEL, (j + 1) * PANEL)
        tile = jnp.where(lane == j, coarse[rows], tile)
        tile = jnp.where(lane == CAND + j, fine[rows], tile)
    tile = tile.astype(BF16)
    for block_at in range(PANEL // ROWS):
        for half in range(2):
            out[block_at * 2 + half, CAND * TILES] = tile[block_at * ROWS : (block_at + 1) * ROWS]

    wide_step = 256
    for s in range(WIDTH // wide_step):
        part = lax.dot_general(
            shares[...], members[:, s * wide_step : (s + 1) * wide_step], (((1,), (0,)), ((), ())),
            preferred_element_type=F32,
        ).astype(BF16)
        for t in range(wide_step // LANE):
            half, tile_at = divmod(s * (wide_step // LANE) + t, TILES)
            for j in range(CAND):
                for block_at in range(PANEL // ROWS):
                    row = j * PANEL + block_at * ROWS
                    out[block_at * 2 + half, j * TILES + tile_at] = part[row : row + ROWS, t * LANE : (t + 1) * LANE]


def score(group, owners, panels, points, surcharge):
    shape = (N_PTS, SEND_TILES, ROWS, LANE)
    return pl.pallas_call(
        functools.partial(score_kernel, group, len(panels)),
        grid=(1,),
        in_specs=[smem_spec()] + [pl.BlockSpec(memory_space=pl.ANY)] * (len(panels) + 1)
        + [pl.BlockSpec((1, CAND * PANEL, 1), lambda g: (group, 0, 0))],
        out_specs=whole(shape),
        out_shape=jax.ShapeDtypeStruct(shape, BF16),
        scratch_shapes=[
            pltpu.VMEM((GROUP, WIDTH), BF16),
            pltpu.VMEM((CAND * PANEL, WIDTH), BF16),
            pltpu.VMEM((CAND * PANEL, GROUP), BF16),
            pltpu.SemaphoreType.DMA((8,)),
        ],
        compiler_params=params(32),
        cost_estimate=pl.CostEstimate(flops=2 << 30, bytes_accessed=6 * MIB, transcendentals=1 << 19),
    )(owners, *panels, points, surcharge)


def spread_kernel(rows, count, places, *refs):
    sources, (lanes, own, own_weights, out1, out2, out3, total) = refs[:count], refs[count:]
    total[...] = jnp.zeros_like(total)
    for n, source in enumerate(sources):

        def add(s, carry, n=n, source=source):
            for j in range(CAND):
                at = places[(n * N_PTS + s) * CAND + j] * TILES
                total[pl.ds(at, TILES)] += source[s, j * TILES : (j + 1) * TILES].astype(F32)
            return carry

        lax.fori_loop(0, N_PTS, add, 0, unroll=2)
    panel = lax.broadcasted_iota(jnp.int32, (CHIPS * PAN_DEV, LANE), 0)
    weights = jnp.zeros((ROWS, CHIPS * PAN_DEV), F32)
    for n in range(count * N_PTS):
        chosen = jnp.where(panel == lanes[n : n + 1, :], 1.0, 0.0).astype(BF16)
        weights = weights + lax.dot_general(
            sources[n // N_PTS][n % N_PTS, CAND * TILES], chosen, (((1,), (1,)), ((), ())),
            preferred_element_type=F32,
        )
    own[...] = total[0:DENSE]
    coarse = weights.astype(BF16)
    fine = (weights - coarse.astype(F32)).astype(BF16)
    own_weights[...] = weights[:, 0:LANE]
    for d, out in ((1, out1), (2, out2), (3, out3)):
        first = DENSE + (d - 1) * rows * TILES
        out[0 : rows * TILES] = total[first : first + rows * TILES].astype(BF16)
        out[rows * TILES, :, 0:PAN_DEV] = coarse[:, d * PAN_DEV : (d + 1) * PAN_DEV]
        out[rows * TILES, :, PAN_DEV:LANE] = fine[:, d * PAN_DEV : (d + 1) * PAN_DEV]


def spread(rows, places, lanes, sources):
    chunk = jax.ShapeDtypeStruct((rows * TILES + 1, ROWS, LANE), BF16)
    return pl.pallas_call(
        functools.partial(spread_kernel, rows, len(sources)),
        grid=(1,),
        in_specs=[smem_spec()] + [whole(x.shape) for x in sources] + [whole(lanes.shape)],
        out_specs=[whole((DENSE, ROWS, LANE)), whole((ROWS, LANE))] + [whole(chunk.shape)] * 3,
        out_shape=[
            jax.ShapeDtypeStruct((DENSE, ROWS, LANE), F32), jax.ShapeDtypeStruct((ROWS, LANE), F32),
            chunk, chunk, chunk,
        ],
        scratch_shapes=[pltpu.VMEM(((PAN_DEV + 3 * rows + 1) * TILES, ROWS, LANE), F32)],
        compiler_params=params(48),
        cost_estimate=pl.CostEstimate(flops=1 << 22, bytes_accessed=6 * MIB, transcendentals=0),
    )(places, *sources, lanes)


def finish_kernel(rows, owns, blocks, numbers, *refs):
    arrivals = owns * 3
    own, own_weights, arrived = refs[:owns], refs[owns : 2 * owns], refs[2 * owns : 2 * owns + arrivals]
    lanes, old, out, total, inverse, pair = refs[2 * owns + arrivals :]
    step = pl.program_id(0)

    @pl.when(step == 0)
    def _():
        panel = lax.broadcasted_iota(jnp.int32, (PAN_DEV, LANE), 0)
        total[...] = jnp.zeros_like(total)
        weights = own_weights[0][:, 0:PAN_DEV]
        for more in own_weights[1:]:
            weights = weights + more[:, 0:PAN_DEV]
        for d, source in enumerate(arrived):
            chosen = jnp.where(panel == lanes[d : d + 1, :], 1.0, 0.0).astype(BF16)
            weights = weights + lax.dot_general(
                source[rows * TILES], chosen, (((1,), (1,)), ((), ())), preferred_element_type=F32
            )
            first = 1 + arrivals + d * rows

            def add(n, carry, source=source, first=first):
                at = numbers[first + n] * TILES
                total[pl.ds(at, TILES)] += source[pl.ds(n * TILES, TILES)].astype(F32)
                return carry

            lax.fori_loop(0, numbers[1 + d], add, 0)
        coarse = weights.astype(BF16)
        pair[:, 0:PAN_DEV] = coarse
        pair[:, PAN_DEV:LANE] = (weights - coarse.astype(F32)).astype(BF16)
        scale = 1.0 / (weights + prior_mass)
        for q in range(PAN_DEV):
            inverse[q] = jnp.broadcast_to(scale[:, q : q + 1], (ROWS, LANE))

    here = PAN_DEV // blocks
    for q in range(here):
        for t in range(TILES):
            previous = old[q, :, t * LANE : (t + 1) * LANE].astype(F32)
            fresh = total[(step * here + q) * TILES + t] + prior_mass * previous
            for part in own:
                fresh = fresh + part[q * TILES + t]
            out[q // CAND, (q % CAND) * TILES + t] = (fresh * inverse[step * here + q]).astype(BF16)
    for p in range(here // CAND):
        out[p, CAND * TILES] = pair[...]


def finish(rows, numbers, own, own_weights, arrived, lanes, table):
    blocks = 4
    here = PAN_DEV // blocks
    chunk = whole((rows * TILES + 1, ROWS, LANE))
    last = CAND * TILES + 1
    return pl.pallas_call(
        functools.partial(finish_kernel, rows, len(own), blocks),
        grid_spec=pltpu.PrefetchScalarGridSpec(
            num_scalar_prefetch=1,
            grid=(blocks,),
            in_specs=[pl.BlockSpec((here * TILES, ROWS, LANE), lambda g, n: (g, 0, 0))] * len(own)
            + [whole((ROWS, LANE))] * len(own)
            + [chunk] * len(arrived)
            + [whole(lanes.shape), pl.BlockSpec((here, ROWS, HALF), lambda g, n: (g, n[0] // 2, n[0] % 2))],
            out_specs=pl.BlockSpec((here // CAND, last, ROWS, LANE), lambda g, n: (g, 0, 0, 0)),
            scratch_shapes=[
                pltpu.VMEM((DENSE, ROWS, LANE), F32),
                pltpu.VMEM((PAN_DEV, ROWS, LANE), F32),
                pltpu.VMEM((ROWS, LANE), BF16),
            ],
        ),
        out_shape=jax.ShapeDtypeStruct((N_PTS, last, ROWS, LANE), BF16),
        compiler_params=params(48),
        cost_estimate=pl.CostEstimate(flops=1 << 22, bytes_accessed=8 * MIB, transcendentals=0),
    )(numbers, *own, *own_weights, *arrived, lanes, table)


def place_kernel(me, pieces, out, loads):
    for block_at in range(PANEL // ROWS):
        for half in range(2):
            for q in range(CAND):
                for t in range(TILES):
                    column = half * HALF + t * LANE
                    out[q, block_at * ROWS : (block_at + 1) * ROWS, column : column + LANE] = pieces[
                        block_at * 2 + half, q * TILES + t
                    ]
    lane = lax.broadcasted_iota(jnp.int32, (ROWS, LANE), 1)
    row = lax.broadcasted_iota(jnp.int32, (ROWS, LANE), 0)
    wanted = me[0] * CAND + row
    chosen = jnp.where((row < CAND) & (lane % PAN_DEV == wanted), 1.0, 0.0).astype(BF16)
    for block_at in range(PANEL // ROWS):
        pair = pieces[block_at * 2, CAND * TILES]
        part = lax.dot_general(chosen, pair, (((1,), (1,)), ((), ())), preferred_element_type=F32)
        loads[:, block_at * ROWS : (block_at + 1) * ROWS] = part[0:CAND]


def place(me, pieces):
    return pl.pallas_call(
        place_kernel,
        grid=(1,),
        in_specs=[smem_spec(), whole(pieces.shape)],
        out_specs=[whole((CAND, PANEL, WIDTH)), whole((CAND, PANEL))],
        out_shape=[
            jax.ShapeDtypeStruct((CAND, PANEL, WIDTH), BF16),
            jax.ShapeDtypeStruct((CAND, PANEL), F32),
        ],
        compiler_params=params(32),
        cost_estimate=pl.CostEstimate(flops=1 << 20, bytes_accessed=2 * MIB, transcendentals=0),
    )(me, pieces)


def shift(dy, dk):
    return [(y * 2 + k, ((y + dy) % CHIPS) * 2 + (k + dk) % 2) for y in range(CHIPS) for k in range(2)]


def spread_out(x, place, dz, dx):
    held = [x]
    for d in range(1, SIDE):
        pairs = [
            (ix * SIDE + iz, (ix + d * dx) % SIDE * SIDE + (iz + d * dz) % SIDE)
            for ix in range(SIDE)
            for iz in range(SIDE)
        ]
        held.append(lax.ppermute(x, "pts", pairs))
    held = jnp.stack(held)
    at = (place - jnp.arange(SIDE, dtype=jnp.int32)) % SIDE
    return jnp.stack([jnp.sum(jnp.where((at == n).reshape((SIDE,) + (1,) * x.ndim), held, 0), axis=0) for n in range(SIDE)])


def exchange(x, axis):
    return lax.all_to_all(x, axis, split_axis=0, concat_axis=0, tiled=True)


def at_index(x, n, axis=0):
    return lax.dynamic_index_in_dim(x, n, axis, keepdims=False)


def local(points, centroids, prev_loads, candidates, panel_home):
    me = lax.axis_index("pts")
    here = lax.axis_index("cent")
    chip, core = here // 2, here % 2
    shelf = centroids.reshape(PAN_DEV, PANEL, WIDTH)
    tie = lax.optimization_barrier
    where = here.reshape(1)

    with jax.named_scope("requests"):
        answered = exchange(ask(candidates, panel_home, prev_loads.reshape(PAN_DEV, PANEL)), "cent")
        asked = answered[:, LOAD_TILES, 0, 0:GROUPS_DEV].astype(jnp.int32).reshape(-1)

    with jax.named_scope("gather_panels"):
        ready0, = pick_panels(0, False, asked, where, shelf)
        ready1 = pick_panels(1, True, asked, where, shelf)

    with jax.named_scope("gather_panels"):
        arrived0 = exchange(ready0, "cent")

    with jax.named_scope("loads"):
        wanted_ids, answered = tie((candidates.reshape(REQ), answered))
        slots = jnp.sum(
            jnp.where(wanted_ids[:, None] == jnp.arange(panel_home.shape[0], dtype=jnp.int32), panel_home[None, :], 0),
            axis=1,
        )
        owners = (slots // PAN_DEV).reshape(GROUPS_DEV, CAND)
        seen = (chip - owners // 2) % CHIPS * 2 + (core - owners) % 2
        load_table = answered[:, :LOAD_TILES].reshape(N_CENT * PAN_DEV, PANEL)
        loads = jnp.take(load_table, slots, axis=0, mode="clip").astype(F32)
        surcharge = jnp.log(loads).reshape(GROUPS_DEV, CAND * PANEL, 1)

    with jax.named_scope("all_requests"):
        answered, ready0 = tie((answered, ready0))
        ring = answered[:, LOAD_TILES, 1:3, 0:REQ].astype(jnp.int32)
        ring = ring[:, 0] * PAN_DEV + ring[:, 1]
        line = spread_out(ring, me % SIDE, 1, 0)
        everyone = spread_out(line, me // SIDE, 0, 1).reshape(N_PTS, N_CENT, GROUPS_DEV, CAND)

        numbers = jnp.arange(N_CENT * PAN_DEV, dtype=jnp.int32)
        by_chip = jnp.transpose(everyone.reshape(N_PTS, CHIPS, 2, GROUPS_DEV, CAND), (3, 1, 0, 2, 4))
        by_chip = by_chip.reshape(GROUPS_DEV, CHIPS, 2 * N_PTS * CAND)
        asked_by = jnp.any(by_chip[..., None] == numbers, axis=2).reshape(GROUPS_DEV, CHIPS, N_CENT, PAN_DEV)
        below = jnp.arange(PAN_DEV)[:, None] < jnp.arange(PAN_DEV)[None, :]
        ranks = lax.dot_general(
            asked_by.astype(BF16), below.astype(BF16), (((3,), (0,)), ((), ())), preferred_element_type=F32
        ).astype(jnp.int32)
        lengths = jnp.sum(asked_by.astype(jnp.int32), axis=3)
        off_chip = jnp.arange(N_CENT)[None, :] // 2 != jnp.arange(CHIPS)[:, None]
        too_long = jnp.any(off_chip & (lengths > LISTED))

        pair = jnp.stack([at_index(everyone, at, 1) for at in (here, chip * 2 + 1 - core)])
        pair = jnp.transpose(pair, (2, 0, 1, 3)).reshape(GROUPS_DEV, 2 * N_PTS, CAND)
        owner = pair // PAN_DEV
        relative = (owner // 2 - chip) % CHIPS
        my_ranks = at_index(ranks, chip, 1).reshape(GROUPS_DEV, 1, 1, -1)
        rank = jnp.sum(jnp.where(pair[..., None] == numbers, my_ranks, 0), axis=3)

        def sender(rows, rank):
            at = jnp.where(relative == 0, pair % PAN_DEV, rank)
            known = (owner % 2 == core) & ((relative == 0) | (rank < rows))
            first = jnp.where(relative == 0, 0, PAN_DEV + (relative - 1) * rows)
            places = jnp.where(known, first + at, PAN_DEV + 3 * rows)
            lane = jnp.where(known, relative * PAN_DEV + at, CHIPS * PAN_DEV)
            lanes = jnp.pad(
                jnp.concatenate([lane, lane], axis=2), ((0, 0), (0, 0), (0, LANE - 2 * CAND)),
                constant_values=CHIPS * PAN_DEV,
            )
            return places, lanes

        def receiver(rows, count, panels):
            numbers = jnp.concatenate([me.reshape(1), count, panels[:, :rows].reshape(-1)])
            lane = jnp.where(jnp.arange(PAN_DEV) < count[:, None], panels, PAN_DEV)
            return numbers, jnp.concatenate([lane, lane], axis=1)

        behind = [(chip - d) % CHIPS for d in range(1, CHIPS)]
        named = jnp.stack([at_index(at_index(asked_by[g], y), here) for g in range(GROUPS_DEV) for y in behind])
        order = jnp.stack([at_index(at_index(ranks[g], y), here) for g in range(GROUPS_DEV) for y in behind])
        spots = jnp.arange(PAN_DEV, dtype=jnp.int32)
        listed = jnp.sum(
            jnp.where(named[:, None, :] & (order[:, None, :] == spots[None, :, None]), spots, 0), axis=2
        )
        count = jnp.minimum(jnp.sum(named.astype(jnp.int32), axis=1), LISTED)
        places, lanes = sender(LISTED, rank)
        places = [places[g].reshape(-1) for g in range(GROUPS_DEV)]
        lanes = [lanes[g] for g in range(GROUPS_DEV)]
        numbers, back_lanes = receiver(LISTED, count, listed)
        owners, seen, too_long, places, lanes, numbers, back_lanes = tie(
            (owners, seen, too_long, places, lanes, numbers, back_lanes)
        )

    def to_owners(far):
        return [lax.ppermute(far[d - 1], "cent", shift(d, 0)) for d in range(1, CHIPS)]

    with jax.named_scope("group_0"):
        ready1, arrived0 = tie((ready1, arrived0))
        arrived1 = [ready1[0]] + [lax.ppermute(ready1[n], "cent", shift(n // 2, n % 2)) for n in range(1, N_CENT)]
        pieces0 = score(0, owners[0], [arrived0], points, surcharge)
        mine0 = exchange(pieces0, "pts")
        arrived1, mine0 = tie((arrived1, mine0))
        mate0 = lax.ppermute(mine0, "cent", shift(0, 1))

    with jax.named_scope("group_1"):
        pieces1 = score(1, seen[1], arrived1, points, surcharge)
        mine1 = exchange(pieces1, "pts")

    with jax.named_scope("spread_0"):
        own0, weights0, *far0 = spread(LISTED, places[0], lanes[0], [mine0, mate0])
        back0 = to_owners(far0)
        mine1, back0 = tie((mine1, back0))

    with jax.named_scope("spread_1"):
        mate1 = lax.ppermute(mine1, "cent", shift(0, 1))
        own1, weights1, *far1 = spread(LISTED, places[1], lanes[1], [mine1, mate1])
        back1 = to_owners(far1)

    def from_lists():
        return finish(LISTED, numbers, [own0, own1], [weights0, weights1], back0 + back1, back_lanes, shelf)

    def from_all():
        everything = jnp.broadcast_to(spots, (CHIPS - 1, PAN_DEV))
        count = jnp.full((CHIPS - 1,), PAN_DEV, jnp.int32)
        places, lanes = sender(PAN_DEV, pair % PAN_DEV)
        sources = [mine0, mate0, mine1, mate1]
        own, weights, *far = spread(PAN_DEV, places.reshape(-1), lanes.reshape(-1, LANE), sources)
        numbers, back_lanes = receiver(PAN_DEV, count, everything)
        return finish(PAN_DEV, numbers, [own], [weights], to_owners(far), back_lanes, shelf)

    with jax.named_scope("finish"):
        fresh = lax.cond(too_long, from_all, from_lists)

    with jax.named_scope("place"):
        new_centroids, new_loads = place(me.reshape(1), exchange(fresh, "pts"))
    return new_centroids.reshape(CAND * PANEL, WIDTH), new_loads.reshape(CAND * PANEL)


def solution(mesh):
    placed = (P(("pts", "cent"), None), P("cent", None), P("cent"), P(("pts", "cent"), None), P())
    return jax.shard_map(
        local,
        mesh=mesh,
        in_specs=placed,
        out_specs=(P(("cent", "pts"), None), P(("cent", "pts"))),
        check_vma=False,
    )
```

time: 188 us -> 202 us (1.074)
  blocking collectives: 57.7 us -> 25 us
  starting transfers between devices: 26.5 us -> 50.6 us
  Pallas kernels: 23.9 us -> 39.5 us
  local copies, waits for them, and re-layouts: 4.74 us -> 11.7 us
    all_to_all x2 -> x1, blocking collectives: 57.7 us -> 25 us  [exchange(): return lax.all_to_all(x, axis, split_axis=0, concat_axis=0, tiled=True)]
    ppermute x4 -> x15, waiting for transfers between devices: 31.5 us -> 50.1 us  [the longest x6 24.9 us: to_owners(): lax.ppermute(far[d - 1], 'cent', shift(d, 0))]
    all_to_all x2 -> x4, waiting for transfers between devices: 31 us -> 15.1 us  [exchange(): return lax.all_to_all(x, axis, split_axis=0, concat_axis=0, tiled=True)]
    pallas_call x4 -> x8, Pallas kernels: 22.7 us -> 38.3 us  [the longest x2 13.7 us: score(): pl.pallas_call(functools.partial(score_kernel, group, len(panels)), grid=...]
    all_to_all x2 -> x4, starting transfers between devices: 12 us -> 25.6 us  [exchange(): return lax.all_to_all(x, axis, split_axis=0, concat_axis=0, tiled=True)]
    ppermute x4 -> x15, starting transfers between devices: 3.56 us -> 13.1 us  [the longest x7 7.24 us: local(): lax.ppermute(ready1[n], 'cent', shift(n // 2, n % 2))]
    unnamed x0 -> x22, local copies, waits for them, and re-layouts: none -> 6.47 us
  transfers between devices with their start and end apart: 12 -> 25, of which waited for: 7 -> 11; matrix products, arithmetic and copies ran while one was open for 3% -> 4% of each run, Pallas kernels for 0% -> 8%
where the time goes in v5:
time: 202 us; the launch traced here: 200 us
  waiting for transfers between devices  68.3 us (34%)
  starting transfers between devices  50.6 us (25%)
  Pallas kernels  39.5 us (20%)
  blocking collectives  25 us (12%)
  local copies, waits for them, and re-layouts  11.7 us (6%)
  other arithmetic  3.45 us (2%)
    all_to_all x4, starting transfers between devices, exchange(): return lax.all_to_all(x, axis, split_axis=0, concat_axis=0, tiled=True)  25.6 us
    all_to_all x1, blocking collectives, exchange(): return lax.all_to_all(x, axis, split_axis=0, concat_axis=0, tiled=True)  25 us
    ppermute x6, waiting for transfers between devices, to_owners(): lax.ppermute(far[d - 1], 'cent', shift(d, 0))  24.9 us
    ppermute x7, waiting for transfers between devices, local(): lax.ppermute(ready1[n], 'cent', shift(n // 2, n % 2))  22.4 us
    all_to_all x4, waiting for transfers between devices, exchange(): return lax.all_to_all(x, axis, split_axis=0, concat_axis=0, tiled=True)  15.1 us
    pallas_call x2, Pallas kernels, score(): pl.pallas_call(functools.partial(score_kernel, group, len(panels)), grid=...  13.7 us
    ppermute x6, starting transfers between devices, spread_out(): held.append(lax.ppermute(x, 'pts', pairs))  11.9 us
    pallas_call x2, Pallas kernels, pick_panels(): pl.pallas_call(functools.partial(pick_kernel, group), out_shape=out, in_s...  8.32 us
  transfers between devices with their start and end apart: 25, of which 11 were waited for; matrix products, arithmetic and copies ran while one was open for 4% of the time, Pallas kernels for 8%

profile of v5, /device:TPU:24, one launch (start us, length us, event | category | flops | bytes accessed | tf_op | source)
XLA Modules:
  0.0 200.5 jit_solution(4701073610941117444)
XLA Ops:
  4.1 4.7 %all-to-all-start = ((bf16[8,5,16,128]{3,2,1,0:T(8,128)(2,1)}), bf16[8,5,16,128]{3,2,1,0:T(8,128)(2,1)S(1)}, u32[]{:S(2)}, u32[]{:S(2)}) async-start(bf16[8,5,16,128]{3,2,1,0:T(8,128)(2,1)} %requests.1), calls=%async_computation | async-start | bytes 327680 | tf_op jit(solution)/shard_map/requests/all_to_all | solution.py:390
  9.7 3.5 %all-to-all-done = bf16[8,5,16,128]{3,2,1,0:T(8,128)(2,1)S(1)} async-done(((bf16[8,5,16,128]{3,2,1,0:T(8,128)(2,1)}), bf16[8,5,16,128]{3,2,1,0:T(8,128)(2,1)S(1)}, u32[]{:S(2)}, u32[]{:S(2)}) %all-to-all-start) | async-done | bytes 163872 | tf_op jit(solution)/shard_map/requests/all_to_all | solution.py:390
  14.9 4.2 %gather_panels.2 = bf16[8,128,1024]{2,1,0:T(8,128)(2,1)} custom-call(s32[16]{0:T(128)} %reshape.278.ids, s32[1]{0:T(128)} %bitcast.4.place, bf16[64,128,1024]{2,1,0:T(8,128)(2,1)} %bitcast.85), custom_call_target="tpu_custom_call" | custom-call | bytes 4194304 | tf_op jit(solution)/shard_map/gather_panels/pallas_call | solution.py:115
  19.1 5.7 %all-to-all-start.1 = ((bf16[8,128,1024]{2,1,0:T(8,128)(2,1)}), bf16[8,128,1024]{2,1,0:T(8,128)(2,1)S(1)}, u32[]{:S(2)}, u32[]{:S(2)}) async-start(bf16[8,128,1024]{2,1,0:T(8,128)(2,1)} %gather_panels.2), calls=%async_computation.1 | async-start | bytes 4194304 | tf_op jit(solution)/shard_map/gather_panels/all_to_all | solution.py:390
  24.8 4.0 %collective-permute-start.5 = (s32[8,8]{1,0:T(8,128)S(1)}, s32[8,8]{1,0:T(8,128)S(1)}, u32[]{:S(2)}, u32[]{:S(2)}) collective-permute-start(s32[8,8]{1,0:T(8,128)S(1)} %get-tuple-element.226), channel_id=1, source_target_pairs={{0,24},{8,0},{16,8},{24,16},{32,56},{40,32},{48,40},{56,48},{64,88... | collective-permute-start | bytes 776 | tf_op jit(solution)/shard_map/all_requests/ppermute | solution.py:383
  30.7 3.1 %collective-permute-done.4 = s32[8,8]{1,0:T(8,128)S(1)} collective-permute-done((s32[8,8]{1,0:T(8,128)S(1)}, s32[8,8]{1,0:T(8,128)S(1)}, u32[]{:S(2)}, u32[]{:S(2)}) %collective-permute-start.4) | collective-permute-done | bytes 288 | tf_op jit(solution)/shard_map/all_requests/ppermute | solution.py:383
  33.9 3.3 %collective-permute-start.7 = (s32[4,8,8]{2,1,0:T(8,128)S(1)}, s32[4,8,8]{2,1,0:T(8,128)S(1)}, u32[]{:S(2)}, u32[]{:S(2)}) collective-permute-start(s32[4,8,8]{2,1,0:T(8,128)S(1)} %get-tuple-element.223), channel_id=1, source_target_pairs={{0,64},{8,72},{16,80},{24,88},{32,96},{40,104},{48,112},{56,120},{... | collective-permute-start | bytes 3080 | tf_op jit(solution)/shard_map/all_requests/ppermute | solution.py:383
  40.5 4.1 %gather_panels.3 = (bf16[128,1024]{1,0:T(8,128)(2,1)}, bf16[128,1024]{1,0:T(8,128)(2,1)}, bf16[128,1024]{1,0:T(8,128)(2,1)}, bf16[128,1024]{1,0:T(8,128)(2,1)}, ...) custom-call(s32[16]{0:T(128)} %reshape.278.ids, ...), custom_call_target="tpu_custom_call" | custom-call | bytes 4194304 | tf_op jit(solution)/shard_map/gather_panels/pallas_call | solution.py:115
  52.1 6.7 %group_0.1 = bf16[16,17,16,128]{3,2,1,0:T(8,128)(2,1)} custom-call(s32[4]{0:T(128)S(1)} %slice_bitcast_fusion.1.owners, bf16[8,128,1024]{2,1,0:T(8,128)(2,1)S(1)} %all-to-all-done.1.refs_0_, bf16[2048,1024]{1,0:T(8,128)(2,1)S(1)} %copy-done.3, f32[2,512,1]{2,1,0:T(8,128)S(1)} %log.15.refs_2_.refs_9_), custom_call_target="tpu_custom_call" | custom-call | flops 2147483648 | bytes 6291456 | tf_op jit(solution)/shard_map/group_0/pallas_call | solution.py:199
  58.9 8.0 %all-to-all-start.2 = ((bf16[16,17,16,128]{3,2,1,0:T(8,128)(2,1)}), bf16[16,17,16,128]{3,2,1,0:T(8,128)(2,1)}, u32[]{:S(2)}, u32[]{:S(2)}) async-start(bf16[16,17,16,128]{3,2,1,0:T(8,128)(2,1)} %group_0.1), calls=%async_computation.2 | async-start | bytes 2228224 | tf_op jit(solution)/shard_map/group_0/all_to_all | solution.py:390
  76.2 16.1 %collective-permute-done.11.refs_3_ = bf16[128,1024]{1,0:T(8,128)(2,1)S(1)} collective-permute-done((bf16[128,1024]{1,0:T(8,128)(2,1)}, bf16[128,1024]{1,0:T(8,128)(2,1)S(1)}, u32[]{:S(2)}, u32[]{:S(2)}) %collective-permute-start.11) | collective-permute-done | bytes 262176 | tf_op jit(solution)/shard_map/group_0/ppermute | solution.py:492
  92.3 4.3 %collective-permute-done.15.refs_7_ = bf16[128,1024]{1,0:T(8,128)(2,1)S(1)} collective-permute-done((bf16[128,1024]{1,0:T(8,128)(2,1)S(1)}, bf16[128,1024]{1,0:T(8,128)(2,1)S(1)}, u32[]{:S(2)}, u32[]{:S(2)}) %collective-permute-start.15) | collective-permute-done | bytes 262176 | tf_op jit(solution)/shard_map/group_0/ppermute | solution.py:492
  98.9 7.0 %group_1.1 = bf16[16,17,16,128]{3,2,1,0:T(8,128)(2,1)} custom-call(s32[4]{0:T(128)S(1)} %slice_bitcast_fusion.owners, bf16[128,1024]{1,0:T(8,128)(2,1)S(1)} %copy-done.5, bf16[128,1024]{1,0:T(8,128)(2,1)S(1)} %collective-permute-done.9.refs_1_, bf16[128,1024]{1,0:T(8,128)(2,1)S(1)} %collective-permute-done.10.refs_2_, ...), custom_call_target="tpu_custom_call" | custom-call | flops 2147483648 | bytes 6291456 | tf_op jit(solution)/shard_map/group_1/pallas_call | solution.py:199
  105.9 7.2 %all-to-all-start.3 = ((bf16[16,17,16,128]{3,2,1,0:T(8,128)(2,1)}), bf16[16,17,16,128]{3,2,1,0:T(8,128)(2,1)S(1)}, u32[]{:S(2)}, u32[]{:S(2)}) async-start(bf16[16,17,16,128]{3,2,1,0:T(8,128)(2,1)} %group_1.1), calls=%async_computation.3 | async-start | bytes 2228224 | tf_op jit(solution)/shard_map/group_1/all_to_all | solution.py:390
  113.2 4.6 %spread_0.1 = (f32[256,16,128]{2,1,0:T(8,128)}, f32[16,128]{1,0:T(8,128)S(1)}, bf16[97,16,128]{2,1,0:T(8,128)(2,1)S(1)}, bf16[97,16,128]{2,1,0:T(8,128)(2,1)S(1)}, bf16[97,16,128]{2,1,0:T(8,128)(2,1)S(1)}) custom-call(s32[128]{0:T(128)S(1)} %squeeze.71.places, bf16[16,17,16,128]{3,2,1,0:T(8,128)(2,1)} %all-to-all-done.2.refs_0_, ...), custom_call_target="tpu_custom_call" | custom-call | flops 4194304 | bytes 6291456 | tf_op jit(solution)/shard_map/spread_0/pallas_call | solution.py:250
  120.6 11.6 %all-to-all-done.3.refs_0_ = bf16[16,17,16,128]{3,2,1,0:T(8,128)(2,1)S(1)} async-done(((bf16[16,17,16,128]{3,2,1,0:T(8,128)(2,1)}), bf16[16,17,16,128]{3,2,1,0:T(8,128)(2,1)S(1)}, u32[]{:S(2)}, u32[]{:S(2)}) %all-to-all-start.3) | async-done | bytes 1114144 | tf_op jit(solution)/shard_map/group_1/all_to_all | solution.py:390
  132.2 6.9 %collective-permute-done.19 = bf16[97,16,128]{2,1,0:T(8,128)(2,1)} collective-permute-done((bf16[97,16,128]{2,1,0:T(8,128)(2,1)S(1)}, bf16[97,16,128]{2,1,0:T(8,128)(2,1)}, u32[]{:S(2)}, u32[]{:S(2)}) %collective-permute-start.19) | collective-permute-done | bytes 397344 | tf_op jit(solution)/shard_map/spread_0/ppermute | solution.py:488
  139.1 2.7 %collective-permute-done.20.refs_1_ = bf16[16,17,16,128]{3,2,1,0:T(8,128)(2,1)S(1)} collective-permute-done((bf16[16,17,16,128]{3,2,1,0:T(8,128)(2,1)S(1)}, bf16[16,17,16,128]{3,2,1,0:T(8,128)(2,1)S(1)}, u32[]{:S(2)}, u32[]{:S(2)}) %collective-permute-start.20) | collective-permute-done | bytes 1114144 | tf_op jit(solution)/shard_map/spread_1/ppermute | solution.py:508
  141.9 3.6 %spread_1.1 = (f32[256,16,128]{2,1,0:T(8,128)}, f32[16,128]{1,0:T(8,128)S(1)}, bf16[97,16,128]{2,1,0:T(8,128)(2,1)S(1)}, bf16[97,16,128]{2,1,0:T(8,128)(2,1)S(1)}, bf16[97,16,128]{2,1,0:T(8,128)(2,1)S(1)}) custom-call(s32[128]{0:T(128)S(1)} %squeeze.72.places, bf16[16,17,16,128]{3,2,1,0:T(8,128)(2,1)S(1)} %all-to-all-done.3.refs_0_, ...), custom_call_target="tpu_custom_call" | custom-call | flops 4194304 | bytes 6291456 | tf_op jit(solution)/shard_map/spread_1/pallas_call | solution.py:250
  149.5 8.1 %collective-permute-done.21 = bf16[97,16,128]{2,1,0:T(8,128)(2,1)} collective-permute-done((bf16[97,16,128]{2,1,0:T(8,128)(2,1)S(1)}, bf16[97,16,128]{2,1,0:T(8,128)(2,1)}, u32[]{:S(2)}, u32[]{:S(2)}) %collective-permute-start.21) | collective-permute-done | bytes 397344 | tf_op jit(solution)/shard_map/spread_1/ppermute | solution.py:488
  160.2 7.3 %collective-permute-done.23 = bf16[97,16,128]{2,1,0:T(8,128)(2,1)} collective-permute-done((bf16[97,16,128]{2,1,0:T(8,128)(2,1)S(1)}, bf16[97,16,128]{2,1,0:T(8,128)(2,1)}, u32[]{:S(2)}, u32[]{:S(2)}) %collective-permute-start.23) | collective-permute-done | bytes 397344 | tf_op jit(solution)/shard_map/spread_1/ppermute | solution.py:488
  167.6 6.6 %conditional.1 = (bf16[16,17,16,128]{3,2,1,0:T(8,128)(2,1)}) conditional(s32[]{:T(128)} %convert_element_type.45, (s32[151]{0:T(256)S(1)}, f32[256,16,128]{2,1,0:T(8,128)}, f32[256,16,128]{2,1,0:T(8,128)}, f32[16,128]{1,0:T(8,128)S(1)}, f32[16,128]{1,0:T(8,128)S(1)}, /*index=5*/bf16[97,16,128]{2,1,0:T(8,128)(2,1)S(1)}, ...), branch_computations={%region_15.16_spmd, %region_16.17_spmd} | conditional | flops 8402632 | bytes 31832944 | solution.py:525
  167.6 6.6 %branch_0_fun.1 = bf16[16,17,16,128]{3,2,1,0:T(8,128)(2,1)} custom-call(s32[151]{0:T(256)S(1)} %get-tuple-element.34.numbers, f32[256,16,128]{2,1,0:T(8,128)} %get-tuple-element.35.refs_0_, f32[256,16,128]{2,1,0:T(8,128)} %get-tuple-element.36.refs_1_, f32[16,128]{1,0:T(8,128)S(1)} %get-tuple-element.56.refs_2_, f32[16,128]{1,0:T(8,128)S(1)} %get-tuple-element.57.refs_3_, ...), custom_call_target="tpu_custom_call" | custom-call | flops 4194304 | bytes 8388608 | tf_op jit(solution)/shard_map/finish/cond/branch_0_fun/pallas_call | solution.py:315
  174.2 25.0 %all_to_all.25.pieces = bf16[16,17,16,128]{3,2,1,0:T(8,128)(2,1)S(1)} all-to-all(bf16[16,17,16,128]{3,2,1,0:T(8,128)(2,1)} %get-tuple-element.245), channel_id=1, replica_groups=mesh['pts'=16,'cent'=8] {'pts'}, dimensions={0} | all-to-all | bytes 2228224 | tf_op jit(solution)/shard_map/place/all_to_all | solution.py:390
  (132 shorter events, 40.3 us)
Async XLA Ops:
  4.1 9.1 %all-to-all-start = ((bf16[8,5,16,128]{3,2,1,0:T(8,128)(2,1)}), bf16[8,5,16,128]{3,2,1,0:T(8,128)(2,1)S(1)}, u32[]{:S(2)}, u32[]{:S(2)}) async-start(bf16[8,5,16,128]{3,2,1,0:T(8,128)(2,1)} %requests.1), calls=%async_computation | async-start | bytes 327680 | tf_op jit(solution)/shard_map/requests/all_to_all | solution.py:390
  19.1 30.8 %all-to-all-start.1 = ((bf16[8,128,1024]{2,1,0:T(8,128)(2,1)}), bf16[8,128,1024]{2,1,0:T(8,128)(2,1)S(1)}, u32[]{:S(2)}, u32[]{:S(2)}) async-start(bf16[8,128,1024]{2,1,0:T(8,128)(2,1)} %gather_panels.2), calls=%async_computation.1 | async-start | bytes 4194304 | tf_op jit(solution)/shard_map/gather_panels/all_to_all | solution.py:390
  24.8 5.9 %collective-permute-start.5 = (s32[8,8]{1,0:T(8,128)S(1)}, s32[8,8]{1,0:T(8,128)S(1)}, u32[]{:S(2)}, u32[]{:S(2)}) collective-permute-start(s32[8,8]{1,0:T(8,128)S(1)} %get-tuple-element.226), channel_id=1, source_target_pairs={{0,24},{8,0},{16,8},{24,16},{32,56},{40,32},{48,40},{56,48},{64,88... | collective-permute-start | bytes 776 | tf_op jit(solution)/shard_map/all_requests/ppermute | solution.py:383
  28.7 5.1 %collective-permute-start.4 = (s32[8,8]{1,0:T(8,128)S(1)}, s32[8,8]{1,0:T(8,128)S(1)}, u32[]{:S(2)}, u32[]{:S(2)}) collective-permute-start(s32[8,8]{1,0:T(8,128)S(1)} %get-tuple-element.226), channel_id=1, source_target_pairs={{0,16},{8,24},{16,0},{24,8},{32,48},{40,56},{48,32},{56,40},{64,80... | collective-permute-start | bytes 776 | tf_op jit(solution)/shard_map/all_requests/ppermute | solution.py:383
  28.8 5.0 %collective-permute-start.3 = (s32[8,8]{1,0:T(8,128)S(1)}, s32[8,8]{1,0:T(8,128)S(1)}, u32[]{:S(2)}, u32[]{:S(2)}) collective-permute-start(s32[8,8]{1,0:T(8,128)S(1)} %get-tuple-element.226), channel_id=1, source_target_pairs={{0,8},{8,16},{16,24},{24,0},{32,40},{40,48},{48,56},{56,32},{64,72... | collective-permute-start | bytes 776 | tf_op jit(solution)/shard_map/all_requests/ppermute | solution.py:383
  33.9 11.0 %collective-permute-start.7 = (s32[4,8,8]{2,1,0:T(8,128)S(1)}, s32[4,8,8]{2,1,0:T(8,128)S(1)}, u32[]{:S(2)}, u32[]{:S(2)}) collective-permute-start(s32[4,8,8]{2,1,0:T(8,128)S(1)} %get-tuple-element.223), channel_id=1, source_target_pairs={{0,64},{8,72},{16,80},{24,88},{32,96},{40,104},{48,112},{56,120},{... | collective-permute-start | bytes 3080 | tf_op jit(solution)/shard_map/all_requests/ppermute | solution.py:383
  37.2 7.8 %collective-permute-start.6 = (s32[4,8,8]{2,1,0:T(8,128)S(1)}, s32[4,8,8]{2,1,0:T(8,128)S(1)}, u32[]{:S(2)}, u32[]{:S(2)}) collective-permute-start(s32[4,8,8]{2,1,0:T(8,128)S(1)} %get-tuple-element.223), channel_id=1, source_target_pairs={{0,32},{8,40},{16,48},{24,56},{32,64},{40,72},{48,80},{56,88},{64,... | collective-permute-start | bytes 3080 | tf_op jit(solution)/shard_map/all_requests/ppermute | solution.py:383
  37.9 7.1 %collective-permute-start.8 = (s32[4,8,8]{2,1,0:T(8,128)S(1)}, s32[4,8,8]{2,1,0:T(8,128)S(1)}, u32[]{:S(2)}, u32[]{:S(2)}) collective-permute-start(s32[4,8,8]{2,1,0:T(8,128)S(1)} %get-tuple-element.223), channel_id=1, source_target_pairs={{0,96},{8,104},{16,112},{24,120},{32,0},{40,8},{48,16},{56,24},{64... | collective-permute-start | bytes 3080 | tf_op jit(solution)/shard_map/all_requests/ppermute | solution.py:383
  58.9 37.7 %all-to-all-start.2 = ((bf16[16,17,16,128]{3,2,1,0:T(8,128)(2,1)}), bf16[16,17,16,128]{3,2,1,0:T(8,128)(2,1)}, u32[]{:S(2)}, u32[]{:S(2)}) async-start(bf16[16,17,16,128]{3,2,1,0:T(8,128)(2,1)} %group_0.1), calls=%async_computation.2 | async-start | bytes 2228224 | tf_op jit(solution)/shard_map/group_0/all_to_all | solution.py:390
  66.9 5.8 %collective-permute-start.9 = (bf16[128,1024]{1,0:T(8,128)(2,1)S(1)}, bf16[128,1024]{1,0:T(8,128)(2,1)S(1)}, u32[]{:S(2)}, u32[]{:S(2)}) collective-permute-start(bf16[128,1024]{1,0:T(8,128)(2,1)S(1)} %copy-done.12), channel_id=1, source_target_pairs={{0,1},{1,0},{2,3},{3,2},{4,5},{5,4},{6,7},{7,6},{8,9},{9,8},{10,11... | collective-permute-start | bytes 786440 | tf_op jit(solution)/shard_map/group_0/ppermute | solution.py:492
  67.0 9.2 %collective-permute-start.10 = (bf16[128,1024]{1,0:T(8,128)(2,1)S(1)}, bf16[128,1024]{1,0:T(8,128)(2,1)S(1)}, u32[]{:S(2)}, u32[]{:S(2)}) collective-permute-start(bf16[128,1024]{1,0:T(8,128)(2,1)S(1)} %copy-done.11), channel_id=1, source_target_pairs={{0,2},{1,3},{2,4},{3,5},{4,6},{5,7},{6,0},{7,1},{8,10},{9,11},{10,... | collective-permute-start | bytes 786440 | tf_op jit(solution)/shard_map/group_0/ppermute | solution.py:492
  69.2 23.2 %collective-permute-start.11 = (bf16[128,1024]{1,0:T(8,128)(2,1)}, bf16[128,1024]{1,0:T(8,128)(2,1)S(1)}, u32[]{:S(2)}, u32[]{:S(2)}) collective-permute-start(bf16[128,1024]{1,0:T(8,128)(2,1)} %get-tuple-element.157), channel_id=1, source_target_pairs={{0,3},{1,2},{2,5},{3,4},{4,7},{5,6},{6,1},{7,0},{8,11},{9,10},{10,... | collective-permute-start | bytes 786440 | tf_op jit(solution)/shard_map/group_0/ppermute | solution.py:492
  69.5 22.8 %collective-permute-start.12 = (bf16[128,1024]{1,0:T(8,128)(2,1)}, bf16[128,1024]{1,0:T(8,128)(2,1)S(1)}, u32[]{:S(2)}, u32[]{:S(2)}) collective-permute-start(bf16[128,1024]{1,0:T(8,128)(2,1)} %get-tuple-element.158), channel_id=1, source_target_pairs={{0,4},{1,5},{2,6},{3,7},{4,0},{5,1},{6,2},{7,3},{8,12},{9,13},{10,... | collective-permute-start | bytes 786440 | tf_op jit(solution)/shard_map/group_0/ppermute | solution.py:492
  70.9 21.4 %collective-permute-start.13 = (bf16[128,1024]{1,0:T(8,128)(2,1)}, bf16[128,1024]{1,0:T(8,128)(2,1)S(1)}, u32[]{:S(2)}, u32[]{:S(2)}) collective-permute-start(bf16[128,1024]{1,0:T(8,128)(2,1)} %get-tuple-element.159), channel_id=1, source_target_pairs={{0,5},{1,4},{2,7},{3,6},{4,1},{5,0},{6,3},{7,2},{8,13},{9,12},{10,... | collective-permute-start | bytes 786440 | tf_op jit(solution)/shard_map/group_0/ppermute | solution.py:492
  72.7 19.6 %collective-permute-start.14 = (bf16[128,1024]{1,0:T(8,128)(2,1)S(1)}, bf16[128,1024]{1,0:T(8,128)(2,1)S(1)}, u32[]{:S(2)}, u32[]{:S(2)}) collective-permute-start(bf16[128,1024]{1,0:T(8,128)(2,1)S(1)} %copy-done.10), channel_id=1, source_target_pairs={{0,6},{1,7},{2,0},{3,1},{4,2},{5,3},{6,4},{7,5},{8,14},{9,15},{10,... | collective-permute-start | bytes 786440 | tf_op jit(solution)/shard_map/group_0/ppermute | solution.py:492
  76.2 20.4 %collective-permute-start.15 = (bf16[128,1024]{1,0:T(8,128)(2,1)S(1)}, bf16[128,1024]{1,0:T(8,128)(2,1)S(1)}, u32[]{:S(2)}, u32[]{:S(2)}) collective-permute-start(bf16[128,1024]{1,0:T(8,128)(2,1)S(1)} %copy-done.9), channel_id=1, source_target_pairs={{0,7},{1,6},{2,1},{3,0},{4,3},{5,2},{6,5},{7,4},{8,15},{9,14},{10,... | collective-permute-start | bytes 786440 | tf_op jit(solution)/shard_map/group_0/ppermute | solution.py:492
  96.6 16.6 %collective-permute-start.16 = (bf16[16,17,16,128]{3,2,1,0:T(8,128)(2,1)}, bf16[16,17,16,128]{3,2,1,0:T(8,128)(2,1)}, u32[]{:S(2)}, u32[]{:S(2)}) collective-permute-start(bf16[16,17,16,128]{3,2,1,0:T(8,128)(2,1)} %all-to-all-done.2.refs_0_), channel_id=1, source_target_pairs={{0,1},{1,0},{2,3},{3,2},{4,5},{5,4},{6,7},{7,6},{8,9},{9,8},{10,11... | collective-permute-start | bytes 3342344 | tf_op jit(solution)/shard_map/group_0/ppermute | solution.py:496
  105.9 26.3 %all-to-all-start.3 = ((bf16[16,17,16,128]{3,2,1,0:T(8,128)(2,1)}), bf16[16,17,16,128]{3,2,1,0:T(8,128)(2,1)S(1)}, u32[]{:S(2)}, u32[]{:S(2)}) async-start(bf16[16,17,16,128]{3,2,1,0:T(8,128)(2,1)} %group_1.1), calls=%async_computation.3 | async-start | bytes 2228224 | tf_op jit(solution)/shard_map/group_1/all_to_all | solution.py:390
  117.8 14.4 %collective-permute-start.17 = (bf16[97,16,128]{2,1,0:T(8,128)(2,1)S(1)}, bf16[97,16,128]{2,1,0:T(8,128)(2,1)S(1)}, u32[]{:S(2)}, u32[]{:S(2)}) collective-permute-start(bf16[97,16,128]{2,1,0:T(8,128)(2,1)S(1)} %get-tuple-element.177), channel_id=1, source_target_pairs={{0,2},{1,3},{2,4},{3,5},{4,6},{5,7},{6,0},{7,1},{8,10},{9,11},{10,... | collective-permute-start | bytes 1191944 | tf_op jit(solution)/shard_map/spread_0/ppermute | solution.py:488
  118.1 14.1 %collective-permute-start.18 = (bf16[97,16,128]{2,1,0:T(8,128)(2,1)S(1)}, bf16[97,16,128]{2,1,0:T(8,128)(2,1)S(1)}, u32[]{:S(2)}, u32[]{:S(2)}) collective-permute-start(bf16[97,16,128]{2,1,0:T(8,128)(2,1)S(1)} %get-tuple-element.178), channel_id=1, source_target_pairs={{0,4},{1,5},{2,6},{3,7},{4,0},{5,1},{6,2},{7,3},{8,12},{9,13},{10,... | collective-permute-start | bytes 1191944 | tf_op jit(solution)/shard_map/spread_0/ppermute | solution.py:488
  119.6 19.5 %collective-permute-start.19 = (bf16[97,16,128]{2,1,0:T(8,128)(2,1)S(1)}, bf16[97,16,128]{2,1,0:T(8,128)(2,1)}, u32[]{:S(2)}, u32[]{:S(2)}) collective-permute-start(bf16[97,16,128]{2,1,0:T(8,128)(2,1)S(1)} %get-tuple-element.179), channel_id=1, source_target_pairs={{0,6},{1,7},{2,0},{3,1},{4,2},{5,3},{6,4},{7,5},{8,14},{9,15},{10,... | collective-permute-start | bytes 1191944 | tf_op jit(solution)/shard_map/spread_0/ppermute | solution.py:488
  145.4 12.2 %collective-permute-start.21 = (bf16[97,16,128]{2,1,0:T(8,128)(2,1)S(1)}, bf16[97,16,128]{2,1,0:T(8,128)(2,1)}, u32[]{:S(2)}, u32[]{:S(2)}) collective-permute-start(bf16[97,16,128]{2,1,0:T(8,128)(2,1)S(1)} %get-tuple-element.188), channel_id=1, source_target_pairs={{0,2},{1,3},{2,4},{3,5},{4,6},{5,7},{6,0},{7,1},{8,10},{9,11},{10,... | collective-permute-start | bytes 1191944 | tf_op jit(solution)/shard_map/spread_1/ppermute | solution.py:488
  146.5 13.7 %collective-permute-start.22 = (bf16[97,16,128]{2,1,0:T(8,128)(2,1)S(1)}, bf16[97,16,128]{2,1,0:T(8,128)(2,1)}, u32[]{:S(2)}, u32[]{:S(2)}) collective-permute-start(bf16[97,16,128]{2,1,0:T(8,128)(2,1)S(1)} %get-tuple-element.189), channel_id=1, source_target_pairs={{0,4},{1,5},{2,6},{3,7},{4,0},{5,1},{6,2},{7,3},{8,12},{9,13},{10,... | collective-permute-start | bytes 1191944 | tf_op jit(solution)/shard_map/spread_1/ppermute | solution.py:488
  147.5 20.0 %collective-permute-start.23 = (bf16[97,16,128]{2,1,0:T(8,128)(2,1)S(1)}, bf16[97,16,128]{2,1,0:T(8,128)(2,1)}, u32[]{:S(2)}, u32[]{:S(2)}) collective-permute-start(bf16[97,16,128]{2,1,0:T(8,128)(2,1)S(1)} %get-tuple-element.190), channel_id=1, source_target_pairs={{0,6},{1,7},{2,0},{3,1},{4,2},{5,3},{6,4},{7,5},{8,14},{9,15},{10,... | collective-permute-start | bytes 1191944 | tf_op jit(solution)/shard_map/spread_1/ppermute | solution.py:488
  (12 other events, 98.2 us)

commit v6 on v4

--- a/solution.py
+++ b/solution.py
@@ -24,6 +24,7 @@
 TILES = HALF // LANE
 SEND_TILES = REQ * TILES + 1
 DENSE = PAN_DEV * TILES
+LOAD_TILES = PAN_DEV // ROWS
 LISTED = 36
 
 sharpness_divisor = 16.0
@@ -39,20 +40,71 @@
     return pltpu.CompilerParams(vmem_limit_bytes=mib * MIB)
 
 
-def pick_kernel(ids, table, out, held, sems):
-    def fetch(n):
-        return pltpu.make_async_copy(table.at[ids[n]], held.at[n], sems.at[0, n])
-
-    def put(n):
-        return pltpu.make_async_copy(held.at[n], out.at[n], sems.at[1, n])
-
-    for n in range(ids.shape[0]):
-        fetch(n).start()
-    for n in range(ids.shape[0]):
-        fetch(n).wait()
-        put(n).start()
-    for n in range(ids.shape[0]):
-        put(n).wait()
+def whole(shape):
+    return pl.BlockSpec(shape, lambda *_: (0,) * len(shape))
+
+
+def smem_spec():
+    return pl.BlockSpec(memory_space=pltpu.SMEM)
+
+
+def vmem_spec():
+    return pl.BlockSpec(memory_space=pltpu.VMEM)
+
+
+def hbm_spec():
+    return pl.BlockSpec(memory_space=pltpu.HBM)
+
+
+def ask_kernel(candidates_in, home_in, loads_in, out, candidates, home, loads, sems):
+    copies = [
+        pltpu.make_async_copy(source, target, sems.at[n])
+        for n, (source, target) in enumerate(((candidates_in, candidates), (home_in, home), (loads_in, loads)))
+    ]
+    for copy in copies:
+        copy.start()
+    for copy in copies:
+        copy.wait()
+    row = lax.broadcasted_iota(jnp.int32, (ROWS, LANE), 0)
+    lane = lax.broadcasted_iota(jnp.int32, (ROWS, LANE), 1)
+    slots = [home[candidates[n // CAND, n % CAND]] for n in range(REQ)]
+    common = jnp.zeros((ROWS, LANE), F32)
+    for n, slot in enumerate(slots):
+        common = jnp.where((row == 1) & (lane == n), (slot // PAN_DEV).astype(F32), common)
+        common = jnp.where((row == 2) & (lane == n), (slot % PAN_DEV).astype(F32), common)
+    for o in range(N_CENT):
+        tile = common
+        for n, slot in enumerate(slots):
+            here = jnp.where(slot // PAN_DEV == o, slot % PAN_DEV, 0).astype(F32)
+            tile = jnp.where((row == 0) & (lane == n // CAND), tile + here, tile)
+        for t in range(LOAD_TILES):
+            out[o, t] = loads[t * ROWS : (t + 1) * ROWS]
+        out[o, LOAD_TILES] = tile.astype(BF16)
+
+
+def ask(candidates, home, loads):
+    return pl.pallas_call(
+        ask_kernel,
+        in_specs=[hbm_spec()] * 3,
+        out_specs=vmem_spec(),
+        out_shape=jax.ShapeDtypeStruct((N_CENT, LOAD_TILES + 1, ROWS, LANE), BF16),
+        scratch_shapes=[
+            pltpu.SMEM(candidates.shape, jnp.int32),
+            pltpu.SMEM(home.shape, jnp.int32),
+            pltpu.VMEM(loads.shape, BF16),
+            pltpu.SemaphoreType.DMA((3,)),
+        ],
+        compiler_params=params(60),
+        cost_estimate=pl.CostEstimate(flops=1 << 16, bytes_accessed=1 << 18, transcendentals=0),
+    )(candidates, home, loads)
+
+
+def pick_kernel(ids, table, out, sems):
+    copies = [pltpu.make_async_copy(table.at[ids[n]], out.at[n], sems.at[n]) for n in range(out.shape[0])]
+    for copy in copies:
+        copy.start()
+    for copy in copies:
+        copy.wait()
 
 
 def pick_panels(ids, table):
@@ -60,110 +112,98 @@
     return pl.pallas_call(
         pick_kernel,
         out_shape=jax.ShapeDtypeStruct((count, PANEL, WIDTH), BF16),
-        in_specs=[pl.BlockSpec(memory_space=pltpu.SMEM), pl.BlockSpec(memory_space=pltpu.HBM)],
-        out_specs=pl.BlockSpec(memory_space=pltpu.HBM),
-        scratch_shapes=[pltpu.VMEM((count, PANEL, WIDTH), BF16), pltpu.SemaphoreType.DMA((2, count))],
-        compiler_params=params(60),
+        in_specs=[smem_spec(), hbm_spec()],
+        out_specs=vmem_spec(),
+        scratch_shapes=[pltpu.SemaphoreType.DMA((count,))],
+        compiler_params=params(56),
         cost_estimate=pl.CostEstimate(flops=0, bytes_accessed=4 * count * PANEL * WIDTH, transcendentals=0),
     )(ids, table)
 
 
-def whole(shape):
-    return pl.BlockSpec(shape, lambda *_: (0,) * len(shape))
-
-
-def smem_spec():
-    return pl.BlockSpec(memory_space=pltpu.SMEM)
-
-
-def score_kernel(target, points, c0, c1, c2, c3, surcharge, out, centers, shares, marks):
-    del target
-    group = pl.program_id(0)
-    for j, panel in enumerate((c0, c1, c2, c3)):
-        centers[j * PANEL : (j + 1) * PANEL, :] = panel[0]
-    wide = centers[...].astype(F32)
-    squares = jnp.sum(wide * wide, axis=1, keepdims=True)
-    bias = squares * (1.0 / sharpness_divisor) + evenness_coefficient * surcharge[0]
+def score_kernel(target, points, arrived, surcharge, out, members, centers, shares, sems):
     step = 256
-    weights = jnp.zeros((CAND * PANEL, LANE), F32)
-    for s in range(GROUP // step):
-        block = points[s * step : (s + 1) * step, :]
-        inner = lax.dot_general(centers[...], block, (((1,), (1,)), ((), ())), preferred_element_type=F32)
-        logits = inner * (2.0 / sharpness_divisor) - bias
-        highest = jnp.max(logits, axis=0, keepdims=True)
-        raised = jnp.exp(logits - highest)
-        scale = 1.0 / jnp.sum(raised, axis=0, keepdims=True)
-        share = (raised * scale).astype(BF16)
-        shares[:, s * step : (s + 1) * step] = share
-        rounded = share.astype(F32)
-        for part in range(step // LANE):
-            weights = weights + rounded[:, part * LANE : (part + 1) * LANE]
-    weight = jnp.sum(weights, axis=1, keepdims=True)
-    coarse = weight.astype(BF16).astype(F32)
-    fine = weight - coarse
+    steps = GROUP // step
+
+    def land(n):
+        rows = pl.ds(n * PANEL, PANEL)
+        return pltpu.make_async_copy(arrived.at[target[n]], centers.at[rows], sems.at[0, n])
+
+    def bring(n):
+        rows = pl.ds(n * step, step)
+        return pltpu.make_async_copy(points.at[rows], members.at[rows], sems.at[1, n])
+
+    for group in range(GROUPS_DEV):
+        for j in range(CAND):
+            land(group * CAND + j).start()
+        for s in range(steps):
+            bring(group * steps + s).start()
     lane = lax.broadcasted_iota(jnp.int32, (PANEL, LANE), 1)
-
-    @pl.when(group == 0)
-    def _():
-        marks[...] = jnp.zeros_like(marks)
-
-    tile = marks[...]
-    for j in range(CAND):
-        place = group * CAND + j
-        rows = slice(j * PANEL, (j + 1) * PANEL)
-        tile = jnp.where(lane == place, coarse[rows], tile)
-        tile = jnp.where(lane == REQ + place, fine[rows], tile)
-    marks[...] = tile
-
-    wide_step = 256
-    for s in range(WIDTH // wide_step):
-        part = lax.dot_general(
-            shares[...], points[:, s * wide_step : (s + 1) * wide_step], (((1,), (0,)), ((), ())),
-            preferred_element_type=F32,
-        ).astype(BF16)
-        for t in range(wide_step // LANE):
-            column = s * (wide_step // LANE) + t
-            half, tile_at = divmod(column, TILES)
-            for j in range(CAND):
-                for block_at in range(PANEL // ROWS):
-                    row = j * PANEL + block_at * ROWS
-                    out[block_at * 2 + half, (group * CAND + j) * TILES + tile_at] = part[
-                        row : row + ROWS, t * LANE : (t + 1) * LANE
-                    ]
-
-    @pl.when(group == GROUPS_DEV - 1)
-    def _():
-        last = marks[...].astype(BF16)
-        for block_at in range(PANEL // ROWS):
-            for half in range(2):
-                out[block_at * 2 + half, REQ * TILES] = last[block_at * ROWS : (block_at + 1) * ROWS]
+    tile = jnp.zeros((PANEL, LANE), F32)
+    for group in range(GROUPS_DEV):
+        for j in range(CAND):
+            land(group * CAND + j).wait()
+        mine = centers[group * CAND * PANEL : (group + 1) * CAND * PANEL, :]
+        wide = mine.astype(F32)
+        squares = jnp.sum(wide * wide, axis=1, keepdims=True)
+        bias = squares * (1.0 / sharpness_divisor) + evenness_coefficient * surcharge[group]
+        weights = jnp.zeros((CAND * PANEL, LANE), F32)
+        for s in range(steps):
+            bring(group * steps + s).wait()
+            block = members[group * GROUP + s * step : group * GROUP + (s + 1) * step, :]
+            inner = lax.dot_general(mine, block, (((1,), (1,)), ((), ())), preferred_element_type=F32)
+            logits = inner * (2.0 / sharpness_divisor) - bias
+            highest = jnp.max(logits, axis=0, keepdims=True)
+            raised = jnp.exp(logits - highest)
+            scale = 1.0 / jnp.sum(raised, axis=0, keepdims=True)
+            share = (raised * scale).astype(BF16)
+            shares[:, s * step : (s + 1) * step] = share
+            rounded = share.astype(F32)
+            for part in range(step // LANE):
+                weights = weights + rounded[:, part * LANE : (part + 1) * LANE]
+        weight = jnp.sum(weights, axis=1, keepdims=True)
+        coarse = weight.astype(BF16).astype(F32)
+        fine = weight - coarse
+        for j in range(CAND):
+            rows = slice(j * PANEL, (j + 1) * PANEL)
+            tile = jnp.where(lane == group * CAND + j, coarse[rows], tile)
+            tile = jnp.where(lane == REQ + group * CAND + j, fine[rows], tile)
+        wide_step = 256
+        for s in range(WIDTH // wide_step):
+            part = lax.dot_general(
+                shares[...],
+                members[group * GROUP : (group + 1) * GROUP, s * wide_step : (s + 1) * wide_step],
+                (((1,), (0,)), ((), ())),
+                preferred_element_type=F32,
+            ).astype(BF16)
+            for t in range(wide_step // LANE):
+                half, tile_at = divmod(s * (wide_step // LANE) + t, TILES)
+                for j in range(CAND):
+                    for block_at in range(PANEL // ROWS):
+                        row = j * PANEL + block_at * ROWS
+                        out[block_at * 2 + half, (group * CAND + j) * TILES + tile_at] = part[
+                            row : row + ROWS, t * LANE : (t + 1) * LANE
+                        ]
+    tile = tile.astype(BF16)
+    for block_at in range(PANEL // ROWS):
+        for half in range(2):
+            out[block_at * 2 + half, REQ * TILES] = tile[block_at * ROWS : (block_at + 1) * ROWS]
 
 
 def score(target, points, arrived, surcharge):
-    def panel(j):
-        return pl.BlockSpec((1, PANEL, WIDTH), lambda g, t: (t[g * CAND + j], 0, 0))
-
     return pl.pallas_call(
         score_kernel,
-        grid_spec=pltpu.PrefetchScalarGridSpec(
-            num_scalar_prefetch=1,
-            grid=(GROUPS_DEV,),
-            in_specs=[
-                pl.BlockSpec((GROUP, WIDTH), lambda g, t: (g, 0)),
-                panel(0), panel(1), panel(2), panel(3),
-                pl.BlockSpec((1, CAND * PANEL, 1), lambda g, t: (g, 0, 0)),
-            ],
-            out_specs=pl.BlockSpec((N_PTS, SEND_TILES, ROWS, LANE), lambda g, t: (0, 0, 0, 0)),
-            scratch_shapes=[
-                pltpu.VMEM((CAND * PANEL, WIDTH), BF16),
-                pltpu.VMEM((CAND * PANEL, GROUP), BF16),
-                pltpu.VMEM((PANEL, LANE), F32),
-            ],
-        ),
+        in_specs=[smem_spec(), hbm_spec(), hbm_spec(), vmem_spec()],
+        out_specs=vmem_spec(),
         out_shape=jax.ShapeDtypeStruct((N_PTS, SEND_TILES, ROWS, LANE), BF16),
+        scratch_shapes=[
+            pltpu.VMEM((GROUPS_DEV * GROUP, WIDTH), BF16),
+            pltpu.VMEM((GROUPS_DEV * CAND * PANEL, WIDTH), BF16),
+            pltpu.VMEM((CAND * PANEL, GROUP), BF16),
+            pltpu.SemaphoreType.DMA((2, 8)),
+        ],
         compiler_params=params(48),
-        cost_estimate=pl.CostEstimate(flops=4294967296, bytes_accessed=10 * MIB, transcendentals=1 << 20),
-    )(target, points, arrived, arrived, arrived, arrived, surcharge)
+        cost_estimate=pl.CostEstimate(flops=4 << 30, bytes_accessed=10 * MIB, transcendentals=1 << 20),
+    )(target, points, arrived, surcharge)
 
 
 def spread_kernel(rows, places, mine, mate, lanes, own, own_weights, out1, out2, out3, total):
@@ -200,20 +240,23 @@
     chunk = jax.ShapeDtypeStruct((rows * TILES + 1, ROWS, LANE), BF16)
     return pl.pallas_call(
         functools.partial(spread_kernel, rows),
-        grid=(1,),
-        in_specs=[smem_spec()] + [whole(mine.shape)] * 2 + [whole((2 * N_PTS, LANE))],
-        out_specs=[whole((DENSE, ROWS, LANE)), whole((ROWS, LANE))] + [whole(chunk.shape)] * 3,
+        in_specs=[smem_spec()] + [vmem_spec()] * 3,
+        out_specs=[vmem_spec()] * 5,
         out_shape=[
             jax.ShapeDtypeStruct((DENSE, ROWS, LANE), F32), jax.ShapeDtypeStruct((ROWS, LANE), F32),
             chunk, chunk, chunk,
         ],
         scratch_shapes=[pltpu.VMEM(((PAN_DEV + 3 * rows + 1) * TILES, ROWS, LANE), F32)],
-        compiler_params=params(48),
+        compiler_params=params(16),
         cost_estimate=pl.CostEstimate(flops=1 << 22, bytes_accessed=8 * MIB, transcendentals=0),
     )(places, mine, mate, lanes)
 
 
-def finish_kernel(rows, numbers, own, own_weights, in1, in2, in3, lanes, old, out, total):
+def finish_kernel(rows, numbers, own, own_weights, in1, in2, in3, lanes, table, out, total, old, sem):
+    row = pl.multiple_of(numbers[0] // 2 * ROWS, ROWS)
+    column = pl.multiple_of(numbers[0] % 2 * HALF, HALF)
+    fetch = pltpu.make_async_copy(table.at[:, pl.ds(row, ROWS), pl.ds(column, HALF)], old, sem)
+    fetch.start()
     weights = own_weights[:, 0:PAN_DEV]
     panel = lax.broadcasted_iota(jnp.int32, (PAN_DEV, LANE), 0)
     total[...] = own[...]
@@ -231,6 +274,7 @@
 
         lax.fori_loop(0, numbers[1 + d], add, 0)
     inverse = 1.0 / (weights + prior_mass)
+    fetch.wait()
     for q in range(PAN_DEV):
         scale = jnp.broadcast_to(inverse[:, q : q + 1], (ROWS, LANE))
         for t in range(TILES):
@@ -245,21 +289,16 @@
 
 
 def finish(rows, numbers, own, own_weights, arrived, lanes, table):
-    chunk = whole((rows * TILES + 1, ROWS, LANE))
-    fresh = (N_PTS, CAND * TILES + 1, ROWS, LANE)
     return pl.pallas_call(
         functools.partial(finish_kernel, rows),
-        grid_spec=pltpu.PrefetchScalarGridSpec(
-            num_scalar_prefetch=1,
-            grid=(1,),
-            in_specs=[
-                whole((DENSE, ROWS, LANE)), whole((ROWS, LANE)), chunk, chunk, chunk, whole((CHIPS - 1, LANE)),
-                pl.BlockSpec((PAN_DEV, ROWS, HALF), lambda g, n: (0, n[0] // 2, n[0] % 2)),
-            ],
-            out_specs=whole(fresh),
-            scratch_shapes=[pltpu.VMEM((DENSE, ROWS, LANE), F32)],
-        ),
-        out_shape=jax.ShapeDtypeStruct(fresh, BF16),
+        in_specs=[smem_spec()] + [vmem_spec()] * 6 + [hbm_spec()],
+        out_specs=vmem_spec(),
+        out_shape=jax.ShapeDtypeStruct((N_PTS, CAND * TILES + 1, ROWS, LANE), BF16),
+        scratch_shapes=[
+            pltpu.VMEM((DENSE, ROWS, LANE), F32),
+            pltpu.VMEM((PAN_DEV, ROWS, HALF), BF16),
+            pltpu.SemaphoreType.DMA,
+        ],
         compiler_params=params(48),
         cost_estimate=pl.CostEstimate(flops=1 << 22, bytes_accessed=6 * MIB, transcendentals=0),
     )(numbers, own, own_weights, *arrived, lanes, table)
@@ -281,7 +320,7 @@
     for block_at in range(PANEL // ROWS):
         pair = pieces[block_at * 2, CAND * TILES]
         part = lax.dot_general(chosen, pair, (((1,), (1,)), ((), ())), preferred_element_type=F32)
-        loads[:, block_at * ROWS : (block_at + 1) * ROWS] = part[0:8]
+        loads[:, block_at * ROWS : (block_at + 1) * ROWS] = part[0:CAND]
 
 
 def place(me, pieces):
@@ -289,10 +328,10 @@
         place_kernel,
         grid=(1,),
         in_specs=[smem_spec(), whole(pieces.shape)],
-        out_specs=[whole((CAND, PANEL, WIDTH)), whole((8, PANEL))],
+        out_specs=[whole((CAND, PANEL, WIDTH)), whole((CAND, PANEL))],
         out_shape=[
             jax.ShapeDtypeStruct((CAND, PANEL, WIDTH), BF16),
-            jax.ShapeDtypeStruct((8, PANEL), F32),
+            jax.ShapeDtypeStruct((CAND, PANEL), F32),
         ],
         compiler_params=params(32),
         cost_estimate=pl.CostEstimate(flops=1 << 20, bytes_accessed=2 * MIB, transcendentals=0),
@@ -328,36 +367,23 @@
     shelf = centroids.reshape(PAN_DEV, PANEL, WIDTH)
 
     with jax.named_scope("requests"):
-        wanted_ids = candidates.reshape(REQ)
+        answered = exchange(ask(candidates, panel_home, prev_loads.reshape(PAN_DEV, PANEL)), "cent")
+        asked = answered[:, LOAD_TILES, 0, 0:GROUPS_DEV].astype(jnp.int32).reshape(-1)
+
+    with jax.named_scope("gather_panels"):
+        ready = pick_panels(asked, shelf)
+        arrived = exchange(ready.reshape(N_CENT, GROUPS_DEV, PANEL, WIDTH), "cent")
+        arrived = arrived.reshape(N_CENT * GROUPS_DEV, PANEL, WIDTH)
+
+    with jax.named_scope("own_requests"):
         slots = jnp.sum(
-            jnp.where(wanted_ids[:, None] == jnp.arange(panel_home.shape[0], dtype=jnp.int32), panel_home[None, :], 0),
+            jnp.where(candidates.reshape(REQ)[:, None] == jnp.arange(panel_home.shape[0], dtype=jnp.int32), panel_home[None, :], 0),
             axis=1,
         )
-        owners, local_ids = slots // PAN_DEV, slots % PAN_DEV
-        target = owners * GROUPS_DEV + jnp.arange(REQ, dtype=jnp.int32) // CAND
-        spots = jnp.arange(N_CENT * GROUPS_DEV, dtype=jnp.int32)
-        wanted = jnp.sum(jnp.where(target[None, :] == spots[:, None], local_ids[None, :], 0), axis=1)
-        ask = jnp.stack(
-            [
-                jnp.pad(wanted.reshape(N_CENT, GROUPS_DEV), ((0, 0), (0, LANE - GROUPS_DEV))),
-                jnp.broadcast_to(jnp.pad(owners, (0, LANE - REQ)), (N_CENT, LANE)),
-                jnp.broadcast_to(jnp.pad(local_ids, (0, LANE - REQ)), (N_CENT, LANE)),
-            ],
-            axis=1,
-        ).astype(BF16)
-        ask = jnp.pad(ask, ((0, 0), (0, ROWS - 3), (0, 0))).reshape(N_CENT, 1, ROWS, LANE)
-        table = jnp.broadcast_to(
-            prev_loads.reshape(1, PAN_DEV // ROWS, ROWS, LANE), (N_CENT, PAN_DEV // ROWS, ROWS, LANE)
-        )
-        answered = exchange(jnp.concatenate([table, ask], axis=1), "cent")
-        asked = answered[:, PAN_DEV // ROWS, 0, 0:GROUPS_DEV].astype(jnp.int32).reshape(-1)
-
-    with jax.named_scope("gather_panels"):
-        arrived = exchange(pick_panels(asked, shelf).reshape(N_CENT, GROUPS_DEV, PANEL, WIDTH), "cent")
-        arrived = arrived.reshape(N_CENT * GROUPS_DEV, PANEL, WIDTH)
+        target = slots // PAN_DEV * GROUPS_DEV + jnp.arange(REQ, dtype=jnp.int32) // CAND
 
     with jax.named_scope("all_requests"):
-        ring = answered[:, PAN_DEV // ROWS, 1:3, 0:REQ].astype(jnp.int32)
+        ring = answered[:, LOAD_TILES, 1:3, 0:REQ].astype(jnp.int32)
         ring = ring[:, 0] * PAN_DEV + ring[:, 1]
         line = spread_out(ring, me % SIDE, 1, 0)
         everyone = spread_out(line, me // SIDE, 0, 1).reshape(N_PTS, N_CENT, REQ)
@@ -410,7 +436,7 @@
         target, too_long, short = lax.optimization_barrier((target, too_long, short))
 
     with jax.named_scope("loads"):
-        load_table = answered[:, : PAN_DEV // ROWS].reshape(N_CENT * PAN_DEV, PANEL)
+        load_table = answered[:, :LOAD_TILES].reshape(N_CENT * PAN_DEV, PANEL)
         loads = jnp.take(load_table, slots, axis=0, mode="clip").astype(F32)
         surcharge = jnp.log(loads).reshape(GROUPS_DEV, CAND * PANEL, 1)
 
@@ -436,7 +462,7 @@
 
     with jax.named_scope("place"):
         new_centroids, new_loads = place(me.reshape(1), exchange(fresh, "pts"))
-    return new_centroids.reshape(CAND * PANEL, WIDTH), new_loads[0:CAND].reshape(CAND * PANEL)
+    return new_centroids.reshape(CAND * PANEL, WIDTH), new_loads.reshape(CAND * PANEL)
 
 
 def solution(mesh):

time: 188 us -> 187 us (level)
  Pallas kernels: 23.9 us -> 27.1 us
  waiting for transfers between devices: 67.5 us -> 64.6 us
    pallas_call x3 -> x4, Pallas kernels: 17.2 us -> 20.5 us  [the longest x1 11.7 us: score(): pl.pallas_call(score_kernel, in_specs=[smem_spec(), hbm_spec(), hbm_spec(...]
    all_to_all x2, waiting for transfers between devices: 31 us -> 28.2 us  [exchange(): return lax.all_to_all(x, axis, split_axis=0, concat_axis=0, tiled=True)]
  transfers between devices with their start and end apart: 12 -> 12, of which waited for: 7 -> 7; matrix products, arithmetic and copies ran while one was open for 3% -> 4% of each run, Pallas kernels for 0% -> 0%
where the time goes in v6:
time: 187 us
  waiting for transfers between devices  64.6 us (35%)
  blocking collectives  59.2 us (32%)
  starting transfers between devices  27.4 us (15%)
  Pallas kernels  27.1 us (14%)
  other arithmetic  3.8 us (2%)
  local copies, waits for them, and re-layouts  3.31 us (2%)
    all_to_all x2, blocking collectives, exchange(): return lax.all_to_all(x, axis, split_axis=0, concat_axis=0, tiled=True)  59.2 us
    all_to_all x2, waiting for transfers between devices, exchange(): return lax.all_to_all(x, axis, split_axis=0, concat_axis=0, tiled=True)  28.2 us
    ppermute x3, waiting for transfers between devices, sum_over_chips(): lax.ppermute(far[d - 1], 'cent', shift(d, 0))  27.8 us
    ppermute x6, starting transfers between devices, spread_out(): held.append(lax.ppermute(x, 'pts', pairs))  12.1 us
    all_to_all x2, starting transfers between devices, exchange(): return lax.all_to_all(x, axis, split_axis=0, concat_axis=0, tiled=True)  11.7 us
    pallas_call x1, Pallas kernels, score(): pl.pallas_call(score_kernel, in_specs=[smem_spec(), hbm_spec(), hbm_spec(...  11.7 us
    pallas_call x1, Pallas kernels, pick_panels(): pl.pallas_call(pick_kernel, out_shape=jax.ShapeDtypeStruct((count, PANEL,...  5.45 us
    ppermute x6, waiting for transfers between devices, spread_out(): held.append(lax.ppermute(x, 'pts', pairs))  4.9 us
  transfers between devices with their start and end apart: 12, of which 7 were waited for; matrix products, arithmetic and copies ran while one was open for 4% of the time, Pallas kernels for 0%

profile of v6, /device:TPU:24, one launch (start us, length us, event | category | flops | bytes accessed | tf_op | source)
XLA Modules:
  0.0 187.2 jit_solution(5235122882630790045)
XLA Ops:
  0.6 1.5 requests.1
  2.2 4.7 %all-to-all-start = ((bf16[8,5,16,128]{3,2,1,0:T(8,128)(2,1)}), bf16[8,5,16,128]{3,2,1,0:T(8,128)(2,1)S(1)}, u32[]{:S(2)}, u32[]{:S(2)}) async-start(bf16[8,5,16,128]{3,2,1,0:T(8,128)(2,1)} %requests.1), calls=%async_computation | async-start | bytes 327680 | tf_op jit(solution)/shard_map/requests/all_to_all | solution.py:360
  8.8 2.5 %all-to-all-done = bf16[8,5,16,128]{3,2,1,0:T(8,128)(2,1)S(1)} async-done(((bf16[8,5,16,128]{3,2,1,0:T(8,128)(2,1)}), bf16[8,5,16,128]{3,2,1,0:T(8,128)(2,1)S(1)}, u32[]{:S(2)}, u32[]{:S(2)}) %all-to-all-start) | async-done | bytes 163872 | tf_op jit(solution)/shard_map/requests/all_to_all | solution.py:360
  11.9 5.5 %gather_panels.1 = bf16[16,128,1024]{2,1,0:T(8,128)(2,1)} custom-call(s32[16]{0:T(128)} %reshape.238.ids, bf16[64,128,1024]{2,1,0:T(8,128)(2,1)} %bitcast.57), custom_call_target="tpu_custom_call" | custom-call | bytes 8388608 | tf_op jit(solution)/shard_map/gather_panels/pallas_call | solution.py:112
  17.4 7.0 %all-to-all-start.1 = ((bf16[8,2,128,1024]{3,2,1,0:T(8,128)(2,1)}), bf16[8,2,128,1024]{3,2,1,0:T(8,128)(2,1)}, u32[]{:S(2)}, u32[]{:S(2)}) async-start(bf16[8,2,128,1024]{3,2,1,0:T(8,128)(2,1)} %bitcast.60), calls=%async_computation.1 | async-start | bytes 8388608 | tf_op jit(solution)/shard_map/gather_panels/all_to_all | solution.py:360
  24.4 3.9 %collective-permute-start.8 = (s32[8,8]{1,0:T(8,128)S(1)}, s32[8,8]{1,0:T(8,128)S(1)}, u32[]{:S(2)}, u32[]{:S(2)}) collective-permute-start(s32[8,8]{1,0:T(8,128)S(1)} %get-tuple-element.141), channel_id=1, source_target_pairs={{0,24},{8,0},{16,8},{24,16},{32,56},{40,32},{48,40},{56,48},{64,88... | collective-permute-start | bytes 776 | tf_op jit(solution)/shard_map/all_requests/ppermute | solution.py:353
  28.3 1.0 collective-permute-start.6
  29.9 3.5 %collective-permute-done.7 = s32[8,8]{1,0:T(8,128)S(1)} collective-permute-done((s32[8,8]{1,0:T(8,128)S(1)}, s32[8,8]{1,0:T(8,128)S(1)}, u32[]{:S(2)}, u32[]{:S(2)}) %collective-permute-start.7) | collective-permute-done | bytes 288 | tf_op jit(solution)/shard_map/all_requests/ppermute | solution.py:353
  33.5 3.9 %collective-permute-start.10 = (s32[4,8,8]{2,1,0:T(8,128)S(1)}, s32[4,8,8]{2,1,0:T(8,128)S(1)}, u32[]{:S(2)}, u32[]{:S(2)}) collective-permute-start(s32[4,8,8]{2,1,0:T(8,128)S(1)} %get-tuple-element.138), channel_id=1, source_target_pairs={{0,64},{8,72},{16,80},{24,88},{32,96},{40,104},{48,112},{56,120},{... | collective-permute-start | bytes 3080 | tf_op jit(solution)/shard_map/all_requests/ppermute | solution.py:353
  37.5 3.2 %collective-permute-start.11 = (s32[4,8,8]{2,1,0:T(8,128)S(1)}, s32[4,8,8]{2,1,0:T(8,128)S(1)}, u32[]{:S(2)}, u32[]{:S(2)}) collective-permute-start(s32[4,8,8]{2,1,0:T(8,128)S(1)} %get-tuple-element.138), channel_id=1, source_target_pairs={{0,96},{8,104},{16,112},{24,120},{32,0},{40,8},{48,16},{56,24},{64... | collective-permute-start | bytes 3080 | tf_op jit(solution)/shard_map/all_requests/ppermute | solution.py:353
  41.1 1.3 collective-permute-done.9
  46.3 25.7 %all-to-all-done.1 = bf16[8,2,128,1024]{3,2,1,0:T(8,128)(2,1)} async-done(((bf16[8,2,128,1024]{3,2,1,0:T(8,128)(2,1)}), bf16[8,2,128,1024]{3,2,1,0:T(8,128)(2,1)}, u32[]{:S(2)}, u32[]{:S(2)}) %all-to-all-start.1) | async-done | bytes 4194336 | tf_op jit(solution)/shard_map/gather_panels/all_to_all | solution.py:360
  72.0 11.7 %score.1 = bf16[16,33,16,128]{3,2,1,0:T(8,128)(2,1)S(1)} custom-call(s32[8]{0:T(128)S(1)} %fusion.27.target, bf16[2048,1024]{1,0:T(8,128)(2,1)} %points.1, bf16[16,128,1024]{2,1,0:T(8,128)(2,1)} %bitcast.34.arrived, f32[2,512,1]{2,1,0:T(8,128)S(1)} %log.15.surcharge), custom_call_target="tpu_custom_call" | custom-call | flops 4294967296 | bytes 10485760 | tf_op jit(solution)/shard_map/score/pallas_call | solution.py:193
  83.7 37.4 %all_to_all.20 = bf16[16,33,16,128]{3,2,1,0:T(8,128)(2,1)S(1)} all-to-all(bf16[16,33,16,128]{3,2,1,0:T(8,128)(2,1)S(1)} %score.1), channel_id=1, replica_groups=mesh['pts'=16,'cent'=8] {'pts'}, dimensions={0} | all-to-all | bytes 4325376 | tf_op jit(solution)/shard_map/split_pieces/all_to_all | solution.py:360
  121.8 3.7 %collective-permute-done.12 = bf16[16,33,16,128]{3,2,1,0:T(8,128)(2,1)} collective-permute-done((bf16[16,33,16,128]{3,2,1,0:T(8,128)(2,1)S(1)}, bf16[16,33,16,128]{3,2,1,0:T(8,128)(2,1)}, u32[]{:S(2)}, u32[]{:S(2)}) %collective-permute-start.12) | collective-permute-done | bytes 2162720 | tf_op jit(solution)/shard_map/split_pieces/ppermute | solution.py:448
  125.5 38.7 %conditional.1 = (bf16[16,17,16,128]{3,2,1,0:T(8,128)(2,1)}) conditional(s32[]{:T(128)} %convert_element_type.43, (s32[256]{0:T(256)S(1)}, bf16[16,33,16,128]{3,2,1,0:T(8,128)(2,1)S(1)}, bf16[16,33,16,128]{3,2,1,0:T(8,128)(2,1)}, s32[32,128]{1,0:T(8,128)S(1)}, s32[112]{0:T(128)S(1)}, /*index=5*/s32[3,128]{1,0:T(4,128)S(1)}, ...), branch_computations={%region_15.16_spmd, %region_16.17_spmd} | conditional | flops 8396488 | bytes 36002384 | solution.py:461
  125.5 4.2 %branch_0_fun.2 = (f32[256,16,128]{2,1,0:T(8,128)S(1)}, f32[16,128]{1,0:T(8,128)S(1)}, bf16[145,16,128]{2,1,0:T(8,128)(2,1)S(1)}, bf16[145,16,128]{2,1,0:T(8,128)(2,1)S(1)}, bf16[145,16,128]{2,1,0:T(8,128)(2,1)S(1)}) custom-call(s32[256]{0:T(256)S(1)} %get-tuple-element.20.places, bf16[16,33,16,128]{3,2,1,0:T(8,128)(2,1)S(1)} %get-tuple-element.21.mine, ...), custom_call_target="tpu_custom_call" | custom-call | flops 4194304 | bytes 8388608 | tf_op jit(solution)/shard_map/sum_over_chips/cond/branch_0_fun/pallas_call | solution.py:241
  129.7 2.2 %collective-permute-start = (bf16[145,16,128]{2,1,0:T(8,128)(2,1)S(1)}, bf16[145,16,128]{2,1,0:T(8,128)(2,1)S(1)}, u32[]{:S(2)}, u32[]{:S(2)}) collective-permute-start(bf16[145,16,128]{2,1,0:T(8,128)(2,1)S(1)} %get-tuple-element.42), channel_id=1, source_target_pairs={{0,2},{1,3},{2,4},{3,5},{4,6},{5,7},{6,0},{7,1},{8,10},{9,11},{10,... | collective-permute-start | bytes 1781768 | tf_op jit(solution)/shard_map/sum_over_chips/cond/branch_0_fun/ppermute | solution.py:452
  132.1 1.2 collective-permute-start.2
  133.3 24.3 %collective-permute-done.in1 = bf16[145,16,128]{2,1,0:T(8,128)(2,1)S(1)} collective-permute-done((bf16[145,16,128]{2,1,0:T(8,128)(2,1)S(1)}, bf16[145,16,128]{2,1,0:T(8,128)(2,1)S(1)}, u32[]{:S(2)}, u32[]{:S(2)}) %collective-permute-start) | collective-permute-done | bytes 593952 | tf_op jit(solution)/shard_map/sum_over_chips/cond/branch_0_fun/ppermute | solution.py:452
  157.6 3.5 %collective-permute-done.2.in3 = bf16[145,16,128]{2,1,0:T(8,128)(2,1)S(1)} collective-permute-done((bf16[145,16,128]{2,1,0:T(8,128)(2,1)S(1)}, bf16[145,16,128]{2,1,0:T(8,128)(2,1)S(1)}, u32[]{:S(2)}, u32[]{:S(2)}) %collective-permute-start.2) | collective-permute-done | bytes 593952 | tf_op jit(solution)/shard_map/sum_over_chips/cond/branch_0_fun/ppermute | solution.py:452
  161.1 3.1 %branch_0_fun.3 = bf16[16,17,16,128]{3,2,1,0:T(8,128)(2,1)} custom-call(s32[112]{0:T(128)S(1)} %get-tuple-element.19.numbers, f32[256,16,128]{2,1,0:T(8,128)S(1)} %get-tuple-element.40.own, f32[16,128]{1,0:T(8,128)S(1)} %get-tuple-element.41.own_weights, bf16[145,16,128]{2,1,0:T(8,128)(2,1)S(1)} %collective-permute-done.in1, ...), custom_call_target="tpu_custom_call" | custom-call | flops 4194304 | bytes 6291456 | tf_op jit(solution)/shard_map/sum_over_chips/cond/branch_0_fun/pallas_call | solution.py:292
  164.2 21.8 %all_to_all.21.pieces = bf16[16,17,16,128]{3,2,1,0:T(8,128)(2,1)S(1)} all-to-all(bf16[16,17,16,128]{3,2,1,0:T(8,128)(2,1)} %get-tuple-element.146), channel_id=1, replica_groups=mesh['pts'=16,'cent'=8] {'pts'}, dimensions={0} | all-to-all | bytes 2228224 | tf_op jit(solution)/shard_map/place/all_to_all | solution.py:360
  186.0 1.2 place.1
  (71 shorter events, 7.5 us)
Async XLA Ops:
  2.2 9.1 %all-to-all-start = ((bf16[8,5,16,128]{3,2,1,0:T(8,128)(2,1)}), bf16[8,5,16,128]{3,2,1,0:T(8,128)(2,1)S(1)}, u32[]{:S(2)}, u32[]{:S(2)}) async-start(bf16[8,5,16,128]{3,2,1,0:T(8,128)(2,1)} %requests.1), calls=%async_computation | async-start | bytes 327680 | tf_op jit(solution)/shard_map/requests/all_to_all | solution.py:360
  17.4 54.7 %all-to-all-start.1 = ((bf16[8,2,128,1024]{3,2,1,0:T(8,128)(2,1)}), bf16[8,2,128,1024]{3,2,1,0:T(8,128)(2,1)}, u32[]{:S(2)}, u32[]{:S(2)}) async-start(bf16[8,2,128,1024]{3,2,1,0:T(8,128)(2,1)} %bitcast.60), calls=%async_computation.1 | async-start | bytes 8388608 | tf_op jit(solution)/shard_map/gather_panels/all_to_all | solution.py:360
  24.4 5.5 %collective-permute-start.8 = (s32[8,8]{1,0:T(8,128)S(1)}, s32[8,8]{1,0:T(8,128)S(1)}, u32[]{:S(2)}, u32[]{:S(2)}) collective-permute-start(s32[8,8]{1,0:T(8,128)S(1)} %get-tuple-element.141), channel_id=1, source_target_pairs={{0,24},{8,0},{16,8},{24,16},{32,56},{40,32},{48,40},{56,48},{64,88... | collective-permute-start | bytes 776 | tf_op jit(solution)/shard_map/all_requests/ppermute | solution.py:353
  28.3 5.1 %collective-permute-start.7 = (s32[8,8]{1,0:T(8,128)S(1)}, s32[8,8]{1,0:T(8,128)S(1)}, u32[]{:S(2)}, u32[]{:S(2)}) collective-permute-start(s32[8,8]{1,0:T(8,128)S(1)} %get-tuple-element.141), channel_id=1, source_target_pairs={{0,16},{8,24},{16,0},{24,8},{32,48},{40,56},{48,32},{56,40},{64,80... | collective-permute-start | bytes 776 | tf_op jit(solution)/shard_map/all_requests/ppermute | solution.py:353
  28.3 5.1 %collective-permute-start.6 = (s32[8,8]{1,0:T(8,128)S(1)}, s32[8,8]{1,0:T(8,128)S(1)}, u32[]{:S(2)}, u32[]{:S(2)}) collective-permute-start(s32[8,8]{1,0:T(8,128)S(1)} %get-tuple-element.141), channel_id=1, source_target_pairs={{0,8},{8,16},{16,24},{24,0},{32,40},{40,48},{48,56},{56,32},{64,72... | collective-permute-start | bytes 776 | tf_op jit(solution)/shard_map/all_requests/ppermute | solution.py:353
  33.5 7.5 %collective-permute-start.10 = (s32[4,8,8]{2,1,0:T(8,128)S(1)}, s32[4,8,8]{2,1,0:T(8,128)S(1)}, u32[]{:S(2)}, u32[]{:S(2)}) collective-permute-start(s32[4,8,8]{2,1,0:T(8,128)S(1)} %get-tuple-element.138), channel_id=1, source_target_pairs={{0,64},{8,72},{16,80},{24,88},{32,96},{40,104},{48,112},{56,120},{... | collective-permute-start | bytes 3080 | tf_op jit(solution)/shard_map/all_requests/ppermute | solution.py:353
  37.5 4.9 %collective-permute-start.9 = (s32[4,8,8]{2,1,0:T(8,128)S(1)}, s32[4,8,8]{2,1,0:T(8,128)S(1)}, u32[]{:S(2)}, u32[]{:S(2)}) collective-permute-start(s32[4,8,8]{2,1,0:T(8,128)S(1)} %get-tuple-element.138), channel_id=1, source_target_pairs={{0,32},{8,40},{16,48},{24,56},{32,64},{40,72},{48,80},{56,88},{64,... | collective-permute-start | bytes 3080 | tf_op jit(solution)/shard_map/all_requests/ppermute | solution.py:353
  37.5 4.9 %collective-permute-start.11 = (s32[4,8,8]{2,1,0:T(8,128)S(1)}, s32[4,8,8]{2,1,0:T(8,128)S(1)}, u32[]{:S(2)}, u32[]{:S(2)}) collective-permute-start(s32[4,8,8]{2,1,0:T(8,128)S(1)} %get-tuple-element.138), channel_id=1, source_target_pairs={{0,96},{8,104},{16,112},{24,120},{32,0},{40,8},{48,16},{56,24},{64... | collective-permute-start | bytes 3080 | tf_op jit(solution)/shard_map/all_requests/ppermute | solution.py:353
  121.1 4.4 %collective-permute-start.12 = (bf16[16,33,16,128]{3,2,1,0:T(8,128)(2,1)S(1)}, bf16[16,33,16,128]{3,2,1,0:T(8,128)(2,1)}, u32[]{:S(2)}, u32[]{:S(2)}) collective-permute-start(bf16[16,33,16,128]{3,2,1,0:T(8,128)(2,1)S(1)} %all_to_all.20), channel_id=1, source_target_pairs={{0,1},{1,0},{2,3},{3,2},{4,5},{5,4},{6,7},{7,6},{8,9},{9,8},{10,11... | collective-permute-start | bytes 6488072 | tf_op jit(solution)/shard_map/split_pieces/ppermute | solution.py:448
  129.7 27.9 %collective-permute-start = (bf16[145,16,128]{2,1,0:T(8,128)(2,1)S(1)}, bf16[145,16,128]{2,1,0:T(8,128)(2,1)S(1)}, u32[]{:S(2)}, u32[]{:S(2)}) collective-permute-start(bf16[145,16,128]{2,1,0:T(8,128)(2,1)S(1)} %get-tuple-element.42), channel_id=1, source_target_pairs={{0,2},{1,3},{2,4},{3,5},{4,6},{5,7},{6,0},{7,1},{8,10},{9,11},{10,... | collective-permute-start | bytes 1781768 | tf_op jit(solution)/shard_map/sum_over_chips/cond/branch_0_fun/ppermute | solution.py:452
  131.9 25.7 %collective-permute-start.1 = (bf16[145,16,128]{2,1,0:T(8,128)(2,1)S(1)}, bf16[145,16,128]{2,1,0:T(8,128)(2,1)S(1)}, u32[]{:S(2)}, u32[]{:S(2)}) collective-permute-start(bf16[145,16,128]{2,1,0:T(8,128)(2,1)S(1)} %get-tuple-element.43), channel_id=1, source_target_pairs={{0,4},{1,5},{2,6},{3,7},{4,0},{5,1},{6,2},{7,3},{8,12},{9,13},{10,... | collective-permute-start | bytes 1781768 | tf_op jit(solution)/shard_map/sum_over_chips/cond/branch_0_fun/ppermute | solution.py:452
  132.1 29.0 %collective-permute-start.2 = (bf16[145,16,128]{2,1,0:T(8,128)(2,1)S(1)}, bf16[145,16,128]{2,1,0:T(8,128)(2,1)S(1)}, u32[]{:S(2)}, u32[]{:S(2)}) collective-permute-start(bf16[145,16,128]{2,1,0:T(8,128)(2,1)S(1)} %get-tuple-element.44), channel_id=1, source_target_pairs={{0,6},{1,7},{2,0},{3,1},{4,2},{5,3},{6,4},{7,5},{8,14},{9,15},{10,... | collective-permute-start | bytes 1781768 | tf_op jit(solution)/shard_map/sum_over_chips/cond/branch_0_fun/ppermute | solution.py:452

commit v7 on v6

--- a/solution.py
+++ b/solution.py
@@ -34,6 +34,7 @@
 BF16 = jnp.bfloat16
 F32 = jnp.float32
 MIB = 1 << 20
+LOG2E = 1.4426950408889634
 
 
 def params(mib):
@@ -142,18 +143,19 @@
     for group in range(GROUPS_DEV):
         for j in range(CAND):
             land(group * CAND + j).wait()
+        for s in range(steps):
+            bring(group * steps + s).wait()
         mine = centers[group * CAND * PANEL : (group + 1) * CAND * PANEL, :]
         wide = mine.astype(F32)
         squares = jnp.sum(wide * wide, axis=1, keepdims=True)
-        bias = squares * (1.0 / sharpness_divisor) + evenness_coefficient * surcharge[group]
+        bias = (squares * (1.0 / sharpness_divisor) + evenness_coefficient * surcharge[group]) * LOG2E
         weights = jnp.zeros((CAND * PANEL, LANE), F32)
         for s in range(steps):
-            bring(group * steps + s).wait()
             block = members[group * GROUP + s * step : group * GROUP + (s + 1) * step, :]
             inner = lax.dot_general(mine, block, (((1,), (1,)), ((), ())), preferred_element_type=F32)
-            logits = inner * (2.0 / sharpness_divisor) - bias
+            logits = inner * (2.0 / sharpness_divisor * LOG2E) - bias
             highest = jnp.max(logits, axis=0, keepdims=True)
-            raised = jnp.exp(logits - highest)
+            raised = jnp.exp2(logits - highest)
             scale = 1.0 / jnp.sum(raised, axis=0, keepdims=True)
             share = (raised * scale).astype(BF16)
             shares[:, s * step : (s + 1) * step] = share
@@ -206,50 +208,74 @@
     )(target, points, arrived, surcharge)
 
 
-def spread_kernel(rows, places, mine, mate, lanes, own, own_weights, out1, out2, out3, total):
-    total[...] = jnp.zeros_like(total)
-    sources = (mine, mate)
-    for n, source in enumerate(sources):
-        def add(s, carry, n=n, source=source):
-            for i in range(REQ):
-                at = places[(n * N_PTS + s) * REQ + i] * TILES
-                total[pl.ds(at, TILES)] += source[s, i * TILES : (i + 1) * TILES].astype(F32)
-            return carry
-
-        lax.fori_loop(0, N_PTS, add, 0)
+def add_pieces(places, source, total):
+    def add(s, carry):
+        for i in range(REQ):
+            at = places[s * REQ + i] * TILES
+            total[pl.ds(at, TILES)] += source[s, i * TILES : (i + 1) * TILES].astype(F32)
+        return carry
+
+    lax.fori_loop(0, N_PTS, add, 0)
+
+
+def sum_weights(lanes, source):
     panel = lax.broadcasted_iota(jnp.int32, (CHIPS * PAN_DEV, LANE), 0)
     weights = jnp.zeros((ROWS, CHIPS * PAN_DEV), F32)
-    for n in range(2 * N_PTS):
+    for n in range(N_PTS):
         chosen = jnp.where(panel == lanes[n : n + 1, :], 1.0, 0.0).astype(BF16)
         weights = weights + lax.dot_general(
-            sources[n // N_PTS][n % N_PTS, REQ * TILES], chosen, (((1,), (1,)), ((), ())),
-            preferred_element_type=F32,
+            source[n, REQ * TILES], chosen, (((1,), (1,)), ((), ())), preferred_element_type=F32
         )
-    own[...] = total[0:DENSE]
+    return weights
+
+
+def spread_mine_kernel(places, mine, lanes, total, total_weights):
+    total[...] = jnp.zeros_like(total)
+    add_pieces(places, mine, total)
+    total_weights[...] = sum_weights(lanes, mine)
+
+
+def spread_mate_kernel(rows, places, mate, lanes, total, total_weights, total_out, own_weights, out1, out2, out3):
+    del total
+    add_pieces(places, mate, total_out)
+    weights = total_weights[...] + sum_weights(lanes, mate)
     coarse = weights.astype(BF16)
     fine = (weights - coarse.astype(F32)).astype(BF16)
     own_weights[...] = weights[:, 0:LANE]
     for d, out in ((1, out1), (2, out2), (3, out3)):
         first = DENSE + (d - 1) * rows * TILES
-        out[0 : rows * TILES] = total[first : first + rows * TILES].astype(BF16)
+        out[0 : rows * TILES] = total_out[first : first + rows * TILES].astype(BF16)
         out[rows * TILES, :, 0:PAN_DEV] = coarse[:, d * PAN_DEV : (d + 1) * PAN_DEV]
         out[rows * TILES, :, PAN_DEV:LANE] = fine[:, d * PAN_DEV : (d + 1) * PAN_DEV]
 
 
-def spread(rows, places, mine, mate, lanes):
+def spread_mine(rows, places, lanes, mine):
+    return pl.pallas_call(
+        spread_mine_kernel,
+        in_specs=[smem_spec(), vmem_spec(), vmem_spec()],
+        out_specs=[vmem_spec(), vmem_spec()],
+        out_shape=[
+            jax.ShapeDtypeStruct(((PAN_DEV + 3 * rows + 1) * TILES, ROWS, LANE), F32),
+            jax.ShapeDtypeStruct((ROWS, CHIPS * PAN_DEV), F32),
+        ],
+        compiler_params=params(16),
+        cost_estimate=pl.CostEstimate(flops=1 << 21, bytes_accessed=8 * MIB, transcendentals=0),
+    )(places, mine, lanes)
+
+
+def spread_mate(rows, places, lanes, mate, total, total_weights):
     chunk = jax.ShapeDtypeStruct((rows * TILES + 1, ROWS, LANE), BF16)
     return pl.pallas_call(
-        functools.partial(spread_kernel, rows),
-        in_specs=[smem_spec()] + [vmem_spec()] * 3,
+        functools.partial(spread_mate_kernel, rows),
+        in_specs=[smem_spec()] + [vmem_spec()] * 4,
         out_specs=[vmem_spec()] * 5,
         out_shape=[
-            jax.ShapeDtypeStruct((DENSE, ROWS, LANE), F32), jax.ShapeDtypeStruct((ROWS, LANE), F32),
-            chunk, chunk, chunk,
+            jax.ShapeDtypeStruct(total.shape, F32), jax.ShapeDtypeStruct((ROWS, LANE), F32), chunk, chunk, chunk,
         ],
-        scratch_shapes=[pltpu.VMEM(((PAN_DEV + 3 * rows + 1) * TILES, ROWS, LANE), F32)],
+        input_output_aliases={3: 0},
         compiler_params=params(16),
-        cost_estimate=pl.CostEstimate(flops=1 << 22, bytes_accessed=8 * MIB, transcendentals=0),
-    )(places, mine, mate, lanes)
+        cost_estimate=pl.CostEstimate(flops=1 << 21, bytes_accessed=8 * MIB, transcendentals=0),
+    )(places, mate, lanes, total, total_weights)
 
 
 def finish_kernel(rows, numbers, own, own_weights, in1, in2, in3, lanes, table, out, total, old, sem):
@@ -259,7 +285,7 @@
     fetch.start()
     weights = own_weights[:, 0:PAN_DEV]
     panel = lax.broadcasted_iota(jnp.int32, (PAN_DEV, LANE), 0)
-    total[...] = own[...]
+    total[...] = own[0:DENSE]
     for d, arrived in enumerate((in1, in2, in3)):
         chosen = jnp.where(panel == lanes[d : d + 1, :], 1.0, 0.0).astype(BF16)
         weights = weights + lax.dot_general(
@@ -447,18 +473,29 @@
         mine = exchange(pieces, "pts")
         mate = lax.ppermute(mine, "cent", shift(0, 1))
 
-    def sum_over_chips(rows, places, lanes, numbers, back_lanes):
-        own, own_weights, *far = spread(rows, places, mine, mate, lanes)
+    def half(x, n):
+        return x.reshape(2, -1)[n] if x.ndim == 1 else x.reshape(2, -1, LANE)[n]
+
+    def start_sums(rows, places, lanes):
+        return spread_mine(rows, half(places, 0), half(lanes, 0), mine)
+
+    def sum_over_chips(rows, begun, places, lanes, numbers, back_lanes):
+        own, own_weights, *far = spread_mate(rows, half(places, 1), half(lanes, 1), mate, *begun)
         back = [lax.ppermute(far[d - 1], "cent", shift(d, 0)) for d in range(1, CHIPS)]
         return finish(rows, numbers, own, own_weights, back, back_lanes, shelf)
 
     def send_all():
         everything = jnp.broadcast_to(spots, (CHIPS - 1, PAN_DEV))
         count = jnp.full((CHIPS - 1,), PAN_DEV, jnp.int32)
-        return sum_over_chips(PAN_DEV, *sender(PAN_DEV, pair % PAN_DEV), *receiver(PAN_DEV, count, everything))
+        to = sender(PAN_DEV, pair % PAN_DEV)
+        return sum_over_chips(
+            PAN_DEV, start_sums(PAN_DEV, *to), *to, *receiver(PAN_DEV, count, everything)
+        )
 
     with jax.named_scope("sum_over_chips"):
-        fresh = lax.cond(too_long, send_all, lambda: sum_over_chips(LISTED, *short))
+        begun = start_sums(LISTED, *short[:2])
+        begun, mate = lax.optimization_barrier((begun, mate))
+        fresh = lax.cond(too_long, send_all, lambda: sum_over_chips(LISTED, begun, *short))
 
     with jax.named_scope("place"):
         new_centroids, new_loads = place(me.reshape(1), exchange(fresh, "pts"))

time: 187 us -> 182 us (0.973)
  Pallas kernels: 27.1 us -> 24.4 us
  waiting for transfers between devices: 64.6 us -> 62.3 us
    pallas_call x1, Pallas kernels: 11.7 us -> 7.78 us  [score(): pl.pallas_call(score_kernel, in_specs=[smem_spec(), hbm_spec(), hbm_spec(...]
    ppermute x1, waiting for transfers between devices: 3.7 us -> 1.72 us  [local(): mate = lax.ppermute(mine, 'cent', shift(0, 1))]
    pallas_call x1 -> x2, Pallas kernels: 4.19 us -> 4.86 us  [the longest x1 2.89 us: spread_mate(): pl.pallas_call(functools.partial(spread_mate_kernel, rows), in_specs=[sme...]
  transfers between devices with their start and end apart: 12 -> 12, of which waited for: 7 -> 8; matrix products, arithmetic and copies ran while one was open for 4% -> 4% of each run, Pallas kernels for 0% -> 1%
where the time goes in v7:
time: 182 us; the launch traced here: 181 us
  waiting for transfers between devices  62.3 us (34%)
  blocking collectives  58.5 us (32%)
  starting transfers between devices  27.2 us (15%)
  Pallas kernels  24.4 us (13%)
  other arithmetic  3.79 us (2%)
  local copies, waits for them, and re-layouts  3.15 us (2%)
    all_to_all x2, blocking collectives, exchange(): return lax.all_to_all(x, axis, split_axis=0, concat_axis=0, tiled=True)  58.5 us
    all_to_all x2, waiting for transfers between devices, exchange(): return lax.all_to_all(x, axis, split_axis=0, concat_axis=0, tiled=True)  29.6 us
    ppermute x3, waiting for transfers between devices, sum_over_chips(): lax.ppermute(far[d - 1], 'cent', shift(d, 0))  27.8 us
    ppermute x6, starting transfers between devices, spread_out(): held.append(lax.ppermute(x, 'pts', pairs))  12.6 us
    all_to_all x2, starting transfers between devices, exchange(): return lax.all_to_all(x, axis, split_axis=0, concat_axis=0, tiled=True)  11.1 us
    pallas_call x1, Pallas kernels, score(): pl.pallas_call(score_kernel, in_specs=[smem_spec(), hbm_spec(), hbm_spec(...  7.78 us
    pallas_call x1, Pallas kernels, pick_panels(): pl.pallas_call(pick_kernel, out_shape=jax.ShapeDtypeStruct((count, PANEL,...  5.93 us
  transfers between devices with their start and end apart: 12, of which 8 were waited for; matrix products, arithmetic and copies ran while one was open for 4% of the time, Pallas kernels for 1%

profile of v7, /device:TPU:24, one launch (start us, length us, event | category | flops | bytes accessed | tf_op | source)
XLA Modules:
  0.0 181.3 jit_solution(10792543324135519447)
XLA Ops:
  0.6 1.5 requests.1
  2.2 4.7 %all-to-all-start = ((bf16[8,5,16,128]{3,2,1,0:T(8,128)(2,1)}), bf16[8,5,16,128]{3,2,1,0:T(8,128)(2,1)S(1)}, u32[]{:S(2)}, u32[]{:S(2)}) async-start(bf16[8,5,16,128]{3,2,1,0:T(8,128)(2,1)} %requests.1), calls=%async_computation | async-start | bytes 327680 | tf_op jit(solution)/shard_map/requests/all_to_all | solution.py:386
  8.8 2.5 %all-to-all-done = bf16[8,5,16,128]{3,2,1,0:T(8,128)(2,1)S(1)} async-done(((bf16[8,5,16,128]{3,2,1,0:T(8,128)(2,1)}), bf16[8,5,16,128]{3,2,1,0:T(8,128)(2,1)S(1)}, u32[]{:S(2)}, u32[]{:S(2)}) %all-to-all-start) | async-done | bytes 163872 | tf_op jit(solution)/shard_map/requests/all_to_all | solution.py:386
  11.9 5.9 %gather_panels.1 = bf16[16,128,1024]{2,1,0:T(8,128)(2,1)} custom-call(s32[16]{0:T(128)} %reshape.259.ids, bf16[64,128,1024]{2,1,0:T(8,128)(2,1)} %bitcast.65), custom_call_target="tpu_custom_call" | custom-call | bytes 8388608 | tf_op jit(solution)/shard_map/gather_panels/pallas_call | solution.py:113
  17.8 6.4 %all-to-all-start.1 = ((bf16[8,2,128,1024]{3,2,1,0:T(8,128)(2,1)}), bf16[8,2,128,1024]{3,2,1,0:T(8,128)(2,1)}, u32[]{:S(2)}, u32[]{:S(2)}) async-start(bf16[8,2,128,1024]{3,2,1,0:T(8,128)(2,1)} %bitcast.68), calls=%async_computation.1 | async-start | bytes 8388608 | tf_op jit(solution)/shard_map/gather_panels/all_to_all | solution.py:386
  24.3 1.5 collective-permute-start.6
  25.8 3.7 %collective-permute-start.7 = (s32[8,8]{1,0:T(8,128)S(1)}, s32[8,8]{1,0:T(8,128)S(1)}, u32[]{:S(2)}, u32[]{:S(2)}) collective-permute-start(s32[8,8]{1,0:T(8,128)S(1)} %get-tuple-element.123), channel_id=1, source_target_pairs={{0,16},{8,24},{16,0},{24,8},{32,48},{40,56},{48,32},{56,40},{64,80... | collective-permute-start | bytes 776 | tf_op jit(solution)/shard_map/all_requests/ppermute | solution.py:379
  31.1 1.9 %collective-permute-done.8 = s32[8,8]{1,0:T(8,128)S(1)} collective-permute-done((s32[8,8]{1,0:T(8,128)S(1)}, s32[8,8]{1,0:T(8,128)S(1)}, u32[]{:S(2)}, u32[]{:S(2)}) %collective-permute-start.8) | collective-permute-done | bytes 288 | tf_op jit(solution)/shard_map/all_requests/ppermute | solution.py:379
  33.1 1.9 %collective-permute-start.9 = (s32[4,8,8]{2,1,0:T(8,128)S(1)}, s32[4,8,8]{2,1,0:T(8,128)S(1)}, u32[]{:S(2)}, u32[]{:S(2)}) collective-permute-start(s32[4,8,8]{2,1,0:T(8,128)S(1)} %get-tuple-element.120), channel_id=1, source_target_pairs={{0,32},{8,40},{16,48},{24,56},{32,64},{40,72},{48,80},{56,88},{64,... | collective-permute-start | bytes 3080 | tf_op jit(solution)/shard_map/all_requests/ppermute | solution.py:379
  35.0 2.4 %collective-permute-start.10 = (s32[4,8,8]{2,1,0:T(8,128)S(1)}, s32[4,8,8]{2,1,0:T(8,128)S(1)}, u32[]{:S(2)}, u32[]{:S(2)}) collective-permute-start(s32[4,8,8]{2,1,0:T(8,128)S(1)} %get-tuple-element.120), channel_id=1, source_target_pairs={{0,64},{8,72},{16,80},{24,88},{32,96},{40,104},{48,112},{56,120},{... | collective-permute-start | bytes 3080 | tf_op jit(solution)/shard_map/all_requests/ppermute | solution.py:379
  37.4 2.1 %collective-permute-start.11 = (s32[4,8,8]{2,1,0:T(8,128)S(1)}, s32[4,8,8]{2,1,0:T(8,128)S(1)}, u32[]{:S(2)}, u32[]{:S(2)}) collective-permute-start(s32[4,8,8]{2,1,0:T(8,128)S(1)} %get-tuple-element.120), channel_id=1, source_target_pairs={{0,96},{8,104},{16,112},{24,120},{32,0},{40,8},{48,16},{56,24},{64... | collective-permute-start | bytes 3080 | tf_op jit(solution)/shard_map/all_requests/ppermute | solution.py:379
  44.8 27.1 %all-to-all-done.1 = bf16[8,2,128,1024]{3,2,1,0:T(8,128)(2,1)} async-done(((bf16[8,2,128,1024]{3,2,1,0:T(8,128)(2,1)}), bf16[8,2,128,1024]{3,2,1,0:T(8,128)(2,1)}, u32[]{:S(2)}, u32[]{:S(2)}) %all-to-all-start.1) | async-done | bytes 4194336 | tf_op jit(solution)/shard_map/gather_panels/all_to_all | solution.py:386
  71.9 7.8 %score.1 = bf16[16,33,16,128]{3,2,1,0:T(8,128)(2,1)S(1)} custom-call(s32[8]{0:T(128)S(1)} %fusion.27.target, bf16[2048,1024]{1,0:T(8,128)(2,1)} %points.1, bf16[16,128,1024]{2,1,0:T(8,128)(2,1)} %bitcast.35.arrived, f32[2,512,1]{2,1,0:T(8,128)S(1)} %log.15.surcharge), custom_call_target="tpu_custom_call" | custom-call | flops 4294967296 | bytes 10485760 | tf_op jit(solution)/shard_map/score/pallas_call | solution.py:195
  79.7 36.7 %all_to_all.20.mine = bf16[16,33,16,128]{3,2,1,0:T(8,128)(2,1)S(1)} all-to-all(bf16[16,33,16,128]{3,2,1,0:T(8,128)(2,1)S(1)} %score.1), channel_id=1, replica_groups=mesh['pts'=16,'cent'=8] {'pts'}, dimensions={0} | all-to-all | bytes 4325376 | tf_op jit(solution)/shard_map/split_pieces/all_to_all | solution.py:386
  117.1 2.0 %sum_over_chips.1 = (f32[692,16,128]{2,1,0:T(8,128)S(1)}, f32[16,256]{1,0:T(8,128)S(1)}) custom-call(s32[128]{0:T(128)S(1)} %slice.54.places, bf16[16,33,16,128]{3,2,1,0:T(8,128)(2,1)S(1)} %all_to_all.20.mine, s32[16,128]{1,0:T(8,128)S(1)} %slice.57.lanes), custom_call_target="tpu_custom_call" | custom-call | flops 2097152 | bytes 8388608 | tf_op jit(solution)/shard_map/sum_over_chips/pallas_call | solution.py:253
  119.1 1.7 collective-permute-done.12
  120.8 37.5 %conditional.1 = (bf16[16,17,16,128]{3,2,1,0:T(8,128)(2,1)}) conditional(s32[]{:T(128)} %convert_element_type.43, (s32[256]{0:T(256)S(1)}, s32[32,128]{1,0:T(8,128)S(1)}, bf16[16,33,16,128]{3,2,1,0:T(8,128)(2,1)}, f32[692,16,128]{2,1,0:T(8,128)S(1)}, f32[16,256]{1,0:T(8,128)S(1)}, /*index=5*/s32[112]{0:T(128)S(1)}, s32[3,128]{1,0:T(4,128)S(1)}, ...), branch_computations={%region_15.16_spmd, %region_16.17_spmd} | conditional | flops 8396488 | bytes 69425736 | solution.py:498
  120.8 2.9 %branch_0_fun.2 = (f32[692,16,128]{2,1,0:T(8,128)S(1)}, f32[16,128]{1,0:T(8,128)S(1)}, bf16[145,16,128]{2,1,0:T(8,128)(2,1)S(1)}, bf16[145,16,128]{2,1,0:T(8,128)(2,1)S(1)}, bf16[145,16,128]{2,1,0:T(8,128)(2,1)S(1)}) custom-call(s32[128]{0:T(128)S(1)} %slice.36.places, ...), custom_call_target="tpu_custom_call", output_to_operand_aliasing={{0}: (3, {})} | custom-call | flops 2097152 | bytes 8388608 | tf_op jit(solution)/shard_map/sum_over_chips/cond/branch_0_fun/pallas_call | solution.py:268
  123.7 2.2 %collective-permute-start = (bf16[145,16,128]{2,1,0:T(8,128)(2,1)S(1)}, bf16[145,16,128]{2,1,0:T(8,128)(2,1)S(1)}, u32[]{:S(2)}, u32[]{:S(2)}) collective-permute-start(bf16[145,16,128]{2,1,0:T(8,128)(2,1)S(1)} %get-tuple-element.45), channel_id=1, source_target_pairs={{0,2},{1,3},{2,4},{3,5},{4,6},{5,7},{6,0},{7,1},{8,10},{9,11},{10,... | collective-permute-start | bytes 1781768 | tf_op jit(solution)/shard_map/sum_over_chips/cond/branch_0_fun/ppermute | solution.py:484
  126.1 1.2 collective-permute-start.2
  127.3 24.3 %collective-permute-done.in1 = bf16[145,16,128]{2,1,0:T(8,128)(2,1)S(1)} collective-permute-done((bf16[145,16,128]{2,1,0:T(8,128)(2,1)S(1)}, bf16[145,16,128]{2,1,0:T(8,128)(2,1)S(1)}, u32[]{:S(2)}, u32[]{:S(2)}) %collective-permute-start) | collective-permute-done | bytes 593952 | tf_op jit(solution)/shard_map/sum_over_chips/cond/branch_0_fun/ppermute | solution.py:484
  151.6 3.5 %collective-permute-done.2.in3 = bf16[145,16,128]{2,1,0:T(8,128)(2,1)S(1)} collective-permute-done((bf16[145,16,128]{2,1,0:T(8,128)(2,1)S(1)}, bf16[145,16,128]{2,1,0:T(8,128)(2,1)S(1)}, u32[]{:S(2)}, u32[]{:S(2)}) %collective-permute-start.2) | collective-permute-done | bytes 593952 | tf_op jit(solution)/shard_map/sum_over_chips/cond/branch_0_fun/ppermute | solution.py:484
  155.1 3.1 %branch_0_fun.3 = bf16[16,17,16,128]{3,2,1,0:T(8,128)(2,1)} custom-call(s32[112]{0:T(128)S(1)} %get-tuple-element.21.numbers, f32[692,16,128]{2,1,0:T(8,128)S(1)} %get-tuple-element.43.own, f32[16,128]{1,0:T(8,128)S(1)} %get-tuple-element.44.own_weights, bf16[145,16,128]{2,1,0:T(8,128)(2,1)S(1)} %collective-permute-done.in1, ...), custom_call_target="tpu_custom_call" | custom-call | flops 4194304 | bytes 6291456 | tf_op jit(solution)/shard_map/sum_over_chips/cond/branch_0_fun/pallas_call | solution.py:318
  158.4 21.7 %all_to_all.21.pieces = bf16[16,17,16,128]{3,2,1,0:T(8,128)(2,1)S(1)} all-to-all(bf16[16,17,16,128]{3,2,1,0:T(8,128)(2,1)} %get-tuple-element.128), channel_id=1, replica_groups=mesh['pts'=16,'cent'=8] {'pts'}, dimensions={0} | all-to-all | bytes 2228224 | tf_op jit(solution)/shard_map/place/all_to_all | solution.py:386
  (73 shorter events, 10.9 us)
Async XLA Ops:
  2.2 9.1 %all-to-all-start = ((bf16[8,5,16,128]{3,2,1,0:T(8,128)(2,1)}), bf16[8,5,16,128]{3,2,1,0:T(8,128)(2,1)S(1)}, u32[]{:S(2)}, u32[]{:S(2)}) async-start(bf16[8,5,16,128]{3,2,1,0:T(8,128)(2,1)} %requests.1), calls=%async_computation | async-start | bytes 327680 | tf_op jit(solution)/shard_map/requests/all_to_all | solution.py:386
  17.8 54.1 %all-to-all-start.1 = ((bf16[8,2,128,1024]{3,2,1,0:T(8,128)(2,1)}), bf16[8,2,128,1024]{3,2,1,0:T(8,128)(2,1)}, u32[]{:S(2)}, u32[]{:S(2)}) async-start(bf16[8,2,128,1024]{3,2,1,0:T(8,128)(2,1)} %bitcast.68), calls=%async_computation.1 | async-start | bytes 8388608 | tf_op jit(solution)/shard_map/gather_panels/all_to_all | solution.py:386
  24.3 6.8 %collective-permute-start.6 = (s32[8,8]{1,0:T(8,128)S(1)}, s32[8,8]{1,0:T(8,128)S(1)}, u32[]{:S(2)}, u32[]{:S(2)}) collective-permute-start(s32[8,8]{1,0:T(8,128)S(1)} %get-tuple-element.123), channel_id=1, source_target_pairs={{0,8},{8,16},{16,24},{24,0},{32,40},{40,48},{48,56},{56,32},{64,72... | collective-permute-start | bytes 776 | tf_op jit(solution)/shard_map/all_requests/ppermute | solution.py:379
  25.8 5.3 %collective-permute-start.7 = (s32[8,8]{1,0:T(8,128)S(1)}, s32[8,8]{1,0:T(8,128)S(1)}, u32[]{:S(2)}, u32[]{:S(2)}) collective-permute-start(s32[8,8]{1,0:T(8,128)S(1)} %get-tuple-element.123), channel_id=1, source_target_pairs={{0,16},{8,24},{16,0},{24,8},{32,48},{40,56},{48,32},{56,40},{64,80... | collective-permute-start | bytes 776 | tf_op jit(solution)/shard_map/all_requests/ppermute | solution.py:379
  29.4 3.6 %collective-permute-start.8 = (s32[8,8]{1,0:T(8,128)S(1)}, s32[8,8]{1,0:T(8,128)S(1)}, u32[]{:S(2)}, u32[]{:S(2)}) collective-permute-start(s32[8,8]{1,0:T(8,128)S(1)} %get-tuple-element.123), channel_id=1, source_target_pairs={{0,24},{8,0},{16,8},{24,16},{32,56},{40,32},{48,40},{56,48},{64,88... | collective-permute-start | bytes 776 | tf_op jit(solution)/shard_map/all_requests/ppermute | solution.py:379
  33.1 6.7 %collective-permute-start.9 = (s32[4,8,8]{2,1,0:T(8,128)S(1)}, s32[4,8,8]{2,1,0:T(8,128)S(1)}, u32[]{:S(2)}, u32[]{:S(2)}) collective-permute-start(s32[4,8,8]{2,1,0:T(8,128)S(1)} %get-tuple-element.120), channel_id=1, source_target_pairs={{0,32},{8,40},{16,48},{24,56},{32,64},{40,72},{48,80},{56,88},{64,... | collective-permute-start | bytes 3080 | tf_op jit(solution)/shard_map/all_requests/ppermute | solution.py:379
  35.0 5.2 %collective-permute-start.10 = (s32[4,8,8]{2,1,0:T(8,128)S(1)}, s32[4,8,8]{2,1,0:T(8,128)S(1)}, u32[]{:S(2)}, u32[]{:S(2)}) collective-permute-start(s32[4,8,8]{2,1,0:T(8,128)S(1)} %get-tuple-element.120), channel_id=1, source_target_pairs={{0,64},{8,72},{16,80},{24,88},{32,96},{40,104},{48,112},{56,120},{... | collective-permute-start | bytes 3080 | tf_op jit(solution)/shard_map/all_requests/ppermute | solution.py:379
  37.4 3.7 %collective-permute-start.11 = (s32[4,8,8]{2,1,0:T(8,128)S(1)}, s32[4,8,8]{2,1,0:T(8,128)S(1)}, u32[]{:S(2)}, u32[]{:S(2)}) collective-permute-start(s32[4,8,8]{2,1,0:T(8,128)S(1)} %get-tuple-element.120), channel_id=1, source_target_pairs={{0,96},{8,104},{16,112},{24,120},{32,0},{40,8},{48,16},{56,24},{64... | collective-permute-start | bytes 3080 | tf_op jit(solution)/shard_map/all_requests/ppermute | solution.py:379
  116.4 4.4 %collective-permute-start.12 = (bf16[16,33,16,128]{3,2,1,0:T(8,128)(2,1)S(1)}, bf16[16,33,16,128]{3,2,1,0:T(8,128)(2,1)}, u32[]{:S(2)}, u32[]{:S(2)}) collective-permute-start(bf16[16,33,16,128]{3,2,1,0:T(8,128)(2,1)S(1)} %all_to_all.20.mine), channel_id=1, source_target_pairs={{0,1},{1,0},{2,3},{3,2},{4,5},{5,4},{6,7},{7,6},{8,9},{9,8},{10,11... | collective-permute-start | bytes 6488072 | tf_op jit(solution)/shard_map/split_pieces/ppermute | solution.py:474
  123.7 27.9 %collective-permute-start = (bf16[145,16,128]{2,1,0:T(8,128)(2,1)S(1)}, bf16[145,16,128]{2,1,0:T(8,128)(2,1)S(1)}, u32[]{:S(2)}, u32[]{:S(2)}) collective-permute-start(bf16[145,16,128]{2,1,0:T(8,128)(2,1)S(1)} %get-tuple-element.45), channel_id=1, source_target_pairs={{0,2},{1,3},{2,4},{3,5},{4,6},{5,7},{6,0},{7,1},{8,10},{9,11},{10,... | collective-permute-start | bytes 1781768 | tf_op jit(solution)/shard_map/sum_over_chips/cond/branch_0_fun/ppermute | solution.py:484
  125.9 25.7 %collective-permute-start.1 = (bf16[145,16,128]{2,1,0:T(8,128)(2,1)S(1)}, bf16[145,16,128]{2,1,0:T(8,128)(2,1)S(1)}, u32[]{:S(2)}, u32[]{:S(2)}) collective-permute-start(bf16[145,16,128]{2,1,0:T(8,128)(2,1)S(1)} %get-tuple-element.46), channel_id=1, source_target_pairs={{0,4},{1,5},{2,6},{3,7},{4,0},{5,1},{6,2},{7,3},{8,12},{9,13},{10,... | collective-permute-start | bytes 1781768 | tf_op jit(solution)/shard_map/sum_over_chips/cond/branch_0_fun/ppermute | solution.py:484
  126.1 29.0 %collective-permute-start.2 = (bf16[145,16,128]{2,1,0:T(8,128)(2,1)S(1)}, bf16[145,16,128]{2,1,0:T(8,128)(2,1)S(1)}, u32[]{:S(2)}, u32[]{:S(2)}) collective-permute-start(bf16[145,16,128]{2,1,0:T(8,128)(2,1)S(1)} %get-tuple-element.47), channel_id=1, source_target_pairs={{0,6},{1,7},{2,0},{3,1},{4,2},{5,3},{6,4},{7,5},{8,14},{9,15},{10,... | collective-permute-start | bytes 1781768 | tf_op jit(solution)/shard_map/sum_over_chips/cond/branch_0_fun/ppermute | solution.py:484

commit v8 on v7

--- a/solution.py
+++ b/solution.py
@@ -17,7 +17,6 @@
 N_CENT = 8
 CHIPS = 4
 N_PTS = 16
-SIDE = 4
 ROWS = 16
 HALF = 512
 LANE = 128
@@ -100,34 +99,49 @@
     )(candidates, home, loads)
 
 
-def pick_kernel(ids, table, out, sems):
-    copies = [pltpu.make_async_copy(table.at[ids[n]], out.at[n], sems.at[n]) for n in range(out.shape[0])]
-    for copy in copies:
-        copy.start()
-    for copy in copies:
-        copy.wait()
-
-
-def pick_panels(ids, table):
-    count = ids.shape[0]
-    return pl.pallas_call(
-        pick_kernel,
-        out_shape=jax.ShapeDtypeStruct((count, PANEL, WIDTH), BF16),
-        in_specs=[smem_spec(), hbm_spec()],
-        out_specs=vmem_spec(),
-        scratch_shapes=[pltpu.SemaphoreType.DMA((count,))],
-        compiler_params=params(56),
+def pick_kernel(readers, ids, place, table, *refs):
+    *outs, held, sems = refs
+
+    def fetch(n, g):
+        reader = (place[0] // 2 + readers[n] // 2) % CHIPS * 2 + (place[0] + readers[n]) % 2
+        at = n * GROUPS_DEV + g
+        return pltpu.make_async_copy(table.at[ids[reader * GROUPS_DEV + g]], held.at[at], sems.at[0, at])
+
+    def put(n, g):
+        at = n * GROUPS_DEV + g
+        return pltpu.make_async_copy(held.at[at], outs[n].at[g], sems.at[1, at])
+
+    every = [(n, g) for n in range(len(readers)) for g in range(GROUPS_DEV)]
+    for at in every:
+        fetch(*at).start()
+    for at in every:
+        fetch(*at).wait()
+        put(*at).start()
+    for at in every:
+        put(*at).wait()
+
+
+def pick_panels(readers, ids, place, table):
+    count = len(readers) * GROUPS_DEV
+    return pl.pallas_call(
+        functools.partial(pick_kernel, readers),
+        out_shape=[jax.ShapeDtypeStruct((GROUPS_DEV, PANEL, WIDTH), BF16)] * len(readers),
+        in_specs=[smem_spec(), smem_spec(), hbm_spec()],
+        out_specs=[hbm_spec()] * len(readers),
+        scratch_shapes=[pltpu.VMEM((count, PANEL, WIDTH), BF16), pltpu.SemaphoreType.DMA((2, count))],
+        compiler_params=params(60),
         cost_estimate=pl.CostEstimate(flops=0, bytes_accessed=4 * count * PANEL * WIDTH, transcendentals=0),
-    )(ids, table)
-
-
-def score_kernel(target, points, arrived, surcharge, out, members, centers, shares, sems):
+    )(ids, place, table)
+
+
+def score_kernel(owners, *refs):
+    panels, (points, surcharge, out, members, centers, shares, sems) = refs[:N_CENT], refs[N_CENT:]
     step = 256
     steps = GROUP // step
 
-    def land(n):
+    def land(n, o):
         rows = pl.ds(n * PANEL, PANEL)
-        return pltpu.make_async_copy(arrived.at[target[n]], centers.at[rows], sems.at[0, n])
+        return pltpu.make_async_copy(panels[o].at[n // CAND], centers.at[rows], sems.at[0, n])
 
     def bring(n):
         rows = pl.ds(n * step, step)
@@ -135,14 +149,19 @@
 
     for group in range(GROUPS_DEV):
         for j in range(CAND):
-            land(group * CAND + j).start()
+            for o in range(N_CENT):
+
+                @pl.when(owners[group * CAND + j] == o)
+                def _(n=group * CAND + j, o=o):
+                    land(n, o).start()
+
         for s in range(steps):
             bring(group * steps + s).start()
     lane = lax.broadcasted_iota(jnp.int32, (PANEL, LANE), 1)
     tile = jnp.zeros((PANEL, LANE), F32)
     for group in range(GROUPS_DEV):
         for j in range(CAND):
-            land(group * CAND + j).wait()
+            land(group * CAND + j, 0).wait()
         for s in range(steps):
             bring(group * steps + s).wait()
         mine = centers[group * CAND * PANEL : (group + 1) * CAND * PANEL, :]
@@ -191,10 +210,10 @@
             out[block_at * 2 + half, REQ * TILES] = tile[block_at * ROWS : (block_at + 1) * ROWS]
 
 
-def score(target, points, arrived, surcharge):
+def score(owners, panels, points, surcharge):
     return pl.pallas_call(
         score_kernel,
-        in_specs=[smem_spec(), hbm_spec(), hbm_spec(), vmem_spec()],
+        in_specs=[smem_spec()] + [hbm_spec()] * (N_CENT + 1) + [vmem_spec()],
         out_specs=vmem_spec(),
         out_shape=jax.ShapeDtypeStruct((N_PTS, SEND_TILES, ROWS, LANE), BF16),
         scratch_shapes=[
@@ -203,9 +222,9 @@
             pltpu.VMEM((CAND * PANEL, GROUP), BF16),
             pltpu.SemaphoreType.DMA((2, 8)),
         ],
-        compiler_params=params(48),
+        compiler_params=params(45),
         cost_estimate=pl.CostEstimate(flops=4 << 30, bytes_accessed=10 * MIB, transcendentals=1 << 20),
-    )(target, points, arrived, surcharge)
+    )(owners, *panels, points, surcharge)
 
 
 def add_pieces(places, source, total):
@@ -368,20 +387,6 @@
     return [(y * 2 + k, ((y + dy) % CHIPS) * 2 + (k + dk) % 2) for y in range(CHIPS) for k in range(2)]
 
 
-def spread_out(x, place, dz, dx):
-    held = [x]
-    for d in range(1, SIDE):
-        pairs = [
-            (ix * SIDE + iz, (ix + d * dx) % SIDE * SIDE + (iz + d * dz) % SIDE)
-            for ix in range(SIDE)
-            for iz in range(SIDE)
-        ]
-        held.append(lax.ppermute(x, "pts", pairs))
-    held = jnp.stack(held)
-    at = (place - jnp.arange(SIDE, dtype=jnp.int32)) % SIDE
-    return jnp.stack([jnp.sum(jnp.where((at == n).reshape((SIDE,) + (1,) * x.ndim), held, 0), axis=0) for n in range(SIDE)])
-
-
 def exchange(x, axis):
     return lax.all_to_all(x, axis, split_axis=0, concat_axis=0, tiled=True)
 
@@ -397,22 +402,24 @@
         asked = answered[:, LOAD_TILES, 0, 0:GROUPS_DEV].astype(jnp.int32).reshape(-1)
 
     with jax.named_scope("gather_panels"):
-        ready = pick_panels(asked, shelf)
-        arrived = exchange(ready.reshape(N_CENT, GROUPS_DEV, PANEL, WIDTH), "cent")
-        arrived = arrived.reshape(N_CENT * GROUPS_DEV, PANEL, WIDTH)
+        readers = (4, 5, 2, 6, 1, 3, 7, 0)
+        ready = dict(zip(readers, pick_panels(readers, asked, here.reshape(1), shelf)))
+        arrived = [ready[0]] + [lax.ppermute(ready[n], "cent", shift(n // 2, n % 2)) for n in range(1, N_CENT)]
+        answered, arrived[1] = lax.optimization_barrier((answered, arrived[1]))
 
     with jax.named_scope("own_requests"):
         slots = jnp.sum(
             jnp.where(candidates.reshape(REQ)[:, None] == jnp.arange(panel_home.shape[0], dtype=jnp.int32), panel_home[None, :], 0),
             axis=1,
         )
-        target = slots // PAN_DEV * GROUPS_DEV + jnp.arange(REQ, dtype=jnp.int32) // CAND
+        owners = slots // PAN_DEV
+        seen = (chip - owners // 2) % CHIPS * 2 + (core - owners) % 2
 
     with jax.named_scope("all_requests"):
         ring = answered[:, LOAD_TILES, 1:3, 0:REQ].astype(jnp.int32)
         ring = ring[:, 0] * PAN_DEV + ring[:, 1]
-        line = spread_out(ring, me % SIDE, 1, 0)
-        everyone = spread_out(line, me // SIDE, 0, 1).reshape(N_PTS, N_CENT, REQ)
+        everyone = exchange(jnp.broadcast_to(ring, (N_PTS, N_CENT, REQ)), "pts")
+
         numbers = jnp.arange(N_CENT * PAN_DEV, dtype=jnp.int32)
         by_chip = jnp.transpose(everyone.reshape(N_PTS, CHIPS, 2 * REQ), (1, 0, 2)).reshape(CHIPS, -1)
         asked_by = jnp.any(by_chip[:, :, None] == numbers, axis=1).reshape(CHIPS, N_CENT, PAN_DEV)
@@ -459,7 +466,7 @@
         )
         count = jnp.minimum(jnp.sum(named.astype(jnp.int32), axis=1), LISTED)
         short = sender(LISTED, rank) + receiver(LISTED, count, listed)
-        target, too_long, short = lax.optimization_barrier((target, too_long, short))
+        seen, too_long, short = lax.optimization_barrier((seen, too_long, short))
 
     with jax.named_scope("loads"):
         load_table = answered[:, :LOAD_TILES].reshape(N_CENT * PAN_DEV, PANEL)
@@ -467,7 +474,7 @@
         surcharge = jnp.log(loads).reshape(GROUPS_DEV, CAND * PANEL, 1)
 
     with jax.named_scope("score"):
-        pieces = score(target, points, arrived, surcharge)
+        pieces = score(seen, arrived, points, surcharge)
 
     with jax.named_scope("split_pieces"):
         mine = exchange(pieces, "pts")

time: 182 us -> 179 us (0.984)
  starting transfers between devices: 27.2 us -> 23.4 us
    ppermute x6 -> x7, waiting for transfers between devices: 3.24 us -> 22.7 us  [local(): lax.ppermute(ready[n], 'cent', shift(n // 2, n % 2))]
    all_to_all x2, waiting for transfers between devices: 29.6 us -> 10.4 us  [exchange(): return lax.all_to_all(x, axis, split_axis=0, concat_axis=0, tiled=True)]
    ppermute x6 -> x7, starting transfers between devices: 12.6 us -> 8.15 us  [local(): lax.ppermute(ready[n], 'cent', shift(n // 2, n % 2))]
  transfers between devices with their start and end apart: 12 -> 13, of which waited for: 8 -> 8; matrix products, arithmetic and copies ran while one was open for 4% -> 3% of each run, Pallas kernels for 1% -> 1%
where the time goes in v8:
time: 179 us; the launch traced here: 178 us
  waiting for transfers between devices  63 us (35%)
  blocking collectives  58.2 us (33%)
  Pallas kernels  24.5 us (14%)
  starting transfers between devices  23.4 us (13%)
  local copies, waits for them, and re-layouts  4.77 us (3%)
  other arithmetic  2.82 us (2%)
    all_to_all x2, blocking collectives, exchange(): return lax.all_to_all(x, axis, split_axis=0, concat_axis=0, tiled=True)  58.2 us
    ppermute x3, waiting for transfers between devices, sum_over_chips(): lax.ppermute(far[d - 1], 'cent', shift(d, 0))  28.1 us
    ppermute x7, waiting for transfers between devices, local(): lax.ppermute(ready[n], 'cent', shift(n // 2, n % 2))  22.7 us
    all_to_all x2, starting transfers between devices, exchange(): return lax.all_to_all(x, axis, split_axis=0, concat_axis=0, tiled=True)  11.8 us
    all_to_all x2, waiting for transfers between devices, exchange(): return lax.all_to_all(x, axis, split_axis=0, concat_axis=0, tiled=True)  10.4 us
    ppermute x7, starting transfers between devices, local(): lax.ppermute(ready[n], 'cent', shift(n // 2, n % 2))  8.15 us
    pallas_call x1, Pallas kernels, score(): pl.pallas_call(score_kernel, in_specs=[smem_spec()] + [hbm_spec()] * (N_C...  7.77 us
    pallas_call x1, Pallas kernels, pick_panels(): pl.pallas_call(functools.partial(pick_kernel, readers), out_shape=[jax.Sh...  6 us
  transfers between devices with their start and end apart: 13, of which 8 were waited for; matrix products, arithmetic and copies ran while one was open for 3% of the time, Pallas kernels for 1%

profile of v8, /device:TPU:24, one launch (start us, length us, event | category | flops | bytes accessed | tf_op | source)
XLA Modules:
  0.0 178.2 jit_solution(7270316026271932183)
XLA Ops:
  0.6 1.5 requests.1
  2.2 4.7 %all-to-all-start = ((bf16[8,5,16,128]{3,2,1,0:T(8,128)(2,1)}), bf16[8,5,16,128]{3,2,1,0:T(8,128)(2,1)S(1)}, u32[]{:S(2)}, u32[]{:S(2)}) async-start(bf16[8,5,16,128]{3,2,1,0:T(8,128)(2,1)} %requests.1), calls=%async_computation | async-start | bytes 327680 | tf_op jit(solution)/shard_map/requests/all_to_all | solution.py:391
  7.6 3.7 %all-to-all-done = bf16[8,5,16,128]{3,2,1,0:T(8,128)(2,1)S(1)} async-done(((bf16[8,5,16,128]{3,2,1,0:T(8,128)(2,1)}), bf16[8,5,16,128]{3,2,1,0:T(8,128)(2,1)S(1)}, u32[]{:S(2)}, u32[]{:S(2)}) %all-to-all-start) | async-done | bytes 163872 | tf_op jit(solution)/shard_map/requests/all_to_all | solution.py:391
  11.9 6.0 %gather_panels.1 = (bf16[2,128,1024]{2,1,0:T(8,128)(2,1)}, bf16[2,128,1024]{2,1,0:T(8,128)(2,1)}, bf16[2,128,1024]{2,1,0:T(8,128)(2,1)}, bf16[2,128,1024]{2,1,0:...) custom-call(s32[16]{0:T(128)} %reshape.169.ids, ...), custom_call_target="tpu_custom_call" | custom-call | bytes 8388608 | tf_op jit(solution)/shard_map/gather_panels/pallas_call | solution.py:126
  18.3 2.5 %collective-permute-start.10 = (bf16[2,128,1024]{2,1,0:T(8,128)(2,1)}, bf16[2,128,1024]{2,1,0:T(8,128)(2,1)S(1)}, u32[]{:S(2)}, u32[]{:S(2)}) collective-permute-start(bf16[2,128,1024]{2,1,0:T(8,128)(2,1)} %get-tuple-element.103), channel_id=1, source_target_pairs={{0,5},{1,4},{2,7},{3,6},{4,1},{5,0},{6,3},{7,2},{8,13},{9,12},{10,... | collective-permute-start | bytes 1572872 | tf_op jit(solution)/shard_map/gather_panels/ppermute | solution.py:407
  21.3 2.8 %collective-permute-start.7 = (bf16[2,128,1024]{2,1,0:T(8,128)(2,1)}, bf16[2,128,1024]{2,1,0:T(8,128)(2,1)S(1)}, u32[]{:S(2)}, u32[]{:S(2)}) collective-permute-start(bf16[2,128,1024]{2,1,0:T(8,128)(2,1)} %get-tuple-element.100), channel_id=1, source_target_pairs={{0,2},{1,3},{2,4},{3,5},{4,6},{5,7},{6,0},{7,1},{8,10},{9,11},{10,... | collective-permute-start | bytes 1572872 | tf_op jit(solution)/shard_map/gather_panels/ppermute | solution.py:407
  24.1 1.5 collective-permute-start.8
  26.2 7.1 %all-to-all-start.1 = ((s32[16,8,8]{2,1,0:T(8,128)}), s32[16,8,8]{2,1,0:T(8,128)S(1)}, u32[]{:S(2)}, u32[]{:S(2)}) async-start(s32[16,8,8]{2,1,0:T(8,128)} %broadcast_in_dim.77), calls=%async_computation.1 | async-start | bytes 131072 | tf_op jit(solution)/shard_map/all_requests/all_to_all | solution.py:391
  34.3 6.7 %all-to-all-done.1 = s32[16,8,8]{2,1,0:T(8,128)S(1)} async-done(((s32[16,8,8]{2,1,0:T(8,128)}), s32[16,8,8]{2,1,0:T(8,128)S(1)}, u32[]{:S(2)}, u32[]{:S(2)}) %all-to-all-start.1) | async-done | bytes 4128 | tf_op jit(solution)/shard_map/all_requests/all_to_all | solution.py:391
  45.6 11.5 %collective-permute-done.12.refs_7_ = bf16[2,128,1024]{2,1,0:T(8,128)(2,1)S(1)} collective-permute-done((bf16[2,128,1024]{2,1,0:T(8,128)(2,1)}, bf16[2,128,1024]{2,1,0:T(8,128)(2,1)S(1)}, u32[]{:S(2)}, u32[]{:S(2)}) %collective-permute-start.12) | collective-permute-done | bytes 524320 | tf_op jit(solution)/shard_map/gather_panels/ppermute | solution.py:407
  57.2 10.9 %collective-permute-done.9.refs_4_ = bf16[2,128,1024]{2,1,0:T(8,128)(2,1)S(1)} collective-permute-done((bf16[2,128,1024]{2,1,0:T(8,128)(2,1)}, bf16[2,128,1024]{2,1,0:T(8,128)(2,1)S(1)}, u32[]{:S(2)}, u32[]{:S(2)}) %collective-permute-start.9) | collective-permute-done | bytes 524320 | tf_op jit(solution)/shard_map/gather_panels/ppermute | solution.py:407
  68.1 1.0 copy-done.1
  69.1 7.8 %score.1 = bf16[16,33,16,128]{3,2,1,0:T(8,128)(2,1)S(1)} custom-call(s32[8]{0:T(128)S(1)} %fusion.26.owners, bf16[2,128,1024]{2,1,0:T(8,128)(2,1)S(1)} %copy-done.1, bf16[2,128,1024]{2,1,0:T(8,128)(2,1)S(1)} %collective-permute-done.6.refs_1_, bf16[2,128,1024]{2,1,0:T(8,128)(2,1)S(1)} %collective-permute-done.7.refs_2_, ...), custom_call_target="tpu_custom_call" | custom-call | flops 4294967296 | bytes 10485760 | tf_op jit(solution)/shard_map/score/pallas_call | solution.py:214
  76.9 36.5 %all_to_all.20.mine = bf16[16,33,16,128]{3,2,1,0:T(8,128)(2,1)S(1)} all-to-all(bf16[16,33,16,128]{3,2,1,0:T(8,128)(2,1)S(1)} %score.1), channel_id=1, replica_groups=mesh['pts'=16,'cent'=8] {'pts'}, dimensions={0} | all-to-all | bytes 4325376 | tf_op jit(solution)/shard_map/split_pieces/all_to_all | solution.py:391
  114.1 2.0 %sum_over_chips.1 = (f32[692,16,128]{2,1,0:T(8,128)S(1)}, f32[16,256]{1,0:T(8,128)S(1)}) custom-call(s32[128]{0:T(128)S(1)} %slice.55.places, bf16[16,33,16,128]{3,2,1,0:T(8,128)(2,1)S(1)} %all_to_all.20.mine, s32[16,128]{1,0:T(8,128)S(1)} %slice.57.lanes), custom_call_target="tpu_custom_call" | custom-call | flops 2097152 | bytes 8388608 | tf_op jit(solution)/shard_map/sum_over_chips/pallas_call | solution.py:272
  116.0 1.7 collective-permute-done.13
  117.8 37.5 %conditional.1 = (bf16[16,17,16,128]{3,2,1,0:T(8,128)(2,1)}) conditional(s32[]{:T(128)} %convert_element_type.45, (s32[256]{0:T(256)S(1)}, s32[32,128]{1,0:T(8,128)S(1)}, bf16[16,33,16,128]{3,2,1,0:T(8,128)(2,1)}, f32[692,16,128]{2,1,0:T(8,128)S(1)}, f32[16,256]{1,0:T(8,128)S(1)}, /*index=5*/s32[112]{0:T(128)S(1)}, s32[3,128]{1,0:T(4,128)S(1)}, ...), branch_computations={%region_7.8_spmd, %region_8.9_spmd} | conditional | flops 8396488 | bytes 69425736 | solution.py:505
  117.8 2.9 %branch_0_fun.2 = (f32[692,16,128]{2,1,0:T(8,128)S(1)}, f32[16,128]{1,0:T(8,128)S(1)}, bf16[145,16,128]{2,1,0:T(8,128)(2,1)S(1)}, bf16[145,16,128]{2,1,0:T(8,128)(2,1)S(1)}, bf16[145,16,128]{2,1,0:T(8,128)(2,1)S(1)}) custom-call(s32[128]{0:T(128)S(1)} %slice.36.places, ...), custom_call_target="tpu_custom_call", output_to_operand_aliasing={{0}: (3, {})} | custom-call | flops 2097152 | bytes 8388608 | tf_op jit(solution)/shard_map/sum_over_chips/cond/branch_0_fun/pallas_call | solution.py:287
  120.7 2.4 %collective-permute-start = (bf16[145,16,128]{2,1,0:T(8,128)(2,1)S(1)}, bf16[145,16,128]{2,1,0:T(8,128)(2,1)S(1)}, u32[]{:S(2)}, u32[]{:S(2)}) collective-permute-start(bf16[145,16,128]{2,1,0:T(8,128)(2,1)S(1)} %get-tuple-element.45), channel_id=1, source_target_pairs={{0,2},{1,3},{2,4},{3,5},{4,6},{5,7},{6,0},{7,1},{8,10},{9,11},{10,... | collective-permute-start | bytes 1781768 | tf_op jit(solution)/shard_map/sum_over_chips/cond/branch_0_fun/ppermute | solution.py:491
  124.0 24.8 %collective-permute-done.in1 = bf16[145,16,128]{2,1,0:T(8,128)(2,1)S(1)} collective-permute-done((bf16[145,16,128]{2,1,0:T(8,128)(2,1)S(1)}, bf16[145,16,128]{2,1,0:T(8,128)(2,1)S(1)}, u32[]{:S(2)}, u32[]{:S(2)}) %collective-permute-start) | collective-permute-done | bytes 593952 | tf_op jit(solution)/shard_map/sum_over_chips/cond/branch_0_fun/ppermute | solution.py:491
  148.8 3.4 %collective-permute-done.2.in3 = bf16[145,16,128]{2,1,0:T(8,128)(2,1)S(1)} collective-permute-done((bf16[145,16,128]{2,1,0:T(8,128)(2,1)S(1)}, bf16[145,16,128]{2,1,0:T(8,128)(2,1)S(1)}, u32[]{:S(2)}, u32[]{:S(2)}) %collective-permute-start.2) | collective-permute-done | bytes 593952 | tf_op jit(solution)/shard_map/sum_over_chips/cond/branch_0_fun/ppermute | solution.py:491
  152.2 3.1 %branch_0_fun.3 = bf16[16,17,16,128]{3,2,1,0:T(8,128)(2,1)} custom-call(s32[112]{0:T(128)S(1)} %get-tuple-element.21.numbers, f32[692,16,128]{2,1,0:T(8,128)S(1)} %get-tuple-element.43.own, f32[16,128]{1,0:T(8,128)S(1)} %get-tuple-element.44.own_weights, bf16[145,16,128]{2,1,0:T(8,128)(2,1)S(1)} %collective-permute-done.in1, ...), custom_call_target="tpu_custom_call" | custom-call | flops 4194304 | bytes 6291456 | tf_op jit(solution)/shard_map/sum_over_chips/cond/branch_0_fun/pallas_call | solution.py:337
  155.3 21.7 %all_to_all.21.pieces = bf16[16,17,16,128]{3,2,1,0:T(8,128)(2,1)S(1)} all-to-all(bf16[16,17,16,128]{3,2,1,0:T(8,128)(2,1)} %get-tuple-element.136), channel_id=1, replica_groups=mesh['pts'=16,'cent'=8] {'pts'}, dimensions={0} | all-to-all | bytes 2228224 | tf_op jit(solution)/shard_map/place/all_to_all | solution.py:391
  177.0 1.2 place.1
  (66 shorter events, 9.3 us)
Async XLA Ops:
  2.2 9.1 %all-to-all-start = ((bf16[8,5,16,128]{3,2,1,0:T(8,128)(2,1)}), bf16[8,5,16,128]{3,2,1,0:T(8,128)(2,1)S(1)}, u32[]{:S(2)}, u32[]{:S(2)}) async-start(bf16[8,5,16,128]{3,2,1,0:T(8,128)(2,1)} %requests.1), calls=%async_computation | async-start | bytes 327680 | tf_op jit(solution)/shard_map/requests/all_to_all | solution.py:391
  11.9 6.1 %copy-start.2 = (s32[512]{0:T(512)S(1)}, s32[512]{0:T(512)}, u32[]{:S(2)}) copy-start(s32[512]{0:T(512)} %home_in.1) | copy-start | bytes 6148
  17.9 6.1 %collective-permute-start.6 = (bf16[2,128,1024]{2,1,0:T(8,128)(2,1)}, bf16[2,128,1024]{2,1,0:T(8,128)(2,1)S(1)}, u32[]{:S(2)}, u32[]{:S(2)}) collective-permute-start(bf16[2,128,1024]{2,1,0:T(8,128)(2,1)} %get-tuple-element.92), channel_id=1, source_target_pairs={{0,1},{1,0},{2,3},{3,2},{4,5},{5,4},{6,7},{7,6},{8,9},{9,8},{10,11... | collective-permute-start | bytes 1572872 | tf_op jit(solution)/shard_map/gather_panels/ppermute | solution.py:407
  18.3 25.3 %collective-permute-start.10 = (bf16[2,128,1024]{2,1,0:T(8,128)(2,1)}, bf16[2,128,1024]{2,1,0:T(8,128)(2,1)S(1)}, u32[]{:S(2)}, u32[]{:S(2)}) collective-permute-start(bf16[2,128,1024]{2,1,0:T(8,128)(2,1)} %get-tuple-element.103), channel_id=1, source_target_pairs={{0,5},{1,4},{2,7},{3,6},{4,1},{5,0},{6,3},{7,2},{8,13},{9,12},{10,... | collective-permute-start | bytes 1572872 | tf_op jit(solution)/shard_map/gather_panels/ppermute | solution.py:407
  20.8 24.8 %collective-permute-start.11 = (bf16[2,128,1024]{2,1,0:T(8,128)(2,1)}, bf16[2,128,1024]{2,1,0:T(8,128)(2,1)S(1)}, u32[]{:S(2)}, u32[]{:S(2)}) collective-permute-start(bf16[2,128,1024]{2,1,0:T(8,128)(2,1)} %get-tuple-element.104), channel_id=1, source_target_pairs={{0,6},{1,7},{2,0},{3,1},{4,2},{5,3},{6,4},{7,5},{8,14},{9,15},{10,... | collective-permute-start | bytes 1572872 | tf_op jit(solution)/shard_map/gather_panels/ppermute | solution.py:407
  20.8 36.3 %collective-permute-start.12 = (bf16[2,128,1024]{2,1,0:T(8,128)(2,1)}, bf16[2,128,1024]{2,1,0:T(8,128)(2,1)S(1)}, u32[]{:S(2)}, u32[]{:S(2)}) collective-permute-start(bf16[2,128,1024]{2,1,0:T(8,128)(2,1)} %get-tuple-element.105), channel_id=1, source_target_pairs={{0,7},{1,6},{2,1},{3,0},{4,3},{5,2},{6,5},{7,4},{8,15},{9,14},{10,... | collective-permute-start | bytes 1572872 | tf_op jit(solution)/shard_map/gather_panels/ppermute | solution.py:407
  21.3 35.9 %collective-permute-start.7 = (bf16[2,128,1024]{2,1,0:T(8,128)(2,1)}, bf16[2,128,1024]{2,1,0:T(8,128)(2,1)S(1)}, u32[]{:S(2)}, u32[]{:S(2)}) collective-permute-start(bf16[2,128,1024]{2,1,0:T(8,128)(2,1)} %get-tuple-element.100), channel_id=1, source_target_pairs={{0,2},{1,3},{2,4},{3,5},{4,6},{5,7},{6,0},{7,1},{8,10},{9,11},{10,... | collective-permute-start | bytes 1572872 | tf_op jit(solution)/shard_map/gather_panels/ppermute | solution.py:407
  24.1 33.1 %collective-permute-start.8 = (bf16[2,128,1024]{2,1,0:T(8,128)(2,1)}, bf16[2,128,1024]{2,1,0:T(8,128)(2,1)}, u32[]{:S(2)}, u32[]{:S(2)}) collective-permute-start(bf16[2,128,1024]{2,1,0:T(8,128)(2,1)} %get-tuple-element.101), channel_id=1, source_target_pairs={{0,3},{1,2},{2,5},{3,4},{4,7},{5,6},{6,1},{7,0},{8,11},{9,10},{10,... | collective-permute-start | bytes 1572872 | tf_op jit(solution)/shard_map/gather_panels/ppermute | solution.py:407
  26.2 14.8 %all-to-all-start.1 = ((s32[16,8,8]{2,1,0:T(8,128)}), s32[16,8,8]{2,1,0:T(8,128)S(1)}, u32[]{:S(2)}, u32[]{:S(2)}) async-start(s32[16,8,8]{2,1,0:T(8,128)} %broadcast_in_dim.77), calls=%async_computation.1 | async-start | bytes 131072 | tf_op jit(solution)/shard_map/all_requests/all_to_all | solution.py:391
  43.6 24.4 %collective-permute-start.9 = (bf16[2,128,1024]{2,1,0:T(8,128)(2,1)}, bf16[2,128,1024]{2,1,0:T(8,128)(2,1)S(1)}, u32[]{:S(2)}, u32[]{:S(2)}) collective-permute-start(bf16[2,128,1024]{2,1,0:T(8,128)(2,1)} %get-tuple-element.102), channel_id=1, source_target_pairs={{0,4},{1,5},{2,6},{3,7},{4,0},{5,1},{6,2},{7,3},{8,12},{9,13},{10,... | collective-permute-start | bytes 1572872 | tf_op jit(solution)/shard_map/gather_panels/ppermute | solution.py:407
  68.1 1.0 copy-start.1
  113.4 4.4 %collective-permute-start.13 = (bf16[16,33,16,128]{3,2,1,0:T(8,128)(2,1)S(1)}, bf16[16,33,16,128]{3,2,1,0:T(8,128)(2,1)}, u32[]{:S(2)}, u32[]{:S(2)}) collective-permute-start(bf16[16,33,16,128]{3,2,1,0:T(8,128)(2,1)S(1)} %all_to_all.20.mine), channel_id=1, source_target_pairs={{0,1},{1,0},{2,3},{3,2},{4,5},{5,4},{6,7},{7,6},{8,9},{9,8},{10,11... | collective-permute-start | bytes 6488072 | tf_op jit(solution)/shard_map/split_pieces/ppermute | solution.py:481
  120.7 28.2 %collective-permute-start = (bf16[145,16,128]{2,1,0:T(8,128)(2,1)S(1)}, bf16[145,16,128]{2,1,0:T(8,128)(2,1)S(1)}, u32[]{:S(2)}, u32[]{:S(2)}) collective-permute-start(bf16[145,16,128]{2,1,0:T(8,128)(2,1)S(1)} %get-tuple-element.45), channel_id=1, source_target_pairs={{0,2},{1,3},{2,4},{3,5},{4,6},{5,7},{6,0},{7,1},{8,10},{9,11},{10,... | collective-permute-start | bytes 1781768 | tf_op jit(solution)/shard_map/sum_over_chips/cond/branch_0_fun/ppermute | solution.py:491
  123.1 25.7 %collective-permute-start.1 = (bf16[145,16,128]{2,1,0:T(8,128)(2,1)S(1)}, bf16[145,16,128]{2,1,0:T(8,128)(2,1)S(1)}, u32[]{:S(2)}, u32[]{:S(2)}) collective-permute-start(bf16[145,16,128]{2,1,0:T(8,128)(2,1)S(1)} %get-tuple-element.46), channel_id=1, source_target_pairs={{0,4},{1,5},{2,6},{3,7},{4,0},{5,1},{6,2},{7,3},{8,12},{9,13},{10,... | collective-permute-start | bytes 1781768 | tf_op jit(solution)/shard_map/sum_over_chips/cond/branch_0_fun/ppermute | solution.py:491
  123.3 28.9 %collective-permute-start.2 = (bf16[145,16,128]{2,1,0:T(8,128)(2,1)S(1)}, bf16[145,16,128]{2,1,0:T(8,128)(2,1)S(1)}, u32[]{:S(2)}, u32[]{:S(2)}) collective-permute-start(bf16[145,16,128]{2,1,0:T(8,128)(2,1)S(1)} %get-tuple-element.47), channel_id=1, source_target_pairs={{0,6},{1,7},{2,0},{3,1},{4,2},{5,3},{6,4},{7,5},{8,14},{9,15},{10,... | collective-permute-start | bytes 1781768 | tf_op jit(solution)/shard_map/sum_over_chips/cond/branch_0_fun/ppermute | solution.py:491

commit v9 on v8

--- a/solution.py
+++ b/solution.py
@@ -24,7 +24,7 @@
 SEND_TILES = REQ * TILES + 1
 DENSE = PAN_DEV * TILES
 LOAD_TILES = PAN_DEV // ROWS
-LISTED = 36
+LISTED = 34
 
 sharpness_divisor = 16.0
 evenness_coefficient = 1.0
@@ -75,7 +75,7 @@
     for o in range(N_CENT):
         tile = common
         for n, slot in enumerate(slots):
-            here = jnp.where(slot // PAN_DEV == o, slot % PAN_DEV, 0).astype(F32)
+            here = jnp.where(slot // PAN_DEV == o, slot % PAN_DEV + 1, 0).astype(F32)
             tile = jnp.where((row == 0) & (lane == n // CAND), tile + here, tile)
         for t in range(LOAD_TILES):
             out[o, t] = loads[t * ROWS : (t + 1) * ROWS]
@@ -111,14 +111,22 @@
         at = n * GROUPS_DEV + g
         return pltpu.make_async_copy(held.at[at], outs[n].at[g], sems.at[1, at])
 
-    every = [(n, g) for n in range(len(readers)) for g in range(GROUPS_DEV)]
-    for at in every:
-        fetch(*at).start()
-    for at in every:
-        fetch(*at).wait()
-        put(*at).start()
-    for at in every:
-        put(*at).wait()
+    def each(work):
+        for n, reader in enumerate(readers):
+            at = (place[0] // 2 + reader // 2) % CHIPS * 2 + (place[0] + reader) % 2
+            for g in range(GROUPS_DEV):
+
+                @pl.when(ids[at * GROUPS_DEV + g] >= 0)
+                def _(n=n, g=g):
+                    work(n, g)
+
+    def pass_on(n, g):
+        fetch(n, g).wait()
+        put(n, g).start()
+
+    each(lambda n, g: fetch(n, g).start())
+    each(pass_on)
+    each(lambda n, g: put(n, g).wait())
 
 
 def pick_panels(readers, ids, place, table):
@@ -297,35 +305,52 @@
     )(places, mate, lanes, total, total_weights)
 
 
-def finish_kernel(rows, numbers, own, own_weights, in1, in2, in3, lanes, table, out, total, old, sem):
-    row = pl.multiple_of(numbers[0] // 2 * ROWS, ROWS)
-    column = pl.multiple_of(numbers[0] % 2 * HALF, HALF)
+def begin_kernel(me, own, table, out, old, sem):
+    row = pl.multiple_of(me[0] // 2 * ROWS, ROWS)
+    column = pl.multiple_of(me[0] % 2 * HALF, HALF)
     fetch = pltpu.make_async_copy(table.at[:, pl.ds(row, ROWS), pl.ds(column, HALF)], old, sem)
     fetch.start()
+    fetch.wait()
+    for q in range(PAN_DEV):
+        for t in range(TILES):
+            previous = old[q, :, t * LANE : (t + 1) * LANE].astype(F32)
+            out[q * TILES + t] = own[q * TILES + t] + prior_mass * previous
+
+
+def begin(me, own, table):
+    return pl.pallas_call(
+        begin_kernel,
+        in_specs=[smem_spec(), vmem_spec(), hbm_spec()],
+        out_specs=vmem_spec(),
+        out_shape=jax.ShapeDtypeStruct((DENSE, ROWS, LANE), F32),
+        scratch_shapes=[pltpu.VMEM((PAN_DEV, ROWS, HALF), BF16), pltpu.SemaphoreType.DMA],
+        compiler_params=params(48),
+        cost_estimate=pl.CostEstimate(flops=1 << 22, bytes_accessed=5 * MIB, transcendentals=0),
+    )(me, own, table)
+
+
+def finish_kernel(rows, numbers, begun, own_weights, in1, in2, in3, lanes, out, total):
+    del begun
     weights = own_weights[:, 0:PAN_DEV]
     panel = lax.broadcasted_iota(jnp.int32, (PAN_DEV, LANE), 0)
-    total[...] = own[0:DENSE]
     for d, arrived in enumerate((in1, in2, in3)):
         chosen = jnp.where(panel == lanes[d : d + 1, :], 1.0, 0.0).astype(BF16)
         weights = weights + lax.dot_general(
             arrived[rows * TILES], chosen, (((1,), (1,)), ((), ())), preferred_element_type=F32
         )
-        first = 4 + d * rows
+        first = 3 + d * rows
 
         def add(n, carry, arrived=arrived, first=first):
             at = numbers[first + n] * TILES
             total[pl.ds(at, TILES)] += arrived[pl.ds(n * TILES, TILES)].astype(F32)
             return carry
 
-        lax.fori_loop(0, numbers[1 + d], add, 0)
+        lax.fori_loop(0, numbers[d], add, 0)
     inverse = 1.0 / (weights + prior_mass)
-    fetch.wait()
     for q in range(PAN_DEV):
         scale = jnp.broadcast_to(inverse[:, q : q + 1], (ROWS, LANE))
         for t in range(TILES):
-            previous = old[q, :, t * LANE : (t + 1) * LANE].astype(F32)
-            fresh = (total[q * TILES + t] + prior_mass * previous) * scale
-            out[q // CAND, (q % CAND) * TILES + t] = fresh.astype(BF16)
+            out[q // CAND, (q % CAND) * TILES + t] = (total[q * TILES + t] * scale).astype(BF16)
     coarse = weights.astype(BF16)
     fine = (weights - coarse.astype(F32)).astype(BF16)
     for p in range(N_PTS):
@@ -333,20 +358,19 @@
         out[p, CAND * TILES, :, PAN_DEV:LANE] = fine
 
 
-def finish(rows, numbers, own, own_weights, arrived, lanes, table):
+def finish(rows, numbers, begun, own_weights, arrived, lanes):
     return pl.pallas_call(
         functools.partial(finish_kernel, rows),
-        in_specs=[smem_spec()] + [vmem_spec()] * 6 + [hbm_spec()],
-        out_specs=vmem_spec(),
-        out_shape=jax.ShapeDtypeStruct((N_PTS, CAND * TILES + 1, ROWS, LANE), BF16),
-        scratch_shapes=[
-            pltpu.VMEM((DENSE, ROWS, LANE), F32),
-            pltpu.VMEM((PAN_DEV, ROWS, HALF), BF16),
-            pltpu.SemaphoreType.DMA,
+        in_specs=[smem_spec()] + [vmem_spec()] * 6,
+        out_specs=[vmem_spec(), vmem_spec()],
+        out_shape=[
+            jax.ShapeDtypeStruct((N_PTS, CAND * TILES + 1, ROWS, LANE), BF16),
+            jax.ShapeDtypeStruct(begun.shape, F32),
         ],
-        compiler_params=params(48),
+        input_output_aliases={1: 1},
+        compiler_params=params(32),
         cost_estimate=pl.CostEstimate(flops=1 << 22, bytes_accessed=6 * MIB, transcendentals=0),
-    )(numbers, own, own_weights, *arrived, lanes, table)
+    )(numbers, begun, own_weights, *arrived, lanes)[0]
 
 
 def place_kernel(me, pieces, out, loads):
@@ -399,13 +423,16 @@
 
     with jax.named_scope("requests"):
         answered = exchange(ask(candidates, panel_home, prev_loads.reshape(PAN_DEV, PANEL)), "cent")
-        asked = answered[:, LOAD_TILES, 0, 0:GROUPS_DEV].astype(jnp.int32).reshape(-1)
+        asked = answered[:, LOAD_TILES, 0, 0:GROUPS_DEV].astype(jnp.int32).reshape(-1) - 1
 
     with jax.named_scope("gather_panels"):
-        readers = (4, 5, 2, 6, 1, 3, 7, 0)
-        ready = dict(zip(readers, pick_panels(readers, asked, here.reshape(1), shelf)))
-        arrived = [ready[0]] + [lax.ppermute(ready[n], "cent", shift(n // 2, n % 2)) for n in range(1, N_CENT)]
-        answered, arrived[1] = lax.optimization_barrier((answered, arrived[1]))
+        arrived = {}
+        for readers in ((1, 2, 6, 4), (3, 7, 5, 0)):
+            for n, panels in zip(readers, pick_panels(readers, asked, here.reshape(1), shelf)):
+                arrived[n] = lax.ppermute(panels, "cent", shift(n // 2, n % 2)) if n else panels
+            asked, arrived[1] = lax.optimization_barrier((asked, arrived[1]))
+        answered, arrived[0] = lax.optimization_barrier((answered, arrived[0]))
+        arrived = [arrived[n] for n in range(N_CENT)]
 
     with jax.named_scope("own_requests"):
         slots = jnp.sum(
@@ -452,7 +479,7 @@
             return places, lanes
 
         def receiver(rows, count, panels):
-            numbers = jnp.concatenate([me.reshape(1), count, panels[:, :rows].reshape(-1)])
+            numbers = jnp.concatenate([count, panels[:, :rows].reshape(-1)])
             lane = jnp.where(jnp.arange(PAN_DEV) < jnp.minimum(count, rows)[:, None], panels, PAN_DEV)
             return numbers, jnp.concatenate([lane, lane], axis=1)
 
@@ -489,7 +516,7 @@
     def sum_over_chips(rows, begun, places, lanes, numbers, back_lanes):
         own, own_weights, *far = spread_mate(rows, half(places, 1), half(lanes, 1), mate, *begun)
         back = [lax.ppermute(far[d - 1], "cent", shift(d, 0)) for d in range(1, CHIPS)]
-        return finish(rows, numbers, own, own_weights, back, back_lanes, shelf)
+        return finish(rows, numbers, begin(me.reshape(1), own, shelf), own_weights, back, back_lanes)
 
     def send_all():
         everything = jnp.broadcast_to(spots, (CHIPS - 1, PAN_DEV))

time: 179 us -> 175 us (0.978)
  waiting for transfers between devices: 63 us -> 59.1 us
  starting transfers between devices: 23.4 us -> 21.3 us
    ppermute x3, waiting for transfers between devices: 28.1 us -> 25.6 us  [sum_over_chips(): lax.ppermute(far[d - 1], 'cent', shift(d, 0))]
    ppermute x7, starting transfers between devices: 8.15 us -> 5.68 us  [local(): lax.ppermute(panels, 'cent', shift(n // 2, n % 2))]
    pallas_call x1 -> x2, Pallas kernels: 6 us -> 6 us  [pick_panels(): pl.pallas_call(functools.partial(pick_kernel, readers), out_shape=[jax.Sh...]
  transfers between devices with their start and end apart: 13 -> 13, of which waited for: 8 -> 7; matrix products, arithmetic and copies ran while one was open for 3% -> 3% of each run, Pallas kernels for 1% -> 4%
where the time goes in v9:
time: 175 us; the launch traced here: 174 us
  blocking collectives  59.2 us (34%)
  waiting for transfers between devices  59.1 us (34%)
  Pallas kernels  25.4 us (15%)
  starting transfers between devices  21.3 us (12%)
  local copies, waits for them, and re-layouts  4.81 us (3%)
  other arithmetic  2.82 us (2%)
    all_to_all x2, blocking collectives, exchange(): return lax.all_to_all(x, axis, split_axis=0, concat_axis=0, tiled=True)  59.2 us
    ppermute x3, waiting for transfers between devices, sum_over_chips(): lax.ppermute(far[d - 1], 'cent', shift(d, 0))  25.6 us
    ppermute x7, waiting for transfers between devices, local(): lax.ppermute(panels, 'cent', shift(n // 2, n % 2))  22.9 us
    all_to_all x2, starting transfers between devices, exchange(): return lax.all_to_all(x, axis, split_axis=0, concat_axis=0, tiled=True)  12.6 us
    all_to_all x2, waiting for transfers between devices, exchange(): return lax.all_to_all(x, axis, split_axis=0, concat_axis=0, tiled=True)  8.8 us
    pallas_call x1, Pallas kernels, score(): pl.pallas_call(score_kernel, in_specs=[smem_spec()] + [hbm_spec()] * (N_C...  7.76 us
    pallas_call x2, Pallas kernels, pick_panels(): pl.pallas_call(functools.partial(pick_kernel, readers), out_shape=[jax.Sh...  6 us
    ppermute x7, starting transfers between devices, local(): lax.ppermute(panels, 'cent', shift(n // 2, n % 2))  5.68 us
  transfers between devices with their start and end apart: 13, of which 7 were waited for; matrix products, arithmetic and copies ran while one was open for 3% of the time, Pallas kernels for 4%

profile of v9, /device:TPU:24, one launch (start us, length us, event | category | flops | bytes accessed | tf_op | source)
XLA Modules:
  0.0 174.3 jit_solution(12706805111394032488)
XLA Ops:
  0.6 1.5 requests.1
  2.2 4.7 %all-to-all-start = ((bf16[8,5,16,128]{3,2,1,0:T(8,128)(2,1)}), bf16[8,5,16,128]{3,2,1,0:T(8,128)(2,1)S(1)}, u32[]{:S(2)}, u32[]{:S(2)}) async-start(bf16[8,5,16,128]{3,2,1,0:T(8,128)(2,1)} %requests.1), calls=%async_computation | async-start | bytes 327680 | tf_op jit(solution)/shard_map/requests/all_to_all | solution.py:415
  7.6 3.7 %all-to-all-done = bf16[8,5,16,128]{3,2,1,0:T(8,128)(2,1)S(1)} async-done(((bf16[8,5,16,128]{3,2,1,0:T(8,128)(2,1)}), bf16[8,5,16,128]{3,2,1,0:T(8,128)(2,1)S(1)}, u32[]{:S(2)}, u32[]{:S(2)}) %all-to-all-start) | async-done | bytes 163872 | tf_op jit(solution)/shard_map/requests/all_to_all | solution.py:415
  12.0 3.0 %gather_panels.2 = (bf16[2,128,1024]{2,1,0:T(8,128)(2,1)}, bf16[2,128,1024]{2,1,0:T(8,128)(2,1)}, bf16[2,128,1024]{2,1,0:T(8,128)(2,1)}, bf16[2,128,1024]{2,1,0:T(8,128)(2,1)}) custom-call(s32[16]{0:T(128)} %sub.84.ids, s32[1]{0:T(128)} %bitcast.4.place, bf16[64,128,1024]{2,1,0:T(8,128)(2,1)} %bitcast.48), custom_call_target="tpu_custom_call" | custom-call | bytes 4194304 | tf_op jit(solution)/shard_map/gather_panels/pallas_call | solution.py:134
  15.5 3.2 %collective-permute-start.7 = (bf16[2,128,1024]{2,1,0:T(8,128)(2,1)}, bf16[2,128,1024]{2,1,0:T(8,128)(2,1)S(1)}, u32[]{:S(2)}, u32[]{:S(2)}) collective-permute-start(bf16[2,128,1024]{2,1,0:T(8,128)(2,1)} %get-tuple-element.110), channel_id=1, source_target_pairs={{0,2},{1,3},{2,4},{3,5},{4,6},{5,7},{6,0},{7,1},{8,10},{9,11},{10,... | collective-permute-start | bytes 1572872 | tf_op jit(solution)/shard_map/gather_panels/ppermute | solution.py:432
  19.4 3.0 %gather_panels.3 = (bf16[2,128,1024]{2,1,0:T(8,128)(2,1)}, bf16[2,128,1024]{2,1,0:T(8,128)(2,1)}, bf16[2,128,1024]{2,1,0:T(8,128)(2,1)}, bf16[2,128,1024]{2,1,0:T(8,128)(2,1)}) custom-call(s32[16]{0:T(128)} %sub.84.ids, s32[1]{0:T(128)} %bitcast.4.place, bf16[64,128,1024]{2,1,0:T(8,128)(2,1)} %bitcast.49), custom_call_target="tpu_custom_call" | custom-call | bytes 4194304 | tf_op jit(solution)/shard_map/gather_panels/pallas_call | solution.py:134
  23.0 7.8 %all-to-all-start.1 = ((s32[16,8,8]{2,1,0:T(8,128)}), s32[16,8,8]{2,1,0:T(8,128)S(1)}, u32[]{:S(2)}, u32[]{:S(2)}) async-start(s32[16,8,8]{2,1,0:T(8,128)} %broadcast_in_dim.77), calls=%async_computation.1 | async-start | bytes 131072 | tf_op jit(solution)/shard_map/all_requests/all_to_all | solution.py:415
  31.8 1.6 collective-permute-start.10
  33.4 5.1 %all-to-all-done.1 = s32[16,8,8]{2,1,0:T(8,128)S(1)} async-done(((s32[16,8,8]{2,1,0:T(8,128)}), s32[16,8,8]{2,1,0:T(8,128)S(1)}, u32[]{:S(2)}, u32[]{:S(2)}) %all-to-all-start.1) | async-done | bytes 4128 | tf_op jit(solution)/shard_map/all_requests/all_to_all | solution.py:415
  42.1 11.7 %collective-permute-done.7.refs_2_ = bf16[2,128,1024]{2,1,0:T(8,128)(2,1)S(1)} collective-permute-done((bf16[2,128,1024]{2,1,0:T(8,128)(2,1)}, bf16[2,128,1024]{2,1,0:T(8,128)(2,1)S(1)}, u32[]{:S(2)}, u32[]{:S(2)}) %collective-permute-start.7) | collective-permute-done | bytes 524320 | tf_op jit(solution)/shard_map/gather_panels/ppermute | solution.py:432
  53.7 11.3 %collective-permute-done.12.refs_7_ = bf16[2,128,1024]{2,1,0:T(8,128)(2,1)} collective-permute-done((bf16[2,128,1024]{2,1,0:T(8,128)(2,1)}, bf16[2,128,1024]{2,1,0:T(8,128)(2,1)}, u32[]{:S(2)}, u32[]{:S(2)}) %collective-permute-start.12) | collective-permute-done | bytes 524320 | tf_op jit(solution)/shard_map/gather_panels/ppermute | solution.py:432
  66.1 7.8 %score.1 = bf16[16,33,16,128]{3,2,1,0:T(8,128)(2,1)S(1)} custom-call(s32[8]{0:T(128)S(1)} %fusion.27.owners, bf16[2,128,1024]{2,1,0:T(8,128)(2,1)S(1)} %copy-done.1, bf16[2,128,1024]{2,1,0:T(8,128)(2,1)S(1)} %collective-permute-done.6.refs_1_, bf16[2,128,1024]{2,1,0:T(8,128)(2,1)S(1)} %collective-permute-done.7.refs_2_, ...), custom_call_target="tpu_custom_call" | custom-call | flops 4294967296 | bytes 10485760 | tf_op jit(solution)/shard_map/score/pallas_call | solution.py:222
  73.8 37.2 %all_to_all.20.mine = bf16[16,33,16,128]{3,2,1,0:T(8,128)(2,1)S(1)} all-to-all(bf16[16,33,16,128]{3,2,1,0:T(8,128)(2,1)S(1)} %score.1), channel_id=1, replica_groups=mesh['pts'=16,'cent'=8] {'pts'}, dimensions={0} | all-to-all | bytes 4325376 | tf_op jit(solution)/shard_map/split_pieces/all_to_all | solution.py:415
  111.7 2.0 %sum_over_chips.1 = (f32[668,16,128]{2,1,0:T(8,128)S(1)}, f32[16,256]{1,0:T(8,128)S(1)}) custom-call(s32[128]{0:T(128)S(1)} %slice.55.places, bf16[16,33,16,128]{3,2,1,0:T(8,128)(2,1)S(1)} %all_to_all.20.mine, s32[16,128]{1,0:T(8,128)S(1)} %slice.57.lanes), custom_call_target="tpu_custom_call" | custom-call | flops 2097152 | bytes 8388608 | tf_op jit(solution)/shard_map/sum_over_chips/pallas_call | solution.py:280
  113.7 1.7 collective-permute-done.13
  115.4 35.7 %conditional.1 = (bf16[16,17,16,128]{3,2,1,0:T(8,128)(2,1)}) conditional(s32[]{:T(128)} %convert_element_type.42, (s32[]{:T(128)}, s32[256]{0:T(256)S(1)}, s32[32,128]{1,0:T(8,128)S(1)}, bf16[16,33,16,128]{3,2,1,0:T(8,128)(2,1)}, f32[668,16,128]{2,1,0:T(8,128)S(1)}, /*index=5*/f32[16,256]{1,0:T(8,128)S(1)}, bf16[64,128,1024]{2,1,0:T(8,128)(2,1)}, ...), branch_computations={%region_7.8_spmd, %region_8.9_spmd} | conditional | flops 12590400 | bytes 74668584 | solution.py:532
  115.4 2.9 %branch_0_fun.3 = (f32[668,16,128]{2,1,0:T(8,128)S(1)}, f32[16,128]{1,0:T(8,128)S(1)}, bf16[137,16,128]{2,1,0:T(8,128)(2,1)S(1)}, bf16[137,16,128]{2,1,0:T(8,128)(2,1)S(1)}, bf16[137,16,128]{2,1,0:T(8,128)(2,1)S(1)}) custom-call(s32[128]{0:T(128)S(1)} %slice.36.places, ...), custom_call_target="tpu_custom_call", output_to_operand_aliasing={{0}: (3, {})} | custom-call | flops 2097152 | bytes 8388608 | tf_op jit(solution)/shard_map/sum_over_chips/cond/branch_0_fun/pallas_call | solution.py:295
  118.3 2.1 %collective-permute-start = (bf16[137,16,128]{2,1,0:T(8,128)(2,1)S(1)}, bf16[137,16,128]{2,1,0:T(8,128)(2,1)S(1)}, u32[]{:S(2)}, u32[]{:S(2)}) collective-permute-start(bf16[137,16,128]{2,1,0:T(8,128)(2,1)S(1)} %get-tuple-element.50), channel_id=1, source_target_pairs={{0,2},{1,3},{2,4},{3,5},{4,6},{5,7},{6,0},{7,1},{8,10},{9,11},{10,... | collective-permute-start | bytes 1683464 | tf_op jit(solution)/shard_map/sum_over_chips/cond/branch_0_fun/ppermute | solution.py:518
  121.4 1.4 branch_0_fun.4.begun
  122.8 21.9 %collective-permute-done.in1 = bf16[137,16,128]{2,1,0:T(8,128)(2,1)S(1)} collective-permute-done((bf16[137,16,128]{2,1,0:T(8,128)(2,1)S(1)}, bf16[137,16,128]{2,1,0:T(8,128)(2,1)S(1)}, u32[]{:S(2)}, u32[]{:S(2)}) %collective-permute-start) | collective-permute-done | bytes 561184 | tf_op jit(solution)/shard_map/sum_over_chips/cond/branch_0_fun/ppermute | solution.py:518
  144.8 3.7 %collective-permute-done.2.in3 = bf16[137,16,128]{2,1,0:T(8,128)(2,1)S(1)} collective-permute-done((bf16[137,16,128]{2,1,0:T(8,128)(2,1)S(1)}, bf16[137,16,128]{2,1,0:T(8,128)(2,1)S(1)}, u32[]{:S(2)}, u32[]{:S(2)}) %collective-permute-start.2) | collective-permute-done | bytes 561184 | tf_op jit(solution)/shard_map/sum_over_chips/cond/branch_0_fun/ppermute | solution.py:518
  148.4 2.7 %branch_0_fun.5 = (bf16[16,17,16,128]{3,2,1,0:T(8,128)(2,1)}, f32[256,16,128]{2,1,0:T(8,128)S(1)}) custom-call(s32[105]{0:T(128)S(1)} %get-tuple-element.24.numbers, f32[256,16,128]{2,1,0:T(8,128)S(1)} %branch_0_fun.4.begun, f32[16,128]{1,0:T(8,128)S(1)} %get-tuple-element.49.own_weights, ...), custom_call_target="tpu_custom_call", output_to_operand_aliasing={{1}: (1, {})} | custom-call | flops 4194304 | bytes 6291456 | tf_op jit(solution)/shard_map/sum_over_chips/cond/branch_0_fun/pallas_call | solution.py:362
  151.1 22.0 %all_to_all.21.pieces = bf16[16,17,16,128]{3,2,1,0:T(8,128)(2,1)S(1)} all-to-all(bf16[16,17,16,128]{3,2,1,0:T(8,128)(2,1)} %get-tuple-element.146), channel_id=1, replica_groups=mesh['pts'=16,'cent'=8] {'pts'}, dimensions={0} | all-to-all | bytes 2228224 | tf_op jit(solution)/shard_map/place/all_to_all | solution.py:415
  173.1 1.2 place.1
  (68 shorter events, 9.6 us)
Async XLA Ops:
  2.2 9.1 %all-to-all-start = ((bf16[8,5,16,128]{3,2,1,0:T(8,128)(2,1)}), bf16[8,5,16,128]{3,2,1,0:T(8,128)(2,1)S(1)}, u32[]{:S(2)}, u32[]{:S(2)}) async-start(bf16[8,5,16,128]{3,2,1,0:T(8,128)(2,1)} %requests.1), calls=%async_computation | async-start | bytes 327680 | tf_op jit(solution)/shard_map/requests/all_to_all | solution.py:415
  12.0 3.2 %copy-start.2 = (s32[512]{0:T(512)S(1)}, s32[512]{0:T(512)}, u32[]{:S(2)}) copy-start(s32[512]{0:T(512)} %home_in.1) | copy-start | bytes 6148
  15.0 4.3 %collective-permute-start.6 = (bf16[2,128,1024]{2,1,0:T(8,128)(2,1)}, bf16[2,128,1024]{2,1,0:T(8,128)(2,1)S(1)}, u32[]{:S(2)}, u32[]{:S(2)}) collective-permute-start(bf16[2,128,1024]{2,1,0:T(8,128)(2,1)} %get-tuple-element.100), channel_id=1, source_target_pairs={{0,1},{1,0},{2,3},{3,2},{4,5},{5,4},{6,7},{7,6},{8,9},{9,8},{10,11... | collective-permute-start | bytes 1572872 | tf_op jit(solution)/shard_map/gather_panels/ppermute | solution.py:432
  15.4 25.8 %collective-permute-start.11 = (bf16[2,128,1024]{2,1,0:T(8,128)(2,1)}, bf16[2,128,1024]{2,1,0:T(8,128)(2,1)S(1)}, u32[]{:S(2)}, u32[]{:S(2)}) collective-permute-start(bf16[2,128,1024]{2,1,0:T(8,128)(2,1)} %get-tuple-element.114), channel_id=1, source_target_pairs={{0,6},{1,7},{2,0},{3,1},{4,2},{5,3},{6,4},{7,5},{8,14},{9,15},{10,... | collective-permute-start | bytes 1572872 | tf_op jit(solution)/shard_map/gather_panels/ppermute | solution.py:432
  15.5 38.3 %collective-permute-start.7 = (bf16[2,128,1024]{2,1,0:T(8,128)(2,1)}, bf16[2,128,1024]{2,1,0:T(8,128)(2,1)S(1)}, u32[]{:S(2)}, u32[]{:S(2)}) collective-permute-start(bf16[2,128,1024]{2,1,0:T(8,128)(2,1)} %get-tuple-element.110), channel_id=1, source_target_pairs={{0,2},{1,3},{2,4},{3,5},{4,6},{5,7},{6,0},{7,1},{8,10},{9,11},{10,... | collective-permute-start | bytes 1572872 | tf_op jit(solution)/shard_map/gather_panels/ppermute | solution.py:432
  18.7 35.1 %collective-permute-start.9 = (bf16[2,128,1024]{2,1,0:T(8,128)(2,1)}, bf16[2,128,1024]{2,1,0:T(8,128)(2,1)S(1)}, u32[]{:S(2)}, u32[]{:S(2)}) collective-permute-start(bf16[2,128,1024]{2,1,0:T(8,128)(2,1)} %get-tuple-element.112), channel_id=1, source_target_pairs={{0,4},{1,5},{2,6},{3,7},{4,0},{5,1},{6,2},{7,3},{8,12},{9,13},{10,... | collective-permute-start | bytes 1572872 | tf_op jit(solution)/shard_map/gather_panels/ppermute | solution.py:432
  23.0 15.5 %all-to-all-start.1 = ((s32[16,8,8]{2,1,0:T(8,128)}), s32[16,8,8]{2,1,0:T(8,128)S(1)}, u32[]{:S(2)}, u32[]{:S(2)}) async-start(s32[16,8,8]{2,1,0:T(8,128)} %broadcast_in_dim.77), calls=%async_computation.1 | async-start | bytes 131072 | tf_op jit(solution)/shard_map/all_requests/all_to_all | solution.py:415
  31.8 22.0 %collective-permute-start.10 = (bf16[2,128,1024]{2,1,0:T(8,128)(2,1)}, bf16[2,128,1024]{2,1,0:T(8,128)(2,1)S(1)}, u32[]{:S(2)}, u32[]{:S(2)}) collective-permute-start(bf16[2,128,1024]{2,1,0:T(8,128)(2,1)} %get-tuple-element.113), channel_id=1, source_target_pairs={{0,5},{1,4},{2,7},{3,6},{4,1},{5,0},{6,3},{7,2},{8,13},{9,12},{10,... | collective-permute-start | bytes 1572872 | tf_op jit(solution)/shard_map/gather_panels/ppermute | solution.py:432
  33.4 31.6 %collective-permute-start.12 = (bf16[2,128,1024]{2,1,0:T(8,128)(2,1)}, bf16[2,128,1024]{2,1,0:T(8,128)(2,1)}, u32[]{:S(2)}, u32[]{:S(2)}) collective-permute-start(bf16[2,128,1024]{2,1,0:T(8,128)(2,1)} %get-tuple-element.115), channel_id=1, source_target_pairs={{0,7},{1,6},{2,1},{3,0},{4,3},{5,2},{6,5},{7,4},{8,15},{9,14},{10,... | collective-permute-start | bytes 1572872 | tf_op jit(solution)/shard_map/gather_panels/ppermute | solution.py:432
  41.2 23.8 %collective-permute-start.8 = (bf16[2,128,1024]{2,1,0:T(8,128)(2,1)}, bf16[2,128,1024]{2,1,0:T(8,128)(2,1)S(1)}, u32[]{:S(2)}, u32[]{:S(2)}) collective-permute-start(bf16[2,128,1024]{2,1,0:T(8,128)(2,1)} %get-tuple-element.111), channel_id=1, source_target_pairs={{0,3},{1,2},{2,5},{3,4},{4,7},{5,6},{6,1},{7,0},{8,11},{9,10},{10,... | collective-permute-start | bytes 1572872 | tf_op jit(solution)/shard_map/gather_panels/ppermute | solution.py:432
  65.0 1.0 copy-start.1
  111.0 4.4 %collective-permute-start.13 = (bf16[16,33,16,128]{3,2,1,0:T(8,128)(2,1)S(1)}, bf16[16,33,16,128]{3,2,1,0:T(8,128)(2,1)}, u32[]{:S(2)}, u32[]{:S(2)}) collective-permute-start(bf16[16,33,16,128]{3,2,1,0:T(8,128)(2,1)S(1)} %all_to_all.20.mine), channel_id=1, source_target_pairs={{0,1},{1,0},{2,3},{3,2},{4,5},{5,4},{6,7},{7,6},{8,9},{9,8},{10,11... | collective-permute-start | bytes 6488072 | tf_op jit(solution)/shard_map/split_pieces/ppermute | solution.py:508
  118.3 26.4 %collective-permute-start = (bf16[137,16,128]{2,1,0:T(8,128)(2,1)S(1)}, bf16[137,16,128]{2,1,0:T(8,128)(2,1)S(1)}, u32[]{:S(2)}, u32[]{:S(2)}) collective-permute-start(bf16[137,16,128]{2,1,0:T(8,128)(2,1)S(1)} %get-tuple-element.50), channel_id=1, source_target_pairs={{0,2},{1,3},{2,4},{3,5},{4,6},{5,7},{6,0},{7,1},{8,10},{9,11},{10,... | collective-permute-start | bytes 1683464 | tf_op jit(solution)/shard_map/sum_over_chips/cond/branch_0_fun/ppermute | solution.py:518
  120.4 24.3 %collective-permute-start.1 = (bf16[137,16,128]{2,1,0:T(8,128)(2,1)S(1)}, bf16[137,16,128]{2,1,0:T(8,128)(2,1)S(1)}, u32[]{:S(2)}, u32[]{:S(2)}) collective-permute-start(bf16[137,16,128]{2,1,0:T(8,128)(2,1)S(1)} %get-tuple-element.51), channel_id=1, source_target_pairs={{0,4},{1,5},{2,6},{3,7},{4,0},{5,1},{6,2},{7,3},{8,12},{9,13},{10,... | collective-permute-start | bytes 1683464 | tf_op jit(solution)/shard_map/sum_over_chips/cond/branch_0_fun/ppermute | solution.py:518
  121.3 27.1 %collective-permute-start.2 = (bf16[137,16,128]{2,1,0:T(8,128)(2,1)S(1)}, bf16[137,16,128]{2,1,0:T(8,128)(2,1)S(1)}, u32[]{:S(2)}, u32[]{:S(2)}) collective-permute-start(bf16[137,16,128]{2,1,0:T(8,128)(2,1)S(1)} %get-tuple-element.52), channel_id=1, source_target_pairs={{0,6},{1,7},{2,0},{3,1},{4,2},{5,3},{6,4},{7,5},{8,14},{9,15},{10,... | collective-permute-start | bytes 1683464 | tf_op jit(solution)/shard_map/sum_over_chips/cond/branch_0_fun/ppermute | solution.py:518

commit v10 on v9

--- a/solution.py
+++ b/solution.py
@@ -21,7 +21,7 @@
 HALF = 512
 LANE = 128
 TILES = HALF // LANE
-SEND_TILES = REQ * TILES + 1
+SEND_TILES = CAND * TILES + 1
 DENSE = PAN_DEV * TILES
 LOAD_TILES = PAN_DEV // ROWS
 LISTED = 34
@@ -99,150 +99,145 @@
     )(candidates, home, loads)
 
 
-def pick_kernel(readers, ids, place, table, *refs):
+def pick_kernel(group, ids, place, table, *refs):
     *outs, held, sems = refs
 
-    def fetch(n, g):
-        reader = (place[0] // 2 + readers[n] // 2) % CHIPS * 2 + (place[0] + readers[n]) % 2
-        at = n * GROUPS_DEV + g
-        return pltpu.make_async_copy(table.at[ids[reader * GROUPS_DEV + g]], held.at[at], sems.at[0, at])
-
-    def put(n, g):
-        at = n * GROUPS_DEV + g
-        return pltpu.make_async_copy(held.at[at], outs[n].at[g], sems.at[1, at])
+    def fetch(n, at):
+        return pltpu.make_async_copy(table.at[ids[at]], held.at[n], sems.at[0, n])
+
+    def put(n):
+        return pltpu.make_async_copy(held.at[n], outs[n], sems.at[1, n])
 
     def each(work):
-        for n, reader in enumerate(readers):
+        for n in range(N_CENT - 1):
+            reader = n + 1
             at = (place[0] // 2 + reader // 2) % CHIPS * 2 + (place[0] + reader) % 2
-            for g in range(GROUPS_DEV):
-
-                @pl.when(ids[at * GROUPS_DEV + g] >= 0)
-                def _(n=n, g=g):
-                    work(n, g)
-
-    def pass_on(n, g):
-        fetch(n, g).wait()
-        put(n, g).start()
-
-    each(lambda n, g: fetch(n, g).start())
+
+            @pl.when(ids[at * GROUPS_DEV + group] >= 0)
+            def _(n=n, at=at):
+                work(n, at * GROUPS_DEV + group)
+
+    def pass_on(n, at):
+        fetch(n, at).wait()
+        put(n).start()
+
+    each(lambda n, at: fetch(n, at).start())
     each(pass_on)
-    each(lambda n, g: put(n, g).wait())
-
-
-def pick_panels(readers, ids, place, table):
-    count = len(readers) * GROUPS_DEV
-    return pl.pallas_call(
-        functools.partial(pick_kernel, readers),
-        out_shape=[jax.ShapeDtypeStruct((GROUPS_DEV, PANEL, WIDTH), BF16)] * len(readers),
+    each(lambda n, at: put(n).wait())
+
+
+def pick_panels(group, ids, place, table):
+    count = N_CENT - 1
+    return pl.pallas_call(
+        functools.partial(pick_kernel, group),
+        out_shape=[jax.ShapeDtypeStruct((PANEL, WIDTH), BF16)] * count,
         in_specs=[smem_spec(), smem_spec(), hbm_spec()],
-        out_specs=[hbm_spec()] * len(readers),
+        out_specs=[hbm_spec()] * count,
         scratch_shapes=[pltpu.VMEM((count, PANEL, WIDTH), BF16), pltpu.SemaphoreType.DMA((2, count))],
         compiler_params=params(60),
         cost_estimate=pl.CostEstimate(flops=0, bytes_accessed=4 * count * PANEL * WIDTH, transcendentals=0),
     )(ids, place, table)
 
 
-def score_kernel(owners, *refs):
-    panels, (points, surcharge, out, members, centers, shares, sems) = refs[:N_CENT], refs[N_CENT:]
+def score_kernel(group, owners, *refs):
+    panels, (table, points, surcharge, out, members, centers, shares, sems) = refs[: N_CENT - 1], refs[N_CENT - 1 :]
     step = 256
     steps = GROUP // step
 
-    def land(n, o):
-        rows = pl.ds(n * PANEL, PANEL)
-        return pltpu.make_async_copy(panels[o].at[n // CAND], centers.at[rows], sems.at[0, n])
+    def land(j, source):
+        rows = pl.ds(j * PANEL, PANEL)
+        return pltpu.make_async_copy(source, centers.at[rows], sems.at[0, j])
 
     def bring(n):
         rows = pl.ds(n * step, step)
-        return pltpu.make_async_copy(points.at[rows], members.at[rows], sems.at[1, n])
-
-    for group in range(GROUPS_DEV):
-        for j in range(CAND):
-            for o in range(N_CENT):
-
-                @pl.when(owners[group * CAND + j] == o)
-                def _(n=group * CAND + j, o=o):
-                    land(n, o).start()
-
-        for s in range(steps):
-            bring(group * steps + s).start()
+        return pltpu.make_async_copy(points.at[pl.ds(group * GROUP + n * step, step)], members.at[rows], sems.at[1, n])
+
+    for j in range(CAND):
+
+        @pl.when(owners[j] == 0)
+        def _(j=j):
+            land(j, table.at[owners[CAND + j]]).start()
+
+        for o in range(1, N_CENT):
+
+            @pl.when(owners[j] == o)
+            def _(j=j, o=o):
+                land(j, panels[o - 1]).start()
+
+    for s in range(steps):
+        bring(s).start()
+    for j in range(CAND):
+        land(j, panels[0]).wait()
+    for s in range(steps):
+        bring(s).wait()
+    wide = centers[...].astype(F32)
+    squares = jnp.sum(wide * wide, axis=1, keepdims=True)
+    bias = (squares * (1.0 / sharpness_divisor) + evenness_coefficient * surcharge[group]) * LOG2E
+    weights = jnp.zeros((CAND * PANEL, LANE), F32)
+    for s in range(steps):
+        block = members[s * step : (s + 1) * step, :]
+        inner = lax.dot_general(centers[...], block, (((1,), (1,)), ((), ())), preferred_element_type=F32)
+        logits = inner * (2.0 / sharpness_divisor * LOG2E) - bias
+        highest = jnp.max(logits, axis=0, keepdims=True)
+        raised = jnp.exp2(logits - highest)
+        scale = 1.0 / jnp.sum(raised, axis=0, keepdims=True)
+        share = (raised * scale).astype(BF16)
+        shares[:, s * step : (s + 1) * step] = share
+        rounded = share.astype(F32)
+        for part in range(step // LANE):
+            weights = weights + rounded[:, part * LANE : (part + 1) * LANE]
+    weight = jnp.sum(weights, axis=1, keepdims=True)
+    coarse = weight.astype(BF16).astype(F32)
+    fine = weight - coarse
     lane = lax.broadcasted_iota(jnp.int32, (PANEL, LANE), 1)
     tile = jnp.zeros((PANEL, LANE), F32)
-    for group in range(GROUPS_DEV):
-        for j in range(CAND):
-            land(group * CAND + j, 0).wait()
-        for s in range(steps):
-            bring(group * steps + s).wait()
-        mine = centers[group * CAND * PANEL : (group + 1) * CAND * PANEL, :]
-        wide = mine.astype(F32)
-        squares = jnp.sum(wide * wide, axis=1, keepdims=True)
-        bias = (squares * (1.0 / sharpness_divisor) + evenness_coefficient * surcharge[group]) * LOG2E
-        weights = jnp.zeros((CAND * PANEL, LANE), F32)
-        for s in range(steps):
-            block = members[group * GROUP + s * step : group * GROUP + (s + 1) * step, :]
-            inner = lax.dot_general(mine, block, (((1,), (1,)), ((), ())), preferred_element_type=F32)
-            logits = inner * (2.0 / sharpness_divisor * LOG2E) - bias
-            highest = jnp.max(logits, axis=0, keepdims=True)
-            raised = jnp.exp2(logits - highest)
-            scale = 1.0 / jnp.sum(raised, axis=0, keepdims=True)
-            share = (raised * scale).astype(BF16)
-            shares[:, s * step : (s + 1) * step] = share
-            rounded = share.astype(F32)
-            for part in range(step // LANE):
-                weights = weights + rounded[:, part * LANE : (part + 1) * LANE]
-        weight = jnp.sum(weights, axis=1, keepdims=True)
-        coarse = weight.astype(BF16).astype(F32)
-        fine = weight - coarse
-        for j in range(CAND):
-            rows = slice(j * PANEL, (j + 1) * PANEL)
-            tile = jnp.where(lane == group * CAND + j, coarse[rows], tile)
-            tile = jnp.where(lane == REQ + group * CAND + j, fine[rows], tile)
-        wide_step = 256
-        for s in range(WIDTH // wide_step):
-            part = lax.dot_general(
-                shares[...],
-                members[group * GROUP : (group + 1) * GROUP, s * wide_step : (s + 1) * wide_step],
-                (((1,), (0,)), ((), ())),
-                preferred_element_type=F32,
-            ).astype(BF16)
-            for t in range(wide_step // LANE):
-                half, tile_at = divmod(s * (wide_step // LANE) + t, TILES)
-                for j in range(CAND):
-                    for block_at in range(PANEL // ROWS):
-                        row = j * PANEL + block_at * ROWS
-                        out[block_at * 2 + half, (group * CAND + j) * TILES + tile_at] = part[
-                            row : row + ROWS, t * LANE : (t + 1) * LANE
-                        ]
+    for j in range(CAND):
+        rows = slice(j * PANEL, (j + 1) * PANEL)
+        tile = jnp.where(lane == j, coarse[rows], tile)
+        tile = jnp.where(lane == CAND + j, fine[rows], tile)
+    wide_step = 256
+    for s in range(WIDTH // wide_step):
+        part = lax.dot_general(
+            shares[...], members[:, s * wide_step : (s + 1) * wide_step], (((1,), (0,)), ((), ())),
+            preferred_element_type=F32,
+        ).astype(BF16)
+        for t in range(wide_step // LANE):
+            half, tile_at = divmod(s * (wide_step // LANE) + t, TILES)
+            for j in range(CAND):
+                for block_at in range(PANEL // ROWS):
+                    row = j * PANEL + block_at * ROWS
+                    out[block_at * 2 + half, j * TILES + tile_at] = part[row : row + ROWS, t * LANE : (t + 1) * LANE]
     tile = tile.astype(BF16)
     for block_at in range(PANEL // ROWS):
         for half in range(2):
-            out[block_at * 2 + half, REQ * TILES] = tile[block_at * ROWS : (block_at + 1) * ROWS]
-
-
-def score(owners, panels, points, surcharge):
-    return pl.pallas_call(
-        score_kernel,
+            out[block_at * 2 + half, CAND * TILES] = tile[block_at * ROWS : (block_at + 1) * ROWS]
+
+
+def score(group, owners, panels, table, points, surcharge):
+    return pl.pallas_call(
+        functools.partial(score_kernel, group),
         in_specs=[smem_spec()] + [hbm_spec()] * (N_CENT + 1) + [vmem_spec()],
         out_specs=vmem_spec(),
         out_shape=jax.ShapeDtypeStruct((N_PTS, SEND_TILES, ROWS, LANE), BF16),
         scratch_shapes=[
-            pltpu.VMEM((GROUPS_DEV * GROUP, WIDTH), BF16),
-            pltpu.VMEM((GROUPS_DEV * CAND * PANEL, WIDTH), BF16),
+            pltpu.VMEM((GROUP, WIDTH), BF16),
+            pltpu.VMEM((CAND * PANEL, WIDTH), BF16),
             pltpu.VMEM((CAND * PANEL, GROUP), BF16),
-            pltpu.SemaphoreType.DMA((2, 8)),
+            pltpu.SemaphoreType.DMA((2, 4)),
         ],
-        compiler_params=params(45),
-        cost_estimate=pl.CostEstimate(flops=4 << 30, bytes_accessed=10 * MIB, transcendentals=1 << 20),
-    )(owners, *panels, points, surcharge)
+        compiler_params=params(50),
+        cost_estimate=pl.CostEstimate(flops=2 << 30, bytes_accessed=5 * MIB, transcendentals=1 << 19),
+    )(owners, *panels, table, points, surcharge)
 
 
 def add_pieces(places, source, total):
     def add(s, carry):
-        for i in range(REQ):
-            at = places[s * REQ + i] * TILES
-            total[pl.ds(at, TILES)] += source[s, i * TILES : (i + 1) * TILES].astype(F32)
+        for j in range(CAND):
+            at = places[s * CAND + j] * TILES
+            total[pl.ds(at, TILES)] += source[s, j * TILES : (j + 1) * TILES].astype(F32)
         return carry
 
-    lax.fori_loop(0, N_PTS, add, 0)
+    lax.fori_loop(0, N_PTS, add, 0, unroll=2)
 
 
 def sum_weights(lanes, source):
@@ -251,58 +246,65 @@
     for n in range(N_PTS):
         chosen = jnp.where(panel == lanes[n : n + 1, :], 1.0, 0.0).astype(BF16)
         weights = weights + lax.dot_general(
-            source[n, REQ * TILES], chosen, (((1,), (1,)), ((), ())), preferred_element_type=F32
+            source[n, CAND * TILES], chosen, (((1,), (1,)), ((), ())), preferred_element_type=F32
         )
     return weights
 
 
-def spread_mine_kernel(places, mine, lanes, total, total_weights):
+def spread_first_kernel(places, source, lanes, total, total_weights):
     total[...] = jnp.zeros_like(total)
-    add_pieces(places, mine, total)
-    total_weights[...] = sum_weights(lanes, mine)
-
-
-def spread_mate_kernel(rows, places, mate, lanes, total, total_weights, total_out, own_weights, out1, out2, out3):
-    del total
-    add_pieces(places, mate, total_out)
-    weights = total_weights[...] + sum_weights(lanes, mate)
+    add_pieces(places, source, total)
+    total_weights[...] = sum_weights(lanes, source)
+
+
+def spread_more_kernel(places, source, lanes, total_in, weights_in, total, total_weights):
+    del total_in
+    add_pieces(places, source, total)
+    total_weights[...] = weights_in[...] + sum_weights(lanes, source)
+
+
+def spread_join_kernel(places, source, lanes, total_in, weights_in, total, total_weights):
+    total[...] = total_in[...]
+    total_weights[...] = weights_in[...] + sum_weights(lanes, source)
+    add_pieces(places, source, total)
+
+
+def spread_last_kernel(rows, places, source, lanes, total_in, weights_in, total, own_weights, out1, out2, out3):
+    del total_in
+    add_pieces(places, source, total)
+    weights = weights_in[...] + sum_weights(lanes, source)
     coarse = weights.astype(BF16)
     fine = (weights - coarse.astype(F32)).astype(BF16)
     own_weights[...] = weights[:, 0:LANE]
     for d, out in ((1, out1), (2, out2), (3, out3)):
         first = DENSE + (d - 1) * rows * TILES
-        out[0 : rows * TILES] = total_out[first : first + rows * TILES].astype(BF16)
+        out[0 : rows * TILES] = total[first : first + rows * TILES].astype(BF16)
         out[rows * TILES, :, 0:PAN_DEV] = coarse[:, d * PAN_DEV : (d + 1) * PAN_DEV]
         out[rows * TILES, :, PAN_DEV:LANE] = fine[:, d * PAN_DEV : (d + 1) * PAN_DEV]
 
 
-def spread_mine(rows, places, lanes, mine):
-    return pl.pallas_call(
-        spread_mine_kernel,
-        in_specs=[smem_spec(), vmem_spec(), vmem_spec()],
-        out_specs=[vmem_spec(), vmem_spec()],
-        out_shape=[
-            jax.ShapeDtypeStruct(((PAN_DEV + 3 * rows + 1) * TILES, ROWS, LANE), F32),
-            jax.ShapeDtypeStruct((ROWS, CHIPS * PAN_DEV), F32),
-        ],
+def spread(rows, places, lanes, source, before=None, last=False, join=False):
+    totals = [
+        jax.ShapeDtypeStruct(((PAN_DEV + 3 * rows + 1) * TILES, ROWS, LANE), F32),
+        jax.ShapeDtypeStruct((ROWS, CHIPS * PAN_DEV), F32),
+    ]
+    if last:
+        chunk = jax.ShapeDtypeStruct((rows * TILES + 1, ROWS, LANE), BF16)
+        kernel = functools.partial(spread_last_kernel, rows)
+        out = [totals[0], jax.ShapeDtypeStruct((ROWS, LANE), F32), chunk, chunk, chunk]
+    else:
+        kernel = spread_join_kernel if join else spread_first_kernel if before is None else spread_more_kernel
+        out = totals
+    before = before or []
+    return pl.pallas_call(
+        kernel,
+        in_specs=[smem_spec()] + [vmem_spec()] * (2 + len(before)),
+        out_specs=[vmem_spec()] * len(out),
+        out_shape=out,
+        input_output_aliases={3: 0} if before and not join else {},
         compiler_params=params(16),
-        cost_estimate=pl.CostEstimate(flops=1 << 21, bytes_accessed=8 * MIB, transcendentals=0),
-    )(places, mine, lanes)
-
-
-def spread_mate(rows, places, lanes, mate, total, total_weights):
-    chunk = jax.ShapeDtypeStruct((rows * TILES + 1, ROWS, LANE), BF16)
-    return pl.pallas_call(
-        functools.partial(spread_mate_kernel, rows),
-        in_specs=[smem_spec()] + [vmem_spec()] * 4,
-        out_specs=[vmem_spec()] * 5,
-        out_shape=[
-            jax.ShapeDtypeStruct(total.shape, F32), jax.ShapeDtypeStruct((ROWS, LANE), F32), chunk, chunk, chunk,
-        ],
-        input_output_aliases={3: 0},
-        compiler_params=params(16),
-        cost_estimate=pl.CostEstimate(flops=1 << 21, bytes_accessed=8 * MIB, transcendentals=0),
-    )(places, mate, lanes, total, total_weights)
+        cost_estimate=pl.CostEstimate(flops=1 << 21, bytes_accessed=4 * MIB, transcendentals=0),
+    )(places, source, lanes, *before)
 
 
 def begin_kernel(me, own, table, out, old, sem):
@@ -425,14 +427,14 @@
         answered = exchange(ask(candidates, panel_home, prev_loads.reshape(PAN_DEV, PANEL)), "cent")
         asked = answered[:, LOAD_TILES, 0, 0:GROUPS_DEV].astype(jnp.int32).reshape(-1) - 1
 
+    tie = lax.optimization_barrier
     with jax.named_scope("gather_panels"):
-        arrived = {}
-        for readers in ((1, 2, 6, 4), (3, 7, 5, 0)):
-            for n, panels in zip(readers, pick_panels(readers, asked, here.reshape(1), shelf)):
-                arrived[n] = lax.ppermute(panels, "cent", shift(n // 2, n % 2)) if n else panels
-            asked, arrived[1] = lax.optimization_barrier((asked, arrived[1]))
-        answered, arrived[0] = lax.optimization_barrier((answered, arrived[0]))
-        arrived = [arrived[n] for n in range(N_CENT)]
+        arrived = []
+        for g in range(GROUPS_DEV):
+            ready = pick_panels(g, asked, here.reshape(1), shelf)
+            arrived.append([lax.ppermute(x, "cent", shift((n + 1) // 2, (n + 1) % 2)) for n, x in enumerate(ready)])
+            asked, arrived[g][0] = tie((asked, arrived[g][0]))
+        answered, arrived[1][0] = tie((answered, arrived[1][0]))
 
     with jax.named_scope("own_requests"):
         slots = jnp.sum(
@@ -441,6 +443,8 @@
         )
         owners = slots // PAN_DEV
         seen = (chip - owners // 2) % CHIPS * 2 + (core - owners) % 2
+        seen = jnp.stack([seen.reshape(GROUPS_DEV, CAND), (slots % PAN_DEV).reshape(GROUPS_DEV, CAND)], axis=1)
+        seen = [seen[g].reshape(-1) for g in range(GROUPS_DEV)]
 
     with jax.named_scope("all_requests"):
         ring = answered[:, LOAD_TILES, 1:3, 0:REQ].astype(jnp.int32)
@@ -460,23 +464,27 @@
 
         pair = jnp.stack(
             [lax.dynamic_index_in_dim(everyone, at, 1, keepdims=False) for at in (here, chip * 2 + 1 - core)]
-        ).reshape(2 * N_PTS, REQ)
+        )
+        pair = jnp.transpose(pair.reshape(2, N_PTS, GROUPS_DEV, CAND), (2, 0, 1, 3))
         owner = pair // PAN_DEV
         relative = (owner // 2 - chip) % CHIPS
         my_ranks = lax.dynamic_index_in_dim(ranks, chip, 0, keepdims=False).reshape(-1)
-        rank = jnp.sum(jnp.where(pair[:, :, None] == numbers, my_ranks, 0), axis=2)
+        rank = jnp.sum(jnp.where(pair[..., None] == numbers, my_ranks, 0), axis=4)
         ours = owner % 2 == core
 
         def sender(rows, rank):
             at = jnp.where(relative == 0, pair % PAN_DEV, rank)
             known = ours & ((relative == 0) | (rank < rows))
             first = jnp.where(relative == 0, 0, PAN_DEV + (relative - 1) * rows)
-            places = jnp.where(known, first + at, PAN_DEV + 3 * rows).reshape(-1)
+            places = jnp.where(known, first + at, PAN_DEV + 3 * rows)
             lane = jnp.where(known, relative * PAN_DEV + at, CHIPS * PAN_DEV)
             lanes = jnp.pad(
-                jnp.concatenate([lane, lane], axis=1), ((0, 0), (0, LANE - 2 * REQ)), constant_values=CHIPS * PAN_DEV
+                jnp.concatenate([lane, lane], axis=3), ((0, 0), (0, 0), (0, 0), (0, LANE - 2 * CAND)),
+                constant_values=CHIPS * PAN_DEV,
             )
-            return places, lanes
+            return [
+                (places[g, n].reshape(-1), lanes[g, n]) for g in range(GROUPS_DEV) for n in range(2)
+            ]
 
         def receiver(rows, count, panels):
             numbers = jnp.concatenate([count, panels[:, :rows].reshape(-1)])
@@ -492,29 +500,32 @@
             jnp.where(named[:, None, :] & (order[:, None, :] == spots[None, :, None]), spots, 0), axis=2
         )
         count = jnp.minimum(jnp.sum(named.astype(jnp.int32), axis=1), LISTED)
-        short = sender(LISTED, rank) + receiver(LISTED, count, listed)
-        seen, too_long, short = lax.optimization_barrier((seen, too_long, short))
+        short = sender(LISTED, rank)
+        short_back = receiver(LISTED, count, listed)
+        seen[1], too_long, short, short_back = tie((seen[1], too_long, short, short_back))
 
     with jax.named_scope("loads"):
         load_table = answered[:, :LOAD_TILES].reshape(N_CENT * PAN_DEV, PANEL)
         loads = jnp.take(load_table, slots, axis=0, mode="clip").astype(F32)
         surcharge = jnp.log(loads).reshape(GROUPS_DEV, CAND * PANEL, 1)
 
-    with jax.named_scope("score"):
-        pieces = score(seen, arrived, points, surcharge)
-
-    with jax.named_scope("split_pieces"):
-        mine = exchange(pieces, "pts")
-        mate = lax.ppermute(mine, "cent", shift(0, 1))
-
-    def half(x, n):
-        return x.reshape(2, -1)[n] if x.ndim == 1 else x.reshape(2, -1, LANE)[n]
-
-    def start_sums(rows, places, lanes):
-        return spread_mine(rows, half(places, 0), half(lanes, 0), mine)
-
-    def sum_over_chips(rows, begun, places, lanes, numbers, back_lanes):
-        own, own_weights, *far = spread_mate(rows, half(places, 1), half(lanes, 1), mate, *begun)
+    sources = []
+    for g in range(GROUPS_DEV):
+        with jax.named_scope("score"):
+            pieces = score(g, seen[g], arrived[g], shelf, points, surcharge)
+        with jax.named_scope("split_pieces"):
+            mine = exchange(pieces, "pts")
+            if g == 1:
+                with jax.named_scope("sum_over_chips"):
+                    begun = spread(LISTED, *short[0], sources[0])
+                    begun = spread(LISTED, *short[1], sources[1], before=begun)
+                mine, begun = tie((mine, begun))
+            sources += [mine, lax.ppermute(mine, "cent", shift(0, 1))]
+        if g == 0:
+            arrived[1][0], sources[0] = tie((arrived[1][0], sources[0]))
+
+    def sum_over_chips(rows, to, begun, numbers, back_lanes):
+        own, own_weights, *far = spread(rows, *to[3], sources[3], before=begun, last=True)
         back = [lax.ppermute(far[d - 1], "cent", shift(d, 0)) for d in range(1, CHIPS)]
         return finish(rows, numbers, begin(me.reshape(1), own, shelf), own_weights, back, back_lanes)
 
@@ -522,14 +533,15 @@
         everything = jnp.broadcast_to(spots, (CHIPS - 1, PAN_DEV))
         count = jnp.full((CHIPS - 1,), PAN_DEV, jnp.int32)
         to = sender(PAN_DEV, pair % PAN_DEV)
-        return sum_over_chips(
-            PAN_DEV, start_sums(PAN_DEV, *to), *to, *receiver(PAN_DEV, count, everything)
-        )
+        begun = None
+        for n in range(3):
+            begun = spread(PAN_DEV, *to[n], sources[n], before=begun)
+        return sum_over_chips(PAN_DEV, to, begun, *receiver(PAN_DEV, count, everything))
 
     with jax.named_scope("sum_over_chips"):
-        begun = start_sums(LISTED, *short[:2])
-        begun, mate = lax.optimization_barrier((begun, mate))
-        fresh = lax.cond(too_long, send_all, lambda: sum_over_chips(LISTED, begun, *short))
+        begun = spread(LISTED, *short[2], sources[2], before=begun, join=True)
+        begun, sources[3] = tie((begun, sources[3]))
+        fresh = lax.cond(too_long, send_all, lambda: sum_over_chips(LISTED, short, begun, *short_back))
 
     with jax.named_scope("place"):
         new_centroids, new_loads = place(me.reshape(1), exchange(fresh, "pts"))

time: 175 us -> 181 us (1.034)
  blocking collectives: 59.2 us -> 21.9 us
  starting transfers between devices: 21.3 us -> 43.2 us
  waiting for transfers between devices: 59.1 us -> 66.2 us
  local copies, waits for them, and re-layouts: 4.81 us -> 11.9 us
  Pallas kernels: 25.4 us -> 32.1 us
    all_to_all x2 -> x1, blocking collectives: 59.2 us -> 21.9 us  [exchange(): return lax.all_to_all(x, axis, split_axis=0, concat_axis=0, tiled=True)]
    all_to_all x2 -> x4, waiting for transfers between devices: 8.8 us -> 31.1 us  [exchange(): return lax.all_to_all(x, axis, split_axis=0, concat_axis=0, tiled=True)]
    ppermute x8 -> x16, waiting for transfers between devices: 24.7 us -> 9.36 us  [the longest x14 9.35 us: local(): lax.ppermute(x, 'cent', shift((n + 1) // 2, (n + 1) % 2))]
    all_to_all x2 -> x4, starting transfers between devices: 12.6 us -> 24.8 us  [exchange(): return lax.all_to_all(x, axis, split_axis=0, concat_axis=0, tiled=True)]
    ppermute x8 -> x16, starting transfers between devices: 5.68 us -> 14.3 us  [the longest x14 14.3 us: local(): lax.ppermute(x, 'cent', shift((n + 1) // 2, (n + 1) % 2))]
    unnamed x4 -> x24, local copies, waits for them, and re-layouts: 1.05 us -> 8.26 us
    pallas_call x5 -> x8, Pallas kernels: 18.6 us -> 25.2 us  [the longest x2 12.4 us: score(): pl.pallas_call(functools.partial(score_kernel, group), in_specs=[smem_spe...]
  transfers between devices with their start and end apart: 13 -> 23, of which waited for: 7 -> 8; matrix products, arithmetic and copies ran while one was open for 3% -> 3% of each run, Pallas kernels for 4% -> 11%
where the time goes in v10:
time: 181 us; the launch traced here: 180 us
  waiting for transfers between devices  66.2 us (37%)
  starting transfers between devices  43.2 us (24%)
  Pallas kernels  32.1 us (18%)
  blocking collectives  21.9 us (12%)
  local copies, waits for them, and re-layouts  11.9 us (7%)
  other arithmetic  2.69 us (1%)
    all_to_all x4, waiting for transfers between devices, exchange(): return lax.all_to_all(x, axis, split_axis=0, concat_axis=0, tiled=True)  31.1 us
    ppermute x3, waiting for transfers between devices, sum_over_chips(): lax.ppermute(far[d - 1], 'cent', shift(d, 0))  25.7 us
    all_to_all x4, starting transfers between devices, exchange(): return lax.all_to_all(x, axis, split_axis=0, concat_axis=0, tiled=True)  24.8 us
    all_to_all x1, blocking collectives, exchange(): return lax.all_to_all(x, axis, split_axis=0, concat_axis=0, tiled=True)  21.9 us
    ppermute x14, starting transfers between devices, local(): lax.ppermute(x, 'cent', shift((n + 1) // 2, (n + 1) % 2))  14.3 us
    pallas_call x2, Pallas kernels, score(): pl.pallas_call(functools.partial(score_kernel, group), in_specs=[smem_spe...  12.4 us
    ppermute x14, waiting for transfers between devices, local(): lax.ppermute(x, 'cent', shift((n + 1) // 2, (n + 1) % 2))  9.35 us
    unnamed x24, local copies, waits for them, and re-layouts  8.26 us
  transfers between devices with their start and end apart: 23, of which 8 were waited for; matrix products, arithmetic and copies ran while one was open for 3% of the time, Pallas kernels for 11%

profile of v10, /device:TPU:24, one launch (start us, length us, event | category | flops | bytes accessed | tf_op | source)
XLA Modules:
  0.0 179.7 jit_solution(4640578762629384298)
XLA Ops:
  2.2 4.7 %all-to-all-start = ((bf16[8,5,16,128]{3,2,1,0:T(8,128)(2,1)}), bf16[8,5,16,128]{3,2,1,0:T(8,128)(2,1)S(1)}, u32[]{:S(2)}, u32[]{:S(2)}) async-start(bf16[8,5,16,128]{3,2,1,0:T(8,128)(2,1)} %requests.1), calls=%async_computation | async-start | bytes 327680 | tf_op jit(solution)/shard_map/requests/all_to_all | solution.py:417
  6.9 4.4 %all-to-all-done = bf16[8,5,16,128]{3,2,1,0:T(8,128)(2,1)S(1)} async-done(((bf16[8,5,16,128]{3,2,1,0:T(8,128)(2,1)}), bf16[8,5,16,128]{3,2,1,0:T(8,128)(2,1)S(1)}, u32[]{:S(2)}, u32[]{:S(2)}) %all-to-all-start) | async-done | bytes 163872 | tf_op jit(solution)/shard_map/requests/all_to_all | solution.py:417
  11.9 2.8 %gather_panels.2 = (bf16[128,1024]{1,0:T(8,128)(2,1)}, bf16[128,1024]{1,0:T(8,128)(2,1)}, bf16[128,1024]{1,0:T(8,128)(2,1)}, bf16[128,1024]{1,0:T(8,128)(2,1)}, ...) custom-call(s32[16]{0:T(128)} %sub.89.ids, s32[1]{0:T(128)} %bitcast.8.place, ...), custom_call_target="tpu_custom_call" | custom-call | bytes 3670016 | tf_op jit(solution)/shard_map/gather_panels/pallas_call | solution.py:131
  16.5 2.7 %gather_panels.3 = (bf16[128,1024]{1,0:T(8,128)(2,1)}, bf16[128,1024]{1,0:T(8,128)(2,1)}, bf16[128,1024]{1,0:T(8,128)(2,1)}, bf16[128,1024]{1,0:T(8,128)(2,1)}, ...) custom-call(s32[16]{0:T(128)} %sub.89.ids, s32[1]{0:T(128)} %bitcast.8.place, ...), custom_call_target="tpu_custom_call" | custom-call | bytes 3670016 | tf_op jit(solution)/shard_map/gather_panels/pallas_call | solution.py:131
  19.6 2.1 %collective-permute-start.10 = (bf16[128,1024]{1,0:T(8,128)(2,1)S(1)}, bf16[128,1024]{1,0:T(8,128)(2,1)S(1)}, u32[]{:S(2)}, u32[]{:S(2)}) collective-permute-start(bf16[128,1024]{1,0:T(8,128)(2,1)S(1)} %copy-done.12), channel_id=1, source_target_pairs={{0,4},{1,5},{2,6},{3,7},{4,0},{5,1},{6,2},{7,3},{8,12},{9,13},{10,... | collective-permute-start | bytes 786440 | tf_op jit(solution)/shard_map/gather_panels/ppermute | solution.py:435
  27.0 3.4 %collective-permute-done.10.refs_3_ = bf16[128,1024]{1,0:T(8,128)(2,1)S(1)} collective-permute-done((bf16[128,1024]{1,0:T(8,128)(2,1)S(1)}, bf16[128,1024]{1,0:T(8,128)(2,1)S(1)}, u32[]{:S(2)}, u32[]{:S(2)}) %collective-permute-start.10) | collective-permute-done | bytes 262176 | tf_op jit(solution)/shard_map/gather_panels/ppermute | solution.py:435
  32.2 7.9 %all-to-all-start.1 = ((s32[16,8,8]{2,1,0:T(8,128)}), s32[16,8,8]{2,1,0:T(8,128)S(1)}, u32[]{:S(2)}, u32[]{:S(2)}) async-start(s32[16,8,8]{2,1,0:T(8,128)} %broadcast_in_dim.78), calls=%async_computation.1 | async-start | bytes 131072 | tf_op jit(solution)/shard_map/all_requests/all_to_all | solution.py:417
  41.8 4.6 %collective-permute-done.13.refs_6_ = bf16[128,1024]{1,0:T(8,128)(2,1)S(1)} collective-permute-done((bf16[128,1024]{1,0:T(8,128)(2,1)S(1)}, bf16[128,1024]{1,0:T(8,128)(2,1)S(1)}, u32[]{:S(2)}, u32[]{:S(2)}) %collective-permute-start.13) | collective-permute-done | bytes 262176 | tf_op jit(solution)/shard_map/gather_panels/ppermute | solution.py:435
  46.4 2.0 %collective-permute-start.16 = (bf16[128,1024]{1,0:T(8,128)(2,1)}, bf16[128,1024]{1,0:T(8,128)(2,1)S(1)}, u32[]{:S(2)}, u32[]{:S(2)}) collective-permute-start(bf16[128,1024]{1,0:T(8,128)(2,1)} %get-tuple-element.151), channel_id=1, source_target_pairs={{0,4},{1,5},{2,6},{3,7},{4,0},{5,1},{6,2},{7,3},{8,12},{9,13},{10,... | collective-permute-start | bytes 786440 | tf_op jit(solution)/shard_map/gather_panels/ppermute | solution.py:435
  53.3 6.1 %score.2 = bf16[16,17,16,128]{3,2,1,0:T(8,128)(2,1)} custom-call(s32[8]{0:T(128)S(1)} %squeeze.88.owners, bf16[128,1024]{1,0:T(8,128)(2,1)S(1)} %collective-permute-done.6.refs_0_, bf16[128,1024]{1,0:T(8,128)(2,1)S(1)} %copy-done.4, bf16[128,1024]{1,0:T(8,128)(2,1)S(1)} %copy-done.6, bf16[128,1024]{1,0:T(8,128)(2,1)S(1)} %collective-permute-done.10.refs_3_, ...), custom_call_target="tpu_custom_call" | custom-call | flops 2147483648 | bytes 5242880 | tf_op jit(solution)/shard_map/score/pallas_call | solution.py:217
  59.4 8.4 %all-to-all-start.2 = ((bf16[16,17,16,128]{3,2,1,0:T(8,128)(2,1)}), bf16[16,17,16,128]{3,2,1,0:T(8,128)(2,1)}, u32[]{:S(2)}, u32[]{:S(2)}) async-start(bf16[16,17,16,128]{3,2,1,0:T(8,128)(2,1)} %score.2), calls=%async_computation.2 | async-start | bytes 2228224 | tf_op jit(solution)/shard_map/split_pieces/all_to_all | solution.py:417
  72.8 13.7 %all-to-all-done.2.source = bf16[16,17,16,128]{3,2,1,0:T(8,128)(2,1)} async-done(((bf16[16,17,16,128]{3,2,1,0:T(8,128)(2,1)}), bf16[16,17,16,128]{3,2,1,0:T(8,128)(2,1)}, u32[]{:S(2)}, u32[]{:S(2)}) %all-to-all-start.2) | async-done | bytes 1114144 | tf_op jit(solution)/shard_map/split_pieces/all_to_all | solution.py:417
  86.6 6.3 %score.3 = bf16[16,17,16,128]{3,2,1,0:T(8,128)(2,1)} custom-call(s32[8]{0:T(128)S(1)} %squeeze.79.owners, bf16[128,1024]{1,0:T(8,128)(2,1)S(1)} %collective-permute-done.7.refs_0_, bf16[128,1024]{1,0:T(8,128)(2,1)S(1)} %collective-permute-done.14.refs_1_, bf16[128,1024]{1,0:T(8,128)(2,1)S(1)} %collective-permute-done.15.refs_2_, ...), custom_call_target="tpu_custom_call" | custom-call | flops 2147483648 | bytes 5242880 | tf_op jit(solution)/shard_map/score/pallas_call | solution.py:217
  92.9 3.7 %all-to-all-start.3 = ((bf16[16,17,16,128]{3,2,1,0:T(8,128)(2,1)}), bf16[16,17,16,128]{3,2,1,0:T(8,128)(2,1)S(1)}, u32[]{:S(2)}, u32[]{:S(2)}) async-start(bf16[16,17,16,128]{3,2,1,0:T(8,128)(2,1)} %score.3), calls=%async_computation.3 | async-start | bytes 2228224 | tf_op jit(solution)/shard_map/split_pieces/all_to_all | solution.py:417
  96.6 2.3 %sum_over_chips.3 = (f32[668,16,128]{2,1,0:T(8,128)S(1)}, f32[16,256]{1,0:T(8,128)S(1)}) custom-call(s32[64]{0:T(128)S(1)} %squeeze.80.places, bf16[16,17,16,128]{3,2,1,0:T(8,128)(2,1)} %all-to-all-done.2.source, s32[16,128]{1,0:T(8,128)S(1)} %get-tuple-element.159.lanes), custom_call_target="tpu_custom_call" | custom-call | flops 2097152 | bytes 4194304 | tf_op jit(solution)/shard_map/split_pieces/sum_over_chips/pallas_call | solution.py:299
  100.9 2.4 %copy-done.1 = f32[668,16,128]{2,1,0:T(8,128)} copy-done((f32[668,16,128]{2,1,0:T(8,128)}, f32[668,16,128]{2,1,0:T(8,128)S(1)}, u32[]{:S(2)}) %copy-start.1) | copy-done | bytes 5472280
  103.3 12.9 %all-to-all-done.3.source = bf16[16,17,16,128]{3,2,1,0:T(8,128)(2,1)S(1)} async-done(((bf16[16,17,16,128]{3,2,1,0:T(8,128)(2,1)}), bf16[16,17,16,128]{3,2,1,0:T(8,128)(2,1)S(1)}, u32[]{:S(2)}, u32[]{:S(2)}) %all-to-all-start.3) | async-done | bytes 1114144 | tf_op jit(solution)/shard_map/split_pieces/all_to_all | solution.py:417
  117.0 2.5 %copy-done.2 = f32[668,16,128]{2,1,0:T(8,128)S(1)} copy-done((f32[668,16,128]{2,1,0:T(8,128)S(1)}, f32[668,16,128]{2,1,0:T(8,128)}, u32[]{:S(2)}) %copy-start.2) | copy-done | bytes 5472280
  121.2 35.4 %conditional.1 = (bf16[16,17,16,128]{3,2,1,0:T(8,128)(2,1)}) conditional(s32[]{:T(128)} %convert_element_type.42, (s32[]{:T(128)}, s32[64]{0:T(128)S(1)}, bf16[16,17,16,128]{3,2,1,0:T(8,128)(2,1)S(1)}, s32[16,128]{1,0:T(8,128)S(1)}, f32[668,16,128]{2,1,0:T(8,128)S(1)}, /*index=5*/f32[16,256]{1,0:T(8,128)S(1)}, bf16[64,128,1024]{2,1,0:T(8,128)(2,1)}, ...), branch_computations={%region_7.8_spmd, %region_8.9_spmd} | conditional | flops 16784704 | bytes 74684968 | solution.py:544
  122.6 2.9 %collective-permute-start = (bf16[137,16,128]{2,1,0:T(8,128)(2,1)S(1)}, bf16[137,16,128]{2,1,0:T(8,128)(2,1)S(1)}, u32[]{:S(2)}, u32[]{:S(2)}) collective-permute-start(bf16[137,16,128]{2,1,0:T(8,128)(2,1)S(1)} %get-tuple-element.53), channel_id=1, source_target_pairs={{0,2},{1,3},{2,4},{3,5},{4,6},{5,7},{6,0},{7,1},{8,10},{9,11},{10,... | collective-permute-start | bytes 1683464 | tf_op jit(solution)/shard_map/sum_over_chips/cond/branch_0_fun/ppermute | solution.py:529
  128.1 22.1 %collective-permute-done.in1 = bf16[137,16,128]{2,1,0:T(8,128)(2,1)S(1)} collective-permute-done((bf16[137,16,128]{2,1,0:T(8,128)(2,1)S(1)}, bf16[137,16,128]{2,1,0:T(8,128)(2,1)S(1)}, u32[]{:S(2)}, u32[]{:S(2)}) %collective-permute-start) | collective-permute-done | bytes 561184 | tf_op jit(solution)/shard_map/sum_over_chips/cond/branch_0_fun/ppermute | solution.py:529
  150.2 3.7 %collective-permute-done.2.in3 = bf16[137,16,128]{2,1,0:T(8,128)(2,1)S(1)} collective-permute-done((bf16[137,16,128]{2,1,0:T(8,128)(2,1)S(1)}, bf16[137,16,128]{2,1,0:T(8,128)(2,1)S(1)}, u32[]{:S(2)}, u32[]{:S(2)}) %collective-permute-start.2) | collective-permute-done | bytes 561184 | tf_op jit(solution)/shard_map/sum_over_chips/cond/branch_0_fun/ppermute | solution.py:529
  153.9 2.7 %branch_0_fun.5 = (bf16[16,17,16,128]{3,2,1,0:T(8,128)(2,1)}, f32[256,16,128]{2,1,0:T(8,128)S(1)}) custom-call(s32[105]{0:T(128)S(1)} %get-tuple-element.25.numbers, f32[256,16,128]{2,1,0:T(8,128)S(1)} %branch_0_fun.4.begun, f32[16,128]{1,0:T(8,128)S(1)} %get-tuple-element.52.own_weights, ...), custom_call_target="tpu_custom_call", output_to_operand_aliasing={{1}: (1, {})} | custom-call | flops 4194304 | bytes 6291456 | tf_op jit(solution)/shard_map/sum_over_chips/cond/branch_0_fun/pallas_call | solution.py:364
  156.6 21.9 %all_to_all.25.pieces = bf16[16,17,16,128]{3,2,1,0:T(8,128)(2,1)S(1)} all-to-all(bf16[16,17,16,128]{3,2,1,0:T(8,128)(2,1)} %get-tuple-element.215), channel_id=1, replica_groups=mesh['pts'=16,'cent'=8] {'pts'}, dimensions={0} | all-to-all | bytes 2228224 | tf_op jit(solution)/shard_map/place/all_to_all | solution.py:417
  (115 shorter events, 31.8 us)
Async XLA Ops:
  2.2 9.1 %all-to-all-start = ((bf16[8,5,16,128]{3,2,1,0:T(8,128)(2,1)}), bf16[8,5,16,128]{3,2,1,0:T(8,128)(2,1)S(1)}, u32[]{:S(2)}, u32[]{:S(2)}) async-start(bf16[8,5,16,128]{3,2,1,0:T(8,128)(2,1)} %requests.1), calls=%async_computation | async-start | bytes 327680 | tf_op jit(solution)/shard_map/requests/all_to_all | solution.py:417
  14.7 1.8 %collective-permute-start.6 = (bf16[128,1024]{1,0:T(8,128)(2,1)}, bf16[128,1024]{1,0:T(8,128)(2,1)S(1)}, u32[]{:S(2)}, u32[]{:S(2)}) collective-permute-start(bf16[128,1024]{1,0:T(8,128)(2,1)} %get-tuple-element.131), channel_id=1, source_target_pairs={{0,1},{1,0},{2,3},{3,2},{4,5},{5,4},{6,7},{7,6},{8,9},{9,8},{10,11... | collective-permute-start | bytes 786440 | tf_op jit(solution)/shard_map/gather_panels/ppermute | solution.py:435
  19.2 5.6 %collective-permute-start.7 = (bf16[128,1024]{1,0:T(8,128)(2,1)}, bf16[128,1024]{1,0:T(8,128)(2,1)S(1)}, u32[]{:S(2)}, u32[]{:S(2)}) collective-permute-start(bf16[128,1024]{1,0:T(8,128)(2,1)} %get-tuple-element.133), channel_id=1, source_target_pairs={{0,1},{1,0},{2,3},{3,2},{4,5},{5,4},{6,7},{7,6},{8,9},{9,8},{10,11... | collective-permute-start | bytes 786440 | tf_op jit(solution)/shard_map/gather_panels/ppermute | solution.py:435
  19.6 10.8 %collective-permute-start.10 = (bf16[128,1024]{1,0:T(8,128)(2,1)S(1)}, bf16[128,1024]{1,0:T(8,128)(2,1)S(1)}, u32[]{:S(2)}, u32[]{:S(2)}) collective-permute-start(bf16[128,1024]{1,0:T(8,128)(2,1)S(1)} %copy-done.12), channel_id=1, source_target_pairs={{0,4},{1,5},{2,6},{3,7},{4,0},{5,1},{6,2},{7,3},{8,12},{9,13},{10,... | collective-permute-start | bytes 786440 | tf_op jit(solution)/shard_map/gather_panels/ppermute | solution.py:435
  21.8 18.3 %collective-permute-start.11 = (bf16[128,1024]{1,0:T(8,128)(2,1)}, bf16[128,1024]{1,0:T(8,128)(2,1)S(1)}, u32[]{:S(2)}, u32[]{:S(2)}) collective-permute-start(bf16[128,1024]{1,0:T(8,128)(2,1)} %get-tuple-element.145), channel_id=1, source_target_pairs={{0,5},{1,4},{2,7},{3,6},{4,1},{5,0},{6,3},{7,2},{8,13},{9,12},{10,... | collective-permute-start | bytes 786440 | tf_op jit(solution)/shard_map/gather_panels/ppermute | solution.py:435
  22.9 18.9 %collective-permute-start.12 = (bf16[128,1024]{1,0:T(8,128)(2,1)S(1)}, bf16[128,1024]{1,0:T(8,128)(2,1)S(1)}, u32[]{:S(2)}, u32[]{:S(2)}) collective-permute-start(bf16[128,1024]{1,0:T(8,128)(2,1)S(1)} %copy-done.11), channel_id=1, source_target_pairs={{0,6},{1,7},{2,0},{3,1},{4,2},{5,3},{6,4},{7,5},{8,14},{9,15},{10,... | collective-permute-start | bytes 786440 | tf_op jit(solution)/shard_map/gather_panels/ppermute | solution.py:435
  23.2 23.2 %collective-permute-start.13 = (bf16[128,1024]{1,0:T(8,128)(2,1)S(1)}, bf16[128,1024]{1,0:T(8,128)(2,1)S(1)}, u32[]{:S(2)}, u32[]{:S(2)}) collective-permute-start(bf16[128,1024]{1,0:T(8,128)(2,1)S(1)} %copy-done.10), channel_id=1, source_target_pairs={{0,7},{1,6},{2,1},{3,0},{4,3},{5,2},{6,5},{7,4},{8,15},{9,14},{10,... | collective-permute-start | bytes 786440 | tf_op jit(solution)/shard_map/gather_panels/ppermute | solution.py:435
  24.8 23.7 %collective-permute-start.8 = (bf16[128,1024]{1,0:T(8,128)(2,1)}, bf16[128,1024]{1,0:T(8,128)(2,1)S(1)}, u32[]{:S(2)}, u32[]{:S(2)}) collective-permute-start(bf16[128,1024]{1,0:T(8,128)(2,1)} %get-tuple-element.142), channel_id=1, source_target_pairs={{0,2},{1,3},{2,4},{3,5},{4,6},{5,7},{6,0},{7,1},{8,10},{9,11},{10,... | collective-permute-start | bytes 786440 | tf_op jit(solution)/shard_map/gather_panels/ppermute | solution.py:435
  30.4 19.7 %collective-permute-start.9 = (bf16[128,1024]{1,0:T(8,128)(2,1)}, bf16[128,1024]{1,0:T(8,128)(2,1)S(1)}, u32[]{:S(2)}, u32[]{:S(2)}) collective-permute-start(bf16[128,1024]{1,0:T(8,128)(2,1)} %get-tuple-element.143), channel_id=1, source_target_pairs={{0,3},{1,2},{2,5},{3,4},{4,7},{5,6},{6,1},{7,0},{8,11},{9,10},{10,... | collective-permute-start | bytes 786440 | tf_op jit(solution)/shard_map/gather_panels/ppermute | solution.py:435
  32.2 27.3 %all-to-all-start.1 = ((s32[16,8,8]{2,1,0:T(8,128)}), s32[16,8,8]{2,1,0:T(8,128)S(1)}, u32[]{:S(2)}, u32[]{:S(2)}) async-start(s32[16,8,8]{2,1,0:T(8,128)} %broadcast_in_dim.78), calls=%async_computation.1 | async-start | bytes 131072 | tf_op jit(solution)/shard_map/all_requests/all_to_all | solution.py:417
  40.1 31.0 %collective-permute-start.14 = (bf16[128,1024]{1,0:T(8,128)(2,1)}, bf16[128,1024]{1,0:T(8,128)(2,1)S(1)}, u32[]{:S(2)}, u32[]{:S(2)}) collective-permute-start(bf16[128,1024]{1,0:T(8,128)(2,1)} %get-tuple-element.149), channel_id=1, source_target_pairs={{0,2},{1,3},{2,4},{3,5},{4,6},{5,7},{6,0},{7,1},{8,10},{9,11},{10,... | collective-permute-start | bytes 786440 | tf_op jit(solution)/shard_map/gather_panels/ppermute | solution.py:435
  41.8 44.7 %collective-permute-start.15 = (bf16[128,1024]{1,0:T(8,128)(2,1)}, bf16[128,1024]{1,0:T(8,128)(2,1)S(1)}, u32[]{:S(2)}, u32[]{:S(2)}) collective-permute-start(bf16[128,1024]{1,0:T(8,128)(2,1)} %get-tuple-element.150), channel_id=1, source_target_pairs={{0,3},{1,2},{2,5},{3,4},{4,7},{5,6},{6,1},{7,0},{8,11},{9,10},{10,... | collective-permute-start | bytes 786440 | tf_op jit(solution)/shard_map/gather_panels/ppermute | solution.py:435
  46.4 40.1 %collective-permute-start.16 = (bf16[128,1024]{1,0:T(8,128)(2,1)}, bf16[128,1024]{1,0:T(8,128)(2,1)S(1)}, u32[]{:S(2)}, u32[]{:S(2)}) collective-permute-start(bf16[128,1024]{1,0:T(8,128)(2,1)} %get-tuple-element.151), channel_id=1, source_target_pairs={{0,4},{1,5},{2,6},{3,7},{4,0},{5,1},{6,2},{7,3},{8,12},{9,13},{10,... | collective-permute-start | bytes 786440 | tf_op jit(solution)/shard_map/gather_panels/ppermute | solution.py:435
  49.2 37.4 %collective-permute-start.17 = (bf16[128,1024]{1,0:T(8,128)(2,1)}, bf16[128,1024]{1,0:T(8,128)(2,1)S(1)}, u32[]{:S(2)}, u32[]{:S(2)}) collective-permute-start(bf16[128,1024]{1,0:T(8,128)(2,1)} %get-tuple-element.152), channel_id=1, source_target_pairs={{0,5},{1,4},{2,7},{3,6},{4,1},{5,0},{6,3},{7,2},{8,13},{9,12},{10,... | collective-permute-start | bytes 786440 | tf_op jit(solution)/shard_map/gather_panels/ppermute | solution.py:435
  50.8 35.7 %collective-permute-start.18 = (bf16[128,1024]{1,0:T(8,128)(2,1)}, bf16[128,1024]{1,0:T(8,128)(2,1)S(1)}, u32[]{:S(2)}, u32[]{:S(2)}) collective-permute-start(bf16[128,1024]{1,0:T(8,128)(2,1)} %get-tuple-element.153), channel_id=1, source_target_pairs={{0,6},{1,7},{2,0},{3,1},{4,2},{5,3},{6,4},{7,5},{8,14},{9,15},{10,... | collective-permute-start | bytes 786440 | tf_op jit(solution)/shard_map/gather_panels/ppermute | solution.py:435
  59.4 11.7 %copy-start.9 = (bf16[128,1024]{1,0:T(8,128)(2,1)S(1)}, bf16[128,1024]{1,0:T(8,128)(2,1)}, u32[]{:S(2)}) copy-start(bf16[128,1024]{1,0:T(8,128)(2,1)} %get-tuple-element.154) | copy-start | bytes 786436
  59.4 27.1 %all-to-all-start.2 = ((bf16[16,17,16,128]{3,2,1,0:T(8,128)(2,1)}), bf16[16,17,16,128]{3,2,1,0:T(8,128)(2,1)}, u32[]{:S(2)}, u32[]{:S(2)}) async-start(bf16[16,17,16,128]{3,2,1,0:T(8,128)(2,1)} %score.2), calls=%async_computation.2 | async-start | bytes 2228224 | tf_op jit(solution)/shard_map/split_pieces/all_to_all | solution.py:417
  71.1 15.5 %collective-permute-start.19 = (bf16[128,1024]{1,0:T(8,128)(2,1)S(1)}, bf16[128,1024]{1,0:T(8,128)(2,1)S(1)}, u32[]{:S(2)}, u32[]{:S(2)}) collective-permute-start(bf16[128,1024]{1,0:T(8,128)(2,1)S(1)} %copy-done.9), channel_id=1, source_target_pairs={{0,7},{1,6},{2,1},{3,0},{4,3},{5,2},{6,5},{7,4},{8,15},{9,14},{10,... | collective-permute-start | bytes 786440 | tf_op jit(solution)/shard_map/gather_panels/ppermute | solution.py:435
  86.5 12.4 %collective-permute-start.20 = (bf16[16,17,16,128]{3,2,1,0:T(8,128)(2,1)}, bf16[16,17,16,128]{3,2,1,0:T(8,128)(2,1)}, u32[]{:S(2)}, u32[]{:S(2)}) collective-permute-start(bf16[16,17,16,128]{3,2,1,0:T(8,128)(2,1)} %all-to-all-done.2.source), channel_id=1, source_target_pairs={{0,1},{1,0},{2,3},{3,2},{4,5},{5,4},{6,7},{7,6},{8,9},{9,8},{10,11... | collective-permute-start | bytes 3342344 | tf_op jit(solution)/shard_map/split_pieces/ppermute | solution.py:523
  92.9 23.4 %all-to-all-start.3 = ((bf16[16,17,16,128]{3,2,1,0:T(8,128)(2,1)}), bf16[16,17,16,128]{3,2,1,0:T(8,128)(2,1)S(1)}, u32[]{:S(2)}, u32[]{:S(2)}) async-start(bf16[16,17,16,128]{3,2,1,0:T(8,128)(2,1)} %score.3), calls=%async_computation.3 | async-start | bytes 2228224 | tf_op jit(solution)/shard_map/split_pieces/all_to_all | solution.py:417
  116.3 4.9 %collective-permute-start.21 = (bf16[16,17,16,128]{3,2,1,0:T(8,128)(2,1)S(1)}, bf16[16,17,16,128]{3,2,1,0:T(8,128)(2,1)S(1)}, u32[]{:S(2)}, u32[]{:S(2)}) collective-permute-start(bf16[16,17,16,128]{3,2,1,0:T(8,128)(2,1)S(1)} %all-to-all-done.3.source), channel_id=1, source_target_pairs={{0,1},{1,0},{2,3},{3,2},{4,5},{5,4},{6,7},{7,6},{8,9},{9,8},{10,11... | collective-permute-start | bytes 3342344 | tf_op jit(solution)/shard_map/split_pieces/ppermute | solution.py:523
  122.6 27.6 %collective-permute-start = (bf16[137,16,128]{2,1,0:T(8,128)(2,1)S(1)}, bf16[137,16,128]{2,1,0:T(8,128)(2,1)S(1)}, u32[]{:S(2)}, u32[]{:S(2)}) collective-permute-start(bf16[137,16,128]{2,1,0:T(8,128)(2,1)S(1)} %get-tuple-element.53), channel_id=1, source_target_pairs={{0,2},{1,3},{2,4},{3,5},{4,6},{5,7},{6,0},{7,1},{8,10},{9,11},{10,... | collective-permute-start | bytes 1683464 | tf_op jit(solution)/shard_map/sum_over_chips/cond/branch_0_fun/ppermute | solution.py:529
  125.5 24.7 %collective-permute-start.1 = (bf16[137,16,128]{2,1,0:T(8,128)(2,1)S(1)}, bf16[137,16,128]{2,1,0:T(8,128)(2,1)S(1)}, u32[]{:S(2)}, u32[]{:S(2)}) collective-permute-start(bf16[137,16,128]{2,1,0:T(8,128)(2,1)S(1)} %get-tuple-element.54), channel_id=1, source_target_pairs={{0,4},{1,5},{2,6},{3,7},{4,0},{5,1},{6,2},{7,3},{8,12},{9,13},{10,... | collective-permute-start | bytes 1683464 | tf_op jit(solution)/shard_map/sum_over_chips/cond/branch_0_fun/ppermute | solution.py:529
  126.7 27.2 %collective-permute-start.2 = (bf16[137,16,128]{2,1,0:T(8,128)(2,1)S(1)}, bf16[137,16,128]{2,1,0:T(8,128)(2,1)S(1)}, u32[]{:S(2)}, u32[]{:S(2)}) collective-permute-start(bf16[137,16,128]{2,1,0:T(8,128)(2,1)S(1)} %get-tuple-element.55), channel_id=1, source_target_pairs={{0,6},{1,7},{2,0},{3,1},{4,2},{5,3},{6,4},{7,5},{8,14},{9,15},{10,... | collective-permute-start | bytes 1683464 | tf_op jit(solution)/shard_map/sum_over_chips/cond/branch_0_fun/ppermute | solution.py:529
  (11 other events, 34.4 us)

commit v11 on v10

--- a/solution.py
+++ b/solution.py
@@ -433,8 +433,9 @@
         for g in range(GROUPS_DEV):
             ready = pick_panels(g, asked, here.reshape(1), shelf)
             arrived.append([lax.ppermute(x, "cent", shift((n + 1) // 2, (n + 1) % 2)) for n, x in enumerate(ready)])
-            asked, arrived[g][0] = tie((asked, arrived[g][0]))
-        answered, arrived[1][0] = tie((answered, arrived[1][0]))
+            if g == 0:
+                answered, arrived[g][0] = tie((answered, arrived[g][0]))
+                asked, arrived[g][1] = tie((asked, arrived[g][1]))
 
     with jax.named_scope("own_requests"):
         slots = jnp.sum(
@@ -521,8 +522,6 @@
                     begun = spread(LISTED, *short[1], sources[1], before=begun)
                 mine, begun = tie((mine, begun))
             sources += [mine, lax.ppermute(mine, "cent", shift(0, 1))]
-        if g == 0:
-            arrived[1][0], sources[0] = tie((arrived[1][0], sources[0]))
 
     def sum_over_chips(rows, to, begun, numbers, back_lanes):
         own, own_weights, *far = spread(rows, *to[3], sources[3], before=begun, last=True)

time: 181 us -> 176 us (0.972)
  waiting for transfers between devices: 66.2 us -> 58 us
  starting transfers between devices: 43.2 us -> 47.6 us
    ppermute x14, waiting for transfers between devices: 9.35 us -> 6.03 us  [local(): lax.ppermute(x, 'cent', shift((n + 1) // 2, (n + 1) % 2))]
    all_to_all x4, waiting for transfers between devices: 31.1 us -> 27.8 us  [exchange(): return lax.all_to_all(x, axis, split_axis=0, concat_axis=0, tiled=True)]
    ppermute x14, starting transfers between devices: 14.3 us -> 17 us  [local(): lax.ppermute(x, 'cent', shift((n + 1) // 2, (n + 1) % 2))]
    unnamed x24 -> x10, local copies, waits for them, and re-layouts: 8.26 us -> 6.6 us
  transfers between devices with their start and end apart: 23 -> 23, of which waited for: 8 -> 7; matrix products, arithmetic and copies ran while one was open for 3% -> 4% of each run, Pallas kernels for 11% -> 13%
where the time goes in v11:
time: 176 us; the launch traced here: 175 us
  waiting for transfers between devices  58 us (33%)
  starting transfers between devices  47.6 us (27%)
  Pallas kernels  31.5 us (18%)
  blocking collectives  22 us (12%)
  local copies, waits for them, and re-layouts  11 us (6%)
  other arithmetic  3.37 us (2%)
    all_to_all x4, waiting for transfers between devices, exchange(): return lax.all_to_all(x, axis, split_axis=0, concat_axis=0, tiled=True)  27.8 us
    all_to_all x4, starting transfers between devices, exchange(): return lax.all_to_all(x, axis, split_axis=0, concat_axis=0, tiled=True)  24.8 us
    ppermute x3, waiting for transfers between devices, sum_over_chips(): lax.ppermute(far[d - 1], 'cent', shift(d, 0))  24.1 us
    all_to_all x1, blocking collectives, exchange(): return lax.all_to_all(x, axis, split_axis=0, concat_axis=0, tiled=True)  22 us
    ppermute x14, starting transfers between devices, local(): lax.ppermute(x, 'cent', shift((n + 1) // 2, (n + 1) % 2))  17 us
    pallas_call x2, Pallas kernels, score(): pl.pallas_call(functools.partial(score_kernel, group), in_specs=[smem_spe...  12.3 us
    pallas_call x4, Pallas kernels, spread(): pl.pallas_call(kernel, in_specs=[smem_spec()] + [vmem_spec()] * (2 + len(...  7.37 us
    unnamed x10, local copies, waits for them, and re-layouts  6.6 us
  transfers between devices with their start and end apart: 23, of which 7 were waited for; matrix products, arithmetic and copies ran while one was open for 4% of the time, Pallas kernels for 13%

profile of v11, /device:TPU:24, one launch (start us, length us, event | category | flops | bytes accessed | tf_op | source)
XLA Modules:
  0.0 175.1 jit_solution(17350875263159642713)
XLA Ops:
  2.2 4.7 %all-to-all-start = ((bf16[8,5,16,128]{3,2,1,0:T(8,128)(2,1)}), bf16[8,5,16,128]{3,2,1,0:T(8,128)(2,1)S(1)}, u32[]{:S(2)}, u32[]{:S(2)}) async-start(bf16[8,5,16,128]{3,2,1,0:T(8,128)(2,1)} %requests.1), calls=%async_computation | async-start | bytes 327680 | tf_op jit(solution)/shard_map/requests/all_to_all | solution.py:417
  8.6 2.7 %all-to-all-done = bf16[8,5,16,128]{3,2,1,0:T(8,128)(2,1)S(1)} async-done(((bf16[8,5,16,128]{3,2,1,0:T(8,128)(2,1)}), bf16[8,5,16,128]{3,2,1,0:T(8,128)(2,1)S(1)}, u32[]{:S(2)}, u32[]{:S(2)}) %all-to-all-start) | async-done | bytes 163872 | tf_op jit(solution)/shard_map/requests/all_to_all | solution.py:417
  11.9 2.5 %gather_panels.2 = (bf16[128,1024]{1,0:T(8,128)(2,1)}, bf16[128,1024]{1,0:T(8,128)(2,1)}, bf16[128,1024]{1,0:T(8,128)(2,1)}, bf16[128,1024]{1,0:T(8,128)(2,1)}, ...) custom-call(s32[16]{0:T(128)} %sub.89.ids, s32[1]{0:T(128)} %bitcast.8.place, ...), custom_call_target="tpu_custom_call" | custom-call | bytes 3670016 | tf_op jit(solution)/shard_map/gather_panels/pallas_call | solution.py:131
  24.9 8.1 %all-to-all-start.1 = ((s32[16,8,8]{2,1,0:T(8,128)}), s32[16,8,8]{2,1,0:T(8,128)S(1)}, u32[]{:S(2)}, u32[]{:S(2)}) async-start(s32[16,8,8]{2,1,0:T(8,128)} %broadcast_in_dim.78), calls=%async_computation.1 | async-start | bytes 131072 | tf_op jit(solution)/shard_map/all_requests/all_to_all | solution.py:417
  33.1 2.5 %gather_panels.3 = (bf16[128,1024]{1,0:T(8,128)(2,1)}, bf16[128,1024]{1,0:T(8,128)(2,1)}, bf16[128,1024]{1,0:T(8,128)(2,1)}, bf16[128,1024]{1,0:T(8,128)(2,1)}, ...) custom-call(s32[16]{0:T(128)} %sub.89.ids, s32[1]{0:T(128)} %bitcast.8.place, ...), custom_call_target="tpu_custom_call" | custom-call | bytes 3670016 | tf_op jit(solution)/shard_map/gather_panels/pallas_call | solution.py:131
  35.6 4.5 %collective-permute-done.15.refs_2_ = bf16[128,1024]{1,0:T(8,128)(2,1)S(1)} collective-permute-done((bf16[128,1024]{1,0:T(8,128)(2,1)}, bf16[128,1024]{1,0:T(8,128)(2,1)S(1)}, u32[]{:S(2)}, u32[]{:S(2)}) %collective-permute-start.15) | collective-permute-done | bytes 262176 | tf_op jit(solution)/shard_map/gather_panels/ppermute | solution.py:435
  40.1 3.3 %collective-permute-start.10 = (bf16[128,1024]{1,0:T(8,128)(2,1)}, bf16[128,1024]{1,0:T(8,128)(2,1)S(1)}, u32[]{:S(2)}, u32[]{:S(2)}) collective-permute-start(bf16[128,1024]{1,0:T(8,128)(2,1)} %get-tuple-element.138), channel_id=1, source_target_pairs={{0,3},{1,2},{2,5},{3,4},{4,7},{5,6},{6,1},{7,0},{8,11},{9,10},{10,... | collective-permute-start | bytes 786440 | tf_op jit(solution)/shard_map/gather_panels/ppermute | solution.py:435
  43.4 2.8 %collective-permute-start.12 = (bf16[128,1024]{1,0:T(8,128)(2,1)}, bf16[128,1024]{1,0:T(8,128)(2,1)S(1)}, u32[]{:S(2)}, u32[]{:S(2)}) collective-permute-start(bf16[128,1024]{1,0:T(8,128)(2,1)} %get-tuple-element.140), channel_id=1, source_target_pairs={{0,5},{1,4},{2,7},{3,6},{4,1},{5,0},{6,3},{7,2},{8,13},{9,12},{10,... | collective-permute-start | bytes 786440 | tf_op jit(solution)/shard_map/gather_panels/ppermute | solution.py:435
  48.1 6.1 %score.3 = bf16[16,17,16,128]{3,2,1,0:T(8,128)(2,1)} custom-call(s32[8]{0:T(128)S(1)} %squeeze.88.owners, bf16[128,1024]{1,0:T(8,128)(2,1)S(1)} %collective-permute-done.6.refs_0_, bf16[128,1024]{1,0:T(8,128)(2,1)S(1)} %collective-permute-done.7.refs_1_, bf16[128,1024]{1,0:T(8,128)(2,1)S(1)} %collective-permute-done.15.refs_2_, ...), custom_call_target="tpu_custom_call" | custom-call | flops 2147483648 | bytes 5242880 | tf_op jit(solution)/shard_map/score/pallas_call | solution.py:217
  54.1 8.3 %all-to-all-start.3 = ((bf16[16,17,16,128]{3,2,1,0:T(8,128)(2,1)}), bf16[16,17,16,128]{3,2,1,0:T(8,128)(2,1)}, u32[]{:S(2)}, u32[]{:S(2)}) async-start(bf16[16,17,16,128]{3,2,1,0:T(8,128)(2,1)} %score.3), calls=%async_computation.3 | async-start | bytes 2228224 | tf_op jit(solution)/shard_map/split_pieces/all_to_all | solution.py:417
  66.0 3.2 %collective-permute-start.9 = (bf16[128,1024]{1,0:T(8,128)(2,1)S(1)}, bf16[128,1024]{1,0:T(8,128)(2,1)S(1)}, u32[]{:S(2)}, u32[]{:S(2)}) collective-permute-start(bf16[128,1024]{1,0:T(8,128)(2,1)S(1)} %copy-done.5), channel_id=1, source_target_pairs={{0,2},{1,3},{2,4},{3,5},{4,6},{5,7},{6,0},{7,1},{8,10},{9,11},{10,... | collective-permute-start | bytes 786440 | tf_op jit(solution)/shard_map/gather_panels/ppermute | solution.py:435
  69.7 12.1 %all-to-all-done.3.source = bf16[16,17,16,128]{3,2,1,0:T(8,128)(2,1)} async-done(((bf16[16,17,16,128]{3,2,1,0:T(8,128)(2,1)}), bf16[16,17,16,128]{3,2,1,0:T(8,128)(2,1)}, u32[]{:S(2)}, u32[]{:S(2)}) %all-to-all-start.3) | async-done | bytes 1114144 | tf_op jit(solution)/shard_map/split_pieces/all_to_all | solution.py:417
  81.8 6.2 %score.2 = bf16[16,17,16,128]{3,2,1,0:T(8,128)(2,1)} custom-call(s32[8]{0:T(128)S(1)} %squeeze.79.owners, bf16[128,1024]{1,0:T(8,128)(2,1)S(1)} %collective-permute-done.8.refs_0_, bf16[128,1024]{1,0:T(8,128)(2,1)S(1)} %collective-permute-done.9.refs_1_, bf16[128,1024]{1,0:T(8,128)(2,1)S(1)} %collective-permute-done.10.refs_2_, ...), custom_call_target="tpu_custom_call" | custom-call | flops 2147483648 | bytes 5242880 | tf_op jit(solution)/shard_map/score/pallas_call | solution.py:217
  88.1 3.7 %all-to-all-start.2 = ((bf16[16,17,16,128]{3,2,1,0:T(8,128)(2,1)}), bf16[16,17,16,128]{3,2,1,0:T(8,128)(2,1)S(1)}, u32[]{:S(2)}, u32[]{:S(2)}) async-start(bf16[16,17,16,128]{3,2,1,0:T(8,128)(2,1)} %score.2), calls=%async_computation.2 | async-start | bytes 2228224 | tf_op jit(solution)/shard_map/split_pieces/all_to_all | solution.py:417
  91.8 2.3 %sum_over_chips.3 = (f32[668,16,128]{2,1,0:T(8,128)S(1)}, f32[16,256]{1,0:T(8,128)S(1)}) custom-call(s32[64]{0:T(128)S(1)} %squeeze.80.places, bf16[16,17,16,128]{3,2,1,0:T(8,128)(2,1)} %all-to-all-done.3.source, s32[16,128]{1,0:T(8,128)S(1)} %get-tuple-element.153.lanes), custom_call_target="tpu_custom_call" | custom-call | flops 2097152 | bytes 4194304 | tf_op jit(solution)/shard_map/split_pieces/sum_over_chips/pallas_call | solution.py:299
  96.2 2.4 %copy-done.1 = f32[668,16,128]{2,1,0:T(8,128)} copy-done((f32[668,16,128]{2,1,0:T(8,128)}, f32[668,16,128]{2,1,0:T(8,128)S(1)}, u32[]{:S(2)}) %copy-start.1) | copy-done | bytes 5472280
  98.6 13.0 %all-to-all-done.2.source = bf16[16,17,16,128]{3,2,1,0:T(8,128)(2,1)S(1)} async-done(((bf16[16,17,16,128]{3,2,1,0:T(8,128)(2,1)}), bf16[16,17,16,128]{3,2,1,0:T(8,128)(2,1)S(1)}, u32[]{:S(2)}, u32[]{:S(2)}) %all-to-all-start.2) | async-done | bytes 1114144 | tf_op jit(solution)/shard_map/split_pieces/all_to_all | solution.py:417
  112.3 2.5 %copy-done.2 = f32[668,16,128]{2,1,0:T(8,128)S(1)} copy-done((f32[668,16,128]{2,1,0:T(8,128)S(1)}, f32[668,16,128]{2,1,0:T(8,128)}, u32[]{:S(2)}) %copy-start.2) | copy-done | bytes 5472280
  116.5 35.4 %conditional.1 = (bf16[16,17,16,128]{3,2,1,0:T(8,128)(2,1)}) conditional(s32[]{:T(128)} %convert_element_type.42, (s32[]{:T(128)}, s32[64]{0:T(128)S(1)}, bf16[16,17,16,128]{3,2,1,0:T(8,128)(2,1)S(1)}, s32[16,128]{1,0:T(8,128)S(1)}, f32[668,16,128]{2,1,0:T(8,128)S(1)}, /*index=5*/f32[16,256]{1,0:T(8,128)S(1)}, bf16[64,128,1024]{2,1,0:T(8,128)(2,1)}, ...), branch_computations={%region_7.8_spmd, %region_8.9_spmd} | conditional | flops 16784704 | bytes 74684968 | solution.py:543
  118.0 2.9 %collective-permute-start = (bf16[137,16,128]{2,1,0:T(8,128)(2,1)S(1)}, bf16[137,16,128]{2,1,0:T(8,128)(2,1)S(1)}, u32[]{:S(2)}, u32[]{:S(2)}) collective-permute-start(bf16[137,16,128]{2,1,0:T(8,128)(2,1)S(1)} %get-tuple-element.53), channel_id=1, source_target_pairs={{0,2},{1,3},{2,4},{3,5},{4,6},{5,7},{6,0},{7,1},{8,10},{9,11},{10,... | collective-permute-start | bytes 1683464 | tf_op jit(solution)/shard_map/sum_over_chips/cond/branch_0_fun/ppermute | solution.py:528
  125.1 20.4 %collective-permute-done.in1 = bf16[137,16,128]{2,1,0:T(8,128)(2,1)S(1)} collective-permute-done((bf16[137,16,128]{2,1,0:T(8,128)(2,1)S(1)}, bf16[137,16,128]{2,1,0:T(8,128)(2,1)S(1)}, u32[]{:S(2)}, u32[]{:S(2)}) %collective-permute-start) | collective-permute-done | bytes 561184 | tf_op jit(solution)/shard_map/sum_over_chips/cond/branch_0_fun/ppermute | solution.py:528
  145.6 3.7 %collective-permute-done.2.in3 = bf16[137,16,128]{2,1,0:T(8,128)(2,1)S(1)} collective-permute-done((bf16[137,16,128]{2,1,0:T(8,128)(2,1)S(1)}, bf16[137,16,128]{2,1,0:T(8,128)(2,1)S(1)}, u32[]{:S(2)}, u32[]{:S(2)}) %collective-permute-start.2) | collective-permute-done | bytes 561184 | tf_op jit(solution)/shard_map/sum_over_chips/cond/branch_0_fun/ppermute | solution.py:528
  149.3 2.6 %branch_0_fun.5 = (bf16[16,17,16,128]{3,2,1,0:T(8,128)(2,1)}, f32[256,16,128]{2,1,0:T(8,128)S(1)}) custom-call(s32[105]{0:T(128)S(1)} %get-tuple-element.25.numbers, f32[256,16,128]{2,1,0:T(8,128)S(1)} %branch_0_fun.4.begun, f32[16,128]{1,0:T(8,128)S(1)} %get-tuple-element.52.own_weights, ...), custom_call_target="tpu_custom_call", output_to_operand_aliasing={{1}: (1, {})} | custom-call | flops 4194304 | bytes 6291456 | tf_op jit(solution)/shard_map/sum_over_chips/cond/branch_0_fun/pallas_call | solution.py:364
  151.9 22.0 %all_to_all.25.pieces = bf16[16,17,16,128]{3,2,1,0:T(8,128)(2,1)S(1)} all-to-all(bf16[16,17,16,128]{3,2,1,0:T(8,128)(2,1)} %get-tuple-element.209), channel_id=1, replica_groups=mesh['pts'=16,'cent'=8] {'pts'}, dimensions={0} | all-to-all | bytes 2228224 | tf_op jit(solution)/shard_map/place/all_to_all | solution.py:417
  (101 shorter events, 30.7 us)
Async XLA Ops:
  2.2 9.1 %all-to-all-start = ((bf16[8,5,16,128]{3,2,1,0:T(8,128)(2,1)}), bf16[8,5,16,128]{3,2,1,0:T(8,128)(2,1)S(1)}, u32[]{:S(2)}, u32[]{:S(2)}) async-start(bf16[8,5,16,128]{3,2,1,0:T(8,128)(2,1)} %requests.1), calls=%async_computation | async-start | bytes 327680 | tf_op jit(solution)/shard_map/requests/all_to_all | solution.py:417
  14.4 6.5 %collective-permute-start.6 = (bf16[128,1024]{1,0:T(8,128)(2,1)}, bf16[128,1024]{1,0:T(8,128)(2,1)S(1)}, u32[]{:S(2)}, u32[]{:S(2)}) collective-permute-start(bf16[128,1024]{1,0:T(8,128)(2,1)} %get-tuple-element.128), channel_id=1, source_target_pairs={{0,1},{1,0},{2,3},{3,2},{4,5},{5,4},{6,7},{7,6},{8,9},{9,8},{10,11... | collective-permute-start | bytes 786440 | tf_op jit(solution)/shard_map/gather_panels/ppermute | solution.py:435
  14.6 9.4 %collective-permute-start.7 = (bf16[128,1024]{1,0:T(8,128)(2,1)}, bf16[128,1024]{1,0:T(8,128)(2,1)S(1)}, u32[]{:S(2)}, u32[]{:S(2)}) collective-permute-start(bf16[128,1024]{1,0:T(8,128)(2,1)} %get-tuple-element.134), channel_id=1, source_target_pairs={{0,2},{1,3},{2,4},{3,5},{4,6},{5,7},{6,0},{7,1},{8,10},{9,11},{10,... | collective-permute-start | bytes 786440 | tf_op jit(solution)/shard_map/gather_panels/ppermute | solution.py:435
  16.9 23.2 %collective-permute-start.15 = (bf16[128,1024]{1,0:T(8,128)(2,1)}, bf16[128,1024]{1,0:T(8,128)(2,1)S(1)}, u32[]{:S(2)}, u32[]{:S(2)}) collective-permute-start(bf16[128,1024]{1,0:T(8,128)(2,1)} %get-tuple-element.146), channel_id=1, source_target_pairs={{0,3},{1,2},{2,5},{3,4},{4,7},{5,6},{6,1},{7,0},{8,11},{9,10},{10,... | collective-permute-start | bytes 786440 | tf_op jit(solution)/shard_map/gather_panels/ppermute | solution.py:435
  17.7 25.6 %collective-permute-start.16 = (bf16[128,1024]{1,0:T(8,128)(2,1)}, bf16[128,1024]{1,0:T(8,128)(2,1)S(1)}, u32[]{:S(2)}, u32[]{:S(2)}) collective-permute-start(bf16[128,1024]{1,0:T(8,128)(2,1)} %get-tuple-element.147), channel_id=1, source_target_pairs={{0,4},{1,5},{2,6},{3,7},{4,0},{5,1},{6,2},{7,3},{8,12},{9,13},{10,... | collective-permute-start | bytes 786440 | tf_op jit(solution)/shard_map/gather_panels/ppermute | solution.py:435
  18.7 24.7 %collective-permute-start.17 = (bf16[128,1024]{1,0:T(8,128)(2,1)}, bf16[128,1024]{1,0:T(8,128)(2,1)S(1)}, u32[]{:S(2)}, u32[]{:S(2)}) collective-permute-start(bf16[128,1024]{1,0:T(8,128)(2,1)} %get-tuple-element.148), channel_id=1, source_target_pairs={{0,5},{1,4},{2,7},{3,6},{4,1},{5,0},{6,3},{7,2},{8,13},{9,12},{10,... | collective-permute-start | bytes 786440 | tf_op jit(solution)/shard_map/gather_panels/ppermute | solution.py:435
  20.9 25.3 %collective-permute-start.18 = (bf16[128,1024]{1,0:T(8,128)(2,1)}, bf16[128,1024]{1,0:T(8,128)(2,1)S(1)}, u32[]{:S(2)}, u32[]{:S(2)}) collective-permute-start(bf16[128,1024]{1,0:T(8,128)(2,1)} %get-tuple-element.149), channel_id=1, source_target_pairs={{0,6},{1,7},{2,0},{3,1},{4,2},{5,3},{6,4},{7,5},{8,14},{9,15},{10,... | collective-permute-start | bytes 786440 | tf_op jit(solution)/shard_map/gather_panels/ppermute | solution.py:435
  23.9 22.3 %collective-permute-start.19 = (bf16[128,1024]{1,0:T(8,128)(2,1)}, bf16[128,1024]{1,0:T(8,128)(2,1)S(1)}, u32[]{:S(2)}, u32[]{:S(2)}) collective-permute-start(bf16[128,1024]{1,0:T(8,128)(2,1)} %get-tuple-element.150), channel_id=1, source_target_pairs={{0,7},{1,6},{2,1},{3,0},{4,3},{5,2},{6,5},{7,4},{8,15},{9,14},{10,... | collective-permute-start | bytes 786440 | tf_op jit(solution)/shard_map/gather_panels/ppermute | solution.py:435
  24.9 29.2 %all-to-all-start.1 = ((s32[16,8,8]{2,1,0:T(8,128)}), s32[16,8,8]{2,1,0:T(8,128)S(1)}, u32[]{:S(2)}, u32[]{:S(2)}) async-start(s32[16,8,8]{2,1,0:T(8,128)} %broadcast_in_dim.78), calls=%async_computation.1 | async-start | bytes 131072 | tf_op jit(solution)/shard_map/all_requests/all_to_all | solution.py:417
  40.1 25.5 %collective-permute-start.10 = (bf16[128,1024]{1,0:T(8,128)(2,1)}, bf16[128,1024]{1,0:T(8,128)(2,1)S(1)}, u32[]{:S(2)}, u32[]{:S(2)}) collective-permute-start(bf16[128,1024]{1,0:T(8,128)(2,1)} %get-tuple-element.138), channel_id=1, source_target_pairs={{0,3},{1,2},{2,5},{3,4},{4,7},{5,6},{6,1},{7,0},{8,11},{9,10},{10,... | collective-permute-start | bytes 786440 | tf_op jit(solution)/shard_map/gather_panels/ppermute | solution.py:435
  43.4 22.6 %collective-permute-start.11 = (bf16[128,1024]{1,0:T(8,128)(2,1)}, bf16[128,1024]{1,0:T(8,128)(2,1)S(1)}, u32[]{:S(2)}, u32[]{:S(2)}) collective-permute-start(bf16[128,1024]{1,0:T(8,128)(2,1)} %get-tuple-element.139), channel_id=1, source_target_pairs={{0,4},{1,5},{2,6},{3,7},{4,0},{5,1},{6,2},{7,3},{8,12},{9,13},{10,... | collective-permute-start | bytes 786440 | tf_op jit(solution)/shard_map/gather_panels/ppermute | solution.py:435
  43.4 26.3 %collective-permute-start.12 = (bf16[128,1024]{1,0:T(8,128)(2,1)}, bf16[128,1024]{1,0:T(8,128)(2,1)S(1)}, u32[]{:S(2)}, u32[]{:S(2)}) collective-permute-start(bf16[128,1024]{1,0:T(8,128)(2,1)} %get-tuple-element.140), channel_id=1, source_target_pairs={{0,5},{1,4},{2,7},{3,6},{4,1},{5,0},{6,3},{7,2},{8,13},{9,12},{10,... | collective-permute-start | bytes 786440 | tf_op jit(solution)/shard_map/gather_panels/ppermute | solution.py:435
  46.2 35.6 %collective-permute-start.13 = (bf16[128,1024]{1,0:T(8,128)(2,1)}, bf16[128,1024]{1,0:T(8,128)(2,1)S(1)}, u32[]{:S(2)}, u32[]{:S(2)}) collective-permute-start(bf16[128,1024]{1,0:T(8,128)(2,1)} %get-tuple-element.141), channel_id=1, source_target_pairs={{0,6},{1,7},{2,0},{3,1},{4,2},{5,3},{6,4},{7,5},{8,14},{9,15},{10,... | collective-permute-start | bytes 786440 | tf_op jit(solution)/shard_map/gather_panels/ppermute | solution.py:435
  46.9 34.9 %collective-permute-start.14 = (bf16[128,1024]{1,0:T(8,128)(2,1)}, bf16[128,1024]{1,0:T(8,128)(2,1)S(1)}, u32[]{:S(2)}, u32[]{:S(2)}) collective-permute-start(bf16[128,1024]{1,0:T(8,128)(2,1)} %get-tuple-element.142), channel_id=1, source_target_pairs={{0,7},{1,6},{2,1},{3,0},{4,3},{5,2},{6,5},{7,4},{8,15},{9,14},{10,... | collective-permute-start | bytes 786440 | tf_op jit(solution)/shard_map/gather_panels/ppermute | solution.py:435
  54.1 11.9 %copy-start.5 = (bf16[128,1024]{1,0:T(8,128)(2,1)S(1)}, bf16[128,1024]{1,0:T(8,128)(2,1)}, u32[]{:S(2)}) copy-start(bf16[128,1024]{1,0:T(8,128)(2,1)} %get-tuple-element.137) | copy-start | bytes 786436
  54.1 27.7 %all-to-all-start.3 = ((bf16[16,17,16,128]{3,2,1,0:T(8,128)(2,1)}), bf16[16,17,16,128]{3,2,1,0:T(8,128)(2,1)}, u32[]{:S(2)}, u32[]{:S(2)}) async-start(bf16[16,17,16,128]{3,2,1,0:T(8,128)(2,1)} %score.3), calls=%async_computation.3 | async-start | bytes 2228224 | tf_op jit(solution)/shard_map/split_pieces/all_to_all | solution.py:417
  65.7 16.2 %collective-permute-start.8 = (bf16[128,1024]{1,0:T(8,128)(2,1)}, bf16[128,1024]{1,0:T(8,128)(2,1)S(1)}, u32[]{:S(2)}, u32[]{:S(2)}) collective-permute-start(bf16[128,1024]{1,0:T(8,128)(2,1)} %get-tuple-element.136), channel_id=1, source_target_pairs={{0,1},{1,0},{2,3},{3,2},{4,5},{5,4},{6,7},{7,6},{8,9},{9,8},{10,11... | collective-permute-start | bytes 786440 | tf_op jit(solution)/shard_map/gather_panels/ppermute | solution.py:435
  66.0 15.8 %collective-permute-start.9 = (bf16[128,1024]{1,0:T(8,128)(2,1)S(1)}, bf16[128,1024]{1,0:T(8,128)(2,1)S(1)}, u32[]{:S(2)}, u32[]{:S(2)}) collective-permute-start(bf16[128,1024]{1,0:T(8,128)(2,1)S(1)} %copy-done.5), channel_id=1, source_target_pairs={{0,2},{1,3},{2,4},{3,5},{4,6},{5,7},{6,0},{7,1},{8,10},{9,11},{10,... | collective-permute-start | bytes 786440 | tf_op jit(solution)/shard_map/gather_panels/ppermute | solution.py:435
  81.8 12.3 %collective-permute-start.20 = (bf16[16,17,16,128]{3,2,1,0:T(8,128)(2,1)}, bf16[16,17,16,128]{3,2,1,0:T(8,128)(2,1)}, u32[]{:S(2)}, u32[]{:S(2)}) collective-permute-start(bf16[16,17,16,128]{3,2,1,0:T(8,128)(2,1)} %all-to-all-done.3.source), channel_id=1, source_target_pairs={{0,1},{1,0},{2,3},{3,2},{4,5},{5,4},{6,7},{7,6},{8,9},{9,8},{10,11... | collective-permute-start | bytes 3342344 | tf_op jit(solution)/shard_map/split_pieces/ppermute | solution.py:524
  88.1 23.5 %all-to-all-start.2 = ((bf16[16,17,16,128]{3,2,1,0:T(8,128)(2,1)}), bf16[16,17,16,128]{3,2,1,0:T(8,128)(2,1)S(1)}, u32[]{:S(2)}, u32[]{:S(2)}) async-start(bf16[16,17,16,128]{3,2,1,0:T(8,128)(2,1)} %score.2), calls=%async_computation.2 | async-start | bytes 2228224 | tf_op jit(solution)/shard_map/split_pieces/all_to_all | solution.py:417
  111.6 4.9 %collective-permute-start.21 = (bf16[16,17,16,128]{3,2,1,0:T(8,128)(2,1)S(1)}, bf16[16,17,16,128]{3,2,1,0:T(8,128)(2,1)S(1)}, u32[]{:S(2)}, u32[]{:S(2)}) collective-permute-start(bf16[16,17,16,128]{3,2,1,0:T(8,128)(2,1)S(1)} %all-to-all-done.2.source), channel_id=1, source_target_pairs={{0,1},{1,0},{2,3},{3,2},{4,5},{5,4},{6,7},{7,6},{8,9},{9,8},{10,11... | collective-permute-start | bytes 3342344 | tf_op jit(solution)/shard_map/split_pieces/ppermute | solution.py:524
  118.0 27.6 %collective-permute-start = (bf16[137,16,128]{2,1,0:T(8,128)(2,1)S(1)}, bf16[137,16,128]{2,1,0:T(8,128)(2,1)S(1)}, u32[]{:S(2)}, u32[]{:S(2)}) collective-permute-start(bf16[137,16,128]{2,1,0:T(8,128)(2,1)S(1)} %get-tuple-element.53), channel_id=1, source_target_pairs={{0,2},{1,3},{2,4},{3,5},{4,6},{5,7},{6,0},{7,1},{8,10},{9,11},{10,... | collective-permute-start | bytes 1683464 | tf_op jit(solution)/shard_map/sum_over_chips/cond/branch_0_fun/ppermute | solution.py:528
  120.9 24.7 %collective-permute-start.1 = (bf16[137,16,128]{2,1,0:T(8,128)(2,1)S(1)}, bf16[137,16,128]{2,1,0:T(8,128)(2,1)S(1)}, u32[]{:S(2)}, u32[]{:S(2)}) collective-permute-start(bf16[137,16,128]{2,1,0:T(8,128)(2,1)S(1)} %get-tuple-element.54), channel_id=1, source_target_pairs={{0,4},{1,5},{2,6},{3,7},{4,0},{5,1},{6,2},{7,3},{8,12},{9,13},{10,... | collective-permute-start | bytes 1683464 | tf_op jit(solution)/shard_map/sum_over_chips/cond/branch_0_fun/ppermute | solution.py:528
  122.4 26.9 %collective-permute-start.2 = (bf16[137,16,128]{2,1,0:T(8,128)(2,1)S(1)}, bf16[137,16,128]{2,1,0:T(8,128)(2,1)S(1)}, u32[]{:S(2)}, u32[]{:S(2)}) collective-permute-start(bf16[137,16,128]{2,1,0:T(8,128)(2,1)S(1)} %get-tuple-element.55), channel_id=1, source_target_pairs={{0,6},{1,7},{2,0},{3,1},{4,2},{5,3},{6,4},{7,5},{8,14},{9,15},{10,... | collective-permute-start | bytes 1683464 | tf_op jit(solution)/shard_map/sum_over_chips/cond/branch_0_fun/ppermute | solution.py:528
  (4 other events, 6.6 us)

commit v12 on v11

--- a/solution.py
+++ b/solution.py
@@ -99,14 +99,15 @@
     )(candidates, home, loads)
 
 
-def pick_kernel(group, ids, place, table, *refs):
+def pick_kernel(group, paired, ids, place, table, *refs):
     *outs, held, sems = refs
 
     def fetch(n, at):
         return pltpu.make_async_copy(table.at[ids[at]], held.at[n], sems.at[0, n])
 
     def put(n):
-        return pltpu.make_async_copy(held.at[n], outs[n], sems.at[1, n])
+        target = outs[(n + 1) // 2].at[n and (n + 1) % 2] if paired else outs[n]
+        return pltpu.make_async_copy(held.at[n], target, sems.at[1, n])
 
     def each(work):
         for n in range(N_CENT - 1):
@@ -126,13 +127,16 @@
     each(lambda n, at: put(n).wait())
 
 
-def pick_panels(group, ids, place, table):
+def pick_panels(group, paired, ids, place, table):
     count = N_CENT - 1
-    return pl.pallas_call(
-        functools.partial(pick_kernel, group),
-        out_shape=[jax.ShapeDtypeStruct((PANEL, WIDTH), BF16)] * count,
+    one = jax.ShapeDtypeStruct((PANEL, WIDTH), BF16)
+    pair = jax.ShapeDtypeStruct((2, PANEL, WIDTH), BF16)
+    out = [jax.ShapeDtypeStruct((1, PANEL, WIDTH), BF16), pair, pair, pair] if paired else [one] * count
+    return pl.pallas_call(
+        functools.partial(pick_kernel, group, paired),
+        out_shape=out,
         in_specs=[smem_spec(), smem_spec(), hbm_spec()],
-        out_specs=[hbm_spec()] * count,
+        out_specs=[hbm_spec()] * len(out),
         scratch_shapes=[pltpu.VMEM((count, PANEL, WIDTH), BF16), pltpu.SemaphoreType.DMA((2, count))],
         compiler_params=params(60),
         cost_estimate=pl.CostEstimate(flops=0, bytes_accessed=4 * count * PANEL * WIDTH, transcendentals=0),
@@ -140,7 +144,9 @@
 
 
 def score_kernel(group, owners, *refs):
-    panels, (table, points, surcharge, out, members, centers, shares, sems) = refs[: N_CENT - 1], refs[N_CENT - 1 :]
+    *panels, table, points, surcharge, out, members, centers, shares, sems = refs
+    if len(panels) == CHIPS:
+        panels = [panels[o // 2 - 1].at[0] if o % 2 == 0 else panels[-1].at[o // 2] for o in range(1, N_CENT)]
     step = 256
     steps = GROUP // step
 
@@ -216,7 +222,7 @@
 def score(group, owners, panels, table, points, surcharge):
     return pl.pallas_call(
         functools.partial(score_kernel, group),
-        in_specs=[smem_spec()] + [hbm_spec()] * (N_CENT + 1) + [vmem_spec()],
+        in_specs=[smem_spec()] + [hbm_spec()] * (len(panels) + 2) + [vmem_spec()],
         out_specs=vmem_spec(),
         out_shape=jax.ShapeDtypeStruct((N_PTS, SEND_TILES, ROWS, LANE), BF16),
         scratch_shapes=[
@@ -431,8 +437,13 @@
     with jax.named_scope("gather_panels"):
         arrived = []
         for g in range(GROUPS_DEV):
-            ready = pick_panels(g, asked, here.reshape(1), shelf)
-            arrived.append([lax.ppermute(x, "cent", shift((n + 1) // 2, (n + 1) % 2)) for n, x in enumerate(ready)])
+            ready = pick_panels(g, g == 1, asked, here.reshape(1), shelf)
+            if g == 0:
+                arrived.append([lax.ppermute(x, "cent", shift((n + 1) // 2, (n + 1) % 2)) for n, x in enumerate(ready)])
+            else:
+                direct = [lax.ppermute(ready[d], "cent", shift(d, 0)) for d in range(1, CHIPS)]
+                passed = jnp.concatenate([ready[0]] + [x[1:2] for x in direct])
+                arrived.append(direct + [lax.ppermute(passed, "cent", shift(0, 1))])
             if g == 0:
                 answered, arrived[g][0] = tie((answered, arrived[g][0]))
                 asked, arrived[g][1] = tie((asked, arrived[g][1]))
@@ -515,13 +526,16 @@
         with jax.named_scope("score"):
             pieces = score(g, seen[g], arrived[g], shelf, points, surcharge)
         with jax.named_scope("split_pieces"):
-            mine = exchange(pieces, "pts")
-            if g == 1:
+            if g == 0:
+                sources.append(exchange(pieces, "pts"))
+            else:
                 with jax.named_scope("sum_over_chips"):
+                    sources[0], pieces = tie((sources[0], pieces))
+                    sources.append(lax.ppermute(sources[0], "cent", shift(0, 1)))
                     begun = spread(LISTED, *short[0], sources[0])
                     begun = spread(LISTED, *short[1], sources[1], before=begun)
-                mine, begun = tie((mine, begun))
-            sources += [mine, lax.ppermute(mine, "cent", shift(0, 1))]
+                mine, begun = tie((exchange(pieces, "pts"), begun))
+                sources += [mine, lax.ppermute(mine, "cent", shift(0, 1))]
 
     def sum_over_chips(rows, to, begun, numbers, back_lanes):
         own, own_weights, *far = spread(rows, *to[3], sources[3], before=begun, last=True)

time: 176 us -> 169 us (0.960)
  starting transfers between devices: 47.6 us -> 43.8 us
  waiting for transfers between devices: 58 us -> 55.6 us
    all_to_all x4, waiting for transfers between devices: 27.8 us -> 15.8 us  [exchange(): return lax.all_to_all(x, axis, split_axis=0, concat_axis=0, tiled=True)]
    ppermute x14 -> x7, starting transfers between devices: 17 us -> 6.2 us  [local(): lax.ppermute(x, 'cent', shift((n + 1) // 2, (n + 1) % 2))]
    ppermute x0 -> x5, waiting for transfers between devices: none -> 7.67 us  [the longest x3 6.23 us: local(): lax.ppermute(ready[d], 'cent', shift(d, 0))]
    ppermute x0 -> x5, starting transfers between devices: none -> 6.84 us  [the longest x3 6.42 us: local(): lax.ppermute(ready[d], 'cent', shift(d, 0))]
    all_to_all x4, starting transfers between devices: 24.8 us -> 27.3 us  [exchange(): return lax.all_to_all(x, axis, split_axis=0, concat_axis=0, tiled=True)]
    ppermute x3, starting transfers between devices: 5.76 us -> 3.46 us  [sum_over_chips(): lax.ppermute(far[d - 1], 'cent', shift(d, 0))]
    ppermute x14 -> x7, waiting for transfers between devices: 6.03 us -> 7.99 us  [local(): lax.ppermute(x, 'cent', shift((n + 1) // 2, (n + 1) % 2))]
    unnamed x10 -> x8, local copies, waits for them, and re-layouts: 6.6 us -> 4.97 us
  transfers between devices with their start and end apart: 23 -> 20, of which waited for: 7 -> 8; matrix products, arithmetic and copies ran while one was open for 4% -> 4% of each run, Pallas kernels for 13% -> 13%
where the time goes in v12:
time: 169 us; the launch traced here: 168 us
  waiting for transfers between devices  55.6 us (33%)
  starting transfers between devices  43.8 us (26%)
  Pallas kernels  32.3 us (19%)
  blocking collectives  22 us (13%)
  local copies, waits for them, and re-layouts  9.37 us (6%)
  other arithmetic  3.5 us (2%)
    all_to_all x4, starting transfers between devices, exchange(): return lax.all_to_all(x, axis, split_axis=0, concat_axis=0, tiled=True)  27.3 us
    ppermute x3, waiting for transfers between devices, sum_over_chips(): lax.ppermute(far[d - 1], 'cent', shift(d, 0))  24.1 us
    all_to_all x1, blocking collectives, exchange(): return lax.all_to_all(x, axis, split_axis=0, concat_axis=0, tiled=True)  22 us
    all_to_all x4, waiting for transfers between devices, exchange(): return lax.all_to_all(x, axis, split_axis=0, concat_axis=0, tiled=True)  15.8 us
    pallas_call x2, Pallas kernels, score(): pl.pallas_call(functools.partial(score_kernel, group), in_specs=[smem_spe...  12.2 us
    ppermute x7, waiting for transfers between devices, local(): lax.ppermute(x, 'cent', shift((n + 1) // 2, (n + 1) % 2))  7.99 us
    pallas_call x4, Pallas kernels, spread(): pl.pallas_call(kernel, in_specs=[smem_spec()] + [vmem_spec()] * (2 + len(...  7.4 us
    ppermute x3, starting transfers between devices, local(): lax.ppermute(ready[d], 'cent', shift(d, 0))  6.42 us
  transfers between devices with their start and end apart: 20, of which 8 were waited for; matrix products, arithmetic and copies ran while one was open for 4% of the time, Pallas kernels for 13%

profile of v12, /device:TPU:24, one launch (start us, length us, event | category | flops | bytes accessed | tf_op | source)
XLA Modules:
  0.0 168.4 jit_solution(7325301302424888545)
XLA Ops:
  2.2 4.7 %all-to-all-start = ((bf16[8,5,16,128]{3,2,1,0:T(8,128)(2,1)}), bf16[8,5,16,128]{3,2,1,0:T(8,128)(2,1)S(1)}, u32[]{:S(2)}, u32[]{:S(2)}) async-start(bf16[8,5,16,128]{3,2,1,0:T(8,128)(2,1)} %requests.1), calls=%async_computation | async-start | bytes 327680 | tf_op jit(solution)/shard_map/requests/all_to_all | solution.py:423
  8.6 2.7 %all-to-all-done = bf16[8,5,16,128]{3,2,1,0:T(8,128)(2,1)S(1)} async-done(((bf16[8,5,16,128]{3,2,1,0:T(8,128)(2,1)}), bf16[8,5,16,128]{3,2,1,0:T(8,128)(2,1)S(1)}, u32[]{:S(2)}, u32[]{:S(2)}) %all-to-all-start) | async-done | bytes 163872 | tf_op jit(solution)/shard_map/requests/all_to_all | solution.py:423
  11.9 2.9 %gather_panels.2 = (bf16[128,1024]{1,0:T(8,128)(2,1)}, bf16[128,1024]{1,0:T(8,128)(2,1)}, bf16[128,1024]{1,0:T(8,128)(2,1)}, bf16[128,1024]{1,0:T(8,128)(2,1)}, ...) custom-call(s32[16]{0:T(128)} %sub.89.ids, s32[1]{0:T(128)} %bitcast.8.place, ...), custom_call_target="tpu_custom_call" | custom-call | bytes 3670016 | tf_op jit(solution)/shard_map/gather_panels/pallas_call | solution.py:135
  21.3 8.0 %collective-permute-done.7.refs_1_ = bf16[128,1024]{1,0:T(8,128)(2,1)S(1)} collective-permute-done((bf16[128,1024]{1,0:T(8,128)(2,1)}, bf16[128,1024]{1,0:T(8,128)(2,1)S(1)}, u32[]{:S(2)}, u32[]{:S(2)}) %collective-permute-start.7) | collective-permute-done | bytes 262176 | tf_op jit(solution)/shard_map/gather_panels/ppermute | solution.py:442
  29.9 8.0 %all-to-all-start.1 = ((s32[16,8,8]{2,1,0:T(8,128)}), s32[16,8,8]{2,1,0:T(8,128)S(1)}, u32[]{:S(2)}, u32[]{:S(2)}) async-start(s32[16,8,8]{2,1,0:T(8,128)} %broadcast_in_dim.78), calls=%async_computation.1 | async-start | bytes 131072 | tf_op jit(solution)/shard_map/all_requests/all_to_all | solution.py:423
  37.9 3.0 %gather_panels.3 = (bf16[1,128,1024]{2,1,0:T(8,128)(2,1)}, bf16[2,128,1024]{2,1,0:T(8,128)(2,1)}, bf16[2,128,1024]{2,1,0:T(8,128)(2,1)}, bf16[2,128,1024]{2,1,0:T(8,128)(2,1)}) custom-call(s32[16]{0:T(128)} %sub.89.ids, s32[1]{0:T(128)} %bitcast.8.place, bf16[64,128,1024]{2,1,0:T(8,128)(2,1)} %bitcast.82), custom_call_target="tpu_custom_call" | custom-call | bytes 3670016 | tf_op jit(solution)/shard_map/gather_panels/pallas_call | solution.py:135
  41.9 3.6 %collective-permute-start.13 = (bf16[2,128,1024]{2,1,0:T(8,128)(2,1)}, bf16[2,128,1024]{2,1,0:T(8,128)(2,1)S(1)}, u32[]{:S(2)}, u32[]{:S(2)}) collective-permute-start(bf16[2,128,1024]{2,1,0:T(8,128)(2,1)} %get-tuple-element.142), channel_id=1, source_target_pairs={{0,2},{1,3},{2,4},{3,5},{4,6},{5,7},{6,0},{7,1},{8,10},{9,11},{10,... | collective-permute-start | bytes 1572872 | tf_op jit(solution)/shard_map/gather_panels/ppermute | solution.py:444
  45.4 2.9 %collective-permute-start.14 = (bf16[2,128,1024]{2,1,0:T(8,128)(2,1)}, bf16[2,128,1024]{2,1,0:T(8,128)(2,1)S(1)}, u32[]{:S(2)}, u32[]{:S(2)}) collective-permute-start(bf16[2,128,1024]{2,1,0:T(8,128)(2,1)} %get-tuple-element.143), channel_id=1, source_target_pairs={{0,4},{1,5},{2,6},{3,7},{4,0},{5,1},{6,2},{7,3},{8,12},{9,13},{10,... | collective-permute-start | bytes 1572872 | tf_op jit(solution)/shard_map/gather_panels/ppermute | solution.py:444
  48.3 6.0 %score.2 = bf16[16,17,16,128]{3,2,1,0:T(8,128)(2,1)} custom-call(s32[8]{0:T(128)S(1)} %squeeze.88.owners, bf16[128,1024]{1,0:T(8,128)(2,1)S(1)} %collective-permute-done.6.refs_0_, bf16[128,1024]{1,0:T(8,128)(2,1)S(1)} %collective-permute-done.7.refs_1_, bf16[128,1024]{1,0:T(8,128)(2,1)} %collective-permute-done.8.refs_2_, ...), custom_call_target="tpu_custom_call" | custom-call | flops 2147483648 | bytes 5242880 | tf_op jit(solution)/shard_map/score/pallas_call | solution.py:223
  54.3 7.5 %all-to-all-start.2 = ((bf16[16,17,16,128]{3,2,1,0:T(8,128)(2,1)}), bf16[16,17,16,128]{3,2,1,0:T(8,128)(2,1)}, u32[]{:S(2)}, u32[]{:S(2)}) async-start(bf16[16,17,16,128]{3,2,1,0:T(8,128)(2,1)} %score.2), calls=%async_computation.2 | async-start | bytes 2228224 | tf_op jit(solution)/shard_map/split_pieces/all_to_all | solution.py:423
  64.6 6.2 %collective-permute-done.15.refs_2_ = bf16[2,128,1024]{2,1,0:T(8,128)(2,1)S(1)} collective-permute-done((bf16[2,128,1024]{2,1,0:T(8,128)(2,1)}, bf16[2,128,1024]{2,1,0:T(8,128)(2,1)S(1)}, u32[]{:S(2)}, u32[]{:S(2)}) %collective-permute-start.15) | collective-permute-done | bytes 524320 | tf_op jit(solution)/shard_map/gather_panels/ppermute | solution.py:444
  73.7 6.2 %score.3 = bf16[16,17,16,128]{3,2,1,0:T(8,128)(2,1)} custom-call(s32[8]{0:T(128)S(1)} %squeeze.79.owners, bf16[2,128,1024]{2,1,0:T(8,128)(2,1)S(1)} %collective-permute-done.13.refs_0_, bf16[2,128,1024]{2,1,0:T(8,128)(2,1)S(1)} %collective-permute-done.14.refs_1_, bf16[2,128,1024]{2,1,0:T(8,128)(2,1)S(1)} %collective-permute-done.15.refs_2_, ...), custom_call_target="tpu_custom_call" | custom-call | flops 2147483648 | bytes 5242880 | tf_op jit(solution)/shard_map/score/pallas_call | solution.py:223
  80.2 7.0 %all-to-all-start.3 = ((bf16[16,17,16,128]{3,2,1,0:T(8,128)(2,1)}), bf16[16,17,16,128]{3,2,1,0:T(8,128)(2,1)S(1)}, u32[]{:S(2)}, u32[]{:S(2)}) async-start(bf16[16,17,16,128]{3,2,1,0:T(8,128)(2,1)} %score.3), calls=%async_computation.3 | async-start | bytes 2228224 | tf_op jit(solution)/shard_map/split_pieces/all_to_all | solution.py:423
  87.3 2.3 %sum_over_chips.3 = (f32[668,16,128]{2,1,0:T(8,128)S(1)}, f32[16,256]{1,0:T(8,128)S(1)}) custom-call(s32[64]{0:T(128)S(1)} %squeeze.80.places, bf16[16,17,16,128]{3,2,1,0:T(8,128)(2,1)} %all-to-all-done.2.source, s32[16,128]{1,0:T(8,128)S(1)} %get-tuple-element.151.lanes), custom_call_target="tpu_custom_call" | custom-call | flops 2097152 | bytes 4194304 | tf_op jit(solution)/shard_map/split_pieces/sum_over_chips/pallas_call | solution.py:305
  90.9 2.4 %copy-done.1 = f32[668,16,128]{2,1,0:T(8,128)} copy-done((f32[668,16,128]{2,1,0:T(8,128)}, f32[668,16,128]{2,1,0:T(8,128)S(1)}, u32[]{:S(2)}) %copy-start.1) | copy-done | bytes 5472280
  93.3 13.0 %all-to-all-done.3.source = bf16[16,17,16,128]{3,2,1,0:T(8,128)(2,1)S(1)} async-done(((bf16[16,17,16,128]{3,2,1,0:T(8,128)(2,1)}), bf16[16,17,16,128]{3,2,1,0:T(8,128)(2,1)S(1)}, u32[]{:S(2)}, u32[]{:S(2)}) %all-to-all-start.3) | async-done | bytes 1114144 | tf_op jit(solution)/shard_map/split_pieces/all_to_all | solution.py:423
  107.1 2.5 %copy-done.2 = f32[668,16,128]{2,1,0:T(8,128)S(1)} copy-done((f32[668,16,128]{2,1,0:T(8,128)S(1)}, f32[668,16,128]{2,1,0:T(8,128)}, u32[]{:S(2)}) %copy-start.2) | copy-done | bytes 5472280
  111.2 33.9 %conditional.1 = (bf16[16,17,16,128]{3,2,1,0:T(8,128)(2,1)}) conditional(s32[]{:T(128)} %convert_element_type.42, (s32[]{:T(128)}, s32[64]{0:T(128)S(1)}, bf16[16,17,16,128]{3,2,1,0:T(8,128)(2,1)}, s32[16,128]{1,0:T(8,128)S(1)}, f32[668,16,128]{2,1,0:T(8,128)S(1)}, /*index=5*/f32[16,256]{1,0:T(8,128)S(1)}, bf16[64,128,1024]{2,1,0:T(8,128)(2,1)}, ...), branch_computations={%region_7.8_spmd, %region_8.9_spmd} | conditional | flops 16784704 | bytes 74684968 | solution.py:557
  111.3 2.2 %branch_0_fun.3 = (f32[668,16,128]{2,1,0:T(8,128)S(1)}, f32[16,128]{1,0:T(8,128)S(1)}, bf16[137,16,128]{2,1,0:T(8,128)(2,1)S(1)}, bf16[137,16,128]{2,1,0:T(8,128)(2,1)S(1)}, bf16[137,16,128]{2,1,0:T(8,128)(2,1)S(1)}) custom-call(s32[64]{0:T(128)S(1)} %get-tuple-element.27.places, ...), custom_call_target="tpu_custom_call", output_to_operand_aliasing={{0}: (3, {})} | custom-call | flops 2097152 | bytes 4194304 | tf_op jit(solution)/shard_map/sum_over_chips/cond/branch_0_fun/pallas_call | solution.py:305
  114.1 2.8 %collective-permute-start.1 = (bf16[137,16,128]{2,1,0:T(8,128)(2,1)S(1)}, bf16[137,16,128]{2,1,0:T(8,128)(2,1)S(1)}, u32[]{:S(2)}, u32[]{:S(2)}) collective-permute-start(bf16[137,16,128]{2,1,0:T(8,128)(2,1)S(1)} %get-tuple-element.54), channel_id=1, source_target_pairs={{0,4},{1,5},{2,6},{3,7},{4,0},{5,1},{6,2},{7,3},{8,12},{9,13},{10,... | collective-permute-start | bytes 1683464 | tf_op jit(solution)/shard_map/sum_over_chips/cond/branch_0_fun/ppermute | solution.py:542
  118.3 10.7 %collective-permute-done.in1 = bf16[137,16,128]{2,1,0:T(8,128)(2,1)S(1)} collective-permute-done((bf16[137,16,128]{2,1,0:T(8,128)(2,1)S(1)}, bf16[137,16,128]{2,1,0:T(8,128)(2,1)S(1)}, u32[]{:S(2)}, u32[]{:S(2)}) %collective-permute-start) | collective-permute-done | bytes 561184 | tf_op jit(solution)/shard_map/sum_over_chips/cond/branch_0_fun/ppermute | solution.py:542
  131.2 11.3 %collective-permute-done.2.in3 = bf16[137,16,128]{2,1,0:T(8,128)(2,1)S(1)} collective-permute-done((bf16[137,16,128]{2,1,0:T(8,128)(2,1)S(1)}, bf16[137,16,128]{2,1,0:T(8,128)(2,1)S(1)}, u32[]{:S(2)}, u32[]{:S(2)}) %collective-permute-start.2) | collective-permute-done | bytes 561184 | tf_op jit(solution)/shard_map/sum_over_chips/cond/branch_0_fun/ppermute | solution.py:542
  142.5 2.6 %branch_0_fun.5 = (bf16[16,17,16,128]{3,2,1,0:T(8,128)(2,1)}, f32[256,16,128]{2,1,0:T(8,128)S(1)}) custom-call(s32[105]{0:T(128)S(1)} %get-tuple-element.25.numbers, f32[256,16,128]{2,1,0:T(8,128)S(1)} %branch_0_fun.4.begun, f32[16,128]{1,0:T(8,128)S(1)} %get-tuple-element.52.own_weights, ...), custom_call_target="tpu_custom_call", output_to_operand_aliasing={{1}: (1, {})} | custom-call | flops 4194304 | bytes 6291456 | tf_op jit(solution)/shard_map/sum_over_chips/cond/branch_0_fun/pallas_call | solution.py:370
  145.1 22.0 %all_to_all.25.pieces = bf16[16,17,16,128]{3,2,1,0:T(8,128)(2,1)S(1)} all-to-all(bf16[16,17,16,128]{3,2,1,0:T(8,128)(2,1)} %get-tuple-element.207), channel_id=1, replica_groups=mesh['pts'=16,'cent'=8] {'pts'}, dimensions={0} | all-to-all | bytes 2228224 | tf_op jit(solution)/shard_map/place/all_to_all | solution.py:423
  (98 shorter events, 26.0 us)
Async XLA Ops:
  2.2 9.1 %all-to-all-start = ((bf16[8,5,16,128]{3,2,1,0:T(8,128)(2,1)}), bf16[8,5,16,128]{3,2,1,0:T(8,128)(2,1)S(1)}, u32[]{:S(2)}, u32[]{:S(2)}) async-start(bf16[8,5,16,128]{3,2,1,0:T(8,128)(2,1)} %requests.1), calls=%async_computation | async-start | bytes 327680 | tf_op jit(solution)/shard_map/requests/all_to_all | solution.py:423
  11.3 18.0 %copy-start.3 = (bf16[8,5,16,128]{3,2,1,0:T(8,128)(2,1)}, bf16[8,5,16,128]{3,2,1,0:T(8,128)(2,1)S(1)}, u32[]{:S(2)}) copy-start(bf16[8,5,16,128]{3,2,1,0:T(8,128)(2,1)S(1)} %all-to-all-done) | copy-start | bytes 491524
  14.8 5.2 %collective-permute-start.6 = (bf16[128,1024]{1,0:T(8,128)(2,1)}, bf16[128,1024]{1,0:T(8,128)(2,1)S(1)}, u32[]{:S(2)}, u32[]{:S(2)}) collective-permute-start(bf16[128,1024]{1,0:T(8,128)(2,1)} %get-tuple-element.127), channel_id=1, source_target_pairs={{0,1},{1,0},{2,3},{3,2},{4,5},{5,4},{6,7},{7,6},{8,9},{9,8},{10,11... | collective-permute-start | bytes 786440 | tf_op jit(solution)/shard_map/gather_panels/ppermute | solution.py:442
  14.9 14.3 %collective-permute-start.7 = (bf16[128,1024]{1,0:T(8,128)(2,1)}, bf16[128,1024]{1,0:T(8,128)(2,1)S(1)}, u32[]{:S(2)}, u32[]{:S(2)}) collective-permute-start(bf16[128,1024]{1,0:T(8,128)(2,1)} %get-tuple-element.133), channel_id=1, source_target_pairs={{0,2},{1,3},{2,4},{3,5},{4,6},{5,7},{6,0},{7,1},{8,10},{9,11},{10,... | collective-permute-start | bytes 786440 | tf_op jit(solution)/shard_map/gather_panels/ppermute | solution.py:442
  17.1 24.8 %collective-permute-start.10 = (bf16[128,1024]{1,0:T(8,128)(2,1)}, bf16[128,1024]{1,0:T(8,128)(2,1)S(1)}, u32[]{:S(2)}, u32[]{:S(2)}) collective-permute-start(bf16[128,1024]{1,0:T(8,128)(2,1)} %get-tuple-element.137), channel_id=1, source_target_pairs={{0,5},{1,4},{2,7},{3,6},{4,1},{5,0},{6,3},{7,2},{8,13},{9,12},{10,... | collective-permute-start | bytes 786440 | tf_op jit(solution)/shard_map/gather_panels/ppermute | solution.py:442
  17.3 28.2 %collective-permute-start.11 = (bf16[128,1024]{1,0:T(8,128)(2,1)}, bf16[128,1024]{1,0:T(8,128)(2,1)S(1)}, u32[]{:S(2)}, u32[]{:S(2)}) collective-permute-start(bf16[128,1024]{1,0:T(8,128)(2,1)} %get-tuple-element.138), channel_id=1, source_target_pairs={{0,6},{1,7},{2,0},{3,1},{4,2},{5,3},{6,4},{7,5},{8,14},{9,15},{10,... | collective-permute-start | bytes 786440 | tf_op jit(solution)/shard_map/gather_panels/ppermute | solution.py:442
  18.3 30.0 %collective-permute-start.12 = (bf16[128,1024]{1,0:T(8,128)(2,1)}, bf16[128,1024]{1,0:T(8,128)(2,1)S(1)}, u32[]{:S(2)}, u32[]{:S(2)}) collective-permute-start(bf16[128,1024]{1,0:T(8,128)(2,1)} %get-tuple-element.139), channel_id=1, source_target_pairs={{0,7},{1,6},{2,1},{3,0},{4,3},{5,2},{6,5},{7,4},{8,15},{9,14},{10,... | collective-permute-start | bytes 786440 | tf_op jit(solution)/shard_map/gather_panels/ppermute | solution.py:442
  20.0 28.3 %collective-permute-start.8 = (bf16[128,1024]{1,0:T(8,128)(2,1)}, bf16[128,1024]{1,0:T(8,128)(2,1)}, u32[]{:S(2)}, u32[]{:S(2)}) collective-permute-start(bf16[128,1024]{1,0:T(8,128)(2,1)} %get-tuple-element.135), channel_id=1, source_target_pairs={{0,3},{1,2},{2,5},{3,4},{4,7},{5,6},{6,1},{7,0},{8,11},{9,10},{10,... | collective-permute-start | bytes 786440 | tf_op jit(solution)/shard_map/gather_panels/ppermute | solution.py:442
  29.3 19.1 %collective-permute-start.9 = (bf16[128,1024]{1,0:T(8,128)(2,1)}, bf16[128,1024]{1,0:T(8,128)(2,1)}, u32[]{:S(2)}, u32[]{:S(2)}) collective-permute-start(bf16[128,1024]{1,0:T(8,128)(2,1)} %get-tuple-element.136), channel_id=1, source_target_pairs={{0,4},{1,5},{2,6},{3,7},{4,0},{5,1},{6,2},{7,3},{8,12},{9,13},{10,... | collective-permute-start | bytes 786440 | tf_op jit(solution)/shard_map/gather_panels/ppermute | solution.py:442
  29.9 24.4 %all-to-all-start.1 = ((s32[16,8,8]{2,1,0:T(8,128)}), s32[16,8,8]{2,1,0:T(8,128)S(1)}, u32[]{:S(2)}, u32[]{:S(2)}) async-start(s32[16,8,8]{2,1,0:T(8,128)} %broadcast_in_dim.78), calls=%async_computation.1 | async-start | bytes 131072 | tf_op jit(solution)/shard_map/all_requests/all_to_all | solution.py:423
  37.9 3.0 %slice-start = ((bf16[8,5,16,128]{3,2,1,0:T(8,128)(2,1)}), bf16[8,4,16,128]{3,2,1,0:T(8,128)(2,1)S(1)}, s32[]{:S(2)}) async-start(bf16[8,5,16,128]{3,2,1,0:T(8,128)(2,1)} %copy-done.3), calls=%async_computation.5 | async-start | bytes 262144 | tf_op jit(solution)/shard_map/loads/slice | solution.py:520
  41.9 22.7 %collective-permute-start.13 = (bf16[2,128,1024]{2,1,0:T(8,128)(2,1)}, bf16[2,128,1024]{2,1,0:T(8,128)(2,1)S(1)}, u32[]{:S(2)}, u32[]{:S(2)}) collective-permute-start(bf16[2,128,1024]{2,1,0:T(8,128)(2,1)} %get-tuple-element.142), channel_id=1, source_target_pairs={{0,2},{1,3},{2,4},{3,5},{4,6},{5,7},{6,0},{7,1},{8,10},{9,11},{10,... | collective-permute-start | bytes 1572872 | tf_op jit(solution)/shard_map/gather_panels/ppermute | solution.py:444
  45.4 19.1 %collective-permute-start.14 = (bf16[2,128,1024]{2,1,0:T(8,128)(2,1)}, bf16[2,128,1024]{2,1,0:T(8,128)(2,1)S(1)}, u32[]{:S(2)}, u32[]{:S(2)}) collective-permute-start(bf16[2,128,1024]{2,1,0:T(8,128)(2,1)} %get-tuple-element.143), channel_id=1, source_target_pairs={{0,4},{1,5},{2,6},{3,7},{4,0},{5,1},{6,2},{7,3},{8,12},{9,13},{10,... | collective-permute-start | bytes 1572872 | tf_op jit(solution)/shard_map/gather_panels/ppermute | solution.py:444
  48.3 22.5 %collective-permute-start.15 = (bf16[2,128,1024]{2,1,0:T(8,128)(2,1)}, bf16[2,128,1024]{2,1,0:T(8,128)(2,1)S(1)}, u32[]{:S(2)}, u32[]{:S(2)}) collective-permute-start(bf16[2,128,1024]{2,1,0:T(8,128)(2,1)} %get-tuple-element.144), channel_id=1, source_target_pairs={{0,6},{1,7},{2,0},{3,1},{4,2},{5,3},{6,4},{7,5},{8,14},{9,15},{10,... | collective-permute-start | bytes 1572872 | tf_op jit(solution)/shard_map/gather_panels/ppermute | solution.py:444
  54.3 16.5 %copy-start.4 = (bf16[1,128,1024]{2,1,0:T(8,128)(2,1)S(1)}, bf16[1,128,1024]{2,1,0:T(8,128)(2,1)}, u32[]{:S(2)}) copy-start(bf16[1,128,1024]{2,1,0:T(8,128)(2,1)} %get-tuple-element.145) | copy-start | bytes 786436
  54.3 25.7 %all-to-all-start.2 = ((bf16[16,17,16,128]{3,2,1,0:T(8,128)(2,1)}), bf16[16,17,16,128]{3,2,1,0:T(8,128)(2,1)}, u32[]{:S(2)}, u32[]{:S(2)}) async-start(bf16[16,17,16,128]{3,2,1,0:T(8,128)(2,1)} %score.2), calls=%async_computation.2 | async-start | bytes 2228224 | tf_op jit(solution)/shard_map/split_pieces/all_to_all | solution.py:423
  71.0 2.7 %collective-permute-start.16 = (bf16[4,128,1024]{2,1,0:T(8,128)(2,1)S(1)}, bf16[4,128,1024]{2,1,0:T(8,128)(2,1)S(1)}, u32[]{:S(2)}, u32[]{:S(2)}) collective-permute-start(bf16[4,128,1024]{2,1,0:T(8,128)(2,1)S(1)} %pad_maximum_fusion), channel_id=1, source_target_pairs={{0,1},{1,0},{2,3},{3,2},{4,5},{5,4},{6,7},{7,6},{8,9},{9,8},{10,11... | collective-permute-start | bytes 3145736 | tf_op jit(solution)/shard_map/gather_panels/ppermute | solution.py:446
  80.0 9.6 %collective-permute-start.17 = (bf16[16,17,16,128]{3,2,1,0:T(8,128)(2,1)}, bf16[16,17,16,128]{3,2,1,0:T(8,128)(2,1)S(1)}, u32[]{:S(2)}, u32[]{:S(2)}) collective-permute-start(bf16[16,17,16,128]{3,2,1,0:T(8,128)(2,1)} %all-to-all-done.2.source), channel_id=1, source_target_pairs={{0,1},{1,0},{2,3},{3,2},{4,5},{5,4},{6,7},{7,6},{8,9},{9,8},{10,11... | collective-permute-start | bytes 3342344 | tf_op jit(solution)/shard_map/split_pieces/sum_over_chips/ppermute | solution.py:534
  80.2 26.1 %all-to-all-start.3 = ((bf16[16,17,16,128]{3,2,1,0:T(8,128)(2,1)}), bf16[16,17,16,128]{3,2,1,0:T(8,128)(2,1)S(1)}, u32[]{:S(2)}, u32[]{:S(2)}) async-start(bf16[16,17,16,128]{3,2,1,0:T(8,128)(2,1)} %score.3), calls=%async_computation.3 | async-start | bytes 2228224 | tf_op jit(solution)/shard_map/split_pieces/all_to_all | solution.py:423
  106.3 4.9 %collective-permute-start.18 = (bf16[16,17,16,128]{3,2,1,0:T(8,128)(2,1)S(1)}, bf16[16,17,16,128]{3,2,1,0:T(8,128)(2,1)}, u32[]{:S(2)}, u32[]{:S(2)}) collective-permute-start(bf16[16,17,16,128]{3,2,1,0:T(8,128)(2,1)S(1)} %all-to-all-done.3.source), channel_id=1, source_target_pairs={{0,1},{1,0},{2,3},{3,2},{4,5},{5,4},{6,7},{7,6},{8,9},{9,8},{10,11... | collective-permute-start | bytes 3342344 | tf_op jit(solution)/shard_map/split_pieces/ppermute | solution.py:538
  107.0 2.6 %copy-start.2 = (f32[668,16,128]{2,1,0:T(8,128)S(1)}, f32[668,16,128]{2,1,0:T(8,128)}, u32[]{:S(2)}) copy-start(f32[668,16,128]{2,1,0:T(8,128)} %copy-done.1) | copy-start | bytes 16416772
  113.5 15.6 %collective-permute-start = (bf16[137,16,128]{2,1,0:T(8,128)(2,1)S(1)}, bf16[137,16,128]{2,1,0:T(8,128)(2,1)S(1)}, u32[]{:S(2)}, u32[]{:S(2)}) collective-permute-start(bf16[137,16,128]{2,1,0:T(8,128)(2,1)S(1)} %get-tuple-element.53), channel_id=1, source_target_pairs={{0,2},{1,3},{2,4},{3,5},{4,6},{5,7},{6,0},{7,1},{8,10},{9,11},{10,... | collective-permute-start | bytes 1683464 | tf_op jit(solution)/shard_map/sum_over_chips/cond/branch_0_fun/ppermute | solution.py:542
  114.1 17.1 %collective-permute-start.1 = (bf16[137,16,128]{2,1,0:T(8,128)(2,1)S(1)}, bf16[137,16,128]{2,1,0:T(8,128)(2,1)S(1)}, u32[]{:S(2)}, u32[]{:S(2)}) collective-permute-start(bf16[137,16,128]{2,1,0:T(8,128)(2,1)S(1)} %get-tuple-element.54), channel_id=1, source_target_pairs={{0,4},{1,5},{2,6},{3,7},{4,0},{5,1},{6,2},{7,3},{8,12},{9,13},{10,... | collective-permute-start | bytes 1683464 | tf_op jit(solution)/shard_map/sum_over_chips/cond/branch_0_fun/ppermute | solution.py:542
  116.9 25.6 %collective-permute-start.2 = (bf16[137,16,128]{2,1,0:T(8,128)(2,1)S(1)}, bf16[137,16,128]{2,1,0:T(8,128)(2,1)S(1)}, u32[]{:S(2)}, u32[]{:S(2)}) collective-permute-start(bf16[137,16,128]{2,1,0:T(8,128)(2,1)S(1)} %get-tuple-element.55), channel_id=1, source_target_pairs={{0,6},{1,7},{2,0},{3,1},{4,2},{5,3},{6,4},{7,5},{8,14},{9,15},{10,... | collective-permute-start | bytes 1683464 | tf_op jit(solution)/shard_map/sum_over_chips/cond/branch_0_fun/ppermute | solution.py:542
  (1 other events, 2.4 us)

commit v13 on v12

--- a/solution.py
+++ b/solution.py
@@ -461,7 +461,7 @@
     with jax.named_scope("all_requests"):
         ring = answered[:, LOAD_TILES, 1:3, 0:REQ].astype(jnp.int32)
         ring = ring[:, 0] * PAN_DEV + ring[:, 1]
-        everyone = exchange(jnp.broadcast_to(ring, (N_PTS, N_CENT, REQ)), "pts")
+        everyone = exchange(jnp.broadcast_to(ring[None, :, :, None], (N_PTS, N_CENT, REQ, 128)), "pts")[..., 0]
 
         numbers = jnp.arange(N_CENT * PAN_DEV, dtype=jnp.int32)
         by_chip = jnp.transpose(everyone.reshape(N_PTS, CHIPS, 2 * REQ), (1, 0, 2)).reshape(CHIPS, -1)

time: 169 us -> 166 us (0.982)
  waiting for transfers between devices: 55.6 us -> 52.1 us
  local copies, waits for them, and re-layouts: 9.37 us -> 11.1 us
    ppermute x7, waiting for transfers between devices: 7.99 us -> 4.46 us  [local(): lax.ppermute(x, 'cent', shift((n + 1) // 2, (n + 1) % 2))]
    ppermute x3, waiting for transfers between devices: 6.23 us -> 3.41 us  [local(): lax.ppermute(ready[d], 'cent', shift(d, 0))]
    ppermute x3, starting transfers between devices: 6.42 us -> 4.68 us  [local(): lax.ppermute(ready[d], 'cent', shift(d, 0))]
    unnamed x8 -> x9, local copies, waits for them, and re-layouts: 4.97 us -> 6.47 us
  transfers between devices with their start and end apart: 20 -> 20, of which waited for: 8 -> 9; matrix products, arithmetic and copies ran while one was open for 4% -> 6% of each run, Pallas kernels for 13% -> 13%
where the time goes in v13:
time: 166 us; the launch traced here: 165 us
  waiting for transfers between devices  52.1 us (31%)
  starting transfers between devices  43 us (26%)
  Pallas kernels  31.1 us (19%)
  blocking collectives  21.9 us (13%)
  local copies, waits for them, and re-layouts  11.1 us (7%)
  other arithmetic  3.5 us (2%)
    all_to_all x4, starting transfers between devices, exchange(): return lax.all_to_all(x, axis, split_axis=0, concat_axis=0, tiled=True)  28.5 us
    ppermute x3, waiting for transfers between devices, sum_over_chips(): lax.ppermute(far[d - 1], 'cent', shift(d, 0))  25.5 us
    all_to_all x1, blocking collectives, exchange(): return lax.all_to_all(x, axis, split_axis=0, concat_axis=0, tiled=True)  21.9 us
    all_to_all x4, waiting for transfers between devices, exchange(): return lax.all_to_all(x, axis, split_axis=0, concat_axis=0, tiled=True)  17.2 us
    pallas_call x2, Pallas kernels, score(): pl.pallas_call(functools.partial(score_kernel, group), in_specs=[smem_spe...  12.2 us
    ppermute x7, starting transfers between devices, local(): lax.ppermute(x, 'cent', shift((n + 1) // 2, (n + 1) % 2))  7.52 us
    pallas_call x4, Pallas kernels, spread(): pl.pallas_call(kernel, in_specs=[smem_spec()] + [vmem_spec()] * (2 + len(...  6.59 us
    unnamed x9, local copies, waits for them, and re-layouts  6.47 us
  transfers between devices with their start and end apart: 20, of which 9 were waited for; matrix products, arithmetic and copies ran while one was open for 6% of the time, Pallas kernels for 13%

profile of v13, /device:TPU:24, one launch (start us, length us, event | category | flops | bytes accessed | tf_op | source)
XLA Modules:
  0.0 164.5 jit_solution(9876403047740180697)
XLA Ops:
  2.2 4.7 %all-to-all-start = ((bf16[8,5,16,128]{3,2,1,0:T(8,128)(2,1)}), bf16[8,5,16,128]{3,2,1,0:T(8,128)(2,1)S(1)}, u32[]{:S(2)}, u32[]{:S(2)}) async-start(bf16[8,5,16,128]{3,2,1,0:T(8,128)(2,1)} %requests.1), calls=%async_computation | async-start | bytes 327680 | tf_op jit(solution)/shard_map/requests/all_to_all | solution.py:423
  8.5 2.8 %all-to-all-done = bf16[8,5,16,128]{3,2,1,0:T(8,128)(2,1)S(1)} async-done(((bf16[8,5,16,128]{3,2,1,0:T(8,128)(2,1)}), bf16[8,5,16,128]{3,2,1,0:T(8,128)(2,1)S(1)}, u32[]{:S(2)}, u32[]{:S(2)}) %all-to-all-start) | async-done | bytes 163872 | tf_op jit(solution)/shard_map/requests/all_to_all | solution.py:423
  11.9 2.6 %gather_panels.2 = (bf16[128,1024]{1,0:T(8,128)(2,1)}, bf16[128,1024]{1,0:T(8,128)(2,1)}, bf16[128,1024]{1,0:T(8,128)(2,1)}, bf16[128,1024]{1,0:T(8,128)(2,1)}, ...) custom-call(s32[16]{0:T(128)} %sub.89.ids, s32[1]{0:T(128)} %bitcast.8.place, ...), custom_call_target="tpu_custom_call" | custom-call | bytes 3670016 | tf_op jit(solution)/shard_map/gather_panels/pallas_call | solution.py:135
  14.8 2.0 %collective-permute-start.7 = (bf16[128,1024]{1,0:T(8,128)(2,1)}, bf16[128,1024]{1,0:T(8,128)(2,1)S(1)}, u32[]{:S(2)}, u32[]{:S(2)}) collective-permute-start(bf16[128,1024]{1,0:T(8,128)(2,1)} %get-tuple-element.133), channel_id=1, source_target_pairs={{0,2},{1,3},{2,4},{3,5},{4,6},{5,7},{6,0},{7,1},{8,10},{9,11},{10,... | collective-permute-start | bytes 786440 | tf_op jit(solution)/shard_map/gather_panels/ppermute | solution.py:442
  22.1 8.3 %all-to-all-start.1 = ((s32[16,8,8,128]{3,2,1,0:T(8,128)}), s32[16,8,8,128]{3,2,1,0:T(8,128)}, u32[]{:S(2)}, u32[]{:S(2)}) async-start(s32[16,8,8,128]{3,2,1,0:T(8,128)} %broadcast_in_dim.81), calls=%async_computation.1 | async-start | bytes 1048576 | tf_op jit(solution)/shard_map/all_requests/all_to_all | solution.py:423
  31.7 2.8 %gather_panels.3 = (bf16[1,128,1024]{2,1,0:T(8,128)(2,1)}, bf16[2,128,1024]{2,1,0:T(8,128)(2,1)}, bf16[2,128,1024]{2,1,0:T(8,128)(2,1)}, bf16[2,128,1024]{2,1,0:T(8,128)(2,1)}) custom-call(s32[16]{0:T(128)} %sub.89.ids, s32[1]{0:T(128)} %bitcast.8.place, bf16[64,128,1024]{2,1,0:T(8,128)(2,1)} %bitcast.82), custom_call_target="tpu_custom_call" | custom-call | bytes 3670016 | tf_op jit(solution)/shard_map/gather_panels/pallas_call | solution.py:135
  35.4 2.4 %collective-permute-start.13 = (bf16[2,128,1024]{2,1,0:T(8,128)(2,1)}, bf16[2,128,1024]{2,1,0:T(8,128)(2,1)S(1)}, u32[]{:S(2)}, u32[]{:S(2)}) collective-permute-start(bf16[2,128,1024]{2,1,0:T(8,128)(2,1)} %get-tuple-element.142), channel_id=1, source_target_pairs={{0,2},{1,3},{2,4},{3,5},{4,6},{5,7},{6,0},{7,1},{8,10},{9,11},{10,... | collective-permute-start | bytes 1572872 | tf_op jit(solution)/shard_map/gather_panels/ppermute | solution.py:444
  37.8 2.3 %collective-permute-start.14 = (bf16[2,128,1024]{2,1,0:T(8,128)(2,1)}, bf16[2,128,1024]{2,1,0:T(8,128)(2,1)S(1)}, u32[]{:S(2)}, u32[]{:S(2)}) collective-permute-start(bf16[2,128,1024]{2,1,0:T(8,128)(2,1)} %get-tuple-element.143), channel_id=1, source_target_pairs={{0,4},{1,5},{2,6},{3,7},{4,0},{5,1},{6,2},{7,3},{8,12},{9,13},{10,... | collective-permute-start | bytes 1572872 | tf_op jit(solution)/shard_map/gather_panels/ppermute | solution.py:444
  40.1 4.4 %collective-permute-done.9.refs_3_ = bf16[128,1024]{1,0:T(8,128)(2,1)} collective-permute-done((bf16[128,1024]{1,0:T(8,128)(2,1)}, bf16[128,1024]{1,0:T(8,128)(2,1)}, u32[]{:S(2)}, u32[]{:S(2)}) %collective-permute-start.9) | collective-permute-done | bytes 262176 | tf_op jit(solution)/shard_map/gather_panels/ppermute | solution.py:442
  44.6 6.0 %score.2 = bf16[16,17,16,128]{3,2,1,0:T(8,128)(2,1)} custom-call(s32[8]{0:T(128)S(1)} %squeeze.93.owners, bf16[128,1024]{1,0:T(8,128)(2,1)S(1)} %collective-permute-done.6.refs_0_, bf16[128,1024]{1,0:T(8,128)(2,1)S(1)} %collective-permute-done.7.refs_1_, bf16[128,1024]{1,0:T(8,128)(2,1)} %collective-permute-done.8.refs_2_, ...), custom_call_target="tpu_custom_call" | custom-call | flops 2147483648 | bytes 5242880 | tf_op jit(solution)/shard_map/score/pallas_call | solution.py:223
  50.6 8.4 %all-to-all-start.2 = ((bf16[16,17,16,128]{3,2,1,0:T(8,128)(2,1)}), bf16[16,17,16,128]{3,2,1,0:T(8,128)(2,1)}, u32[]{:S(2)}, u32[]{:S(2)}) async-start(bf16[16,17,16,128]{3,2,1,0:T(8,128)(2,1)} %score.2), calls=%async_computation.2 | async-start | bytes 2228224 | tf_op jit(solution)/shard_map/split_pieces/all_to_all | solution.py:423
  63.1 3.4 %collective-permute-done.15.refs_2_ = bf16[2,128,1024]{2,1,0:T(8,128)(2,1)S(1)} collective-permute-done((bf16[2,128,1024]{2,1,0:T(8,128)(2,1)}, bf16[2,128,1024]{2,1,0:T(8,128)(2,1)S(1)}, u32[]{:S(2)}, u32[]{:S(2)}) %collective-permute-start.15) | collective-permute-done | bytes 524320 | tf_op jit(solution)/shard_map/gather_panels/ppermute | solution.py:444
  69.5 6.2 %score.3 = bf16[16,17,16,128]{3,2,1,0:T(8,128)(2,1)} custom-call(s32[8]{0:T(128)S(1)} %squeeze.83.owners, bf16[2,128,1024]{2,1,0:T(8,128)(2,1)S(1)} %collective-permute-done.13.refs_0_, bf16[2,128,1024]{2,1,0:T(8,128)(2,1)S(1)} %collective-permute-done.14.refs_1_, bf16[2,128,1024]{2,1,0:T(8,128)(2,1)S(1)} %collective-permute-done.15.refs_2_, ...), custom_call_target="tpu_custom_call" | custom-call | flops 2147483648 | bytes 5242880 | tf_op jit(solution)/shard_map/score/pallas_call | solution.py:223
  77.1 7.1 %all-to-all-start.3 = ((bf16[16,17,16,128]{3,2,1,0:T(8,128)(2,1)}), bf16[16,17,16,128]{3,2,1,0:T(8,128)(2,1)S(1)}, u32[]{:S(2)}, u32[]{:S(2)}) async-start(bf16[16,17,16,128]{3,2,1,0:T(8,128)(2,1)} %score.3), calls=%async_computation.3 | async-start | bytes 2228224 | tf_op jit(solution)/shard_map/split_pieces/all_to_all | solution.py:423
  84.2 2.3 %sum_over_chips.3 = (f32[668,16,128]{2,1,0:T(8,128)S(1)}, f32[16,256]{1,0:T(8,128)S(1)}) custom-call(s32[64]{0:T(128)S(1)} %squeeze.85.places, bf16[16,17,16,128]{3,2,1,0:T(8,128)(2,1)} %all-to-all-done.2.source, s32[16,128]{1,0:T(8,128)S(1)} %get-tuple-element.151.lanes), custom_call_target="tpu_custom_call" | custom-call | flops 2097152 | bytes 4194304 | tf_op jit(solution)/shard_map/split_pieces/sum_over_chips/pallas_call | solution.py:305
  87.8 2.4 %copy-done.1 = f32[668,16,128]{2,1,0:T(8,128)} copy-done((f32[668,16,128]{2,1,0:T(8,128)}, f32[668,16,128]{2,1,0:T(8,128)S(1)}, u32[]{:S(2)}) %copy-start.1) | copy-done | bytes 5472280
  90.2 13.1 %all-to-all-done.3.source = bf16[16,17,16,128]{3,2,1,0:T(8,128)(2,1)S(1)} async-done(((bf16[16,17,16,128]{3,2,1,0:T(8,128)(2,1)}), bf16[16,17,16,128]{3,2,1,0:T(8,128)(2,1)S(1)}, u32[]{:S(2)}, u32[]{:S(2)}) %all-to-all-start.3) | async-done | bytes 1114144 | tf_op jit(solution)/shard_map/split_pieces/all_to_all | solution.py:423
  104.0 2.5 %copy-done.2 = f32[668,16,128]{2,1,0:T(8,128)S(1)} copy-done((f32[668,16,128]{2,1,0:T(8,128)S(1)}, f32[668,16,128]{2,1,0:T(8,128)}, u32[]{:S(2)}) %copy-start.2) | copy-done | bytes 5472280
  108.1 33.2 %conditional.1 = (bf16[16,17,16,128]{3,2,1,0:T(8,128)(2,1)}) conditional(s32[]{:T(128)} %convert_element_type.42, (s32[]{:T(128)}, s32[64]{0:T(128)S(1)}, bf16[16,17,16,128]{3,2,1,0:T(8,128)(2,1)S(1)}, s32[16,128]{1,0:T(8,128)S(1)}, f32[668,16,128]{2,1,0:T(8,128)S(1)}, /*index=5*/f32[16,256]{1,0:T(8,128)S(1)}, bf16[64,128,1024]{2,1,0:T(8,128)(2,1)}, ...), branch_computations={%region_7.8_spmd, %region_8.9_spmd} | conditional | flops 16784704 | bytes 74684968 | solution.py:557
  113.1 12.1 %collective-permute-done.in1 = bf16[137,16,128]{2,1,0:T(8,128)(2,1)S(1)} collective-permute-done((bf16[137,16,128]{2,1,0:T(8,128)(2,1)S(1)}, bf16[137,16,128]{2,1,0:T(8,128)(2,1)S(1)}, u32[]{:S(2)}, u32[]{:S(2)}) %collective-permute-start) | collective-permute-done | bytes 561184 | tf_op jit(solution)/shard_map/sum_over_chips/cond/branch_0_fun/ppermute | solution.py:542
  125.2 2.2 %collective-permute-done.1.in2 = bf16[137,16,128]{2,1,0:T(8,128)(2,1)S(1)} collective-permute-done((bf16[137,16,128]{2,1,0:T(8,128)(2,1)S(1)}, bf16[137,16,128]{2,1,0:T(8,128)(2,1)S(1)}, u32[]{:S(2)}, u32[]{:S(2)}) %collective-permute-start.1) | collective-permute-done | bytes 561184 | tf_op jit(solution)/shard_map/sum_over_chips/cond/branch_0_fun/ppermute | solution.py:542
  127.4 11.3 %collective-permute-done.2.in3 = bf16[137,16,128]{2,1,0:T(8,128)(2,1)S(1)} collective-permute-done((bf16[137,16,128]{2,1,0:T(8,128)(2,1)S(1)}, bf16[137,16,128]{2,1,0:T(8,128)(2,1)S(1)}, u32[]{:S(2)}, u32[]{:S(2)}) %collective-permute-start.2) | collective-permute-done | bytes 561184 | tf_op jit(solution)/shard_map/sum_over_chips/cond/branch_0_fun/ppermute | solution.py:542
  138.7 2.7 %branch_0_fun.5 = (bf16[16,17,16,128]{3,2,1,0:T(8,128)(2,1)}, f32[256,16,128]{2,1,0:T(8,128)S(1)}) custom-call(s32[105]{0:T(128)S(1)} %get-tuple-element.25.numbers, f32[256,16,128]{2,1,0:T(8,128)S(1)} %branch_0_fun.4.begun, f32[16,128]{1,0:T(8,128)S(1)} %get-tuple-element.52.own_weights, ...), custom_call_target="tpu_custom_call", output_to_operand_aliasing={{1}: (1, {})} | custom-call | flops 4194304 | bytes 6291456 | tf_op jit(solution)/shard_map/sum_over_chips/cond/branch_0_fun/pallas_call | solution.py:370
  141.4 21.9 %all_to_all.25.pieces = bf16[16,17,16,128]{3,2,1,0:T(8,128)(2,1)S(1)} all-to-all(bf16[16,17,16,128]{3,2,1,0:T(8,128)(2,1)} %get-tuple-element.207), channel_id=1, replica_groups=mesh['pts'=16,'cent'=8] {'pts'}, dimensions={0} | all-to-all | bytes 2228224 | tf_op jit(solution)/shard_map/place/all_to_all | solution.py:423
  (98 shorter events, 28.8 us)
Async XLA Ops:
  2.2 9.1 %all-to-all-start = ((bf16[8,5,16,128]{3,2,1,0:T(8,128)(2,1)}), bf16[8,5,16,128]{3,2,1,0:T(8,128)(2,1)S(1)}, u32[]{:S(2)}, u32[]{:S(2)}) async-start(bf16[8,5,16,128]{3,2,1,0:T(8,128)(2,1)} %requests.1), calls=%async_computation | async-start | bytes 327680 | tf_op jit(solution)/shard_map/requests/all_to_all | solution.py:423
  11.3 20.4 %copy-start.3 = (bf16[8,5,16,128]{3,2,1,0:T(8,128)(2,1)}, bf16[8,5,16,128]{3,2,1,0:T(8,128)(2,1)S(1)}, u32[]{:S(2)}) copy-start(bf16[8,5,16,128]{3,2,1,0:T(8,128)(2,1)S(1)} %all-to-all-done) | copy-start | bytes 491524
  14.6 5.2 %collective-permute-start.6 = (bf16[128,1024]{1,0:T(8,128)(2,1)}, bf16[128,1024]{1,0:T(8,128)(2,1)S(1)}, u32[]{:S(2)}, u32[]{:S(2)}) collective-permute-start(bf16[128,1024]{1,0:T(8,128)(2,1)} %get-tuple-element.127), channel_id=1, source_target_pairs={{0,1},{1,0},{2,3},{3,2},{4,5},{5,4},{6,7},{7,6},{8,9},{9,8},{10,11... | collective-permute-start | bytes 786440 | tf_op jit(solution)/shard_map/gather_panels/ppermute | solution.py:442
  14.8 15.6 %collective-permute-start.7 = (bf16[128,1024]{1,0:T(8,128)(2,1)}, bf16[128,1024]{1,0:T(8,128)(2,1)S(1)}, u32[]{:S(2)}, u32[]{:S(2)}) collective-permute-start(bf16[128,1024]{1,0:T(8,128)(2,1)} %get-tuple-element.133), channel_id=1, source_target_pairs={{0,2},{1,3},{2,4},{3,5},{4,6},{5,7},{6,0},{7,1},{8,10},{9,11},{10,... | collective-permute-start | bytes 786440 | tf_op jit(solution)/shard_map/gather_panels/ppermute | solution.py:442
  16.9 18.6 %collective-permute-start.10 = (bf16[128,1024]{1,0:T(8,128)(2,1)}, bf16[128,1024]{1,0:T(8,128)(2,1)S(1)}, u32[]{:S(2)}, u32[]{:S(2)}) collective-permute-start(bf16[128,1024]{1,0:T(8,128)(2,1)} %get-tuple-element.137), channel_id=1, source_target_pairs={{0,5},{1,4},{2,7},{3,6},{4,1},{5,0},{6,3},{7,2},{8,13},{9,12},{10,... | collective-permute-start | bytes 786440 | tf_op jit(solution)/shard_map/gather_panels/ppermute | solution.py:442
  17.1 20.7 %collective-permute-start.11 = (bf16[128,1024]{1,0:T(8,128)(2,1)}, bf16[128,1024]{1,0:T(8,128)(2,1)S(1)}, u32[]{:S(2)}, u32[]{:S(2)}) collective-permute-start(bf16[128,1024]{1,0:T(8,128)(2,1)} %get-tuple-element.138), channel_id=1, source_target_pairs={{0,6},{1,7},{2,0},{3,1},{4,2},{5,3},{6,4},{7,5},{8,14},{9,15},{10,... | collective-permute-start | bytes 786440 | tf_op jit(solution)/shard_map/gather_panels/ppermute | solution.py:442
  18.2 21.9 %collective-permute-start.12 = (bf16[128,1024]{1,0:T(8,128)(2,1)}, bf16[128,1024]{1,0:T(8,128)(2,1)S(1)}, u32[]{:S(2)}, u32[]{:S(2)}) collective-permute-start(bf16[128,1024]{1,0:T(8,128)(2,1)} %get-tuple-element.139), channel_id=1, source_target_pairs={{0,7},{1,6},{2,1},{3,0},{4,3},{5,2},{6,5},{7,4},{8,15},{9,14},{10,... | collective-permute-start | bytes 786440 | tf_op jit(solution)/shard_map/gather_panels/ppermute | solution.py:442
  19.8 20.4 %collective-permute-start.8 = (bf16[128,1024]{1,0:T(8,128)(2,1)}, bf16[128,1024]{1,0:T(8,128)(2,1)}, u32[]{:S(2)}, u32[]{:S(2)}) collective-permute-start(bf16[128,1024]{1,0:T(8,128)(2,1)} %get-tuple-element.135), channel_id=1, source_target_pairs={{0,3},{1,2},{2,5},{3,4},{4,7},{5,6},{6,1},{7,0},{8,11},{9,10},{10,... | collective-permute-start | bytes 786440 | tf_op jit(solution)/shard_map/gather_panels/ppermute | solution.py:442
  22.1 28.5 %all-to-all-start.1 = ((s32[16,8,8,128]{3,2,1,0:T(8,128)}), s32[16,8,8,128]{3,2,1,0:T(8,128)}, u32[]{:S(2)}, u32[]{:S(2)}) async-start(s32[16,8,8,128]{3,2,1,0:T(8,128)} %broadcast_in_dim.81), calls=%async_computation.1 | async-start | bytes 1048576 | tf_op jit(solution)/shard_map/all_requests/all_to_all | solution.py:423
  30.4 14.2 %collective-permute-start.9 = (bf16[128,1024]{1,0:T(8,128)(2,1)}, bf16[128,1024]{1,0:T(8,128)(2,1)}, u32[]{:S(2)}, u32[]{:S(2)}) collective-permute-start(bf16[128,1024]{1,0:T(8,128)(2,1)} %get-tuple-element.136), channel_id=1, source_target_pairs={{0,4},{1,5},{2,6},{3,7},{4,0},{5,1},{6,2},{7,3},{8,12},{9,13},{10,... | collective-permute-start | bytes 786440 | tf_op jit(solution)/shard_map/gather_panels/ppermute | solution.py:442
  31.7 2.8 %slice-start = ((bf16[8,5,16,128]{3,2,1,0:T(8,128)(2,1)}), bf16[8,4,16,128]{3,2,1,0:T(8,128)(2,1)S(1)}, s32[]{:S(2)}) async-start(bf16[8,5,16,128]{3,2,1,0:T(8,128)(2,1)} %copy-done.3), calls=%async_computation.5 | async-start | bytes 262144 | tf_op jit(solution)/shard_map/loads/slice | solution.py:520
  35.4 27.6 %collective-permute-start.13 = (bf16[2,128,1024]{2,1,0:T(8,128)(2,1)}, bf16[2,128,1024]{2,1,0:T(8,128)(2,1)S(1)}, u32[]{:S(2)}, u32[]{:S(2)}) collective-permute-start(bf16[2,128,1024]{2,1,0:T(8,128)(2,1)} %get-tuple-element.142), channel_id=1, source_target_pairs={{0,2},{1,3},{2,4},{3,5},{4,6},{5,7},{6,0},{7,1},{8,10},{9,11},{10,... | collective-permute-start | bytes 1572872 | tf_op jit(solution)/shard_map/gather_panels/ppermute | solution.py:444
  37.8 25.3 %collective-permute-start.14 = (bf16[2,128,1024]{2,1,0:T(8,128)(2,1)}, bf16[2,128,1024]{2,1,0:T(8,128)(2,1)S(1)}, u32[]{:S(2)}, u32[]{:S(2)}) collective-permute-start(bf16[2,128,1024]{2,1,0:T(8,128)(2,1)} %get-tuple-element.143), channel_id=1, source_target_pairs={{0,4},{1,5},{2,6},{3,7},{4,0},{5,1},{6,2},{7,3},{8,12},{9,13},{10,... | collective-permute-start | bytes 1572872 | tf_op jit(solution)/shard_map/gather_panels/ppermute | solution.py:444
  40.1 26.4 %collective-permute-start.15 = (bf16[2,128,1024]{2,1,0:T(8,128)(2,1)}, bf16[2,128,1024]{2,1,0:T(8,128)(2,1)S(1)}, u32[]{:S(2)}, u32[]{:S(2)}) collective-permute-start(bf16[2,128,1024]{2,1,0:T(8,128)(2,1)} %get-tuple-element.144), channel_id=1, source_target_pairs={{0,6},{1,7},{2,0},{3,1},{4,2},{5,3},{6,4},{7,5},{8,14},{9,15},{10,... | collective-permute-start | bytes 1572872 | tf_op jit(solution)/shard_map/gather_panels/ppermute | solution.py:444
  50.6 16.0 %copy-start.4 = (bf16[1,128,1024]{2,1,0:T(8,128)(2,1)S(1)}, bf16[1,128,1024]{2,1,0:T(8,128)(2,1)}, u32[]{:S(2)}) copy-start(bf16[1,128,1024]{2,1,0:T(8,128)(2,1)} %get-tuple-element.145) | copy-start | bytes 786436
  50.6 26.5 %all-to-all-start.2 = ((bf16[16,17,16,128]{3,2,1,0:T(8,128)(2,1)}), bf16[16,17,16,128]{3,2,1,0:T(8,128)(2,1)}, u32[]{:S(2)}, u32[]{:S(2)}) async-start(bf16[16,17,16,128]{3,2,1,0:T(8,128)(2,1)} %score.2), calls=%async_computation.2 | async-start | bytes 2228224 | tf_op jit(solution)/shard_map/split_pieces/all_to_all | solution.py:423
  66.7 2.7 %collective-permute-start.16 = (bf16[4,128,1024]{2,1,0:T(8,128)(2,1)S(1)}, bf16[4,128,1024]{2,1,0:T(8,128)(2,1)S(1)}, u32[]{:S(2)}, u32[]{:S(2)}) collective-permute-start(bf16[4,128,1024]{2,1,0:T(8,128)(2,1)S(1)} %pad_maximum_fusion), channel_id=1, source_target_pairs={{0,1},{1,0},{2,3},{3,2},{4,5},{5,4},{6,7},{7,6},{8,9},{9,8},{10,11... | collective-permute-start | bytes 3145736 | tf_op jit(solution)/shard_map/gather_panels/ppermute | solution.py:446
  77.1 9.4 %collective-permute-start.17 = (bf16[16,17,16,128]{3,2,1,0:T(8,128)(2,1)}, bf16[16,17,16,128]{3,2,1,0:T(8,128)(2,1)S(1)}, u32[]{:S(2)}, u32[]{:S(2)}) collective-permute-start(bf16[16,17,16,128]{3,2,1,0:T(8,128)(2,1)} %all-to-all-done.2.source), channel_id=1, source_target_pairs={{0,1},{1,0},{2,3},{3,2},{4,5},{5,4},{6,7},{7,6},{8,9},{9,8},{10,11... | collective-permute-start | bytes 3342344 | tf_op jit(solution)/shard_map/split_pieces/sum_over_chips/ppermute | solution.py:534
  77.1 26.2 %all-to-all-start.3 = ((bf16[16,17,16,128]{3,2,1,0:T(8,128)(2,1)}), bf16[16,17,16,128]{3,2,1,0:T(8,128)(2,1)S(1)}, u32[]{:S(2)}, u32[]{:S(2)}) async-start(bf16[16,17,16,128]{3,2,1,0:T(8,128)(2,1)} %score.3), calls=%async_computation.3 | async-start | bytes 2228224 | tf_op jit(solution)/shard_map/split_pieces/all_to_all | solution.py:423
  103.3 4.9 %collective-permute-start.18 = (bf16[16,17,16,128]{3,2,1,0:T(8,128)(2,1)S(1)}, bf16[16,17,16,128]{3,2,1,0:T(8,128)(2,1)S(1)}, u32[]{:S(2)}, u32[]{:S(2)}) collective-permute-start(bf16[16,17,16,128]{3,2,1,0:T(8,128)(2,1)S(1)} %all-to-all-done.3.source), channel_id=1, source_target_pairs={{0,1},{1,0},{2,3},{3,2},{4,5},{5,4},{6,7},{7,6},{8,9},{9,8},{10,11... | collective-permute-start | bytes 3342344 | tf_op jit(solution)/shard_map/split_pieces/ppermute | solution.py:538
  104.0 2.6 %copy-start.2 = (f32[668,16,128]{2,1,0:T(8,128)S(1)}, f32[668,16,128]{2,1,0:T(8,128)}, u32[]{:S(2)}) copy-start(f32[668,16,128]{2,1,0:T(8,128)} %copy-done.1) | copy-start | bytes 16416772
  109.6 15.6 %collective-permute-start = (bf16[137,16,128]{2,1,0:T(8,128)(2,1)S(1)}, bf16[137,16,128]{2,1,0:T(8,128)(2,1)S(1)}, u32[]{:S(2)}, u32[]{:S(2)}) collective-permute-start(bf16[137,16,128]{2,1,0:T(8,128)(2,1)S(1)} %get-tuple-element.53), channel_id=1, source_target_pairs={{0,2},{1,3},{2,4},{3,5},{4,6},{5,7},{6,0},{7,1},{8,10},{9,11},{10,... | collective-permute-start | bytes 1683464 | tf_op jit(solution)/shard_map/sum_over_chips/cond/branch_0_fun/ppermute | solution.py:542
  110.3 17.1 %collective-permute-start.1 = (bf16[137,16,128]{2,1,0:T(8,128)(2,1)S(1)}, bf16[137,16,128]{2,1,0:T(8,128)(2,1)S(1)}, u32[]{:S(2)}, u32[]{:S(2)}) collective-permute-start(bf16[137,16,128]{2,1,0:T(8,128)(2,1)S(1)} %get-tuple-element.54), channel_id=1, source_target_pairs={{0,4},{1,5},{2,6},{3,7},{4,0},{5,1},{6,2},{7,3},{8,12},{9,13},{10,... | collective-permute-start | bytes 1683464 | tf_op jit(solution)/shard_map/sum_over_chips/cond/branch_0_fun/ppermute | solution.py:542
  110.5 28.2 %collective-permute-start.2 = (bf16[137,16,128]{2,1,0:T(8,128)(2,1)S(1)}, bf16[137,16,128]{2,1,0:T(8,128)(2,1)S(1)}, u32[]{:S(2)}, u32[]{:S(2)}) collective-permute-start(bf16[137,16,128]{2,1,0:T(8,128)(2,1)S(1)} %get-tuple-element.55), channel_id=1, source_target_pairs={{0,6},{1,7},{2,0},{3,1},{4,2},{5,3},{6,4},{7,5},{8,14},{9,15},{10,... | collective-permute-start | bytes 1683464 | tf_op jit(solution)/shard_map/sum_over_chips/cond/branch_0_fun/ppermute | solution.py:542
  (1 other events, 2.4 us)

commit v14 on v13

--- a/solution.py
+++ b/solution.py
@@ -24,7 +24,7 @@
 SEND_TILES = CAND * TILES + 1
 DENSE = PAN_DEV * TILES
 LOAD_TILES = PAN_DEV // ROWS
-LISTED = 34
+LISTED = 24
 
 sharpness_divisor = 16.0
 evenness_coefficient = 1.0
@@ -264,23 +264,18 @@
 
 
 def spread_more_kernel(places, source, lanes, total_in, weights_in, total, total_weights):
-    del total_in
+    total[...] = total_in[...]
     add_pieces(places, source, total)
     total_weights[...] = weights_in[...] + sum_weights(lanes, source)
 
 
-def spread_join_kernel(places, source, lanes, total_in, weights_in, total, total_weights):
+def spread_last_kernel(rows, places, source, lanes, total_in, weights_in, total, own, own_weights, out1, out2, out3):
     total[...] = total_in[...]
-    total_weights[...] = weights_in[...] + sum_weights(lanes, source)
-    add_pieces(places, source, total)
-
-
-def spread_last_kernel(rows, places, source, lanes, total_in, weights_in, total, own_weights, out1, out2, out3):
-    del total_in
     add_pieces(places, source, total)
     weights = weights_in[...] + sum_weights(lanes, source)
     coarse = weights.astype(BF16)
     fine = (weights - coarse.astype(F32)).astype(BF16)
+    own[...] = total[0:DENSE]
     own_weights[...] = weights[:, 0:LANE]
     for d, out in ((1, out1), (2, out2), (3, out3)):
         first = DENSE + (d - 1) * rows * TILES
@@ -289,7 +284,7 @@
         out[rows * TILES, :, PAN_DEV:LANE] = fine[:, d * PAN_DEV : (d + 1) * PAN_DEV]
 
 
-def spread(rows, places, lanes, source, before=None, last=False, join=False):
+def spread(rows, places, lanes, source, before=None, last=False):
     totals = [
         jax.ShapeDtypeStruct(((PAN_DEV + 3 * rows + 1) * TILES, ROWS, LANE), F32),
         jax.ShapeDtypeStruct((ROWS, CHIPS * PAN_DEV), F32),
@@ -297,9 +292,10 @@
     if last:
         chunk = jax.ShapeDtypeStruct((rows * TILES + 1, ROWS, LANE), BF16)
         kernel = functools.partial(spread_last_kernel, rows)
-        out = [totals[0], jax.ShapeDtypeStruct((ROWS, LANE), F32), chunk, chunk, chunk]
+        own = jax.ShapeDtypeStruct((DENSE, ROWS, LANE), F32)
+        out = [totals[0], own, jax.ShapeDtypeStruct((ROWS, LANE), F32), chunk, chunk, chunk]
     else:
-        kernel = spread_join_kernel if join else spread_first_kernel if before is None else spread_more_kernel
+        kernel = spread_first_kernel if before is None else spread_more_kernel
         out = totals
     before = before or []
     return pl.pallas_call(
@@ -307,7 +303,7 @@
         in_specs=[smem_spec()] + [vmem_spec()] * (2 + len(before)),
         out_specs=[vmem_spec()] * len(out),
         out_shape=out,
-        input_output_aliases={3: 0} if before and not join else {},
+        input_output_aliases={3: 0} if before else {},
         compiler_params=params(16),
         cost_estimate=pl.CostEstimate(flops=1 << 21, bytes_accessed=4 * MIB, transcendentals=0),
     )(places, source, lanes, *before)
@@ -337,11 +333,9 @@
     )(me, own, table)
 
 
-def finish_kernel(rows, numbers, begun, own_weights, in1, in2, in3, lanes, out, total):
-    del begun
-    weights = own_weights[:, 0:PAN_DEV]
+def take_lists(rows, numbers, weights, arrivals, lanes, total):
     panel = lax.broadcasted_iota(jnp.int32, (PAN_DEV, LANE), 0)
-    for d, arrived in enumerate((in1, in2, in3)):
+    for d, arrived in enumerate(arrivals):
         chosen = jnp.where(panel == lanes[d : d + 1, :], 1.0, 0.0).astype(BF16)
         weights = weights + lax.dot_general(
             arrived[rows * TILES], chosen, (((1,), (1,)), ((), ())), preferred_element_type=F32
@@ -354,6 +348,32 @@
             return carry
 
         lax.fori_loop(0, numbers[d], add, 0)
+    return weights
+
+
+def middle_kernel(rows, numbers, begun, weights0, weights1, own, in1, in2, in3, lanes, total, weights):
+    total[...] = begun[...] + own[...]
+    both = weights0[:, 0:PAN_DEV] + weights1[:, 0:PAN_DEV]
+    weights[:, 0:PAN_DEV] = take_lists(rows, numbers, both, (in1, in2, in3), lanes, total)
+    weights[:, PAN_DEV:LANE] = jnp.zeros((ROWS, LANE - PAN_DEV), F32)
+
+
+def middle(rows, lists, begun, weights0, weights1, own, arrived):
+    numbers, lanes = lists
+    return pl.pallas_call(
+        functools.partial(middle_kernel, rows),
+        in_specs=[smem_spec()] + [vmem_spec()] * 8,
+        out_specs=[vmem_spec(), vmem_spec()],
+        out_shape=[jax.ShapeDtypeStruct(begun.shape, F32), jax.ShapeDtypeStruct((ROWS, LANE), F32)],
+        input_output_aliases={1: 0},
+        compiler_params=params(32),
+        cost_estimate=pl.CostEstimate(flops=1 << 22, bytes_accessed=6 * MIB, transcendentals=0),
+    )(numbers, begun, weights0, weights1, own, *arrived, lanes)
+
+
+def finish_kernel(rows, numbers, begun, own_weights, in1, in2, in3, lanes, out, total):
+    total[...] = begun[...]
+    weights = take_lists(rows, numbers, own_weights[:, 0:PAN_DEV], (in1, in2, in3), lanes, total)
     inverse = 1.0 / (weights + prior_mass)
     for q in range(PAN_DEV):
         scale = jnp.broadcast_to(inverse[:, q : q + 1], (ROWS, LANE))
@@ -464,13 +484,14 @@
         everyone = exchange(jnp.broadcast_to(ring[None, :, :, None], (N_PTS, N_CENT, REQ, 128)), "pts")[..., 0]
 
         numbers = jnp.arange(N_CENT * PAN_DEV, dtype=jnp.int32)
-        by_chip = jnp.transpose(everyone.reshape(N_PTS, CHIPS, 2 * REQ), (1, 0, 2)).reshape(CHIPS, -1)
-        asked_by = jnp.any(by_chip[:, :, None] == numbers, axis=1).reshape(CHIPS, N_CENT, PAN_DEV)
+        by_chip = jnp.transpose(everyone.reshape(N_PTS, CHIPS, 2, GROUPS_DEV, CAND), (3, 1, 0, 2, 4))
+        by_chip = by_chip.reshape(GROUPS_DEV, CHIPS, -1)
+        asked_by = jnp.any(by_chip[..., None] == numbers, axis=2).reshape(GROUPS_DEV, CHIPS, N_CENT, PAN_DEV)
         below = jnp.arange(PAN_DEV)[:, None] < jnp.arange(PAN_DEV)[None, :]
         ranks = lax.dot_general(
-            asked_by.astype(BF16), below.astype(BF16), (((2,), (0,)), ((), ())), preferred_element_type=F32
+            asked_by.astype(BF16), below.astype(BF16), (((3,), (0,)), ((), ())), preferred_element_type=F32
         ).astype(jnp.int32)
-        lengths = jnp.sum(asked_by.astype(jnp.int32), axis=2)
+        lengths = jnp.sum(asked_by.astype(jnp.int32), axis=3)
         off_chip = jnp.arange(N_CENT)[None, :] // 2 != jnp.arange(CHIPS)[:, None]
         too_long = jnp.any(off_chip & (lengths > LISTED))
 
@@ -480,7 +501,7 @@
         pair = jnp.transpose(pair.reshape(2, N_PTS, GROUPS_DEV, CAND), (2, 0, 1, 3))
         owner = pair // PAN_DEV
         relative = (owner // 2 - chip) % CHIPS
-        my_ranks = lax.dynamic_index_in_dim(ranks, chip, 0, keepdims=False).reshape(-1)
+        my_ranks = lax.dynamic_index_in_dim(ranks, chip, 1, keepdims=False).reshape(GROUPS_DEV, 1, 1, 1, -1)
         rank = jnp.sum(jnp.where(pair[..., None] == numbers, my_ranks, 0), axis=4)
         ours = owner % 2 == core
 
@@ -505,15 +526,17 @@
 
         behind = [(chip - d) % CHIPS for d in range(1, CHIPS)]
         pick = lambda x, y: lax.dynamic_index_in_dim(lax.dynamic_index_in_dim(x, y, 0, False), here, 0, False)
-        named = jnp.stack([pick(asked_by, y) for y in behind])
-        order = jnp.stack([pick(ranks, y) for y in behind])
+        named = jnp.stack([pick(asked_by[g], y) for g in range(GROUPS_DEV) for y in behind])
+        order = jnp.stack([pick(ranks[g], y) for g in range(GROUPS_DEV) for y in behind])
         spots = jnp.arange(PAN_DEV, dtype=jnp.int32)
         listed = jnp.sum(
             jnp.where(named[:, None, :] & (order[:, None, :] == spots[None, :, None]), spots, 0), axis=2
         )
         count = jnp.minimum(jnp.sum(named.astype(jnp.int32), axis=1), LISTED)
         short = sender(LISTED, rank)
-        short_back = receiver(LISTED, count, listed)
+        short_back = [
+            receiver(LISTED, count[3 * g : 3 * g + 3], listed[3 * g : 3 * g + 3]) for g in range(GROUPS_DEV)
+        ]
         seen[1], too_long, short, short_back = tie((seen[1], too_long, short, short_back))
 
     with jax.named_scope("loads"):
@@ -521,43 +544,53 @@
         loads = jnp.take(load_table, slots, axis=0, mode="clip").astype(F32)
         surcharge = jnp.log(loads).reshape(GROUPS_DEV, CAND * PANEL, 1)
 
-    sources = []
-    for g in range(GROUPS_DEV):
-        with jax.named_scope("score"):
-            pieces = score(g, seen[g], arrived[g], shelf, points, surcharge)
-        with jax.named_scope("split_pieces"):
-            if g == 0:
-                sources.append(exchange(pieces, "pts"))
-            else:
-                with jax.named_scope("sum_over_chips"):
-                    sources[0], pieces = tie((sources[0], pieces))
-                    sources.append(lax.ppermute(sources[0], "cent", shift(0, 1)))
-                    begun = spread(LISTED, *short[0], sources[0])
-                    begun = spread(LISTED, *short[1], sources[1], before=begun)
-                mine, begun = tie((exchange(pieces, "pts"), begun))
-                sources += [mine, lax.ppermute(mine, "cent", shift(0, 1))]
-
-    def sum_over_chips(rows, to, begun, numbers, back_lanes):
-        own, own_weights, *far = spread(rows, *to[3], sources[3], before=begun, last=True)
-        back = [lax.ppermute(far[d - 1], "cent", shift(d, 0)) for d in range(1, CHIPS)]
-        return finish(rows, numbers, begin(me.reshape(1), own, shelf), own_weights, back, back_lanes)
-
-    def send_all():
+    where = me.reshape(1)
+
+    def to_owners(far):
+        return [lax.ppermute(far[d - 1], "cent", shift(d, 0)) for d in range(1, CHIPS)]
+
+    def swap(x):
+        return lax.ppermute(x, "cent", shift(0, 1))
+
+    with jax.named_scope("group_0"):
+        pieces = score(0, seen[0], arrived[0], shelf, points, surcharge)
+        mine0 = exchange(pieces, "pts")
+    with jax.named_scope("group_1"):
+        pieces = score(1, seen[1], arrived[1], shelf, points, surcharge)
+        mine0, pieces = tie((mine0, pieces))
+        mine1 = exchange(pieces, "pts")
+    with jax.named_scope("sums_0"):
+        mate0 = swap(mine0)
+        begun = spread(LISTED, *short[0], mine0)
+        unused, own0, weights0, *far = spread(LISTED, *short[1], mate0, before=begun, last=True)
+        back0 = to_owners(far)
+        begun = begin(where, own0, shelf)
+        mine1, back0, begun = tie((mine1, back0, begun))
+    with jax.named_scope("sums_1"):
+        mate1 = swap(mine1)
+        own1 = spread(LISTED, *short[2], mine1)
+        unused, own1, weights1, *far = spread(LISTED, *short[3], mate1, before=own1, last=True)
+        back1 = to_owners(far)
+        begun, weights = middle(LISTED, short_back[0], begun, weights0, weights1, own1, back0)
+        begun, weights, back1, mate1 = tie((begun, weights, back1, mate1))
+
+    def from_lists():
+        return finish(LISTED, short_back[1][0], begun, weights, back1, short_back[1][1])
+
+    def from_all():
         everything = jnp.broadcast_to(spots, (CHIPS - 1, PAN_DEV))
-        count = jnp.full((CHIPS - 1,), PAN_DEV, jnp.int32)
-        to = sender(PAN_DEV, pair % PAN_DEV)
-        begun = None
-        for n in range(3):
-            begun = spread(PAN_DEV, *to[n], sources[n], before=begun)
-        return sum_over_chips(PAN_DEV, to, begun, *receiver(PAN_DEV, count, everything))
-
-    with jax.named_scope("sum_over_chips"):
-        begun = spread(LISTED, *short[2], sources[2], before=begun, join=True)
-        begun, sources[3] = tie((begun, sources[3]))
-        fresh = lax.cond(too_long, send_all, lambda: sum_over_chips(LISTED, short, begun, *short_back))
+        numbers, back_lanes = receiver(PAN_DEV, jnp.full((CHIPS - 1,), PAN_DEV, jnp.int32), everything)
+        total = None
+        for n, (to, source) in enumerate(zip(sender(PAN_DEV, pair % PAN_DEV), (mine0, mate0, mine1, mate1))):
+            total = spread(PAN_DEV, *to, source, before=total, last=n == 3)
+        unused, own, own_weights, *far = total
+        return finish(PAN_DEV, numbers, begin(where, own, shelf), own_weights, to_owners(far), back_lanes)
+
+    with jax.named_scope("finish"):
+        fresh = lax.cond(too_long, from_all, from_lists)
 
     with jax.named_scope("place"):
-        new_centroids, new_loads = place(me.reshape(1), exchange(fresh, "pts"))
+        new_centroids, new_loads = place(where, exchange(fresh, "pts"))
     return new_centroids.reshape(CAND * PANEL, WIDTH), new_loads.reshape(CAND * PANEL)
 
 

time: 166 us -> 177 us (1.066)
  Pallas kernels: 31.1 us -> 42.6 us
  local copies, waits for them, and re-layouts: 11.1 us -> 7.76 us
  blocking collectives: 21.9 us -> 24.9 us
    all_to_all x4, waiting for transfers between devices: 17.2 us -> 11 us  [exchange(): return lax.all_to_all(x, axis, split_axis=0, concat_axis=0, tiled=True)]
    pallas_call x4, Pallas kernels: 6.59 us -> 11.1 us  [spread(): pl.pallas_call(kernel, in_specs=[smem_spec()] + [vmem_spec()] * (2 + len(...]
    ppermute x3, waiting for transfers between devices: 3.41 us -> 7.44 us  [local(): lax.ppermute(ready[d], 'cent', shift(d, 0))]
    unnamed x9 -> x11, local copies, waits for them, and re-layouts: 6.47 us -> 2.57 us
    pallas_call x0 -> x1, Pallas kernels: none -> 3.78 us  [middle(): pl.pallas_call(functools.partial(middle_kernel, rows), in_specs=[smem_spe...]
    all_to_all x1, blocking collectives: 21.9 us -> 24.9 us  [exchange(): return lax.all_to_all(x, axis, split_axis=0, concat_axis=0, tiled=True)]
    ppermute x5 -> x8, starting transfers between devices: 2.1 us -> 4.28 us  [the longest x6 4.06 us: to_owners(): lax.ppermute(far[d - 1], 'cent', shift(d, 0))]
    ppermute x5 -> x8, waiting for transfers between devices: 25.5 us -> 25.9 us  [the longest x6 25.2 us: to_owners(): lax.ppermute(far[d - 1], 'cent', shift(d, 0))]
  transfers between devices with their start and end apart: 20 -> 23, of which waited for: 9 -> 14; matrix products, arithmetic and copies ran while one was open for 6% -> 6% of each run, Pallas kernels for 13% -> 17%
where the time goes in v14:
time: 177 us; the launch traced here: 176 us
  waiting for transfers between devices  51.2 us (29%)
  starting transfers between devices  43.8 us (25%)
  Pallas kernels  42.6 us (24%)
  blocking collectives  24.9 us (14%)
  local copies, waits for them, and re-layouts  7.76 us (4%)
  other arithmetic  4.06 us (2%)
    all_to_all x4, starting transfers between devices, exchange(): return lax.all_to_all(x, axis, split_axis=0, concat_axis=0, tiled=True)  28.4 us
    ppermute x6, waiting for transfers between devices, to_owners(): lax.ppermute(far[d - 1], 'cent', shift(d, 0))  25.2 us
    all_to_all x1, blocking collectives, exchange(): return lax.all_to_all(x, axis, split_axis=0, concat_axis=0, tiled=True)  24.9 us
    pallas_call x2, Pallas kernels, score(): pl.pallas_call(functools.partial(score_kernel, group), in_specs=[smem_spe...  12.3 us
    pallas_call x4, Pallas kernels, spread(): pl.pallas_call(kernel, in_specs=[smem_spec()] + [vmem_spec()] * (2 + len(...  11.1 us
    all_to_all x4, waiting for transfers between devices, exchange(): return lax.all_to_all(x, axis, split_axis=0, concat_axis=0, tiled=True)  11 us
    ppermute x3, waiting for transfers between devices, local(): lax.ppermute(ready[d], 'cent', shift(d, 0))  7.44 us
    ppermute x7, starting transfers between devices, local(): lax.ppermute(x, 'cent', shift((n + 1) // 2, (n + 1) % 2))  7.34 us
  transfers between devices with their start and end apart: 23, of which 14 were waited for; matrix products, arithmetic and copies ran while one was open for 6% of the time, Pallas kernels for 17%

profile of v14, /device:TPU:24, one launch (start us, length us, event | category | flops | bytes accessed | tf_op | source)
XLA Modules:
  0.0 176.2 jit_solution(16338648106107538986)
XLA Ops:
  2.2 4.7 %all-to-all-start = ((bf16[8,5,16,128]{3,2,1,0:T(8,128)(2,1)}), bf16[8,5,16,128]{3,2,1,0:T(8,128)(2,1)S(1)}, u32[]{:S(2)}, u32[]{:S(2)}) async-start(bf16[8,5,16,128]{3,2,1,0:T(8,128)(2,1)} %requests.1), calls=%async_computation | async-start | bytes 327680 | tf_op jit(solution)/shard_map/requests/all_to_all | solution.py:443
  7.7 3.6 %all-to-all-done = bf16[8,5,16,128]{3,2,1,0:T(8,128)(2,1)S(1)} async-done(((bf16[8,5,16,128]{3,2,1,0:T(8,128)(2,1)}), bf16[8,5,16,128]{3,2,1,0:T(8,128)(2,1)S(1)}, u32[]{:S(2)}, u32[]{:S(2)}) %all-to-all-start) | async-done | bytes 163872 | tf_op jit(solution)/shard_map/requests/all_to_all | solution.py:443
  11.9 2.8 %gather_panels.2 = (bf16[128,1024]{1,0:T(8,128)(2,1)}, bf16[128,1024]{1,0:T(8,128)(2,1)}, bf16[128,1024]{1,0:T(8,128)(2,1)}, bf16[128,1024]{1,0:T(8,128)(2,1)}, ...) custom-call(s32[16]{0:T(128)} %sub.89.ids, s32[1]{0:T(128)} %bitcast.6.place, ...), custom_call_target="tpu_custom_call" | custom-call | bytes 3670016 | tf_op jit(solution)/shard_map/gather_panels/pallas_call | solution.py:135
  23.2 8.1 %all-to-all-start.1 = ((s32[16,8,8,128]{3,2,1,0:T(8,128)}), s32[16,8,8,128]{3,2,1,0:T(8,128)}, u32[]{:S(2)}, u32[]{:S(2)}) async-start(s32[16,8,8,128]{3,2,1,0:T(8,128)} %broadcast_in_dim.91), calls=%async_computation.1 | async-start | bytes 1048576 | tf_op jit(solution)/shard_map/all_requests/all_to_all | solution.py:443
  31.7 2.8 %gather_panels.3 = (bf16[1,128,1024]{2,1,0:T(8,128)(2,1)}, bf16[2,128,1024]{2,1,0:T(8,128)(2,1)}, bf16[2,128,1024]{2,1,0:T(8,128)(2,1)}, bf16[2,128,1024]{2,1,0:T(8,128)(2,1)}) custom-call(s32[16]{0:T(128)} %sub.89.ids, s32[1]{0:T(128)} %bitcast.6.place, bf16[64,128,1024]{2,1,0:T(8,128)(2,1)} %bitcast.95), custom_call_target="tpu_custom_call" | custom-call | bytes 3670016 | tf_op jit(solution)/shard_map/gather_panels/pallas_call | solution.py:135
  35.4 5.3 %collective-permute-done.5.refs_2_ = bf16[128,1024]{1,0:T(8,128)(2,1)S(1)} collective-permute-done((bf16[128,1024]{1,0:T(8,128)(2,1)}, bf16[128,1024]{1,0:T(8,128)(2,1)S(1)}, u32[]{:S(2)}, u32[]{:S(2)}) %collective-permute-start.5) | collective-permute-done | bytes 262176 | tf_op jit(solution)/shard_map/gather_panels/ppermute | solution.py:462
  40.7 2.9 %collective-permute-start.10 = (bf16[2,128,1024]{2,1,0:T(8,128)(2,1)}, bf16[2,128,1024]{2,1,0:T(8,128)(2,1)S(1)}, u32[]{:S(2)}, u32[]{:S(2)}) collective-permute-start(bf16[2,128,1024]{2,1,0:T(8,128)(2,1)} %get-tuple-element.148), channel_id=1, source_target_pairs={{0,2},{1,3},{2,4},{3,5},{4,6},{5,7},{6,0},{7,1},{8,10},{9,11},{10,... | collective-permute-start | bytes 1572872 | tf_op jit(solution)/shard_map/gather_panels/ppermute | solution.py:464
  44.8 6.0 %group_0.1 = bf16[16,17,16,128]{3,2,1,0:T(8,128)(2,1)} custom-call(s32[8]{0:T(128)S(1)} %squeeze.123.owners, bf16[128,1024]{1,0:T(8,128)(2,1)S(1)} %collective-permute-done.3.refs_0_, bf16[128,1024]{1,0:T(8,128)(2,1)S(1)} %collective-permute-done.4.refs_1_, bf16[128,1024]{1,0:T(8,128)(2,1)S(1)} %collective-permute-done.5.refs_2_, ...), custom_call_target="tpu_custom_call" | custom-call | flops 2147483648 | bytes 5242880 | tf_op jit(solution)/shard_map/group_0/pallas_call | solution.py:223
  50.8 8.0 %all-to-all-start.2 = ((bf16[16,17,16,128]{3,2,1,0:T(8,128)(2,1)}), bf16[16,17,16,128]{3,2,1,0:T(8,128)(2,1)}, u32[]{:S(2)}, u32[]{:S(2)}) async-start(bf16[16,17,16,128]{3,2,1,0:T(8,128)(2,1)} %group_0.1), calls=%async_computation.2 | async-start | bytes 2228224 | tf_op jit(solution)/shard_map/group_0/all_to_all | solution.py:443
  63.3 4.1 %collective-permute-done.10.refs_0_ = bf16[2,128,1024]{2,1,0:T(8,128)(2,1)S(1)} collective-permute-done((bf16[2,128,1024]{2,1,0:T(8,128)(2,1)}, bf16[2,128,1024]{2,1,0:T(8,128)(2,1)S(1)}, u32[]{:S(2)}, u32[]{:S(2)}) %collective-permute-start.10) | collective-permute-done | bytes 524320 | tf_op jit(solution)/shard_map/gather_panels/ppermute | solution.py:464
  67.4 3.3 %collective-permute-done.12.refs_2_ = bf16[2,128,1024]{2,1,0:T(8,128)(2,1)S(1)} collective-permute-done((bf16[2,128,1024]{2,1,0:T(8,128)(2,1)}, bf16[2,128,1024]{2,1,0:T(8,128)(2,1)S(1)}, u32[]{:S(2)}, u32[]{:S(2)}) %collective-permute-start.12) | collective-permute-done | bytes 524320 | tf_op jit(solution)/shard_map/gather_panels/ppermute | solution.py:464
  74.8 6.3 %group_1.1 = bf16[16,17,16,128]{3,2,1,0:T(8,128)(2,1)} custom-call(s32[8]{0:T(128)S(1)} %squeeze.111.owners, bf16[2,128,1024]{2,1,0:T(8,128)(2,1)S(1)} %collective-permute-done.10.refs_0_, bf16[2,128,1024]{2,1,0:T(8,128)(2,1)S(1)} %collective-permute-done.11.refs_1_, bf16[2,128,1024]{2,1,0:T(8,128)(2,1)S(1)} %collective-permute-done.12.refs_2_, ...), custom_call_target="tpu_custom_call" | custom-call | flops 2147483648 | bytes 5242880 | tf_op jit(solution)/shard_map/group_1/pallas_call | solution.py:223
  81.3 7.7 %all-to-all-start.3 = ((bf16[16,17,16,128]{3,2,1,0:T(8,128)(2,1)}), bf16[16,17,16,128]{3,2,1,0:T(8,128)(2,1)}, u32[]{:S(2)}, u32[]{:S(2)}) async-start(bf16[16,17,16,128]{3,2,1,0:T(8,128)(2,1)} %group_1.1), calls=%async_computation.3 | async-start | bytes 2228224 | tf_op jit(solution)/shard_map/group_1/all_to_all | solution.py:443
  92.2 3.7 %sums_0.4 = (f32[548,16,128]{2,1,0:T(8,128)S(1)}, f32[256,16,128]{2,1,0:T(8,128)S(1)}, f32[16,128]{1,0:T(8,128)S(1)}, bf16[97,16,128]{2,1,0:T(8,128)(2,1)}, bf16...) custom-call(s32[64]{0:T(128)S(1)} %squeeze.115.places, ...), custom_call_target="tpu_custom_call", output_to_operand_aliasing={{0}: (3, {})} | custom-call | flops 2097152 | bytes 4194304 | tf_op jit(solution)/shard_map/sums_0/pallas_call | solution.py:301
  98.0 2.8 %sums_0.5.begun = f32[256,16,128]{2,1,0:T(8,128)} custom-call(s32[1]{0:T(128)} %bitcast.4.me, f32[256,16,128]{2,1,0:T(8,128)S(1)} %get-tuple-element.163.own, bf16[64,128,1024]{2,1,0:T(8,128)(2,1)} %bitcast.98), custom_call_target="tpu_custom_call" | custom-call | flops 4194304 | bytes 5242880 | tf_op jit(solution)/shard_map/sums_0/pallas_call | solution.py:325
  100.7 7.4 %all-to-all-done.3.source = bf16[16,17,16,128]{3,2,1,0:T(8,128)(2,1)} async-done(((bf16[16,17,16,128]{3,2,1,0:T(8,128)(2,1)}), bf16[16,17,16,128]{3,2,1,0:T(8,128)(2,1)}, u32[]{:S(2)}, u32[]{:S(2)}) %all-to-all-start.3) | async-done | bytes 1114144 | tf_op jit(solution)/shard_map/group_1/all_to_all | solution.py:443
  110.6 7.3 %collective-permute-done.17.in3 = bf16[97,16,128]{2,1,0:T(8,128)(2,1)S(1)} collective-permute-done((bf16[97,16,128]{2,1,0:T(8,128)(2,1)}, bf16[97,16,128]{2,1,0:T(8,128)(2,1)S(1)}, u32[]{:S(2)}, u32[]{:S(2)}) %collective-permute-start.17) | collective-permute-done | bytes 397344 | tf_op jit(solution)/shard_map/sums_0/ppermute | solution.py:550
  120.9 2.9 %sums_1.4 = (f32[548,16,128]{2,1,0:T(8,128)S(1)}, f32[256,16,128]{2,1,0:T(8,128)S(1)}, f32[16,128]{1,0:T(8,128)S(1)}, bf16[97,16,128]{2,1,0:T(8,128)(2,1)}, bf16...) custom-call(s32[64]{0:T(128)S(1)} %squeeze.119.places, ...), custom_call_target="tpu_custom_call", output_to_operand_aliasing={{0}: (3, {})} | custom-call | flops 2097152 | bytes 4194304 | tf_op jit(solution)/shard_map/sums_1/pallas_call | solution.py:301
  126.5 3.8 %sums_1.5 = (f32[256,16,128]{2,1,0:T(8,128)}, f32[16,128]{1,0:T(8,128)S(1)}) custom-call(s32[75]{0:T(128)S(1)} %get-tuple-element.137.numbers, f32[256,16,128]{2,1,0:T(8,128)} %sums_0.5.begun, f32[16,128]{1,0:T(8,128)S(1)} %get-tuple-element.165.weights0, f32[16,128]{1,0:T(8,128)S(1)} %get-tuple-element.173.weights1, ...), custom_call_target="tpu_custom_call", output_to_operand_aliasing={{0}: (1, {})} | custom-call | flops 4194304 | bytes 6291456 | tf_op jit(solution)/shard_map/sums_1/pallas_call | solution.py:363
  130.3 5.9 %collective-permute-done.19 = bf16[97,16,128]{2,1,0:T(8,128)(2,1)} collective-permute-done((bf16[97,16,128]{2,1,0:T(8,128)(2,1)}, bf16[97,16,128]{2,1,0:T(8,128)(2,1)}, u32[]{:S(2)}, u32[]{:S(2)}) %collective-permute-start.19) | collective-permute-done | bytes 397344 | tf_op jit(solution)/shard_map/sums_1/ppermute | solution.py:550
  138.4 7.4 %collective-permute-done.21 = bf16[97,16,128]{2,1,0:T(8,128)(2,1)} collective-permute-done((bf16[97,16,128]{2,1,0:T(8,128)(2,1)}, bf16[97,16,128]{2,1,0:T(8,128)(2,1)}, u32[]{:S(2)}, u32[]{:S(2)}) %collective-permute-start.21) | collective-permute-done | bytes 397344 | tf_op jit(solution)/shard_map/sums_1/ppermute | solution.py:550
  145.7 4.3 %conditional.1 = (bf16[16,17,16,128]{3,2,1,0:T(8,128)(2,1)}) conditional(s32[]{:T(128)} %convert_element_type.42, (s32[75]{0:T(128)S(1)}, f32[256,16,128]{2,1,0:T(8,128)}, f32[16,128]{1,0:T(8,128)S(1)}, bf16[97,16,128]{2,1,0:T(8,128)(2,1)}, bf16[97,16,128]{2,1,0:T(8,128)(2,1)}, /*index=5*/bf16[97,16,128]{2,1,0:T(8,128)(2,1)}, ...), branch_computations={%region_7.8_spmd, %region_8.9_spmd} | conditional | flops 16784704 | bytes 49912392 | solution.py:590
  145.7 4.3 %branch_0_fun.1 = (bf16[16,17,16,128]{3,2,1,0:T(8,128)(2,1)}, f32[256,16,128]{2,1,0:T(8,128)}) custom-call(s32[75]{0:T(128)S(1)} %get-tuple-element.21.numbers, f32[256,16,128]{2,1,0:T(8,128)} %get-tuple-element.22.begun, f32[16,128]{1,0:T(8,128)S(1)} %get-tuple-element.23.own_weights, ...), custom_call_target="tpu_custom_call", output_to_operand_aliasing={{1}: (1, {})} | custom-call | flops 4194304 | bytes 6291456 | tf_op jit(solution)/shard_map/finish/cond/branch_0_fun/pallas_call | solution.py:390
  150.0 24.9 %all_to_all.25.pieces = bf16[16,17,16,128]{3,2,1,0:T(8,128)(2,1)S(1)} all-to-all(bf16[16,17,16,128]{3,2,1,0:T(8,128)(2,1)} %get-tuple-element.249), channel_id=1, replica_groups=mesh['pts'=16,'cent'=8] {'pts'}, dimensions={0} | all-to-all | bytes 2228224 | tf_op jit(solution)/shard_map/place/all_to_all | solution.py:443
  (119 shorter events, 38.6 us)
Async XLA Ops:
  2.2 9.1 %all-to-all-start = ((bf16[8,5,16,128]{3,2,1,0:T(8,128)(2,1)}), bf16[8,5,16,128]{3,2,1,0:T(8,128)(2,1)S(1)}, u32[]{:S(2)}, u32[]{:S(2)}) async-start(bf16[8,5,16,128]{3,2,1,0:T(8,128)(2,1)} %requests.1), calls=%async_computation | async-start | bytes 327680 | tf_op jit(solution)/shard_map/requests/all_to_all | solution.py:443
  11.3 20.4 %copy-start.4 = (bf16[8,5,16,128]{3,2,1,0:T(8,128)(2,1)}, bf16[8,5,16,128]{3,2,1,0:T(8,128)(2,1)S(1)}, u32[]{:S(2)}) copy-start(bf16[8,5,16,128]{3,2,1,0:T(8,128)(2,1)S(1)} %all-to-all-done) | copy-start | bytes 491524
  14.7 6.1 %collective-permute-start.3 = (bf16[128,1024]{1,0:T(8,128)(2,1)}, bf16[128,1024]{1,0:T(8,128)(2,1)S(1)}, u32[]{:S(2)}, u32[]{:S(2)}) collective-permute-start(bf16[128,1024]{1,0:T(8,128)(2,1)} %get-tuple-element.133), channel_id=1, source_target_pairs={{0,1},{1,0},{2,3},{3,2},{4,5},{5,4},{6,7},{7,6},{8,9},{9,8},{10,11... | collective-permute-start | bytes 786440 | tf_op jit(solution)/shard_map/gather_panels/ppermute | solution.py:462
  15.1 16.2 %collective-permute-start.4 = (bf16[128,1024]{1,0:T(8,128)(2,1)}, bf16[128,1024]{1,0:T(8,128)(2,1)S(1)}, u32[]{:S(2)}, u32[]{:S(2)}) collective-permute-start(bf16[128,1024]{1,0:T(8,128)(2,1)} %get-tuple-element.139), channel_id=1, source_target_pairs={{0,2},{1,3},{2,4},{3,5},{4,6},{5,7},{6,0},{7,1},{8,10},{9,11},{10,... | collective-permute-start | bytes 786440 | tf_op jit(solution)/shard_map/gather_panels/ppermute | solution.py:462
  17.3 23.4 %collective-permute-start.5 = (bf16[128,1024]{1,0:T(8,128)(2,1)}, bf16[128,1024]{1,0:T(8,128)(2,1)S(1)}, u32[]{:S(2)}, u32[]{:S(2)}) collective-permute-start(bf16[128,1024]{1,0:T(8,128)(2,1)} %get-tuple-element.141), channel_id=1, source_target_pairs={{0,3},{1,2},{2,5},{3,4},{4,7},{5,6},{6,1},{7,0},{8,11},{9,10},{10,... | collective-permute-start | bytes 786440 | tf_op jit(solution)/shard_map/gather_panels/ppermute | solution.py:462
  17.6 26.0 %collective-permute-start.6 = (bf16[128,1024]{1,0:T(8,128)(2,1)}, bf16[128,1024]{1,0:T(8,128)(2,1)S(1)}, u32[]{:S(2)}, u32[]{:S(2)}) collective-permute-start(bf16[128,1024]{1,0:T(8,128)(2,1)} %get-tuple-element.142), channel_id=1, source_target_pairs={{0,4},{1,5},{2,6},{3,7},{4,0},{5,1},{6,2},{7,3},{8,12},{9,13},{10,... | collective-permute-start | bytes 786440 | tf_op jit(solution)/shard_map/gather_panels/ppermute | solution.py:462
  19.1 24.6 %collective-permute-start.7 = (bf16[128,1024]{1,0:T(8,128)(2,1)}, bf16[128,1024]{1,0:T(8,128)(2,1)S(1)}, u32[]{:S(2)}, u32[]{:S(2)}) collective-permute-start(bf16[128,1024]{1,0:T(8,128)(2,1)} %get-tuple-element.143), channel_id=1, source_target_pairs={{0,5},{1,4},{2,7},{3,6},{4,1},{5,0},{6,3},{7,2},{8,13},{9,12},{10,... | collective-permute-start | bytes 786440 | tf_op jit(solution)/shard_map/gather_panels/ppermute | solution.py:462
  20.8 23.7 %collective-permute-start.8 = (bf16[128,1024]{1,0:T(8,128)(2,1)}, bf16[128,1024]{1,0:T(8,128)(2,1)}, u32[]{:S(2)}, u32[]{:S(2)}) collective-permute-start(bf16[128,1024]{1,0:T(8,128)(2,1)} %get-tuple-element.144), channel_id=1, source_target_pairs={{0,6},{1,7},{2,0},{3,1},{4,2},{5,3},{6,4},{7,5},{8,14},{9,15},{10,... | collective-permute-start | bytes 786440 | tf_op jit(solution)/shard_map/gather_panels/ppermute | solution.py:462
  23.2 27.6 %all-to-all-start.1 = ((s32[16,8,8,128]{3,2,1,0:T(8,128)}), s32[16,8,8,128]{3,2,1,0:T(8,128)}, u32[]{:S(2)}, u32[]{:S(2)}) async-start(s32[16,8,8,128]{3,2,1,0:T(8,128)} %broadcast_in_dim.91), calls=%async_computation.1 | async-start | bytes 1048576 | tf_op jit(solution)/shard_map/all_requests/all_to_all | solution.py:443
  31.3 13.4 %collective-permute-start.9 = (bf16[128,1024]{1,0:T(8,128)(2,1)}, bf16[128,1024]{1,0:T(8,128)(2,1)}, u32[]{:S(2)}, u32[]{:S(2)}) collective-permute-start(bf16[128,1024]{1,0:T(8,128)(2,1)} %get-tuple-element.145), channel_id=1, source_target_pairs={{0,7},{1,6},{2,1},{3,0},{4,3},{5,2},{6,5},{7,4},{8,15},{9,14},{10,... | collective-permute-start | bytes 786440 | tf_op jit(solution)/shard_map/gather_panels/ppermute | solution.py:462
  40.7 26.7 %collective-permute-start.10 = (bf16[2,128,1024]{2,1,0:T(8,128)(2,1)}, bf16[2,128,1024]{2,1,0:T(8,128)(2,1)S(1)}, u32[]{:S(2)}, u32[]{:S(2)}) collective-permute-start(bf16[2,128,1024]{2,1,0:T(8,128)(2,1)} %get-tuple-element.148), channel_id=1, source_target_pairs={{0,2},{1,3},{2,4},{3,5},{4,6},{5,7},{6,0},{7,1},{8,10},{9,11},{10,... | collective-permute-start | bytes 1572872 | tf_op jit(solution)/shard_map/gather_panels/ppermute | solution.py:464
  43.7 23.8 %collective-permute-start.11 = (bf16[2,128,1024]{2,1,0:T(8,128)(2,1)}, bf16[2,128,1024]{2,1,0:T(8,128)(2,1)S(1)}, u32[]{:S(2)}, u32[]{:S(2)}) collective-permute-start(bf16[2,128,1024]{2,1,0:T(8,128)(2,1)} %get-tuple-element.149), channel_id=1, source_target_pairs={{0,4},{1,5},{2,6},{3,7},{4,0},{5,1},{6,2},{7,3},{8,12},{9,13},{10,... | collective-permute-start | bytes 1572872 | tf_op jit(solution)/shard_map/gather_panels/ppermute | solution.py:464
  43.7 27.1 %collective-permute-start.12 = (bf16[2,128,1024]{2,1,0:T(8,128)(2,1)}, bf16[2,128,1024]{2,1,0:T(8,128)(2,1)S(1)}, u32[]{:S(2)}, u32[]{:S(2)}) collective-permute-start(bf16[2,128,1024]{2,1,0:T(8,128)(2,1)} %get-tuple-element.150), channel_id=1, source_target_pairs={{0,6},{1,7},{2,0},{3,1},{4,2},{5,3},{6,4},{7,5},{8,14},{9,15},{10,... | collective-permute-start | bytes 1572872 | tf_op jit(solution)/shard_map/gather_panels/ppermute | solution.py:464
  50.8 30.2 %all-to-all-start.2 = ((bf16[16,17,16,128]{3,2,1,0:T(8,128)(2,1)}), bf16[16,17,16,128]{3,2,1,0:T(8,128)(2,1)}, u32[]{:S(2)}, u32[]{:S(2)}) async-start(bf16[16,17,16,128]{3,2,1,0:T(8,128)(2,1)} %group_0.1), calls=%async_computation.2 | async-start | bytes 2228224 | tf_op jit(solution)/shard_map/group_0/all_to_all | solution.py:443
  71.9 2.9 %collective-permute-start.13 = (bf16[4,128,1024]{2,1,0:T(8,128)(2,1)}, bf16[4,128,1024]{2,1,0:T(8,128)(2,1)S(1)}, u32[]{:S(2)}, u32[]{:S(2)}) collective-permute-start(bf16[4,128,1024]{2,1,0:T(8,128)(2,1)} %pad_maximum_fusion), channel_id=1, source_target_pairs={{0,1},{1,0},{2,3},{3,2},{4,5},{5,4},{6,7},{7,6},{8,9},{9,8},{10,11... | collective-permute-start | bytes 3145736 | tf_op jit(solution)/shard_map/gather_panels/ppermute | solution.py:466
  81.1 10.1 %collective-permute-start.14 = (bf16[16,17,16,128]{3,2,1,0:T(8,128)(2,1)}, bf16[16,17,16,128]{3,2,1,0:T(8,128)(2,1)S(1)}, u32[]{:S(2)}, u32[]{:S(2)}) collective-permute-start(bf16[16,17,16,128]{3,2,1,0:T(8,128)(2,1)} %all-to-all-done.2.source), channel_id=1, source_target_pairs={{0,1},{1,0},{2,3},{3,2},{4,5},{5,4},{6,7},{7,6},{8,9},{9,8},{10,11... | collective-permute-start | bytes 3342344 | tf_op jit(solution)/shard_map/sums_0/ppermute | solution.py:553
  81.3 26.8 %all-to-all-start.3 = ((bf16[16,17,16,128]{3,2,1,0:T(8,128)(2,1)}), bf16[16,17,16,128]{3,2,1,0:T(8,128)(2,1)}, u32[]{:S(2)}, u32[]{:S(2)}) async-start(bf16[16,17,16,128]{3,2,1,0:T(8,128)(2,1)} %group_1.1), calls=%async_computation.3 | async-start | bytes 2228224 | tf_op jit(solution)/shard_map/group_1/all_to_all | solution.py:443
  95.9 12.3 %collective-permute-start.15 = (bf16[97,16,128]{2,1,0:T(8,128)(2,1)}, bf16[97,16,128]{2,1,0:T(8,128)(2,1)S(1)}, u32[]{:S(2)}, u32[]{:S(2)}) collective-permute-start(bf16[97,16,128]{2,1,0:T(8,128)(2,1)} %get-tuple-element.160), channel_id=1, source_target_pairs={{0,2},{1,3},{2,4},{3,5},{4,6},{5,7},{6,0},{7,1},{8,10},{9,11},{10,... | collective-permute-start | bytes 1191944 | tf_op jit(solution)/shard_map/sums_0/ppermute | solution.py:550
  96.8 13.9 %collective-permute-start.16 = (bf16[97,16,128]{2,1,0:T(8,128)(2,1)}, bf16[97,16,128]{2,1,0:T(8,128)(2,1)S(1)}, u32[]{:S(2)}, u32[]{:S(2)}) collective-permute-start(bf16[97,16,128]{2,1,0:T(8,128)(2,1)} %get-tuple-element.161), channel_id=1, source_target_pairs={{0,4},{1,5},{2,6},{3,7},{4,0},{5,1},{6,2},{7,3},{8,12},{9,13},{10,... | collective-permute-start | bytes 1191944 | tf_op jit(solution)/shard_map/sums_0/ppermute | solution.py:550
  97.0 20.8 %collective-permute-start.17 = (bf16[97,16,128]{2,1,0:T(8,128)(2,1)}, bf16[97,16,128]{2,1,0:T(8,128)(2,1)S(1)}, u32[]{:S(2)}, u32[]{:S(2)}) collective-permute-start(bf16[97,16,128]{2,1,0:T(8,128)(2,1)} %get-tuple-element.162), channel_id=1, source_target_pairs={{0,6},{1,7},{2,0},{3,1},{4,2},{5,3},{6,4},{7,5},{8,14},{9,15},{10,... | collective-permute-start | bytes 1191944 | tf_op jit(solution)/shard_map/sums_0/ppermute | solution.py:550
  117.9 3.0 %collective-permute-start.18 = (bf16[16,17,16,128]{3,2,1,0:T(8,128)(2,1)}, bf16[16,17,16,128]{3,2,1,0:T(8,128)(2,1)S(1)}, u32[]{:S(2)}, u32[]{:S(2)}) collective-permute-start(bf16[16,17,16,128]{3,2,1,0:T(8,128)(2,1)} %all-to-all-done.3.source), channel_id=1, source_target_pairs={{0,1},{1,0},{2,3},{3,2},{4,5},{5,4},{6,7},{7,6},{8,9},{9,8},{10,11... | collective-permute-start | bytes 3342344 | tf_op jit(solution)/shard_map/sums_1/ppermute | solution.py:553
  123.8 12.4 %collective-permute-start.19 = (bf16[97,16,128]{2,1,0:T(8,128)(2,1)}, bf16[97,16,128]{2,1,0:T(8,128)(2,1)}, u32[]{:S(2)}, u32[]{:S(2)}) collective-permute-start(bf16[97,16,128]{2,1,0:T(8,128)(2,1)} %get-tuple-element.181), channel_id=1, source_target_pairs={{0,2},{1,3},{2,4},{3,5},{4,6},{5,7},{6,0},{7,1},{8,10},{9,11},{10,... | collective-permute-start | bytes 1191944 | tf_op jit(solution)/shard_map/sums_1/ppermute | solution.py:550
  124.4 13.9 %collective-permute-start.20 = (bf16[97,16,128]{2,1,0:T(8,128)(2,1)}, bf16[97,16,128]{2,1,0:T(8,128)(2,1)}, u32[]{:S(2)}, u32[]{:S(2)}) collective-permute-start(bf16[97,16,128]{2,1,0:T(8,128)(2,1)} %get-tuple-element.182), channel_id=1, source_target_pairs={{0,4},{1,5},{2,6},{3,7},{4,0},{5,1},{6,2},{7,3},{8,12},{9,13},{10,... | collective-permute-start | bytes 1191944 | tf_op jit(solution)/shard_map/sums_1/ppermute | solution.py:550
  124.7 21.0 %collective-permute-start.21 = (bf16[97,16,128]{2,1,0:T(8,128)(2,1)}, bf16[97,16,128]{2,1,0:T(8,128)(2,1)}, u32[]{:S(2)}, u32[]{:S(2)}) collective-permute-start(bf16[97,16,128]{2,1,0:T(8,128)(2,1)} %get-tuple-element.183), channel_id=1, source_target_pairs={{0,6},{1,7},{2,0},{3,1},{4,2},{5,3},{6,4},{7,5},{8,14},{9,15},{10,... | collective-permute-start | bytes 1191944 | tf_op jit(solution)/shard_map/sums_1/ppermute | solution.py:550
  (5 other events, 21.7 us)

commit v15 on v13

--- a/solution.py
+++ b/solution.py
@@ -264,7 +264,7 @@
 
 
 def spread_more_kernel(places, source, lanes, total_in, weights_in, total, total_weights):
-    del total_in
+    total[...] = total_in[...]
     add_pieces(places, source, total)
     total_weights[...] = weights_in[...] + sum_weights(lanes, source)
 
@@ -276,7 +276,7 @@
 
 
 def spread_last_kernel(rows, places, source, lanes, total_in, weights_in, total, own_weights, out1, out2, out3):
-    del total_in
+    total[...] = total_in[...]
     add_pieces(places, source, total)
     weights = weights_in[...] + sum_weights(lanes, source)
     coarse = weights.astype(BF16)
@@ -338,7 +338,7 @@
 
 
 def finish_kernel(rows, numbers, begun, own_weights, in1, in2, in3, lanes, out, total):
-    del begun
+    total[...] = begun[...]
     weights = own_weights[:, 0:PAN_DEV]
     panel = lax.broadcasted_iota(jnp.int32, (PAN_DEV, LANE), 0)
     for d, arrived in enumerate((in1, in2, in3)):

time: 166 us -> 167 us (level)
  Pallas kernels: 31.1 us -> 32.8 us
  transfers between devices with their start and end apart: 20 -> 20, of which waited for: 9 -> 10; matrix products, arithmetic and copies ran while one was open for 6% -> 6% of each run, Pallas kernels for 13% -> 14%
where the time goes in v15:
time: 167 us; the launch traced here: 165 us
  waiting for transfers between devices  51.2 us (31%)
  starting transfers between devices  42.8 us (26%)
  Pallas kernels  32.8 us (20%)
  blocking collectives  21.9 us (13%)
  local copies, waits for them, and re-layouts  11.1 us (7%)
  other arithmetic  3.5 us (2%)
    all_to_all x4, starting transfers between devices, exchange(): return lax.all_to_all(x, axis, split_axis=0, concat_axis=0, tiled=True)  27.3 us
    ppermute x3, waiting for transfers between devices, sum_over_chips(): lax.ppermute(far[d - 1], 'cent', shift(d, 0))  25.5 us
    all_to_all x1, blocking collectives, exchange(): return lax.all_to_all(x, axis, split_axis=0, concat_axis=0, tiled=True)  21.9 us
    all_to_all x4, waiting for transfers between devices, exchange(): return lax.all_to_all(x, axis, split_axis=0, concat_axis=0, tiled=True)  16.1 us
    pallas_call x2, Pallas kernels, score(): pl.pallas_call(functools.partial(score_kernel, group), in_specs=[smem_spe...  12.2 us
    ppermute x7, starting transfers between devices, local(): lax.ppermute(x, 'cent', shift((n + 1) // 2, (n + 1) % 2))  8.59 us
    pallas_call x4, Pallas kernels, spread(): pl.pallas_call(kernel, in_specs=[smem_spec()] + [vmem_spec()] * (2 + len(...  8.04 us
    unnamed x9, local copies, waits for them, and re-layouts  6.47 us
  transfers between devices with their start and end apart: 20, of which 10 were waited for; matrix products, arithmetic and copies ran while one was open for 6% of the time, Pallas kernels for 14%

profile of v15, /device:TPU:24, one launch (start us, length us, event | category | flops | bytes accessed | tf_op | source)
XLA Modules:
  0.0 165.1 jit_solution(11744736459611397841)
XLA Ops:
  2.2 4.7 %all-to-all-start = ((bf16[8,5,16,128]{3,2,1,0:T(8,128)(2,1)}), bf16[8,5,16,128]{3,2,1,0:T(8,128)(2,1)S(1)}, u32[]{:S(2)}, u32[]{:S(2)}) async-start(bf16[8,5,16,128]{3,2,1,0:T(8,128)(2,1)} %requests.1), calls=%async_computation | async-start | bytes 327680 | tf_op jit(solution)/shard_map/requests/all_to_all | solution.py:423
  8.5 2.8 %all-to-all-done = bf16[8,5,16,128]{3,2,1,0:T(8,128)(2,1)S(1)} async-done(((bf16[8,5,16,128]{3,2,1,0:T(8,128)(2,1)}), bf16[8,5,16,128]{3,2,1,0:T(8,128)(2,1)S(1)}, u32[]{:S(2)}, u32[]{:S(2)}) %all-to-all-start) | async-done | bytes 163872 | tf_op jit(solution)/shard_map/requests/all_to_all | solution.py:423
  11.9 2.7 %gather_panels.2 = (bf16[128,1024]{1,0:T(8,128)(2,1)}, bf16[128,1024]{1,0:T(8,128)(2,1)}, bf16[128,1024]{1,0:T(8,128)(2,1)}, bf16[128,1024]{1,0:T(8,128)(2,1)}, ...) custom-call(s32[16]{0:T(128)} %sub.89.ids, s32[1]{0:T(128)} %bitcast.8.place, ...), custom_call_target="tpu_custom_call" | custom-call | bytes 3670016 | tf_op jit(solution)/shard_map/gather_panels/pallas_call | solution.py:135
  14.8 2.1 %collective-permute-start.7 = (bf16[128,1024]{1,0:T(8,128)(2,1)}, bf16[128,1024]{1,0:T(8,128)(2,1)S(1)}, u32[]{:S(2)}, u32[]{:S(2)}) collective-permute-start(bf16[128,1024]{1,0:T(8,128)(2,1)} %get-tuple-element.133), channel_id=1, source_target_pairs={{0,2},{1,3},{2,4},{3,5},{4,6},{5,7},{6,0},{7,1},{8,10},{9,11},{10,... | collective-permute-start | bytes 786440 | tf_op jit(solution)/shard_map/gather_panels/ppermute | solution.py:442
  22.5 7.4 %all-to-all-start.1 = ((s32[16,8,8,128]{3,2,1,0:T(8,128)}), s32[16,8,8,128]{3,2,1,0:T(8,128)}, u32[]{:S(2)}, u32[]{:S(2)}) async-start(s32[16,8,8,128]{3,2,1,0:T(8,128)} %broadcast_in_dim.81), calls=%async_computation.1 | async-start | bytes 1048576 | tf_op jit(solution)/shard_map/all_requests/all_to_all | solution.py:423
  31.9 2.8 %gather_panels.3 = (bf16[1,128,1024]{2,1,0:T(8,128)(2,1)}, bf16[2,128,1024]{2,1,0:T(8,128)(2,1)}, bf16[2,128,1024]{2,1,0:T(8,128)(2,1)}, bf16[2,128,1024]{2,1,0:T(8,128)(2,1)}) custom-call(s32[16]{0:T(128)} %sub.89.ids, s32[1]{0:T(128)} %bitcast.8.place, bf16[64,128,1024]{2,1,0:T(8,128)(2,1)} %bitcast.82), custom_call_target="tpu_custom_call" | custom-call | bytes 3670016 | tf_op jit(solution)/shard_map/gather_panels/pallas_call | solution.py:135
  37.7 2.6 %collective-permute-start.14 = (bf16[2,128,1024]{2,1,0:T(8,128)(2,1)}, bf16[2,128,1024]{2,1,0:T(8,128)(2,1)S(1)}, u32[]{:S(2)}, u32[]{:S(2)}) collective-permute-start(bf16[2,128,1024]{2,1,0:T(8,128)(2,1)} %get-tuple-element.143), channel_id=1, source_target_pairs={{0,4},{1,5},{2,6},{3,7},{4,0},{5,1},{6,2},{7,3},{8,12},{9,13},{10,... | collective-permute-start | bytes 1572872 | tf_op jit(solution)/shard_map/gather_panels/ppermute | solution.py:444
  40.5 4.2 %collective-permute-done.9.refs_3_ = bf16[128,1024]{1,0:T(8,128)(2,1)} collective-permute-done((bf16[128,1024]{1,0:T(8,128)(2,1)}, bf16[128,1024]{1,0:T(8,128)(2,1)}, u32[]{:S(2)}, u32[]{:S(2)}) %collective-permute-start.9) | collective-permute-done | bytes 262176 | tf_op jit(solution)/shard_map/gather_panels/ppermute | solution.py:442
  44.7 6.0 %score.2 = bf16[16,17,16,128]{3,2,1,0:T(8,128)(2,1)} custom-call(s32[8]{0:T(128)S(1)} %squeeze.93.owners, bf16[128,1024]{1,0:T(8,128)(2,1)S(1)} %collective-permute-done.6.refs_0_, bf16[128,1024]{1,0:T(8,128)(2,1)S(1)} %collective-permute-done.7.refs_1_, bf16[128,1024]{1,0:T(8,128)(2,1)} %collective-permute-done.8.refs_2_, ...), custom_call_target="tpu_custom_call" | custom-call | flops 2147483648 | bytes 5242880 | tf_op jit(solution)/shard_map/score/pallas_call | solution.py:223
  50.7 8.0 %all-to-all-start.2 = ((bf16[16,17,16,128]{3,2,1,0:T(8,128)(2,1)}), bf16[16,17,16,128]{3,2,1,0:T(8,128)(2,1)}, u32[]{:S(2)}, u32[]{:S(2)}) async-start(bf16[16,17,16,128]{3,2,1,0:T(8,128)(2,1)} %score.2), calls=%async_computation.2 | async-start | bytes 2228224 | tf_op jit(solution)/shard_map/split_pieces/all_to_all | solution.py:423
  62.9 3.8 %collective-permute-done.15.refs_2_ = bf16[2,128,1024]{2,1,0:T(8,128)(2,1)S(1)} collective-permute-done((bf16[2,128,1024]{2,1,0:T(8,128)(2,1)}, bf16[2,128,1024]{2,1,0:T(8,128)(2,1)S(1)}, u32[]{:S(2)}, u32[]{:S(2)}) %collective-permute-start.15) | collective-permute-done | bytes 524320 | tf_op jit(solution)/shard_map/gather_panels/ppermute | solution.py:444
  69.6 6.2 %score.3 = bf16[16,17,16,128]{3,2,1,0:T(8,128)(2,1)} custom-call(s32[8]{0:T(128)S(1)} %squeeze.83.owners, bf16[2,128,1024]{2,1,0:T(8,128)(2,1)S(1)} %collective-permute-done.13.refs_0_, bf16[2,128,1024]{2,1,0:T(8,128)(2,1)S(1)} %collective-permute-done.14.refs_1_, bf16[2,128,1024]{2,1,0:T(8,128)(2,1)S(1)} %collective-permute-done.15.refs_2_, ...), custom_call_target="tpu_custom_call" | custom-call | flops 2147483648 | bytes 5242880 | tf_op jit(solution)/shard_map/score/pallas_call | solution.py:223
  76.8 7.2 %all-to-all-start.3 = ((bf16[16,17,16,128]{3,2,1,0:T(8,128)(2,1)}), bf16[16,17,16,128]{3,2,1,0:T(8,128)(2,1)S(1)}, u32[]{:S(2)}, u32[]{:S(2)}) async-start(bf16[16,17,16,128]{3,2,1,0:T(8,128)(2,1)} %score.3), calls=%async_computation.3 | async-start | bytes 2228224 | tf_op jit(solution)/shard_map/split_pieces/all_to_all | solution.py:423
  83.9 2.3 %sum_over_chips.3 = (f32[668,16,128]{2,1,0:T(8,128)S(1)}, f32[16,256]{1,0:T(8,128)S(1)}) custom-call(s32[64]{0:T(128)S(1)} %squeeze.85.places, bf16[16,17,16,128]{3,2,1,0:T(8,128)(2,1)} %all-to-all-done.2.source, s32[16,128]{1,0:T(8,128)S(1)} %get-tuple-element.151.lanes), custom_call_target="tpu_custom_call" | custom-call | flops 2097152 | bytes 4194304 | tf_op jit(solution)/shard_map/split_pieces/sum_over_chips/pallas_call | solution.py:305
  88.2 2.4 %copy-done.1 = f32[668,16,128]{2,1,0:T(8,128)} copy-done((f32[668,16,128]{2,1,0:T(8,128)}, f32[668,16,128]{2,1,0:T(8,128)S(1)}, u32[]{:S(2)}) %copy-start.1) | copy-done | bytes 5472280
  90.6 12.4 %all-to-all-done.3.source = bf16[16,17,16,128]{3,2,1,0:T(8,128)(2,1)S(1)} async-done(((bf16[16,17,16,128]{3,2,1,0:T(8,128)(2,1)}), bf16[16,17,16,128]{3,2,1,0:T(8,128)(2,1)S(1)}, u32[]{:S(2)}, u32[]{:S(2)}) %all-to-all-start.3) | async-done | bytes 1114144 | tf_op jit(solution)/shard_map/split_pieces/all_to_all | solution.py:423
  103.7 2.5 %copy-done.2 = f32[668,16,128]{2,1,0:T(8,128)S(1)} copy-done((f32[668,16,128]{2,1,0:T(8,128)S(1)}, f32[668,16,128]{2,1,0:T(8,128)}, u32[]{:S(2)}) %copy-start.2) | copy-done | bytes 5472280
  107.9 34.1 %conditional.1 = (bf16[16,17,16,128]{3,2,1,0:T(8,128)(2,1)}) conditional(s32[]{:T(128)} %convert_element_type.42, (s32[]{:T(128)}, s32[64]{0:T(128)S(1)}, bf16[16,17,16,128]{3,2,1,0:T(8,128)(2,1)S(1)}, s32[16,128]{1,0:T(8,128)S(1)}, f32[668,16,128]{2,1,0:T(8,128)S(1)}, /*index=5*/f32[16,256]{1,0:T(8,128)S(1)}, bf16[64,128,1024]{2,1,0:T(8,128)(2,1)}, ...), branch_computations={%region_7.8_spmd, %region_8.9_spmd} | conditional | flops 16784704 | bytes 74684968 | solution.py:557
  107.9 2.2 %branch_0_fun.3 = (f32[668,16,128]{2,1,0:T(8,128)S(1)}, f32[16,128]{1,0:T(8,128)S(1)}, bf16[137,16,128]{2,1,0:T(8,128)(2,1)S(1)}, bf16[137,16,128]{2,1,0:T(8,128)(2,1)S(1)}, bf16[137,16,128]{2,1,0:T(8,128)(2,1)S(1)}) custom-call(s32[64]{0:T(128)S(1)} %get-tuple-element.27.places, ...), custom_call_target="tpu_custom_call", output_to_operand_aliasing={{0}: (3, {})} | custom-call | flops 2097152 | bytes 4194304 | tf_op jit(solution)/shard_map/sum_over_chips/cond/branch_0_fun/pallas_call | solution.py:305
  113.6 12.1 %collective-permute-done.in1 = bf16[137,16,128]{2,1,0:T(8,128)(2,1)S(1)} collective-permute-done((bf16[137,16,128]{2,1,0:T(8,128)(2,1)S(1)}, bf16[137,16,128]{2,1,0:T(8,128)(2,1)S(1)}, u32[]{:S(2)}, u32[]{:S(2)}) %collective-permute-start) | collective-permute-done | bytes 561184 | tf_op jit(solution)/shard_map/sum_over_chips/cond/branch_0_fun/ppermute | solution.py:542
  125.6 2.2 %collective-permute-done.1.in2 = bf16[137,16,128]{2,1,0:T(8,128)(2,1)S(1)} collective-permute-done((bf16[137,16,128]{2,1,0:T(8,128)(2,1)S(1)}, bf16[137,16,128]{2,1,0:T(8,128)(2,1)S(1)}, u32[]{:S(2)}, u32[]{:S(2)}) %collective-permute-start.1) | collective-permute-done | bytes 561184 | tf_op jit(solution)/shard_map/sum_over_chips/cond/branch_0_fun/ppermute | solution.py:542
  127.8 11.3 %collective-permute-done.2.in3 = bf16[137,16,128]{2,1,0:T(8,128)(2,1)S(1)} collective-permute-done((bf16[137,16,128]{2,1,0:T(8,128)(2,1)S(1)}, bf16[137,16,128]{2,1,0:T(8,128)(2,1)S(1)}, u32[]{:S(2)}, u32[]{:S(2)}) %collective-permute-start.2) | collective-permute-done | bytes 561184 | tf_op jit(solution)/shard_map/sum_over_chips/cond/branch_0_fun/ppermute | solution.py:542
  139.1 2.9 %branch_0_fun.5 = (bf16[16,17,16,128]{3,2,1,0:T(8,128)(2,1)}, f32[256,16,128]{2,1,0:T(8,128)S(1)}) custom-call(s32[105]{0:T(128)S(1)} %get-tuple-element.25.numbers, f32[256,16,128]{2,1,0:T(8,128)S(1)} %branch_0_fun.4.begun, f32[16,128]{1,0:T(8,128)S(1)} %get-tuple-element.52.own_weights, ...), custom_call_target="tpu_custom_call", output_to_operand_aliasing={{1}: (1, {})} | custom-call | flops 4194304 | bytes 6291456 | tf_op jit(solution)/shard_map/sum_over_chips/cond/branch_0_fun/pallas_call | solution.py:370
  142.0 21.9 %all_to_all.25.pieces = bf16[16,17,16,128]{3,2,1,0:T(8,128)(2,1)S(1)} all-to-all(bf16[16,17,16,128]{3,2,1,0:T(8,128)(2,1)} %get-tuple-element.207), channel_id=1, replica_groups=mesh['pts'=16,'cent'=8] {'pts'}, dimensions={0} | all-to-all | bytes 2228224 | tf_op jit(solution)/shard_map/place/all_to_all | solution.py:423
  (98 shorter events, 30.9 us)
Async XLA Ops:
  2.2 9.1 %all-to-all-start = ((bf16[8,5,16,128]{3,2,1,0:T(8,128)(2,1)}), bf16[8,5,16,128]{3,2,1,0:T(8,128)(2,1)S(1)}, u32[]{:S(2)}, u32[]{:S(2)}) async-start(bf16[8,5,16,128]{3,2,1,0:T(8,128)(2,1)} %requests.1), calls=%async_computation | async-start | bytes 327680 | tf_op jit(solution)/shard_map/requests/all_to_all | solution.py:423
  11.3 20.6 %copy-start.3 = (bf16[8,5,16,128]{3,2,1,0:T(8,128)(2,1)}, bf16[8,5,16,128]{3,2,1,0:T(8,128)(2,1)S(1)}, u32[]{:S(2)}) copy-start(bf16[8,5,16,128]{3,2,1,0:T(8,128)(2,1)S(1)} %all-to-all-done) | copy-start | bytes 491524
  14.6 5.3 %collective-permute-start.6 = (bf16[128,1024]{1,0:T(8,128)(2,1)}, bf16[128,1024]{1,0:T(8,128)(2,1)S(1)}, u32[]{:S(2)}, u32[]{:S(2)}) collective-permute-start(bf16[128,1024]{1,0:T(8,128)(2,1)} %get-tuple-element.127), channel_id=1, source_target_pairs={{0,1},{1,0},{2,3},{3,2},{4,5},{5,4},{6,7},{7,6},{8,9},{9,8},{10,11... | collective-permute-start | bytes 786440 | tf_op jit(solution)/shard_map/gather_panels/ppermute | solution.py:442
  14.8 15.1 %collective-permute-start.7 = (bf16[128,1024]{1,0:T(8,128)(2,1)}, bf16[128,1024]{1,0:T(8,128)(2,1)S(1)}, u32[]{:S(2)}, u32[]{:S(2)}) collective-permute-start(bf16[128,1024]{1,0:T(8,128)(2,1)} %get-tuple-element.133), channel_id=1, source_target_pairs={{0,2},{1,3},{2,4},{3,5},{4,6},{5,7},{6,0},{7,1},{8,10},{9,11},{10,... | collective-permute-start | bytes 786440 | tf_op jit(solution)/shard_map/gather_panels/ppermute | solution.py:442
  17.0 18.7 %collective-permute-start.10 = (bf16[128,1024]{1,0:T(8,128)(2,1)}, bf16[128,1024]{1,0:T(8,128)(2,1)S(1)}, u32[]{:S(2)}, u32[]{:S(2)}) collective-permute-start(bf16[128,1024]{1,0:T(8,128)(2,1)} %get-tuple-element.137), channel_id=1, source_target_pairs={{0,5},{1,4},{2,7},{3,6},{4,1},{5,0},{6,3},{7,2},{8,13},{9,12},{10,... | collective-permute-start | bytes 786440 | tf_op jit(solution)/shard_map/gather_panels/ppermute | solution.py:442
  17.6 20.1 %collective-permute-start.11 = (bf16[128,1024]{1,0:T(8,128)(2,1)}, bf16[128,1024]{1,0:T(8,128)(2,1)S(1)}, u32[]{:S(2)}, u32[]{:S(2)}) collective-permute-start(bf16[128,1024]{1,0:T(8,128)(2,1)} %get-tuple-element.138), channel_id=1, source_target_pairs={{0,6},{1,7},{2,0},{3,1},{4,2},{5,3},{6,4},{7,5},{8,14},{9,15},{10,... | collective-permute-start | bytes 786440 | tf_op jit(solution)/shard_map/gather_panels/ppermute | solution.py:442
  18.6 21.6 %collective-permute-start.12 = (bf16[128,1024]{1,0:T(8,128)(2,1)}, bf16[128,1024]{1,0:T(8,128)(2,1)S(1)}, u32[]{:S(2)}, u32[]{:S(2)}) collective-permute-start(bf16[128,1024]{1,0:T(8,128)(2,1)} %get-tuple-element.139), channel_id=1, source_target_pairs={{0,7},{1,6},{2,1},{3,0},{4,3},{5,2},{6,5},{7,4},{8,15},{9,14},{10,... | collective-permute-start | bytes 786440 | tf_op jit(solution)/shard_map/gather_panels/ppermute | solution.py:442
  19.9 20.6 %collective-permute-start.8 = (bf16[128,1024]{1,0:T(8,128)(2,1)}, bf16[128,1024]{1,0:T(8,128)(2,1)}, u32[]{:S(2)}, u32[]{:S(2)}) collective-permute-start(bf16[128,1024]{1,0:T(8,128)(2,1)} %get-tuple-element.135), channel_id=1, source_target_pairs={{0,3},{1,2},{2,5},{3,4},{4,7},{5,6},{6,1},{7,0},{8,11},{9,10},{10,... | collective-permute-start | bytes 786440 | tf_op jit(solution)/shard_map/gather_panels/ppermute | solution.py:442
  22.5 28.2 %all-to-all-start.1 = ((s32[16,8,8,128]{3,2,1,0:T(8,128)}), s32[16,8,8,128]{3,2,1,0:T(8,128)}, u32[]{:S(2)}, u32[]{:S(2)}) async-start(s32[16,8,8,128]{3,2,1,0:T(8,128)} %broadcast_in_dim.81), calls=%async_computation.1 | async-start | bytes 1048576 | tf_op jit(solution)/shard_map/all_requests/all_to_all | solution.py:423
  30.0 14.7 %collective-permute-start.9 = (bf16[128,1024]{1,0:T(8,128)(2,1)}, bf16[128,1024]{1,0:T(8,128)(2,1)}, u32[]{:S(2)}, u32[]{:S(2)}) collective-permute-start(bf16[128,1024]{1,0:T(8,128)(2,1)} %get-tuple-element.136), channel_id=1, source_target_pairs={{0,4},{1,5},{2,6},{3,7},{4,0},{5,1},{6,2},{7,3},{8,12},{9,13},{10,... | collective-permute-start | bytes 786440 | tf_op jit(solution)/shard_map/gather_panels/ppermute | solution.py:442
  31.9 2.8 %slice-start = ((bf16[8,5,16,128]{3,2,1,0:T(8,128)(2,1)}), bf16[8,4,16,128]{3,2,1,0:T(8,128)(2,1)S(1)}, s32[]{:S(2)}) async-start(bf16[8,5,16,128]{3,2,1,0:T(8,128)(2,1)} %copy-done.3), calls=%async_computation.5 | async-start | bytes 262144 | tf_op jit(solution)/shard_map/loads/slice | solution.py:520
  35.7 27.2 %collective-permute-start.13 = (bf16[2,128,1024]{2,1,0:T(8,128)(2,1)}, bf16[2,128,1024]{2,1,0:T(8,128)(2,1)S(1)}, u32[]{:S(2)}, u32[]{:S(2)}) collective-permute-start(bf16[2,128,1024]{2,1,0:T(8,128)(2,1)} %get-tuple-element.142), channel_id=1, source_target_pairs={{0,2},{1,3},{2,4},{3,5},{4,6},{5,7},{6,0},{7,1},{8,10},{9,11},{10,... | collective-permute-start | bytes 1572872 | tf_op jit(solution)/shard_map/gather_panels/ppermute | solution.py:444
  37.7 25.2 %collective-permute-start.14 = (bf16[2,128,1024]{2,1,0:T(8,128)(2,1)}, bf16[2,128,1024]{2,1,0:T(8,128)(2,1)S(1)}, u32[]{:S(2)}, u32[]{:S(2)}) collective-permute-start(bf16[2,128,1024]{2,1,0:T(8,128)(2,1)} %get-tuple-element.143), channel_id=1, source_target_pairs={{0,4},{1,5},{2,6},{3,7},{4,0},{5,1},{6,2},{7,3},{8,12},{9,13},{10,... | collective-permute-start | bytes 1572872 | tf_op jit(solution)/shard_map/gather_panels/ppermute | solution.py:444
  40.3 26.4 %collective-permute-start.15 = (bf16[2,128,1024]{2,1,0:T(8,128)(2,1)}, bf16[2,128,1024]{2,1,0:T(8,128)(2,1)S(1)}, u32[]{:S(2)}, u32[]{:S(2)}) collective-permute-start(bf16[2,128,1024]{2,1,0:T(8,128)(2,1)} %get-tuple-element.144), channel_id=1, source_target_pairs={{0,6},{1,7},{2,0},{3,1},{4,2},{5,3},{6,4},{7,5},{8,14},{9,15},{10,... | collective-permute-start | bytes 1572872 | tf_op jit(solution)/shard_map/gather_panels/ppermute | solution.py:444
  50.7 16.0 %copy-start.4 = (bf16[1,128,1024]{2,1,0:T(8,128)(2,1)S(1)}, bf16[1,128,1024]{2,1,0:T(8,128)(2,1)}, u32[]{:S(2)}) copy-start(bf16[1,128,1024]{2,1,0:T(8,128)(2,1)} %get-tuple-element.145) | copy-start | bytes 786436
  50.7 26.0 %all-to-all-start.2 = ((bf16[16,17,16,128]{3,2,1,0:T(8,128)(2,1)}), bf16[16,17,16,128]{3,2,1,0:T(8,128)(2,1)}, u32[]{:S(2)}, u32[]{:S(2)}) async-start(bf16[16,17,16,128]{3,2,1,0:T(8,128)(2,1)} %score.2), calls=%async_computation.2 | async-start | bytes 2228224 | tf_op jit(solution)/shard_map/split_pieces/all_to_all | solution.py:423
  66.9 2.7 %collective-permute-start.16 = (bf16[4,128,1024]{2,1,0:T(8,128)(2,1)S(1)}, bf16[4,128,1024]{2,1,0:T(8,128)(2,1)S(1)}, u32[]{:S(2)}, u32[]{:S(2)}) collective-permute-start(bf16[4,128,1024]{2,1,0:T(8,128)(2,1)S(1)} %pad_maximum_fusion), channel_id=1, source_target_pairs={{0,1},{1,0},{2,3},{3,2},{4,5},{5,4},{6,7},{7,6},{8,9},{9,8},{10,11... | collective-permute-start | bytes 3145736 | tf_op jit(solution)/shard_map/gather_panels/ppermute | solution.py:446
  76.7 9.5 %collective-permute-start.17 = (bf16[16,17,16,128]{3,2,1,0:T(8,128)(2,1)}, bf16[16,17,16,128]{3,2,1,0:T(8,128)(2,1)S(1)}, u32[]{:S(2)}, u32[]{:S(2)}) collective-permute-start(bf16[16,17,16,128]{3,2,1,0:T(8,128)(2,1)} %all-to-all-done.2.source), channel_id=1, source_target_pairs={{0,1},{1,0},{2,3},{3,2},{4,5},{5,4},{6,7},{7,6},{8,9},{9,8},{10,11... | collective-permute-start | bytes 3342344 | tf_op jit(solution)/shard_map/split_pieces/sum_over_chips/ppermute | solution.py:534
  76.8 26.2 %all-to-all-start.3 = ((bf16[16,17,16,128]{3,2,1,0:T(8,128)(2,1)}), bf16[16,17,16,128]{3,2,1,0:T(8,128)(2,1)S(1)}, u32[]{:S(2)}, u32[]{:S(2)}) async-start(bf16[16,17,16,128]{3,2,1,0:T(8,128)(2,1)} %score.3), calls=%async_computation.3 | async-start | bytes 2228224 | tf_op jit(solution)/shard_map/split_pieces/all_to_all | solution.py:423
  103.0 4.9 %collective-permute-start.18 = (bf16[16,17,16,128]{3,2,1,0:T(8,128)(2,1)S(1)}, bf16[16,17,16,128]{3,2,1,0:T(8,128)(2,1)S(1)}, u32[]{:S(2)}, u32[]{:S(2)}) collective-permute-start(bf16[16,17,16,128]{3,2,1,0:T(8,128)(2,1)S(1)} %all-to-all-done.3.source), channel_id=1, source_target_pairs={{0,1},{1,0},{2,3},{3,2},{4,5},{5,4},{6,7},{7,6},{8,9},{9,8},{10,11... | collective-permute-start | bytes 3342344 | tf_op jit(solution)/shard_map/split_pieces/ppermute | solution.py:538
  103.7 2.6 %copy-start.2 = (f32[668,16,128]{2,1,0:T(8,128)S(1)}, f32[668,16,128]{2,1,0:T(8,128)}, u32[]{:S(2)}) copy-start(f32[668,16,128]{2,1,0:T(8,128)} %copy-done.1) | copy-start | bytes 16416772
  110.1 15.6 %collective-permute-start = (bf16[137,16,128]{2,1,0:T(8,128)(2,1)S(1)}, bf16[137,16,128]{2,1,0:T(8,128)(2,1)S(1)}, u32[]{:S(2)}, u32[]{:S(2)}) collective-permute-start(bf16[137,16,128]{2,1,0:T(8,128)(2,1)S(1)} %get-tuple-element.53), channel_id=1, source_target_pairs={{0,2},{1,3},{2,4},{3,5},{4,6},{5,7},{6,0},{7,1},{8,10},{9,11},{10,... | collective-permute-start | bytes 1683464 | tf_op jit(solution)/shard_map/sum_over_chips/cond/branch_0_fun/ppermute | solution.py:542
  110.7 17.1 %collective-permute-start.1 = (bf16[137,16,128]{2,1,0:T(8,128)(2,1)S(1)}, bf16[137,16,128]{2,1,0:T(8,128)(2,1)S(1)}, u32[]{:S(2)}, u32[]{:S(2)}) collective-permute-start(bf16[137,16,128]{2,1,0:T(8,128)(2,1)S(1)} %get-tuple-element.54), channel_id=1, source_target_pairs={{0,4},{1,5},{2,6},{3,7},{4,0},{5,1},{6,2},{7,3},{8,12},{9,13},{10,... | collective-permute-start | bytes 1683464 | tf_op jit(solution)/shard_map/sum_over_chips/cond/branch_0_fun/ppermute | solution.py:542
  111.1 28.0 %collective-permute-start.2 = (bf16[137,16,128]{2,1,0:T(8,128)(2,1)S(1)}, bf16[137,16,128]{2,1,0:T(8,128)(2,1)S(1)}, u32[]{:S(2)}, u32[]{:S(2)}) collective-permute-start(bf16[137,16,128]{2,1,0:T(8,128)(2,1)S(1)} %get-tuple-element.55), channel_id=1, source_target_pairs={{0,6},{1,7},{2,0},{3,1},{4,2},{5,3},{6,4},{7,5},{8,14},{9,15},{10,... | collective-permute-start | bytes 1683464 | tf_op jit(solution)/shard_map/sum_over_chips/cond/branch_0_fun/ppermute | solution.py:542
  (1 other events, 2.4 us)
